TPU v7x, 32 devices: a whole 2x2x4 slice. The times are simulated.
32 devices in a mesh: section: 2 (over core), dp: 4 (over z), mp: 4 (over y, x).
Axes of the slice: x: 2, y: 2, z: 4, core: 2. Of those that a mesh axis runs over, the one named last changes fastest.
Arguments:
- inputs: bfloat16 [8192, 768], P(('dp', 'mp')), may hold values from -6 to 6
- cotangent: bfloat16 [8192, 768], P(('dp', 'mp')), may hold values from -6 to 6
- doc_ids: int32 [8192], P('dp'), may hold values from -1 to 3, as said below
- norm_gain: float32 [2, 768], P('section'), may hold values from 0.25 to 1.75
- norm_bias: float32 [2, 768], P('section'), may hold values from -1.5 to 1.5
- w_query: bfloat16 [2, 768, 768], P('section', 'dp', 'mp'), may hold values from -0.21875 to 0.21875
- w_key: bfloat16 [2, 768, 768], P('section', 'dp', 'mp'), may hold values from -0.21875 to 0.21875
- w_value: bfloat16 [2, 768, 768], P('section', 'dp', 'mp'), may hold values from -0.21875 to 0.21875
- inner_gain: float32 [2, 768], P('section', 'mp'), may hold values from 0.25 to 1.75
- inner_bias: float32 [2, 768], P('section', 'mp'), may hold values from -1.5 to 1.5
- w_output: bfloat16 [2, 768, 768], P('section', 'mp', 'dp'), may hold values from -0.21875 to 0.21875
- feed_gain: float32 [2, 768], P('section'), may hold values from 0.25 to 1.75
- feed_bias: float32 [2, 768], P('section'), may hold values from -1.5 to 1.5
- w_up: bfloat16 [2, 768, 3072], P('section', 'dp', 'mp'), may hold values from -0.21875 to 0.21875
- middle_gain: float32 [2, 3072], P('section', 'mp'), may hold values from 0.25 to 1.75
- middle_bias: float32 [2, 3072], P('section', 'mp'), may hold values from -1.5 to 1.5
- w_down: bfloat16 [2, 3072, 768], P('section', 'mp', 'dp'), may hold values from -0.109375 to 0.109375
Outputs:
- layer_outputs: bfloat16 [2, 8192, 768], P('section', ('dp', 'mp'))
- input_grads: bfloat16 [2, 8192, 768], P('section', ('dp', 'mp'))
- grad_norm_gain: float32 [2, 768], P('section', ('dp', 'mp'))
- grad_norm_bias: float32 [2, 768], P('section', ('dp', 'mp'))
- grad_query: float32 [2, 768, 768], P('section', 'dp', 'mp')
- grad_key: float32 [2, 768, 768], P('section', 'dp', 'mp')
- grad_value: float32 [2, 768, 768], P('section', 'dp', 'mp')
- grad_inner_gain: float32 [2, 768], P('section', ('mp', 'dp'))
- grad_inner_bias: float32 [2, 768], P('section', ('mp', 'dp'))
- grad_output: float32 [2, 768, 768], P('section', 'mp', 'dp')
- grad_feed_gain: float32 [2, 768], P('section', ('dp', 'mp'))
- grad_feed_bias: float32 [2, 768], P('section', ('dp', 'mp'))
- grad_up: float32 [2, 768, 3072], P('section', 'dp', 'mp')
- grad_middle_gain: float32 [2, 3072], P('section', ('mp', 'dp'))
- grad_middle_bias: float32 [2, 3072], P('section', ('mp', 'dp'))
- grad_down: float32 [2, 3072, 768], P('section', 'mp', 'dp')
Inputs may be any that keep to these rules, and one draw needn't show every extreme that they name: `doc_ids`: along the 1024 rows of each micro-batch document numbers never fall; padding rows (-1) come last; each micro-batch holds documents 0 to 3 and some padding, and document 2 starts within the first 256 rows and ends within the last 256 rows.
All inputs are finite; a program needn't handle non-finite values.
Results may differ from a plain program's by a relative error of at most 0.028.
Values may be sent and summed in bfloat16 or wider, within the bound.
No kernel may reach another device: no remote copies, remote signals or barrier semaphores. Data moves between devices by JAX's collectives and lax.ppermute only.
A program may use at most 192 MiB of HBM per device.

v0:
```python
from functools import partial

import jax
import jax.numpy as jnp
from jax import lax
from jax.sharding import PartitionSpec as P

D = 768
HEAD_DIM = 64
FF = 3072
MICRO = 2


EPS = 1e-05


def from_behind(x, axis, by):
    count = lax.axis_size(axis)
    pairs = [(i, i + by) for i in range(count) if 0 <= i + by < count]
    return lax.ppermute(x, axis, pairs)


def layer_norm(values, gain_vec, bias_vec):
    row_mean = jnp.mean(values, axis=-1, keepdims=True)
    spread = jnp.mean(values * values, axis=-1, keepdims=True) - row_mean * row_mean
    return (values - row_mean) * lax.rsqrt(spread + EPS) * gain_vec + bias_vec


def dot_plain(first_mat, second_mat):
    return jnp.dot(first_mat, second_mat, preferred_element_type=jnp.float32)


def dot_second_turned(first_mat, second_mat):
    return lax.dot_general(
        first_mat, second_mat, (((1,), (1,)), ((), ())), preferred_element_type=jnp.float32
    )


def dot_first_turned(first_mat, second_mat):
    return lax.dot_general(
        first_mat, second_mat, (((0,), (0,)), ((), ())), preferred_element_type=jnp.float32
    )


def spread_rows(row_block):
    return lax.all_gather(row_block, "mp", axis=0, tiled=True)


def settle_rows(partial_rows):
    return lax.psum_scatter(
        partial_rows.astype(jnp.bfloat16), "mp", scatter_dimension=0, tiled=True
    ).astype(jnp.float32)


def row_totals(total_one, total_two):
    return lax.psum((total_one, total_two), "mp")


def split_norm(values, gain_vec, bias_vec, feature_count):
    total_one, total_two = row_totals(jnp.sum(values, axis=-1), jnp.sum(values * values, axis=-1))
    row_mean = total_one[:, None] / feature_count
    spread = total_two[:, None] / feature_count - row_mean * row_mean
    scaled = lax.rsqrt(spread + EPS)
    normal = (values - row_mean) * scaled
    return (normal * gain_vec + bias_vec, normal, scaled)


def split_norm_back(upstream, normal, scaled, gain_vec, feature_count):
    inner_grad = upstream * gain_vec
    total_one, total_two = row_totals(
        jnp.sum(inner_grad, axis=-1), jnp.sum(inner_grad * normal, axis=-1)
    )
    back_grad = scaled * (
        inner_grad
        - total_one[:, None] / feature_count
        - normal * total_two[:, None] / feature_count
    )
    return (back_grad, jnp.sum(upstream * normal, axis=0), jnp.sum(upstream, axis=0))


def masked_scores(query_block, key_rows, label_block, key_labels, score_scale):
    scores = (
        jnp.einsum("qhd,khd->hqk", query_block, key_rows, preferred_element_type=jnp.float32)
        * score_scale
    )
    return jnp.where((label_block[:, None] == key_labels[None, :])[None], scores, -1e30)


def attend(query, key_rows, value_rows, query_labels, key_labels, score_scale):
    row_count, head_count, head_size = query.shape
    block_len = min(512, row_count)

    def one_block(row_start):
        query_block = lax.dynamic_slice_in_dim(query, row_start, block_len, 0)
        label_block = lax.dynamic_slice_in_dim(query_labels, row_start, block_len, 0)
        scores = masked_scores(query_block, key_rows, label_block, key_labels, score_scale)
        row_peak = jnp.max(scores, axis=-1, keepdims=True)
        exp_terms = jnp.exp(scores - row_peak)
        row_total = jnp.sum(exp_terms, axis=-1, keepdims=True)
        prob_block = (exp_terms / row_total).astype(jnp.bfloat16)
        out_block = jnp.einsum(
            "hqk,khd->qhd", prob_block, value_rows, preferred_element_type=jnp.float32
        )
        return (out_block, row_peak[..., 0] + jnp.log(row_total[..., 0]))

    row_starts = jnp.arange(row_count // block_len, dtype=jnp.int32) * block_len
    out_blocks, logsum = lax.map(one_block, row_starts)
    return (out_blocks.reshape(row_count, head_count * head_size), logsum)


def attend_back(
    query, key_rows, value_rows, query_labels, key_labels, logsum, grad_out, score_scale
):
    row_count, head_count, head_size = query.shape
    key_count = key_rows.shape[0]
    block_len = min(512, row_count)

    def one_block(carry, block_index):
        key_grad, value_grad = carry
        row_start = block_index * block_len
        query_block = lax.dynamic_slice_in_dim(query, row_start, block_len, 0)
        label_block = lax.dynamic_slice_in_dim(query_labels, row_start, block_len, 0)
        grad_block = lax.dynamic_slice_in_dim(grad_out, row_start, block_len, 0)
        scores = masked_scores(query_block, key_rows, label_block, key_labels, score_scale)
        prob_block = jnp.exp(scores - logsum[block_index][..., None])
        prob_grad = jnp.einsum(
            "qhd,khd->hqk", grad_block, value_rows, preferred_element_type=jnp.float32
        )
        row_delta = jnp.sum(prob_block * prob_grad, axis=-1, keepdims=True)
        score_grad = (prob_block * (prob_grad - row_delta)).astype(jnp.bfloat16)
        query_grad = (
            jnp.einsum("hqk,khd->qhd", score_grad, key_rows, preferred_element_type=jnp.float32)
            * score_scale
        )
        key_grad = (
            key_grad
            + jnp.einsum(
                "hqk,qhd->khd", score_grad, query_block, preferred_element_type=jnp.float32
            )
            * score_scale
        )
        value_grad = value_grad + jnp.einsum(
            "hqk,qhd->khd",
            prob_block.astype(jnp.bfloat16),
            grad_block,
            preferred_element_type=jnp.float32,
        )
        return ((key_grad, value_grad), query_grad)

    zero_grad = jnp.zeros(key_rows.shape, jnp.float32)
    (key_grad, value_grad), query_grad = lax.scan(
        one_block, (zero_grad, zero_grad), jnp.arange(row_count // block_len, dtype=jnp.int32)
    )
    return (
        query_grad.reshape(row_count, head_count * head_size),
        key_grad.reshape(key_count, head_count * head_size),
        value_grad.reshape(key_count, head_count * head_size),
    )


def layer_forward(layer_input, labels, row_mask, matrices, small_params):
    query_mat, key_mat, value_mat, output_mat, up_mat, down_mat = matrices
    (
        first_gain,
        first_bias,
        inner_gain,
        inner_bias,
        second_gain,
        second_bias,
        middle_gain,
        middle_bias,
    ) = small_params
    head_rows = spread_rows(layer_norm(layer_input, first_gain, first_bias).astype(jnp.bfloat16))
    row_count = head_rows.shape[0]
    head_count = query_mat.shape[1] // HEAD_DIM
    score_scale = HEAD_DIM ** (-0.5)
    query = (
        dot_plain(head_rows, query_mat)
        .astype(jnp.bfloat16)
        .reshape(row_count, head_count, HEAD_DIM)
    )
    key_rows = (
        dot_plain(head_rows, key_mat).astype(jnp.bfloat16).reshape(row_count, head_count, HEAD_DIM)
    )
    value_rows = (
        dot_plain(head_rows, value_mat)
        .astype(jnp.bfloat16)
        .reshape(row_count, head_count, HEAD_DIM)
    )
    mixed, logsum = attend(query, key_rows, value_rows, labels, labels, score_scale)
    inner_out, mixed_normal, mixed_scaled = split_norm(mixed, inner_gain, inner_bias, D)
    inner_rows = inner_out.astype(jnp.bfloat16)
    mid_input = layer_input + settle_rows(dot_plain(inner_rows, output_mat))
    feed_rows = spread_rows(layer_norm(mid_input, second_gain, second_bias).astype(jnp.bfloat16))
    pre_act = dot_plain(feed_rows, up_mat)
    middle_out, middle_normal, middle_scaled = split_norm(
        jax.nn.gelu(pre_act, approximate=False), middle_gain, middle_bias, FF
    )
    middle_rows = middle_out.astype(jnp.bfloat16)
    result = mid_input + settle_rows(dot_plain(middle_rows, down_mat))
    layer_output = (row_mask * result).astype(jnp.bfloat16)
    kept_state = (
        layer_input,
        head_rows,
        query,
        key_rows,
        value_rows,
        logsum,
        mixed_normal,
        mixed_scaled,
        inner_rows,
        mid_input,
        feed_rows,
        pre_act,
        middle_normal,
        middle_scaled,
        middle_rows,
    )
    return (layer_output, kept_state)


def layer_backward(upstream, kept_state, labels, row_mask, matrices, small_params):
    query_mat, key_mat, value_mat, output_mat, up_mat, down_mat = matrices
    (
        first_gain,
        first_bias,
        inner_gain,
        inner_bias,
        second_gain,
        second_bias,
        middle_gain,
        middle_bias,
    ) = small_params
    (
        layer_input,
        head_rows,
        query,
        key_rows,
        value_rows,
        logsum,
        mixed_normal,
        mixed_scaled,
        inner_rows,
        mid_input,
        feed_rows,
        pre_act,
        middle_normal,
        middle_scaled,
        middle_rows,
    ) = kept_state
    score_scale = HEAD_DIM ** (-0.5)
    result_grad = row_mask * upstream
    feed_grad_rows = spread_rows(result_grad.astype(jnp.bfloat16))
    middle_grad = dot_second_turned(feed_grad_rows, down_mat)
    grad_down = dot_first_turned(middle_rows, feed_grad_rows)
    act_grad, grad_middle_gain, grad_middle_bias = split_norm_back(
        middle_grad, middle_normal, middle_scaled, middle_gain, FF
    )
    gelu_out, gelu_back = jax.vjp(partial(jax.nn.gelu, approximate=False), pre_act)
    pre_grad = gelu_back(act_grad)[0].astype(jnp.bfloat16)
    grad_up = dot_first_turned(feed_rows, pre_grad)
    second_in_grad = settle_rows(dot_second_turned(pre_grad, up_mat))
    norm_out, second_back = jax.vjp(layer_norm, mid_input, second_gain, second_bias)
    mid_back, grad_second_gain, grad_second_bias = second_back(second_in_grad)
    mid_grad = result_grad + mid_back
    branch_grad_rows = spread_rows(mid_grad.astype(jnp.bfloat16))
    inner_grad = dot_second_turned(branch_grad_rows, output_mat)
    grad_output = dot_first_turned(inner_rows, branch_grad_rows)
    mixed_grad, grad_inner_gain, grad_inner_bias = split_norm_back(
        inner_grad, mixed_normal, mixed_scaled, inner_gain, D
    )
    mixed_grad = mixed_grad.astype(jnp.bfloat16).reshape(query.shape)
    query_full, key_full, value_full = attend_back(
        query, key_rows, value_rows, labels, labels, logsum, mixed_grad, score_scale
    )
    query_grad = query_full.astype(jnp.bfloat16)
    key_grad = key_full.astype(jnp.bfloat16)
    value_grad = value_full.astype(jnp.bfloat16)
    grad_query = dot_first_turned(head_rows, query_grad)
    grad_key = dot_first_turned(head_rows, key_grad)
    grad_value = dot_first_turned(head_rows, value_grad)
    head_grad = settle_rows(
        dot_second_turned(query_grad, query_mat)
        + dot_second_turned(key_grad, key_mat)
        + dot_second_turned(value_grad, value_mat)
    )
    first_out, first_back = jax.vjp(layer_norm, layer_input, first_gain, first_bias)
    input_back, grad_first_gain, grad_first_bias = first_back(head_grad)
    grads = (
        grad_first_gain,
        grad_first_bias,
        grad_query,
        grad_key,
        grad_value,
        grad_inner_gain,
        grad_inner_bias,
        grad_output,
        grad_second_gain,
        grad_second_bias,
        grad_up,
        grad_middle_gain,
        grad_middle_bias,
        grad_down,
    )
    return (mid_grad + input_back, grads)


def on_device(
    inputs,
    cotangent,
    doc_ids,
    norm_gain,
    norm_bias,
    w_query,
    w_key,
    w_value,
    inner_gain,
    inner_bias,
    w_output,
    feed_gain,
    feed_bias,
    w_up,
    middle_gain,
    middle_bias,
    w_down,
):
    section_first = lax.axis_index("section") == 0
    lane_index = lax.axis_index("mp")
    lane_count = lax.axis_size("mp")
    slice_len = inputs.shape[0] // MICRO
    row_count = lane_count * slice_len
    label_grid = doc_ids.reshape(lane_count, MICRO, slice_len)
    small_params = (
        norm_gain[0],
        norm_bias[0],
        inner_gain[0],
        inner_bias[0],
        feed_gain[0],
        feed_bias[0],
        middle_gain[0],
        middle_bias[0],
    )

    def fetch_matrices():
        matrices = (
            lax.all_gather(w_query[0], "dp", axis=0, tiled=True),
            lax.all_gather(w_key[0], "dp", axis=0, tiled=True),
            lax.all_gather(w_value[0], "dp", axis=0, tiled=True),
            lax.all_gather(w_output[0], "dp", axis=1, tiled=True),
            lax.all_gather(w_up[0], "dp", axis=0, tiled=True),
            lax.all_gather(w_down[0], "dp", axis=1, tiled=True),
        )
        return (matrices, small_params)

    def labels_of(micro_index):
        return label_grid[:, micro_index].reshape(row_count)

    def rows_of(array, micro_index):
        return array[micro_index * slice_len : (micro_index + 1) * slice_len]

    def pick(lower_tree, upper_tree):
        return jnp.where(section_first, lower_tree, upper_tree)

    def mask_of(labels):
        own_labels = lax.dynamic_slice_in_dim(labels, lane_index * slice_len, slice_len)
        return (own_labels >= 0).astype(jnp.float32)[:, None]

    received = jnp.zeros((slice_len, inputs.shape[1]), jnp.bfloat16)
    tick_outputs = []
    tick_inputs = []
    tick_states = []
    for tick_index in range(MICRO + 1):
        lower_micro = min(tick_index, MICRO - 1)
        upper_micro = max(tick_index - 1, 0)
        layer_input = jnp.where(section_first, rows_of(inputs, lower_micro), received)
        labels = jnp.where(section_first, labels_of(lower_micro), labels_of(upper_micro))
        matrices, params_now = fetch_matrices()
        layer_output, kept_state = layer_forward(
            layer_input.astype(jnp.float32), labels, mask_of(labels), matrices, params_now
        )
        tick_outputs.append(layer_output)
        tick_inputs.append(layer_input)
        tick_states.append(kept_state)
        if tick_index < MICRO:
            received = from_behind(layer_output, "section", 1)
    section_outputs = [
        pick(tick_outputs[micro_index], tick_outputs[micro_index + 1])
        for micro_index in range(MICRO)
    ]
    section_inputs = [
        pick(tick_inputs[micro_index], tick_inputs[micro_index + 1]) for micro_index in range(MICRO)
    ]
    received_grad = jnp.zeros((slice_len, inputs.shape[1]), jnp.bfloat16)
    tick_grads = []
    accum = None
    for tick_index in range(MICRO + 1):
        lower_micro = max(tick_index - 1, 0)
        upper_micro = min(tick_index, MICRO - 1)
        labels = jnp.where(section_first, labels_of(lower_micro), labels_of(upper_micro))
        row_mask = mask_of(labels)
        layer_input = pick(section_inputs[lower_micro], section_inputs[upper_micro])
        upstream = jnp.where(
            section_first,
            received_grad.astype(jnp.float32),
            rows_of(cotangent, upper_micro).astype(jnp.float32),
        )
        matrices, params_now = fetch_matrices()
        unused_output, kept_state = layer_forward(
            layer_input.astype(jnp.float32), labels, row_mask, matrices, params_now
        )
        input_grad, grads = layer_backward(
            upstream, kept_state, labels, row_mask, matrices, params_now
        )
        tick_weight = jnp.where(section_first, float(tick_index >= 1), float(tick_index < MICRO))
        grads = jax.tree.map(lambda grad_leaf: tick_weight * grad_leaf, grads)
        if tick_index == 0:
            accum = grads
        else:
            accum = jax.tree.map(lambda total_old, total_new: total_old + total_new, accum, grads)
        grad_rows = input_grad.astype(jnp.bfloat16)
        tick_grads.append(grad_rows)
        if tick_index < MICRO:
            received_grad = from_behind(grad_rows, "section", -1)
    section_grads = [
        pick(tick_grads[micro_index + 1], tick_grads[micro_index]) for micro_index in range(MICRO)
    ]
    (
        grad_first_gain,
        grad_first_bias,
        grad_query,
        grad_key,
        grad_value,
        grad_inner_gain,
        grad_inner_bias,
        grad_output,
        grad_second_gain,
        grad_second_bias,
        grad_up,
        grad_middle_gain,
        grad_middle_bias,
        grad_down,
    ) = accum
    summed = (
        lax.psum_scatter(
            grad_query.astype(jnp.bfloat16), "dp", scatter_dimension=0, tiled=True
        ).astype(jnp.float32),
        lax.psum_scatter(
            grad_key.astype(jnp.bfloat16), "dp", scatter_dimension=0, tiled=True
        ).astype(jnp.float32),
        lax.psum_scatter(
            grad_value.astype(jnp.bfloat16), "dp", scatter_dimension=0, tiled=True
        ).astype(jnp.float32),
        lax.psum_scatter(
            grad_output.astype(jnp.bfloat16), "dp", scatter_dimension=1, tiled=True
        ).astype(jnp.float32),
        lax.psum_scatter(
            grad_up.astype(jnp.bfloat16), "dp", scatter_dimension=0, tiled=True
        ).astype(jnp.float32),
        lax.psum_scatter(
            grad_down.astype(jnp.bfloat16), "dp", scatter_dimension=1, tiled=True
        ).astype(jnp.float32),
        lax.psum_scatter(
            grad_inner_gain.astype(jnp.bfloat16), "dp", scatter_dimension=0, tiled=True
        ).astype(jnp.float32),
        lax.psum_scatter(
            grad_inner_bias.astype(jnp.bfloat16), "dp", scatter_dimension=0, tiled=True
        ).astype(jnp.float32),
        lax.psum_scatter(
            grad_middle_gain.astype(jnp.bfloat16), "dp", scatter_dimension=0, tiled=True
        ).astype(jnp.float32),
        lax.psum_scatter(
            grad_middle_bias.astype(jnp.bfloat16), "dp", scatter_dimension=0, tiled=True
        ).astype(jnp.float32),
    )
    norm_sums = (
        lax.psum_scatter(grad_first_gain, ("dp", "mp"), scatter_dimension=0, tiled=True),
        lax.psum_scatter(grad_first_bias, ("dp", "mp"), scatter_dimension=0, tiled=True),
        lax.psum_scatter(grad_second_gain, ("dp", "mp"), scatter_dimension=0, tiled=True),
        lax.psum_scatter(grad_second_bias, ("dp", "mp"), scatter_dimension=0, tiled=True),
    )
    layer_outputs = jnp.concatenate(section_outputs, axis=0)[None]
    input_grads = jnp.concatenate(section_grads, axis=0)[None]
    return (
        layer_outputs,
        input_grads,
        norm_sums[0][None],
        norm_sums[1][None],
        summed[0][None],
        summed[1][None],
        summed[2][None],
        summed[6][None],
        summed[7][None],
        summed[3][None],
        norm_sums[2][None],
        norm_sums[3][None],
        summed[4][None],
        summed[8][None],
        summed[9][None],
        summed[5][None],
    )


def solution(mesh):
    placed = (
        P(("dp", "mp"), None),
        P(("dp", "mp"), None),
        P("dp"),
        P("section", None),
        P("section", None),
        P("section", "dp", "mp"),
        P("section", "dp", "mp"),
        P("section", "dp", "mp"),
        P("section", "mp"),
        P("section", "mp"),
        P("section", "mp", "dp"),
        P("section", None),
        P("section", None),
        P("section", "dp", "mp"),
        P("section", "mp"),
        P("section", "mp"),
        P("section", "mp", "dp"),
    )
    return jax.shard_map(
        on_device,
        mesh=mesh,
        in_specs=placed,
        out_specs=(
            P("section", ("dp", "mp"), None),
            P("section", ("dp", "mp"), None),
            P("section", ("dp", "mp")),
            P("section", ("dp", "mp")),
            P("section", "dp", "mp"),
            P("section", "dp", "mp"),
            P("section", "dp", "mp"),
            P("section", ("mp", "dp")),
            P("section", ("mp", "dp")),
            P("section", "mp", "dp"),
            P("section", ("dp", "mp")),
            P("section", ("dp", "mp")),
            P("section", "dp", "mp"),
            P("section", ("mp", "dp")),
            P("section", ("mp", "dp")),
            P("section", "mp", "dp"),
        ),
        check_vma=False,
    )
```

profile of v0, /device:TPU:0, one launch (start us, length us, event | category | flops | bytes accessed | tf_op | source)
XLA Modules:
  0.0 1729.8 jit_solution(3163629524772860632)
XLA Ops:
  14.6 21.3 %all-gather.3 = bf16[1,192,768]{1,0,2:T(2,128)(2,1)S(1)} all-gather(bf16[1,192,192]{1,0,2:T(2,128)(2,1)S(1)} %copy.89), channel_id=5, replica_groups=mesh['section'=2,'dp'=4,'mp'=4] {'dp'}, dimensions={2}, use_global_device_ids=true | all-gather | bytes 368640 | tf_op jit(solution)/shard_map/all_gather | solution.py:349
  36.4 15.4 all-gather
  51.8 14.7 all-gather.1
  66.5 14.2 all-gather.2
  88.1 26.5 %while.111 = (s32[]{:T(128)}, f32[2,512,3,64]{1,3,2,0:T(8,128)S(1)}, s32[2]{0:T(128)S(1)}, s32[1024]{0:T(1024)S(1)}, bf16[1024,3,64]{0,2,1:T(8,128)(2,1)}, /*ind...) while((s32[]{:T(128)}, f32[2,512,3,64]{1,3,2,0:T(8,128)S(1)}, ...), condition=%wide.region_5.6_spmd, body=%wide.region_2.5_spmd.sunk | while | flops 412615680 | bytes 15032487 | solution.py:107
  91.1 6.3 fusion.658
  115.6 10.2 all-reduce.18
  128.5 28.1 %reduce-scatter.26.cloned.1.call-done = bf16[256,768]{1,0:T(8,128)(2,1)} async-done(((bf16[1024,768]{1,0:T(8,128)(2,1)}), bf16[256,768]{1,0:T(8,128)(2,1)}) %reduce-scatter.26.cloned.1.call-update) | async-done | bytes 393232 | tf_op jit(solution)/shard_map/reduce_scatter | solution.py:50
  160.8 29.9 %all-gather.29.cloned.1.call-done = bf16[1024,768]{1,0:T(8,128)(2,1)} async-done(((bf16[256,768]{1,0:T(8,128)(2,1)}), bf16[1024,768]{1,0:T(8,128)(2,1)}) %all-gather.29.cloned.1.call-update) | async-done | bytes 1572880 | tf_op jit(solution)/shard_map/all_gather | solution.py:46
  190.8 10.9 fusion.445
  201.7 9.1 all-reduce.17
  210.8 11.6 all-gather.65.cloned.1.call-done
  227.9 30.1 %reduce-scatter.28.cloned.1.call-done = bf16[256,768]{1,0:T(8,128)(2,1)} async-done(((bf16[1024,768]{1,0:T(8,128)(2,1)}), bf16[256,768]{1,0:T(8,128)(2,1)}) %reduce-scatter.28.cloned.1.call-update) | async-done | bytes 393232 | tf_op jit(solution)/shard_map/reduce_scatter | solution.py:50
  266.3 29.7 %all-gather.31.cloned.1.call-done = bf16[1024,768]{1,0:T(8,128)(2,1)} async-done(((bf16[256,768]{1,0:T(8,128)(2,1)}), bf16[1024,768]{1,0:T(8,128)(2,1)}) %all-gather.31.cloned.1.call-update) | async-done | bytes 1572880 | tf_op jit(solution)/shard_map/all_gather | solution.py:46
  303.4 26.6 %while.112 = (s32[]{:T(128)}, f32[2,512,3,64]{1,3,2,0:T(8,128)S(1)}, s32[2]{0:T(128)S(1)}, s32[1024]{0:T(1024)S(1)}, bf16[1024,3,64]{0,2,1:T(8,128)(2,1)}, /*ind...) while((s32[]{:T(128)}, f32[2,512,3,64]{1,3,2,0:T(8,128)S(1)}, ...), condition=%wide.region_23.24_spmd, body=%wide.region_20.23_spmd.sunk | while | flops 412615680 | bytes 15032487 | solution.py:107
  306.4 6.3 fusion.663
  319.7 6.3 fusion.663
  337.8 18.9 %while.114 = (s32[]{:T(128)}, f32[2,512,3,64]{1,3,2,0:T(8,128)}, f32[2,3,512]{2,1,0:T(4,128)S(1)}, s32[2]{0:T(128)S(1)}, s32[1024]{0:T(1024)S(1)}, /*index=5*/bf...) while((s32[]{:T(128)}, f32[2,512,3,64]{1,3,2,0:T(8,128)}, ...), condition=%wide.region_59.60_spmd, body=%wide.region_56.59_spmd.sunk | while | flops 422050304 | bytes 28709100 | solution.py:107
  358.4 15.4 all-reduce.16
  380.9 27.0 %reduce-scatter.30.cloned.1.call-done = bf16[256,768]{1,0:T(8,128)(2,1)} async-done(((bf16[1024,768]{1,0:T(8,128)(2,1)}), bf16[256,768]{1,0:T(8,128)(2,1)}) %reduce-scatter.30.cloned.1.call-update) | async-done | bytes 393232 | tf_op jit(solution)/shard_map/reduce_scatter | solution.py:50
  409.2 32.5 %reduce-scatter.38.cloned.1.call-done = bf16[256,768]{1,0:T(8,128)(2,1)} async-done(((bf16[1024,768]{1,0:T(8,128)(2,1)}), bf16[256,768]{1,0:T(8,128)(2,1)}) %reduce-scatter.38.cloned.1.call-update) | async-done | bytes 393232 | tf_op jit(solution)/shard_map/reduce_scatter | solution.py:50
  446.1 30.3 %all-gather.33.cloned.1.call-done = bf16[1024,768]{1,0:T(8,128)(2,1)} async-done(((bf16[256,768]{1,0:T(8,128)(2,1)}), bf16[1024,768]{1,0:T(8,128)(2,1)}) %all-gather.33.cloned.1.call-update) | async-done | bytes 1572880 | tf_op jit(solution)/shard_map/all_gather | solution.py:46
  476.4 10.9 fusion.444
  487.3 22.2 %all-gather.41.cloned.1.call-done = bf16[1024,768]{1,0:T(8,128)(2,1)} async-done(((bf16[256,768]{1,0:T(8,128)(2,1)}), bf16[1024,768]{1,0:T(8,128)(2,1)}) %all-gather.41.cloned.1.call-update) | async-done | bytes 1572880 | tf_op jit(solution)/shard_map/all_gather | solution.py:46
  509.5 11.9 multiply_reduce_fusion.11
  521.4 15.6 all-reduce.15
  543.5 39.6 %reduce-scatter.32.cloned.1.call-done = bf16[256,768]{1,0:T(8,128)(2,1)} async-done(((bf16[1024,768]{1,0:T(8,128)(2,1)}), bf16[256,768]{1,0:T(8,128)(2,1)}) %reduce-scatter.32.cloned.1.call-update) | async-done | bytes 393232 | tf_op jit(solution)/shard_map/reduce_scatter | solution.py:50
  605.0 15.6 all-gather.55.cloned.1.call-done
  626.6 18.9 %while.116 = (s32[]{:T(128)}, f32[2,512,3,64]{1,3,2,0:T(8,128)}, f32[2,3,512]{2,1,0:T(4,128)S(1)}, s32[2]{0:T(128)S(1)}, s32[1024]{0:T(1024)S(1)}, /*index=5*/bf...) while((s32[]{:T(128)}, f32[2,512,3,64]{1,3,2,0:T(8,128)}, ...), condition=%wide.region_127.128_spmd, body=%wide.region_124.127_spmd.sunk | while | flops 422050304 | bytes 28709100 | solution.py:107
  646.1 7.8 all-gather.47.cloned.1.call-done
  659.9 18.9 %while.115 = (s32[]{:T(128)}, f32[2,512,3,64]{1,3,2,0:T(8,128)}, f32[2,3,512]{2,1,0:T(4,128)S(1)}, s32[2]{0:T(128)S(1)}, s32[1024]{0:T(1024)S(1)}, /*index=5*/bf...) while((s32[]{:T(128)}, f32[2,512,3,64]{1,3,2,0:T(8,128)}, ...), condition=%wide.region_93.94_spmd, body=%wide.region_90.93_spmd.sunk | while | flops 422050304 | bytes 28709100 | solution.py:107
  680.9 15.4 all-reduce.14
  709.0 28.1 %reduce-scatter.40.cloned.1.call-done = bf16[256,768]{1,0:T(8,128)(2,1)} async-done(((bf16[1024,768]{1,0:T(8,128)(2,1)}), bf16[256,768]{1,0:T(8,128)(2,1)}) %reduce-scatter.40.cloned.1.call-update) | async-done | bytes 393232 | tf_op jit(solution)/shard_map/reduce_scatter | solution.py:50
  739.2 31.8 %reduce-scatter.44.cloned.1.call-done = bf16[256,768]{1,0:T(8,128)(2,1)} async-done(((bf16[1024,768]{1,0:T(8,128)(2,1)}), bf16[256,768]{1,0:T(8,128)(2,1)}) %reduce-scatter.44.cloned.1.call-update) | async-done | bytes 393232 | tf_op jit(solution)/shard_map/reduce_scatter | solution.py:50
  777.1 29.3 %all-gather.45.cloned.1.call-done = bf16[1024,768]{1,0:T(8,128)(2,1)} async-done(((bf16[256,768]{1,0:T(8,128)(2,1)}), bf16[1024,768]{1,0:T(8,128)(2,1)}) %all-gather.45.cloned.1.call-update) | async-done | bytes 1572880 | tf_op jit(solution)/shard_map/all_gather | solution.py:46
  810.1 29.6 %all-gather.49.cloned.1.call-done = bf16[1024,768]{1,0:T(8,128)(2,1)} async-done(((bf16[256,768]{1,0:T(8,128)(2,1)}), bf16[1024,768]{1,0:T(8,128)(2,1)}) %all-gather.49.cloned.1.call-update) | async-done | bytes 1572880 | tf_op jit(solution)/shard_map/all_gather | solution.py:46
  839.7 12.4 multiply_reduce_fusion.9
  852.0 16.1 all-reduce.13
  870.3 26.3 %while.117 = (s32[]{:T(128)}, f32[1024,3,64]{0,2,1:T(8,128)S(1)}, f32[1024,3,64]{0,2,1:T(8,128)}, bf16[2,512,3,64]{1,3,2,0:T(8,128)(2,1)}, s32[2]{0:T(128)S(1)},...) while((s32[]{:T(128)}, f32[1024,3,64]{0,2,1:T(8,128)S(1)}, ...), condition=%wide.region_84.85_spmd.clone, body=%wide.region_82.84_spmd.clone.sunk | while | flops 1031830016 | bytes 67428808 | solution.py:151
  902.1 30.5 %reduce-scatter.42.cloned.1.call-done = bf16[256,768]{1,0:T(8,128)(2,1)} async-done(((bf16[1024,768]{1,0:T(8,128)(2,1)}), bf16[256,768]{1,0:T(8,128)(2,1)}) %reduce-scatter.42.cloned.1.call-update) | async-done | bytes 393232 | tf_op jit(solution)/shard_map/reduce_scatter | solution.py:50
  941.0 30.6 %all-gather.51.cloned.1.call-done = bf16[1024,768]{1,0:T(8,128)(2,1)} async-done(((bf16[256,768]{1,0:T(8,128)(2,1)}), bf16[1024,768]{1,0:T(8,128)(2,1)}) %all-gather.51.cloned.1.call-update) | async-done | bytes 1572880 | tf_op jit(solution)/shard_map/all_gather | solution.py:46
  985.0 15.0 all-reduce.12
  1012.6 28.2 %reduce-scatter.46.cloned.1.call-done = bf16[256,768]{1,0:T(8,128)(2,1)} async-done(((bf16[1024,768]{1,0:T(8,128)(2,1)}), bf16[256,768]{1,0:T(8,128)(2,1)}) %reduce-scatter.46.cloned.1.call-update) | async-done | bytes 393232 | tf_op jit(solution)/shard_map/reduce_scatter | solution.py:50
  1042.9 31.8 %reduce-scatter.50.cloned.1.call-done = bf16[256,768]{1,0:T(8,128)(2,1)} async-done(((bf16[1024,768]{1,0:T(8,128)(2,1)}), bf16[256,768]{1,0:T(8,128)(2,1)}) %reduce-scatter.50.cloned.1.call-update) | async-done | bytes 393232 | tf_op jit(solution)/shard_map/reduce_scatter | solution.py:50
  1082.3 28.2 %all-gather.53.cloned.1.call-done = bf16[1024,768]{1,0:T(8,128)(2,1)} async-done(((bf16[256,768]{1,0:T(8,128)(2,1)}), bf16[1024,768]{1,0:T(8,128)(2,1)}) %all-gather.53.cloned.1.call-update) | async-done | bytes 1572880 | tf_op jit(solution)/shard_map/all_gather | solution.py:46
  1114.1 29.7 %all-gather.57.cloned.1.call-done = bf16[1024,768]{1,0:T(8,128)(2,1)} async-done(((bf16[256,768]{1,0:T(8,128)(2,1)}), bf16[1024,768]{1,0:T(8,128)(2,1)}) %all-gather.57.cloned.1.call-update) | async-done | bytes 1572880 | tf_op jit(solution)/shard_map/all_gather | solution.py:46
  1143.7 12.4 multiply_reduce_fusion.7
  1156.1 17.0 all-reduce.11
  1176.2 27.6 %while.118 = (s32[]{:T(128)}, f32[1024,3,64]{0,2,1:T(8,128)S(1)}, f32[1024,3,64]{0,2,1:T(8,128)}, bf16[2,512,3,64]{1,3,2,0:T(8,128)(2,1)}, s32[2]{0:T(128)S(1)},...) while((s32[]{:T(128)}, f32[1024,3,64]{0,2,1:T(8,128)S(1)}, ...), condition=%wide.region_118.119_spmd.clone, body=%wide.region_116.118_spmd.clone.sunk | while | flops 1031830016 | bytes 65855912 | solution.py:151
  1211.7 27.9 %reduce-scatter.48.cloned.1.call-done = bf16[256,768]{1,0:T(8,128)(2,1)} async-done(((bf16[1024,768]{1,0:T(8,128)(2,1)}), bf16[256,768]{1,0:T(8,128)(2,1)}) %reduce-scatter.48.cloned.1.call-update) | async-done | bytes 393232 | tf_op jit(solution)/shard_map/reduce_scatter | solution.py:50
  1251.1 26.5 %while.113 = (s32[]{:T(128)}, f32[2,512,3,64]{1,3,2,0:T(8,128)S(1)}, s32[2]{0:T(128)S(1)}, s32[1024]{0:T(1024)S(1)}, bf16[1024,3,64]{0,2,1:T(8,128)(2,1)}, /*ind...) while((s32[]{:T(128)}, f32[2,512,3,64]{1,3,2,0:T(8,128)S(1)}, ...), condition=%wide.region_41.42_spmd, body=%wide.region_38.41_spmd.sunk | while | flops 412615680 | bytes 15032487 | solution.py:107
  1254.1 6.3 fusion.668
  1293.5 16.3 all-reduce.10
  1323.1 27.9 %reduce-scatter.52.cloned.1.call-done = bf16[256,768]{1,0:T(8,128)(2,1)} async-done(((bf16[1024,768]{1,0:T(8,128)(2,1)}), bf16[256,768]{1,0:T(8,128)(2,1)}) %reduce-scatter.52.cloned.1.call-update) | async-done | bytes 393232 | tf_op jit(solution)/shard_map/reduce_scatter | solution.py:50
  1353.2 31.7 %reduce-scatter.34.cloned.1.call-done = bf16[256,768]{1,0:T(8,128)(2,1)} async-done(((bf16[1024,768]{1,0:T(8,128)(2,1)}), bf16[256,768]{1,0:T(8,128)(2,1)}) %reduce-scatter.34.cloned.1.call-update) | async-done | bytes 393232 | tf_op jit(solution)/shard_map/reduce_scatter | solution.py:50
  1426.7 26.7 %all-gather.37.cloned.1.call-done = bf16[1024,768]{1,0:T(8,128)(2,1)} async-done(((bf16[256,768]{1,0:T(8,128)(2,1)}), bf16[1024,768]{1,0:T(8,128)(2,1)}) %all-gather.37.cloned.1.call-update) | async-done | bytes 1572880 | tf_op jit(solution)/shard_map/all_gather | solution.py:46
  1453.4 10.9 fusion.443
  1464.3 15.6 all-reduce.9
  1482.3 31.3 %while.119 = (s32[]{:T(128)}, f32[1024,3,64]{0,2,1:T(8,128)}, f32[1024,3,64]{0,2,1:T(8,128)}, bf16[2,512,3,64]{1,3,2,0:T(8,128)(2,1)}, s32[2]{0:T(128)S(1)}, /*i...) while((s32[]{:T(128)}, f32[1024,3,64]{0,2,1:T(8,128)}, ...), condition=%wide.region_152.153_spmd.clone, body=%wide.region_150.152_spmd.clone.sunk | while | flops 1031830016 | bytes 75293216 | solution.py:151
  1546.1 12.0 all-reduce.19
  1563.9 15.0 reduce-scatter.58.cloned.1.call-done
  1580.4 19.4 %reduce-scatter.60.cloned.1.call-done = bf16[192,192]{1,0:T(8,128)(2,1)} async-done(((bf16[768,192]{1,0:T(8,128)(2,1)}), bf16[192,192]{1,0:T(8,128)(2,1)}) %reduce-scatter.60.cloned.1.call-update) | async-done | bytes 73744 | tf_op jit(solution)/shard_map/reduce_scatter | solution.py:450
  1601.4 30.4 %reduce-scatter.54.cloned.1.call-done = bf16[256,768]{1,0:T(8,128)(2,1)} async-done(((bf16[1024,768]{1,0:T(8,128)(2,1)}), bf16[256,768]{1,0:T(8,128)(2,1)}) %reduce-scatter.54.cloned.1.call-update) | async-done | bytes 393232 | tf_op jit(solution)/shard_map/reduce_scatter | solution.py:50
  1636.4 76.1 %all-reduce.8 = (f32[768]{0:T(1024)}, f32[768]{0:T(1024)}, f32[768]{0:T(1024)}, f32[768]{0:T(1024)S(1)}) all-reduce(f32[768]{0:T(1024)} %multiply_add_fusion.3, f32[768]{0:T(1024)} %multiply_add_fusion.2, f32[768]{0:T(1024)} %multiply_add_fusion.1, ...), channel_id=23, replica_groups=mesh['section'=2,'dp'=4,'mp'=4] {'dp','mp'}, use_global_device_ids=true, to_apply=%region_159.160.clone | all-reduce | flops 3072 | bytes 24576
  (1136 shorter events, 492.7 us)
Async XLA Ops:
  8.0 72.7 %all-gather.27.cloned.1.call-start = ((), (), s32[]{:S(2)}) async-start(), calls=%async_computation.21 | async-start | bytes 1966080 | tf_op jit(solution)/shard_map/all_gather | solution.py:46
  8.9 255.0 %copy-start.144 = (f32[768]{0:T(1024)}, f32[768]{0:T(1024)S(1)}, u32[]{:S(2)}) copy-start(f32[768]{0:T(1024)S(1)} %reduce.12) | copy-start | bytes 9220
  9.6 254.3 %copy-start.168 = (f32[768]{0:T(1024)}, f32[768]{0:T(1024)S(1)}, u32[]{:S(2)}) copy-start(f32[768]{0:T(1024)S(1)} %reduce.13) | copy-start | bytes 9220
  12.8 143.8 %reduce-scatter.26.cloned.1.call-start = ((), (), s32[]{:S(2)}) async-start(), calls=%async_computation.22 | async-start | bytes 1966080 | tf_op jit(solution)/shard_map/reduce_scatter | solution.py:50
  51.8 606.4 %copy-start.16 = (bf16[1,768,192]{2,1,0:T(8,128)(2,1)}, bf16[1,768,192]{2,1,0:T(8,128)(2,1)S(1)}, u32[]{:S(2)}) copy-start(bf16[1,768,192]{2,1,0:T(8,128)(2,1)S(1)} %all-gather) | copy-start | bytes 884740
  66.5 589.6 %copy-start.19 = (bf16[1,768,192]{2,1,0:T(8,128)(2,1)}, bf16[1,768,192]{2,1,0:T(8,128)(2,1)S(1)}, u32[]{:S(2)}) copy-start(bf16[1,768,192]{2,1,0:T(8,128)(2,1)S(1)} %all-gather.1) | copy-start | bytes 884740
  80.7 573.2 %copy-start.13 = (bf16[1,768,192]{2,1,0:T(8,128)(2,1)}, bf16[1,768,192]{2,1,0:T(8,128)(2,1)S(1)}, u32[]{:S(2)}) copy-start(bf16[1,768,192]{2,1,0:T(8,128)(2,1)S(1)} %all-gather.2) | copy-start | bytes 884740
  80.7 184.5 %copy-start.99 = (s32[4,1,256]{2,1,0:T(1,128)}, s32[4,1,256]{2,1,0:T(1,128)S(1)}, u32[]{:S(2)}) copy-start(s32[4,1,256]{2,1,0:T(1,128)S(1)} %get-tuple-element.979) | copy-start | bytes 12292
  127.8 33.1 %all-gather.63.cloned.1.call-start = ((), (), s32[]{:S(2)}) async-start(), calls=%async_computation.58 | async-start | bytes 1474560 | tf_op jit(solution)/shard_map/all_gather | solution.py:350
  128.3 62.4 %all-gather.29.cloned.1.call-start = ((), (), s32[]{:S(2)}) async-start(), calls=%async_computation.23 | async-start | bytes 1966080 | tf_op jit(solution)/shard_map/all_gather | solution.py:46
  159.9 62.6 %all-gather.65.cloned.1.call-start = ((), (), s32[]{:S(2)}) async-start(), calls=%async_computation.59 | async-start | bytes 1474560 | tf_op jit(solution)/shard_map/all_gather | solution.py:351
  160.4 97.6 %reduce-scatter.28.cloned.1.call-start = ((), (), s32[]{:S(2)}) async-start(), calls=%async_computation.24 | async-start | bytes 1966080 | tf_op jit(solution)/shard_map/reduce_scatter | solution.py:50
  227.7 68.3 %all-gather.31.cloned.1.call-start = ((), (), s32[]{:S(2)}) async-start(), calls=%async_computation.25 | async-start | bytes 1966080 | tf_op jit(solution)/shard_map/all_gather | solution.py:46
  260.1 3.1 collective-permute-start
  263.5 325.0 %copy-start.22 = (bf16[256,768]{1,0:T(8,128)(2,1)}, bf16[256,768]{1,0:T(8,128)(2,1)S(1)}, u32[]{:S(2)}) copy-start(bf16[256,768]{1,0:T(8,128)(2,1)S(1)} %get-tuple-element.947) | copy-start | bytes 1179652
  265.1 66.6 %all-gather.39.cloned.1.call-start = ((), (), s32[]{:S(2)}) async-start(), calls=%async_computation.33 | async-start | bytes 1966080 | tf_op jit(solution)/shard_map/all_gather | solution.py:46
  265.9 142.0 %reduce-scatter.30.cloned.1.call-start = ((), (), s32[]{:S(2)}) async-start(), calls=%async_computation.26 | async-start | bytes 1966080 | tf_op jit(solution)/shard_map/reduce_scatter | solution.py:50
  376.9 64.8 %reduce-scatter.38.cloned.1.call-start = ((), (), s32[]{:S(2)}) async-start(), calls=%async_computation.34 | async-start | bytes 1966080 | tf_op jit(solution)/shard_map/reduce_scatter | solution.py:50
  380.9 95.5 %all-gather.33.cloned.1.call-start = ((), (), s32[]{:S(2)}) async-start(), calls=%async_computation.27 | async-start | bytes 1966080 | tf_op jit(solution)/shard_map/all_gather | solution.py:46
  445.5 64.0 %all-gather.41.cloned.1.call-start = ((), (), s32[]{:S(2)}) async-start(), calls=%async_computation.35 | async-start | bytes 1966080 | tf_op jit(solution)/shard_map/all_gather | solution.py:46
  446.1 137.1 %reduce-scatter.32.cloned.1.call-start = ((), (), s32[]{:S(2)}) async-start(), calls=%async_computation.28 | async-start | bytes 1966080 | tf_op jit(solution)/shard_map/reduce_scatter | solution.py:50
  542.3 47.5 %all-gather.43.cloned.1.call-start = ((), (), s32[]{:S(2)}) async-start(), calls=%async_computation.36 | async-start | bytes 1966080 | tf_op jit(solution)/shard_map/all_gather | solution.py:46
  542.9 77.7 %all-gather.55.cloned.1.call-start = ((), (), s32[]{:S(2)}) async-start(), calls=%async_computation.47 | async-start | bytes 1966080 | tf_op jit(solution)/shard_map/all_gather | solution.py:46
  585.2 3.0 collective-permute-start.1
  589.7 64.2 %all-gather.47.cloned.1.call-start = ((), (), s32[]{:S(2)}) async-start(), calls=%async_computation.40 | async-start | bytes 1966080 | tf_op jit(solution)/shard_map/all_gather | solution.py:46
  598.9 97.3 %copy-start.192 = (f32[1024]{0:T(1024)}, f32[1024]{0:T(1024)S(1)}, u32[]{:S(2)}) copy-start(f32[1024]{0:T(1024)S(1)} %get-tuple-element.996) | copy-start | bytes 12292
  598.9 97.3 %copy-start.194 = (f32[1024]{0:T(1024)}, f32[1024]{0:T(1024)S(1)}, u32[]{:S(2)}) copy-start(f32[1024]{0:T(1024)S(1)} %get-tuple-element.997) | copy-start | bytes 12292
  604.9 132.1 %reduce-scatter.40.cloned.1.call-start = ((), (), s32[]{:S(2)}) async-start(), calls=%async_computation.37 | async-start | bytes 1966080 | tf_op jit(solution)/shard_map/reduce_scatter | solution.py:50
  706.0 65.0 %reduce-scatter.44.cloned.1.call-start = ((), (), s32[]{:S(2)}) async-start(), calls=%async_computation.41 | async-start | bytes 1966080 | tf_op jit(solution)/shard_map/reduce_scatter | solution.py:50
  707.0 403.5 %copy-start.183 = (f32[1024]{0:T(1024)}, f32[1024]{0:T(1024)S(1)}, u32[]{:S(2)}) copy-start(f32[1024]{0:T(1024)S(1)} %get-tuple-element.994) | copy-start | bytes 12292
  707.0 403.5 %copy-start.186 = (f32[1024]{0:T(1024)}, f32[1024]{0:T(1024)S(1)}, u32[]{:S(2)}) copy-start(f32[1024]{0:T(1024)S(1)} %get-tuple-element.995) | copy-start | bytes 12292
  708.9 97.5 %all-gather.45.cloned.1.call-start = ((), (), s32[]{:S(2)}) async-start(), calls=%async_computation.38 | async-start | bytes 1966080 | tf_op jit(solution)/shard_map/all_gather | solution.py:46
  775.5 64.2 %all-gather.49.cloned.1.call-start = ((), (), s32[]{:S(2)}) async-start(), calls=%async_computation.42 | async-start | bytes 1966080 | tf_op jit(solution)/shard_map/all_gather | solution.py:46
  776.2 156.3 %reduce-scatter.42.cloned.1.call-start = ((), (), s32[]{:S(2)}) async-start(), calls=%async_computation.39 | async-start | bytes 1966080 | tf_op jit(solution)/shard_map/reduce_scatter | solution.py:50
  902.0 69.6 %all-gather.51.cloned.1.call-start = ((), (), s32[]{:S(2)}) async-start(), calls=%async_computation.43 | async-start | bytes 1966080 | tf_op jit(solution)/shard_map/all_gather | solution.py:46
  936.2 3.6 collective-permute-start.2
  940.7 100.1 %reduce-scatter.46.cloned.1.call-start = ((), (), s32[]{:S(2)}) async-start(), calls=%async_computation.44 | async-start | bytes 1966080 | tf_op jit(solution)/shard_map/reduce_scatter | solution.py:50
  1009.7 65.0 %reduce-scatter.50.cloned.1.call-start = ((), (), s32[]{:S(2)}) async-start(), calls=%async_computation.48 | async-start | bytes 1966080 | tf_op jit(solution)/shard_map/reduce_scatter | solution.py:50
  1012.5 97.9 %all-gather.53.cloned.1.call-start = ((), (), s32[]{:S(2)}) async-start(), calls=%async_computation.45 | async-start | bytes 1966080 | tf_op jit(solution)/shard_map/all_gather | solution.py:46
  1079.6 64.2 %all-gather.57.cloned.1.call-start = ((), (), s32[]{:S(2)}) async-start(), calls=%async_computation.49 | async-start | bytes 1966080 | tf_op jit(solution)/shard_map/all_gather | solution.py:46
  1080.3 128.5 %all-gather.35.cloned.1.call-start = ((), (), s32[]{:S(2)}) async-start(), calls=%async_computation.29 | async-start | bytes 1966080 | tf_op jit(solution)/shard_map/all_gather | solution.py:46
  1082.2 157.4 %reduce-scatter.48.cloned.1.call-start = ((), (), s32[]{:S(2)}) async-start(), calls=%async_computation.46 | async-start | bytes 1966080 | tf_op jit(solution)/shard_map/reduce_scatter | solution.py:50
  1208.6 74.0 %all-gather.59.cloned.1.call-start = ((), (), s32[]{:S(2)}) async-start(), calls=%async_computation.50 | async-start | bytes 1966080 | tf_op jit(solution)/shard_map/all_gather | solution.py:46
  1245.6 4.5 collective-permute-start.3
  1250.9 100.1 %reduce-scatter.52.cloned.1.call-start = ((), (), s32[]{:S(2)}) async-start(), calls=%async_computation.51 | async-start | bytes 1966080 | tf_op jit(solution)/shard_map/reduce_scatter | solution.py:50
  1320.0 64.9 %reduce-scatter.34.cloned.1.call-start = ((), (), s32[]{:S(2)}) async-start(), calls=%async_computation.30 | async-start | bytes 1966080 | tf_op jit(solution)/shard_map/reduce_scatter | solution.py:50
  1323.1 97.2 %all-gather.61.cloned.1.call-start = ((), (), s32[]{:S(2)}) async-start(), calls=%async_computation.52 | async-start | bytes 1966080 | tf_op jit(solution)/shard_map/all_gather | solution.py:46
  1389.3 64.0 %all-gather.37.cloned.1.call-start = ((), (), s32[]{:S(2)}) async-start(), calls=%async_computation.31 | async-start | bytes 1966080 | tf_op jit(solution)/shard_map/all_gather | solution.py:46
  1389.9 145.4 %reduce-scatter.66.cloned.1.call-start = ((), (), s32[]{:S(2)}) async-start(), calls=%async_computation.61 | async-start | bytes 1474560
  1407.7 129.9 %reduce-scatter.62.cloned.1.call-start = ((), (), s32[]{:S(2)}) async-start(), calls=%async_computation.57 | async-start | bytes 1474560 | tf_op jit(solution)/shard_map/reduce_scatter | solution.py:456
  1419.9 140.7 %reduce-scatter.64.cloned.1.call-start = ((), (), s32[]{:S(2)}) async-start(), calls=%async_computation.60 | async-start | bytes 491520
  1479.9 82.4 %reduce-scatter.56.cloned.1.call-start = ((), (), s32[]{:S(2)}) async-start(), calls=%async_computation.54 | async-start | bytes 491520 | tf_op jit(solution)/shard_map/reduce_scatter | solution.py:444
  1518.4 60.5 %reduce-scatter.58.cloned.1.call-start = ((), (), s32[]{:S(2)}) async-start(), calls=%async_computation.55 | async-start | bytes 491520 | tf_op jit(solution)/shard_map/reduce_scatter | solution.py:447
  1522.8 77.0 %reduce-scatter.60.cloned.1.call-start = ((), (), s32[]{:S(2)}) async-start(), calls=%async_computation.56 | async-start | bytes 491520 | tf_op jit(solution)/shard_map/reduce_scatter | solution.py:450
  1527.8 104.0 %reduce-scatter.54.cloned.1.call-start = ((), (), s32[]{:S(2)}) async-start(), calls=%async_computation.53 | async-start | bytes 1966080 | tf_op jit(solution)/shard_map/reduce_scatter | solution.py:50
  1532.0 186.2 %reduce-scatter.36.cloned.1.call-start = ((), (), s32[]{:S(2)}) async-start(), calls=%async_computation.32 | async-start | bytes 1966080 | tf_op jit(solution)/shard_map/reduce_scatter | solution.py:50
  1545.3 171.6 %copy-start.207 = (f32[256]{0:T(256)S(1)}, f32[256]{0:T(256)}, u32[]{:S(2)}) copy-start(f32[256]{0:T(256)} %copy-done.206) | copy-start | bytes 3076
  1545.3 172.9 %copy-start.45 = (bf16[256,768]{1,0:T(8,128)(2,1)S(1)}, bf16[256,768]{1,0:T(8,128)(2,1)}, u32[]{:S(2)}) copy-start(bf16[256,768]{1,0:T(8,128)(2,1)} %copy-done.43) | copy-start | bytes 1179652
  1545.4 172.8 %copy-start.92 = (bf16[256,768]{1,0:T(8,128)(2,1)S(1)}, bf16[256,768]{1,0:T(8,128)(2,1)}, u32[]{:S(2)}) copy-start(bf16[256,768]{1,0:T(8,128)(2,1)} %reduce-scatter.34.cloned.1.call-done) | copy-start | bytes 1179652
  1545.4 172.8 %copy-start.125 = (bf16[256,768]{1,0:T(8,128)(2,1)S(1)}, bf16[256,768]{1,0:T(8,128)(2,1)}, u32[]{:S(2)}) copy-start(bf16[256,768]{1,0:T(8,128)(2,1)} %copy-done.124) | copy-start | bytes 1179652
  1545.4 172.8 %copy-start.212 = (f32[256]{0:T(256)S(1)}, f32[256]{0:T(256)}, u32[]{:S(2)}) copy-start(f32[256]{0:T(256)} %copy-done.210) | copy-start | bytes 3076
  1545.4 174.2 %copy-start.117 = (bf16[256,768]{1,0:T(8,128)(2,1)S(1)}, bf16[256,768]{1,0:T(8,128)(2,1)}, u32[]{:S(2)}) copy-start(bf16[256,768]{1,0:T(8,128)(2,1)} %get-tuple-element.920) | copy-start | bytes 1179652
  1545.4 175.1 %copy-start.97 = (f32[256,768]{1,0:T(8,128)S(1)}, f32[256,768]{1,0:T(8,128)}, u32[]{:S(2)}) copy-start(f32[256,768]{1,0:T(8,128)} %get-tuple-element.923) | copy-start | bytes 2359300
  1545.4 175.1 %copy-start.127 = (bf16[256,768]{1,0:T(8,128)(2,1)S(1)}, bf16[256,768]{1,0:T(8,128)(2,1)}, u32[]{:S(2)}) copy-start(bf16[256,768]{1,0:T(8,128)(2,1)} %copy-done.126) | copy-start | bytes 1179652
  (304 other events, 6040.3 us)
Sparse Core Ops, SparseCore 0:
  12.9 33.6 all-gather.26
  127.9 28.6 reduce-scatter.25
  227.9 30.1 reduce-scatter.27
  377.0 30.8 reduce-scatter.29
  410.7 30.9 reduce-scatter.37
  542.4 40.7 reduce-scatter.31
  706.1 30.8 reduce-scatter.39
  740.1 30.9 reduce-scatter.43
  902.1 30.3 reduce-scatter.41
  1009.9 30.8 reduce-scatter.45
  1043.8 30.8 reduce-scatter.49
  1208.8 30.8 reduce-scatter.47
  1320.1 30.8 reduce-scatter.51
  1353.9 30.9 reduce-scatter.33
Sparse Core Ops, SparseCore 1:
  129.8 27.8 all-gather.62
  160.0 30.7 all-gather.28
  192.2 30.2 all-gather.64
  265.2 30.8 all-gather.30
  298.5 30.8 all-gather.38
  445.6 30.8 all-gather.32
  478.7 30.8 all-gather.40
  545.2 33.2 all-gather.42
  589.7 30.8 all-gather.54
  623.0 30.8 all-gather.46
  775.6 30.8 all-gather.44
  808.9 30.8 all-gather.48
  940.8 30.8 all-gather.50
  1079.7 30.8 all-gather.52
  1112.9 30.8 all-gather.56
  1145.6 30.9 all-gather.34
  1251.0 31.5 all-gather.58
  1389.4 30.8 all-gather.60
  1422.5 30.8 all-gather.36
  1455.7 29.2 reduce-scatter.65
  1487.1 27.8 reduce-scatter.61
  1517.1 19.1 reduce-scatter.63
  1538.5 18.8 reduce-scatter.55
  1559.7 19.1 reduce-scatter.57
  1581.1 18.7 reduce-scatter.59
  1602.8 28.9 reduce-scatter.53
  1634.8 31.1 reduce-scatter.35
where the time goes:
time: 1740 us; the launch traced here: 1730 us
  waiting for transfers between devices  794 us (46%)
  matrix products  344 us (20%)
  blocking collectives  299 us (17%)
  other arithmetic  146 us (8%)
  local copies, waits for them, and re-layouts  74.4 us (4%)
  loops' own time  40.1 us (2%)
  between operations  21.7 us (1%)
    reduce_scatter x15, waiting for transfers between devices, settle_rows(): lax.psum_scatter(partial_rows.astype(jnp.bfloat16), 'mp', scatter_dimensi...  426 us
    all_gather x18, waiting for transfers between devices, spread_rows(): return lax.all_gather(row_block, 'mp', axis=0, tiled=True)  313 us
    psum x10, blocking collectives, row_totals(): return lax.psum((total_one, total_two), 'mp')  146 us
    dot_general x33, matrix products, dot_plain(): return jnp.dot(first_mat, second_mat, preferred_element_type=jnp.float32)  133 us
    unnamed x2, blocking collectives  88.2 us
    dot_general x18, matrix products, dot_second_turned(): lax.dot_general(first_mat, second_mat, (((1,), (1,)), ((), ())), preferre...  45.3 us
    sub x6, matrix products, one_block(): exp_terms = jnp.exp(scores - row_peak)  37.9 us
    dot_general x12, matrix products, one_block(): jnp.einsum('hqk,khd->qhd', prob_block, value_rows, preferred_element_type...  36.9 us
  transfers between devices with their start and end apart: 45, of which 34 were waited for; matrix products, arithmetic and copies ran while one was open for 18% of the time, Pallas kernels for 0%

commit v1 on v0

v1 whole, which is shorter than its diff:
```python
from functools import partial

import jax
import jax.numpy as jnp
from jax import lax
from jax.sharding import PartitionSpec as P

D = 768
HEAD_DIM = 64
FF = 3072
MICRO = 2
LANES = 4

EPS = 1e-05
SCALE = HEAD_DIM ** (-0.5)
BOTH = ("section", "mp")
Y_PAIRS = [[0, 2], [1, 3]]


def core_swap(x):
    return lax.ppermute(x, "section", [(0, 1), (1, 0)])


def x_swap(x):
    return lax.ppermute(x, "mp", [(i, i ^ 1) for i in range(LANES)])


def layer_norm(values, gain_vec, bias_vec):
    row_mean = jnp.mean(values, axis=-1, keepdims=True)
    spread = jnp.mean(values * values, axis=-1, keepdims=True) - row_mean * row_mean
    return (values - row_mean) * lax.rsqrt(spread + EPS) * gain_vec + bias_vec


def dot_plain(first_mat, second_mat):
    return jnp.dot(first_mat, second_mat, preferred_element_type=jnp.float32)


def dot_second_turned(first_mat, second_mat):
    return lax.dot_general(
        first_mat, second_mat, (((1,), (1,)), ((), ())), preferred_element_type=jnp.float32
    )


def dot_first_turned(first_mat, second_mat):
    return lax.dot_general(
        first_mat, second_mat, (((0,), (0,)), ((), ())), preferred_element_type=jnp.float32
    )


def spread_rows(own):
    far = x_swap(own)
    return jnp.concatenate([own, core_swap(own), far, core_swap(far)], axis=0)


def settle_rows(partial_rows):
    parts = partial_rows.astype(jnp.bfloat16).reshape(4, -1, partial_rows.shape[-1])
    far = (parts[2].astype(jnp.float32) + core_swap(parts[3]).astype(jnp.float32)).astype(
        jnp.bfloat16
    )
    far = x_swap(far)
    near = parts[0].astype(jnp.float32) + core_swap(parts[1]).astype(jnp.float32)
    return near + far.astype(jnp.float32)


def turned(parts):
    return parts


def row_totals(*totals):
    stacked = jnp.stack(totals).reshape(len(totals), 2, 2, -1)
    stacked = stacked + core_swap(stacked)[:, :, ::-1]
    stacked = stacked + x_swap(stacked)[:, ::-1]
    return tuple(stacked.reshape(len(totals), -1))


def split_norm(values, gain_vec, bias_vec, feature_count):
    total_one, total_two = row_totals(jnp.sum(values, axis=-1), jnp.sum(values * values, axis=-1))
    row_mean = total_one[:, None] / feature_count
    spread = total_two[:, None] / feature_count - row_mean * row_mean
    scaled = lax.rsqrt(spread + EPS)
    normal = (values - row_mean) * scaled
    return (normal * gain_vec + bias_vec, normal, scaled)


def split_norm_back(upstream, normal, scaled, gain_vec, feature_count):
    inner_grad = upstream * gain_vec
    total_one, total_two = row_totals(
        jnp.sum(inner_grad, axis=-1), jnp.sum(inner_grad * normal, axis=-1)
    )
    back_grad = scaled * (
        inner_grad
        - total_one[:, None] / feature_count
        - normal * total_two[:, None] / feature_count
    )
    return (back_grad, jnp.sum(upstream * normal, axis=0), jnp.sum(upstream, axis=0))


def masked_scores(query, key_rows, labels):
    scores = (
        jnp.einsum("qhd,khd->hqk", query, key_rows, preferred_element_type=jnp.float32) * SCALE
    )
    return jnp.where((labels[:, None] == labels[None, :])[None], scores, -1e30)


def attend(query, key_rows, value_rows, labels):
    row_count, head_count, head_size = query.shape
    scores = masked_scores(query, key_rows, labels)
    row_peak = jnp.max(scores, axis=-1, keepdims=True)
    exp_terms = jnp.exp(scores - row_peak)
    row_total = jnp.sum(exp_terms, axis=-1, keepdims=True)
    prob = (exp_terms / row_total).astype(jnp.bfloat16)
    out = jnp.einsum("hqk,khd->qhd", prob, value_rows, preferred_element_type=jnp.float32)
    return out.reshape(row_count, -1), row_peak + jnp.log(row_total)


def attend_back(query, key_rows, value_rows, labels, logsum, grad_out):
    row_count = query.shape[0]
    scores = masked_scores(query, key_rows, labels)
    prob = jnp.exp(scores - logsum)
    prob_grad = jnp.einsum(
        "qhd,khd->hqk", grad_out, value_rows, preferred_element_type=jnp.float32
    )
    row_delta = jnp.sum(prob * prob_grad, axis=-1, keepdims=True)
    score_grad = (prob * (prob_grad - row_delta)).astype(jnp.bfloat16)
    ein = partial(jnp.einsum, preferred_element_type=jnp.float32)
    query_grad = ein("hqk,khd->qhd", score_grad, key_rows) * SCALE
    key_grad = ein("hqk,qhd->khd", score_grad, query) * SCALE
    value_grad = ein("hqk,qhd->khd", prob.astype(jnp.bfloat16), grad_out)
    return tuple(
        item.astype(jnp.bfloat16).reshape(row_count, -1)
        for item in (query_grad, key_grad, value_grad)
    )


def layer_forward(layer_input, labels, row_mask, matrices, small_params):
    qkv_mat, output_mat, up_mat, down_mat = matrices
    (
        first_gain,
        first_bias,
        inner_gain,
        inner_bias,
        second_gain,
        second_bias,
        middle_gain,
        middle_bias,
    ) = small_params
    head_rows = spread_rows(layer_norm(layer_input, first_gain, first_bias).astype(jnp.bfloat16))
    row_count = head_rows.shape[0]
    qkv = dot_plain(head_rows, qkv_mat).astype(jnp.bfloat16)
    query, key_rows, value_rows = (
        item.reshape(row_count, -1, HEAD_DIM) for item in jnp.split(qkv, 3, axis=1)
    )
    mixed, logsum = attend(query, key_rows, value_rows, labels)
    inner_out, mixed_normal, mixed_scaled = split_norm(mixed, inner_gain, inner_bias, D)
    inner_rows = inner_out.astype(jnp.bfloat16)
    mid_input = layer_input + settle_rows(dot_plain(inner_rows, output_mat))
    feed_rows = spread_rows(layer_norm(mid_input, second_gain, second_bias).astype(jnp.bfloat16))
    pre_act = dot_plain(feed_rows, up_mat)
    middle_out, middle_normal, middle_scaled = split_norm(
        jax.nn.gelu(pre_act, approximate=False), middle_gain, middle_bias, FF
    )
    middle_rows = middle_out.astype(jnp.bfloat16)
    result = mid_input + settle_rows(dot_plain(middle_rows, down_mat))
    layer_output = (row_mask * result).astype(jnp.bfloat16)
    kept_state = (
        layer_input,
        head_rows,
        query,
        key_rows,
        value_rows,
        logsum,
        mixed_normal,
        mixed_scaled,
        inner_rows,
        mid_input,
        feed_rows,
        pre_act,
        middle_normal,
        middle_scaled,
        middle_rows,
    )
    return (layer_output, kept_state)


def layer_backward(upstream, kept_state, labels, row_mask, matrices, small_params):
    qkv_mat, output_mat, up_mat, down_mat = matrices
    (
        first_gain,
        first_bias,
        inner_gain,
        inner_bias,
        second_gain,
        second_bias,
        middle_gain,
        middle_bias,
    ) = small_params
    (
        layer_input,
        head_rows,
        query,
        key_rows,
        value_rows,
        logsum,
        mixed_normal,
        mixed_scaled,
        inner_rows,
        mid_input,
        feed_rows,
        pre_act,
        middle_normal,
        middle_scaled,
        middle_rows,
    ) = kept_state
    result_grad = row_mask * upstream
    feed_grad_rows = spread_rows(result_grad.astype(jnp.bfloat16))
    middle_grad = dot_second_turned(feed_grad_rows, down_mat)
    grad_down = dot_first_turned(middle_rows, feed_grad_rows)
    act_grad, grad_middle_gain, grad_middle_bias = split_norm_back(
        middle_grad, middle_normal, middle_scaled, middle_gain, FF
    )
    gelu_out, gelu_back = jax.vjp(partial(jax.nn.gelu, approximate=False), pre_act)
    pre_grad = gelu_back(act_grad)[0].astype(jnp.bfloat16)
    grad_up = dot_first_turned(feed_rows, pre_grad)
    second_in_grad = settle_rows(dot_second_turned(pre_grad, up_mat))
    norm_out, second_back = jax.vjp(layer_norm, mid_input, second_gain, second_bias)
    mid_back, grad_second_gain, grad_second_bias = second_back(second_in_grad)
    mid_grad = result_grad + mid_back
    branch_grad_rows = spread_rows(mid_grad.astype(jnp.bfloat16))
    inner_grad = dot_second_turned(branch_grad_rows, output_mat)
    grad_output = dot_first_turned(inner_rows, branch_grad_rows)
    mixed_grad, grad_inner_gain, grad_inner_bias = split_norm_back(
        inner_grad, mixed_normal, mixed_scaled, inner_gain, D
    )
    mixed_grad = mixed_grad.astype(jnp.bfloat16).reshape(query.shape)
    qkv_grad = jnp.concatenate(
        attend_back(query, key_rows, value_rows, labels, logsum, mixed_grad), axis=1
    )
    grad_qkv = dot_first_turned(head_rows, qkv_grad)
    head_grad = settle_rows(dot_second_turned(qkv_grad, qkv_mat))
    first_out, first_back = jax.vjp(layer_norm, layer_input, first_gain, first_bias)
    input_back, grad_first_gain, grad_first_bias = first_back(head_grad)
    outer = jnp.stack([grad_first_gain, grad_first_bias, grad_second_gain, grad_second_bias])
    grads = (
        grad_qkv,
        grad_output,
        grad_up,
        grad_down,
        grad_inner_gain,
        grad_inner_bias,
        grad_middle_gain,
        grad_middle_bias,
        outer,
    )
    return ((mid_grad + input_back).astype(jnp.bfloat16), grads)


def on_device(
    inputs,
    cotangent,
    doc_ids,
    norm_gain,
    norm_bias,
    w_query,
    w_key,
    w_value,
    inner_gain,
    inner_bias,
    w_output,
    feed_gain,
    feed_bias,
    w_up,
    middle_gain,
    middle_bias,
    w_down,
):
    core = lax.axis_index("section")
    lane = lax.axis_index("mp")
    lane_x = lane % 2
    lane_y = lane // 2
    slice_len = inputs.shape[0] // MICRO
    rank = 2 * core + lane_x

    def rows_of(array, micro_index):
        return lax.dynamic_slice_in_dim(array, micro_index * slice_len, slice_len, 0)

    def own_slice(array):
        sent = lax.ppermute(
            rows_of(array, 1 - lane_y),
            BOTH,
            [(s * 4 + r, s * 4 + (r ^ 2)) for s in range(2) for r in range(4) if s == r // 2],
        )
        return jnp.where(core == lane_y, rows_of(array, lane_y), sent)

    def placed(array, layer):
        got = [
            lax.ppermute(
                array,
                BOTH,
                [(s * 4 + 2 * m + x, layer * 4 + 2 * s + x) for s in range(2) for x in range(2)],
            )
            for m in range(MICRO)
        ]
        return jnp.concatenate(got, axis=0)

    label_grid = lax.dynamic_index_in_dim(
        doc_ids.reshape(LANES, MICRO, slice_len), lane_y, 1, keepdims=False
    )
    order = jnp.stack([rank, 2 * (1 - core) + lane_x, rank ^ 1, 2 * (1 - core) + (1 - lane_x)])
    labels = jnp.take(label_grid, order, axis=0).reshape(-1)
    row_mask = (labels[:slice_len] >= 0).astype(jnp.float32)[:, None]

    def by_layer(own, other):
        return (jnp.where(core == 0, own, other), jnp.where(core == 0, other, own))

    def fetch(block, axis):
        whole = lax.all_gather(block, "dp", axis=axis, tiled=True)
        both = lax.all_gather(whole, "mp", axis=0, axis_index_groups=Y_PAIRS)
        own = lax.dynamic_index_in_dim(both, core, 0, keepdims=False)
        other = core_swap(lax.dynamic_index_in_dim(both, 1 - core, 0, keepdims=False))
        return by_layer(own, other)

    def fetch_vector(block, split):
        if not split:
            return by_layer(block, core_swap(block))
        both = lax.all_gather(block, "mp", axis=0, axis_index_groups=Y_PAIRS)
        own = lax.dynamic_index_in_dim(both, core, 0, keepdims=False)
        other = core_swap(lax.dynamic_index_in_dim(both, 1 - core, 0, keepdims=False))
        return by_layer(own, other)

    w_qkv = jnp.concatenate([w_query[0], w_key[0], w_value[0]], axis=1)
    matrices = list(
        zip(fetch(w_qkv, 0), fetch(w_output[0], 1), fetch(w_up[0], 0), fetch(w_down[0], 1))
    )
    small_params = list(
        zip(
            fetch_vector(norm_gain[0], False),
            fetch_vector(norm_bias[0], False),
            fetch_vector(inner_gain[0], True),
            fetch_vector(inner_bias[0], True),
            fetch_vector(feed_gain[0], False),
            fetch_vector(feed_bias[0], False),
            fetch_vector(middle_gain[0], True),
            fetch_vector(middle_bias[0], True),
        )
    )

    lower_in = own_slice(inputs)
    upstream = own_slice(cotangent)
    lower_out, lower_state = layer_forward(
        lower_in.astype(jnp.float32), labels, row_mask, matrices[0], small_params[0]
    )
    upper_out, upper_state = layer_forward(
        lower_out.astype(jnp.float32), labels, row_mask, matrices[1], small_params[1]
    )
    upper_grad, upper_grads = layer_backward(
        upstream.astype(jnp.float32), upper_state, labels, row_mask, matrices[1], small_params[1]
    )
    lower_grad, lower_grads = layer_backward(
        upper_grad.astype(jnp.float32), lower_state, labels, row_mask, matrices[0], small_params[0]
    )

    def spread_pair(lower_array, upper_array):
        lower_part, upper_part = placed(lower_array, 0), placed(upper_array, 1)
        return jnp.where(core == 0, lower_part, upper_part)[None]

    def collect(lower, upper, axis):
        lower, upper = lower.astype(jnp.bfloat16), upper.astype(jnp.bfloat16)
        own = jnp.where(core == 0, lower, upper)
        other = core_swap(jnp.where(core == 0, upper, lower))
        first, second = by_layer(own, other)
        both = jnp.stack([first, second])
        whole = lax.psum_scatter(
            both, "mp", scatter_dimension=0, axis_index_groups=Y_PAIRS, tiled=False
        )
        return lax.psum_scatter(whole, "dp", scatter_dimension=axis, tiled=True).astype(
            jnp.float32
        )[None]

    grads = [
        collect(lower, upper, axis)
        for lower, upper, axis in zip(lower_grads[:8], upper_grads[:8], (0, 1, 0, 1, 0, 0, 0, 0))
    ]
    outer = jnp.where(core == 0, lower_grads[8], upper_grads[8]) + core_swap(
        jnp.where(core == 0, upper_grads[8], lower_grads[8])
    )
    outer = lax.psum_scatter(outer, ("dp", "mp"), scatter_dimension=1, tiled=True)
    grad_query, grad_key, grad_value = jnp.split(grads[0], 3, axis=2)
    return (
        spread_pair(lower_out, upper_out),
        spread_pair(lower_grad, upper_grad),
        outer[0][None],
        outer[1][None],
        grad_query,
        grad_key,
        grad_value,
        grads[4],
        grads[5],
        grads[1],
        outer[2][None],
        outer[3][None],
        grads[2],
        grads[6],
        grads[7],
        grads[3],
    )


def solution(mesh):
    placed = (
        P(("dp", "mp"), None),
        P(("dp", "mp"), None),
        P("dp"),
        P("section", None),
        P("section", None),
        P("section", "dp", "mp"),
        P("section", "dp", "mp"),
        P("section", "dp", "mp"),
        P("section", "mp"),
        P("section", "mp"),
        P("section", "mp", "dp"),
        P("section", None),
        P("section", None),
        P("section", "dp", "mp"),
        P("section", "mp"),
        P("section", "mp"),
        P("section", "mp", "dp"),
    )
    return jax.shard_map(
        on_device,
        mesh=mesh,
        in_specs=placed,
        out_specs=(
            P("section", ("dp", "mp"), None),
            P("section", ("dp", "mp"), None),
            P("section", ("dp", "mp")),
            P("section", ("dp", "mp")),
            P("section", "dp", "mp"),
            P("section", "dp", "mp"),
            P("section", "dp", "mp"),
            P("section", ("mp", "dp")),
            P("section", ("mp", "dp")),
            P("section", "mp", "dp"),
            P("section", ("dp", "mp")),
            P("section", ("dp", "mp")),
            P("section", "dp", "mp"),
            P("section", ("mp", "dp")),
            P("section", ("mp", "dp")),
            P("section", "mp", "dp"),
        ),
        check_vma=False,
    )
```

time: 1740 us -> 951 us (0.55)
  waiting for transfers between devices: 794 us -> 472 us
  matrix products: 344 us -> 124 us
  blocking collectives: 299 us -> 104 us
  other arithmetic: 146 us -> 86.8 us
  starting transfers between devices: 10.2 us -> 59.8 us
  loops' own time: 40.1 us -> 0 us
    reduce_scatter x19 -> x5, waiting for transfers between devices: 460 us -> 58.7 us  [the longest x4 30.8 us: collect(): lax.psum_scatter(both, 'mp', scatter_dimension=0, axis_index_groups=Y_PAI...]
    all_gather x20 -> x5, waiting for transfers between devices: 325 us -> 49.2 us  [the longest x3 42.5 us: fetch(): both = lax.all_gather(whole, 'mp', axis=0, axis_index_groups=Y_PAIRS)]
    ppermute x4 -> x95, waiting for transfers between devices: 4.44 us -> 183 us  [the longest x24 153 us: x_swap(): return lax.ppermute(x, 'mp', [(i, i ^ 1) for i in range(LANES)])]
    unnamed x43 -> x18, waiting for transfers between devices: 4.65 us -> 181 us
    psum x10 -> x0, blocking collectives: 146 us -> none  [row_totals(): return lax.psum((total_one, total_two), 'mp')]
    dot_general x33 -> x8, matrix products: 133 us -> 41.2 us  [dot_plain(): return jnp.dot(first_mat, second_mat, preferred_element_type=jnp.float32)]
    unnamed x2, blocking collectives: 88.2 us -> 21.8 us
    ppermute x4 -> x95, starting transfers between devices: 6.7 us -> 58.5 us  [the longest x24 24.1 us: x_swap(): return lax.ppermute(x, 'mp', [(i, i ^ 1) for i in range(LANES)])]
  transfers between devices with their start and end apart: 45 -> 109, of which waited for: 34 -> 57; matrix products, arithmetic and copies ran while one was open for 18% -> 18% of each run, Pallas kernels for 0% -> 0%
where the time goes in v1:
time: 951 us; the launch traced here: 941 us
  waiting for transfers between devices  472 us (50%)
  matrix products  124 us (13%)
  blocking collectives  104 us (11%)
  other arithmetic  86.8 us (9%)
  local copies, waits for them, and re-layouts  74.3 us (8%)
  starting transfers between devices  59.8 us (6%)
  between operations  19.7 us (2%)
    unnamed x18, waiting for transfers between devices  181 us
    ppermute x24, waiting for transfers between devices, x_swap(): return lax.ppermute(x, 'mp', [(i, i ^ 1) for i in range(LANES)])  153 us
    all_gather x2, blocking collectives, fetch(): whole = lax.all_gather(block, 'dp', axis=axis, tiled=True)  52.2 us
    all_gather x3, waiting for transfers between devices, fetch(): both = lax.all_gather(whole, 'mp', axis=0, axis_index_groups=Y_PAIRS)  42.5 us
    dot_general x8, matrix products, dot_plain(): return jnp.dot(first_mat, second_mat, preferred_element_type=jnp.float32)  41.2 us
    unnamed x498, local copies, waits for them, and re-layouts  38.9 us
    reduce_scatter x4, waiting for transfers between devices, collect(): lax.psum_scatter(both, 'mp', scatter_dimension=0, axis_index_groups=Y_PAI...  30.8 us
    reduce_scatter x1, waiting for transfers between devices, collect(): lax.psum_scatter(whole, 'dp', scatter_dimension=axis, tiled=True)  27.9 us
  transfers between devices with their start and end apart: 109, of which 57 were waited for; matrix products, arithmetic and copies ran while one was open for 18% of the time, Pallas kernels for 0%

profile of v1, /device:TPU:0, one launch (start us, length us, event | category | flops | bytes accessed | tf_op | source)
XLA Modules:
  0.0 940.8 jit_solution(5955662880289259574)
XLA Ops:
  8.4 23.9 %all_gather.48 = bf16[768,576]{1,0:T(8,128)(2,1)} all-gather(bf16[192,576]{1,0:T(8,128)(2,1)S(1)} %pad_maximum_fusion.34), channel_id=1, replica_groups=mesh['section'=2,'dp'=4,'mp'=4] {'dp'}, dimensions={0}, use_global_device_ids=true | all-gather | bytes 1105920 | tf_op jit(solution)/shard_map/all_gather | solution.py:316
  33.3 3.4 collective-permute-start
  37.4 7.9 all-gather.7
  45.3 4.7 all-gather.8
  54.6 9.2 all-gather.17.cloned.1.call-done
  67.0 28.2 %all-gather.1 = bf16[1,192,768]{1,0,2:T(2,128)(2,1)S(1)} all-gather(bf16[1,192,192]{1,0,2:T(2,128)(2,1)S(1)} %copy.97), channel_id=3, replica_groups=mesh['section'=2,'dp'=4,'mp'=4] {'dp'}, dimensions={2}, use_global_device_ids=true | all-gather | bytes 368640 | tf_op jit(solution)/shard_map/all_gather | solution.py:316
  95.8 8.5 all-gather.2
  110.1 3.2 fusion.156
  115.2 2.8 copy-done
  129.1 6.7 all-gather.23.cloned.1.call-done
  143.3 8.8 collective-permute-done.14
  153.5 18.9 %all-gather.21.cloned.1.call-done = bf16[2,768,768]{2,1,0:T(8,128)(2,1)} async-done(((bf16[1,768,768]{2,1,0:T(8,128)(2,1)}), bf16[2,768,768]{2,1,0:T(8,128)(2,1)}) %all-gather.21.cloned.1.call-update) | async-done | bytes 2359312 | tf_op jit(solution)/shard_map/all_gather | solution.py:317
  176.7 9.8 %collective-permute-done.18 = bf16[256,768]{1,0:T(8,128)(2,1)S(1)} collective-permute-done((bf16[256,768]{1,0:T(8,128)(2,1)S(1)}, bf16[256,768]{1,0:T(8,128)(2,1)S(1)}, u32[]{:S(2)}, u32[]{:S(2)}) %collective-permute-start.18) | collective-permute-done | bytes 393248 | tf_op jit(solution)/shard_map/ppermute | solution.py:25
  186.6 4.4 all-gather.9
  191.1 4.4 all-gather.10
  195.6 14.4 %all-gather.25.cloned.1.call-done = bf16[2,768,768]{2,1,0:T(8,128)(2,1)} async-done(((bf16[1,768,768]{2,1,0:T(8,128)(2,1)}), bf16[2,768,768]{2,1,0:T(8,128)(2,1)}) %all-gather.25.cloned.1.call-update) | async-done | bytes 2359312 | tf_op jit(solution)/shard_map/all_gather | solution.py:317
  212.4 12.6 %multiply_reduce_fusion.7 = (f32[1024]{0:T(1024)S(1)}, f32[1024]{0:T(1024)S(1)}, f32[1024,768]{0,1:T(8,128)}, f32[1024,768]{0,1:T(8,128)}, f32[1024,768]{0,1:T(8,128)}) fusion(bf16[768,768]{1,0:T(8,128)(2,1)} %collective-permute-done.20, pred[]{:T(512)S(6)} %eq.16, bf16[2,768,768]{2,1,0:T(8,128)(2,1)} %all-gather.21.cloned.1.call-done, s32[]{:T(128)S(6)} %select_n.401, ...), kind=kOutput, calls=%fused_computation.50 | convolution fusion | flops 1267529728 | bytes 13377541 | tf_op jit(solution)/shard_map/dot_general | solution.py:35
  230.7 4.0 convolution_convert_fusion.6
  239.4 3.2 collective-permute-done.49
  242.6 6.5 collective-permute-done.28
  252.3 9.0 collective-permute-done.32
  265.7 3.4 fusion.158
  270.9 2.8 copy-done.1
  287.7 9.5 %collective-permute-done.38 = bf16[256,768]{1,0:T(8,128)(2,1)S(1)} collective-permute-done((bf16[256,768]{1,0:T(8,128)(2,1)S(1)}, bf16[256,768]{1,0:T(8,128)(2,1)S(1)}, u32[]{:S(2)}, u32[]{:S(2)}) %collective-permute-start.38) | collective-permute-done | bytes 393248 | tf_op jit(solution)/shard_map/ppermute | solution.py:25
  300.7 10.0 %collective-permute-done.40 = bf16[256,768]{1,0:T(8,128)(2,1)S(1)} collective-permute-done((bf16[256,768]{1,0:T(8,128)(2,1)S(1)}, bf16[256,768]{1,0:T(8,128)(2,1)S(1)}, u32[]{:S(2)}, u32[]{:S(2)}) %collective-permute-start.40) | collective-permute-done | bytes 393248 | tf_op jit(solution)/shard_map/ppermute | solution.py:25
  311.3 6.3 collective-permute-done.51
  317.6 13.9 %multiply_reduce_fusion.6 = (f32[1024]{0:T(1024)S(1)}, f32[1024]{0:T(1024)S(1)}, f32[1024,768]{0,1:T(8,128)}, f32[1024,768]{0,1:T(8,128)}, f32[1024,768]{0,1:T(8,128)}) fusion(bf16[768,768]{1,0:T(8,128)(2,1)} %collective-permute-done.20, pred[]{:T(512)S(6)} %eq.16, bf16[2,768,768]{2,1,0:T(8,128)(2,1)S(1)} %copy-done.58, s32[]{:T(128)S(6)} %select_n.401, ...), kind=kOutput, calls=%fused_computation.35 | convolution fusion | flops 1267529728 | bytes 13377541 | tf_op jit(solution)/shard_map/dot_general | solution.py:35
  335.3 5.4 fusion.160
  344.0 3.5 multiply_reduce_fusion.2
  356.5 3.3 collective-permute-done.54
  359.8 5.1 add_convert_fusion.1
  365.0 3.4 convolution_convert_fusion.3
  368.6 3.1 convolution_convert_fusion.4
  374.9 9.8 %collective-permute-done.57 = bf16[256,768]{1,0:T(8,128)(2,1)S(1)} collective-permute-done((bf16[256,768]{1,0:T(8,128)(2,1)S(1)}, bf16[256,768]{1,0:T(8,128)(2,1)S(1)}, u32[]{:S(2)}, u32[]{:S(2)}) %collective-permute-start.57) | collective-permute-done | bytes 393248 | tf_op jit(solution)/shard_map/ppermute | solution.py:25
  385.8 6.4 collective-permute-done.46
  394.0 9.9 %collective-permute-done.59 = bf16[256,768]{1,0:T(8,128)(2,1)S(1)} collective-permute-done((bf16[256,768]{1,0:T(8,128)(2,1)S(1)}, bf16[256,768]{1,0:T(8,128)(2,1)S(1)}, u32[]{:S(2)}, u32[]{:S(2)}) %collective-permute-start.59) | collective-permute-done | bytes 393248 | tf_op jit(solution)/shard_map/ppermute | solution.py:25
  409.6 3.3 collective-permute-done.62
  414.4 6.2 multiply_reduce_fusion.1
  422.8 5.7 multiply_convert_fusion.1
  428.5 4.2 fusion.24
  442.5 10.8 %collective-permute-done.65 = bf16[256,768]{1,0:T(8,128)(2,1)S(1)} collective-permute-done((bf16[256,768]{1,0:T(8,128)(2,1)S(1)}, bf16[256,768]{1,0:T(8,128)(2,1)S(1)}, u32[]{:S(2)}, u32[]{:S(2)}) %collective-permute-start.65) | collective-permute-done | bytes 393248 | tf_op jit(solution)/shard_map/ppermute | solution.py:25
  455.8 10.0 %collective-permute-done.67 = bf16[256,768]{1,0:T(8,128)(2,1)S(1)} collective-permute-done((bf16[256,768]{1,0:T(8,128)(2,1)S(1)}, bf16[256,768]{1,0:T(8,128)(2,1)S(1)}, u32[]{:S(2)}, u32[]{:S(2)}) %collective-permute-start.67) | collective-permute-done | bytes 393248 | tf_op jit(solution)/shard_map/ppermute | solution.py:25
  467.6 3.7 fusion.161
  473.7 3.5 multiply_reduce_fusion.3
  487.4 3.3 collective-permute-done.70
  490.8 5.3 add_convert_fusion
  500.7 11.0 %collective-permute-done.73 = bf16[256,768]{1,0:T(8,128)(2,1)S(1)} collective-permute-done((bf16[256,768]{1,0:T(8,128)(2,1)S(1)}, bf16[256,768]{1,0:T(8,128)(2,1)S(1)}, u32[]{:S(2)}, u32[]{:S(2)}) %collective-permute-start.73) | collective-permute-done | bytes 393248 | tf_op jit(solution)/shard_map/ppermute | solution.py:25
  514.4 10.2 %collective-permute-done.75 = bf16[256,768]{1,0:T(8,128)(2,1)S(1)} collective-permute-done((bf16[256,768]{1,0:T(8,128)(2,1)S(1)}, bf16[256,768]{1,0:T(8,128)(2,1)S(1)}, u32[]{:S(2)}, u32[]{:S(2)}) %collective-permute-start.75) | collective-permute-done | bytes 393248 | tf_op jit(solution)/shard_map/ppermute | solution.py:25
  534.3 6.1 multiply_reduce_fusion
  542.5 5.5 multiply_convert_fusion
  548.1 4.2 fusion.26
  567.4 3.0 convolution_convert_fusion.9
  570.5 2.9 broadcast_select_fusion
  578.7 2.9 convolution_convert_fusion.11
  594.6 9.7 %collective-permute-done.81 = bf16[256,768]{1,0:T(8,128)(2,1)S(1)} collective-permute-done((bf16[256,768]{1,0:T(8,128)(2,1)S(1)}, bf16[256,768]{1,0:T(8,128)(2,1)S(1)}, u32[]{:S(2)}, u32[]{:S(2)}) %collective-permute-start.81) | collective-permute-done | bytes 393248 | tf_op jit(solution)/shard_map/ppermute | solution.py:25
  615.3 5.0 collective-permute-start.47
  624.2 30.5 %reduce-scatter.26.cloned.1.call-done = bf16[1,768,768]{2,1,0:T(8,128)(2,1)} async-done(((bf16[2,768,768]{2,1,0:T(8,128)(2,1)}), bf16[1,768,768]{2,1,0:T(8,128)(2,1)}) %reduce-scatter.26.cloned.1.call-update) | async-done | bytes 1179664 | tf_op jit(solution)/shard_map/reduce_scatter | solution.py:372
  670.9 9.2 all-reduce.9
  686.6 12.6 %all-reduce.8 = (bf16[192]{0:T(256)(128)(2,1)}, bf16[192]{0:T(256)(128)(2,1)}, bf16[768]{0:T(1024)(128)(2,1)}, bf16[768]{0:T(1024)(128)(2,1)}) all-reduce(bf16[192]{0:T(256)(128)(2,1)} %fusion.102, bf16[192]{0:T(256)(128)(2,1)} %fusion.103, ...), channel_id=13, replica_groups=mesh['section'=2,'dp'=4,'mp'=4] {'dp'}, use_global_device_ids=true, to_apply=%region_52.53.clone | all-reduce | flops 1920 | bytes 7680
  710.7 111.6 %reduce-scatter.28.cloned.1.call-done = f32[48,4]{1,0:T(8,128)} async-done(((f32[768,4]{1,0:T(8,128)}), f32[48,4]{1,0:T(8,128)}) %reduce-scatter.28.cloned.1.call-update) | async-done | bytes 784
  827.8 17.2 %reduce-scatter.32.cloned.1.call-done = bf16[192,192]{1,0:T(8,128)(2,1)} async-done(((bf16[768,192]{1,0:T(8,128)(2,1)}), bf16[192,192]{1,0:T(8,128)(2,1)}) %reduce-scatter.32.cloned.1.call-update) | async-done | bytes 73744
  846.6 24.9 %reduce-scatter.30.cloned.1.call-done = bf16[192,576]{1,0:T(8,128)(2,1)} async-done(((bf16[768,576]{1,0:T(8,128)(2,1)}), bf16[192,576]{1,0:T(8,128)(2,1)}) %reduce-scatter.30.cloned.1.call-update) | async-done | bytes 221200
  875.1 26.7 %reduce-scatter.34.cloned.1.call-done = bf16[192,768]{1,0:T(8,128)(2,1)} async-done(((bf16[768,768]{1,0:T(8,128)(2,1)}), bf16[192,768]{1,0:T(8,128)(2,1)}) %reduce-scatter.34.cloned.1.call-update) | async-done | bytes 294928
  904.0 27.9 %reduce-scatter.24.cloned.1.call-done = bf16[192,768]{1,0:T(8,128)(2,1)} async-done(((bf16[768,768]{1,0:T(8,128)(2,1)}), bf16[192,768]{1,0:T(8,128)(2,1)}) %reduce-scatter.24.cloned.1.call-update) | async-done | bytes 294928 | tf_op jit(solution)/shard_map/reduce_scatter | solution.py:375
  (925 shorter events, 253.7 us)
Async XLA Ops:
  7.2 56.6 %all-gather.17.cloned.1.call-start = ((), (), s32[]{:S(2)}) async-start(), calls=%async_computation.14 | async-start | bytes 2949120 | tf_op jit(solution)/shard_map/all_gather | solution.py:317
  32.4 74.7 %all-gather.19.cloned.1.call-start = ((), (), s32[]{:S(2)}) async-start(), calls=%async_computation.15 | async-start | bytes 1474560 | tf_op jit(solution)/shard_map/all_gather | solution.py:316
  33.1 102.6 %all-gather.23.cloned.1.call-start = ((), (), s32[]{:S(2)}) async-start(), calls=%async_computation.17 | async-start | bytes 1474560 | tf_op jit(solution)/shard_map/all_gather | solution.py:316
  33.3 18.8 %collective-permute-start = (bf16[256,768]{1,0:T(8,128)(2,1)S(1)}, bf16[256,768]{1,0:T(8,128)(2,1)S(1)}, u32[]{:S(2)}, u32[]{:S(2)}) collective-permute-start(bf16[256,768]{1,0:T(8,128)(2,1)S(1)} %constant_dynamic-slice_fusion.11), channel_id=1, source_target_pairs={{0,2},{1,3},{18,16},{19,17},{4,6},{5,7},{22,20},{23,21},{8,10},{9,... | collective-permute-start | bytes 1179656 | tf_op jit(solution)/shard_map/ppermute | solution.py:287
  36.8 15.2 %collective-permute-start.1 = (f32[768]{0:T(1024)S(1)}, f32[768]{0:T(1024)S(1)}, u32[]{:S(2)}, u32[]{:S(2)}) collective-permute-start(f32[768]{0:T(1024)S(1)} %reduce.6), channel_id=1, source_target_pairs={{0,16},{16,0},{1,17},{17,1},{2,18},{18,2},{3,19},{19,3},{4,20},{20... | collective-permute-start | bytes 9224 | tf_op jit(solution)/shard_map/ppermute | solution.py:21
  36.9 15.1 %collective-permute-start.2 = (f32[768]{0:T(1024)S(1)}, f32[768]{0:T(1024)S(1)}, u32[]{:S(2)}, u32[]{:S(2)}) collective-permute-start(f32[768]{0:T(1024)S(1)} %reduce.7), channel_id=1, source_target_pairs={{0,16},{16,0},{1,17},{17,1},{2,18},{18,2},{3,19},{19,3},{4,20},{20... | collective-permute-start | bytes 9224 | tf_op jit(solution)/shard_map/ppermute | solution.py:21
  50.6 71.2 %collective-permute-start.9 = (f32[192]{0:T(256)}, f32[192]{0:T(256)}, u32[]{:S(2)}, u32[]{:S(2)}) collective-permute-start(f32[192]{0:T(256)} %bitcast.23), channel_id=1, source_target_pairs={{0,16},{16,0},{1,17},{17,1},{2,18},{18,2},{3,19},{19,3},{4,20},{20... | collective-permute-start | bytes 2312 | tf_op jit(solution)/shard_map/ppermute | solution.py:21
  50.6 73.7 %collective-permute-start.10 = (f32[192]{0:T(256)}, f32[192]{0:T(256)}, u32[]{:S(2)}, u32[]{:S(2)}) collective-permute-start(f32[192]{0:T(256)} %bitcast.26), channel_id=1, source_target_pairs={{0,16},{16,0},{1,17},{17,1},{2,18},{18,2},{3,19},{19,3},{4,20},{20... | collective-permute-start | bytes 2312 | tf_op jit(solution)/shard_map/ppermute | solution.py:21
  51.1 121.3 %all-gather.21.cloned.1.call-start = ((), (), s32[]{:S(2)}) async-start(), calls=%async_computation.16 | async-start | bytes 3538944 | tf_op jit(solution)/shard_map/all_gather | solution.py:317
  53.6 50.7 %collective-permute-start.4 = (bf16[256,768]{1,0:T(8,128)(2,1)}, bf16[256,768]{1,0:T(8,128)(2,1)}, u32[]{:S(2)}, u32[]{:S(2)}) collective-permute-start(bf16[256,768]{1,0:T(8,128)(2,1)} %fusion.43), channel_id=1, source_target_pairs={{0,1},{1,0},{2,3},{3,2},{4,5},{5,4},{6,7},{7,6},{8,9},{9,8},{10,11... | collective-permute-start | bytes 1179656 | tf_op jit(solution)/shard_map/ppermute | solution.py:25
  66.8 40.5 %collective-permute-start.6 = (bf16[768,576]{0,1:T(8,128)(2,1)}, bf16[768,576]{0,1:T(8,128)(2,1)}, u32[]{:S(2)}, u32[]{:S(2)}) collective-permute-start(bf16[768,576]{0,1:T(8,128)(2,1)} %bitcast.280), channel_id=1, source_target_pairs={{0,16},{16,0},{1,17},{17,1},{2,18},{18,2},{3,19},{19,3},{4,20},{20... | collective-permute-start | bytes 2654216 | tf_op jit(solution)/shard_map/ppermute | solution.py:21
  107.1 102.9 %all-gather.25.cloned.1.call-start = ((), (), s32[]{:S(2)}) async-start(), calls=%async_computation.18 | async-start | bytes 3538944 | tf_op jit(solution)/shard_map/all_gather | solution.py:317
  107.2 19.7 %collective-permute-start.11 = (bf16[192,768]{1,0:T(8,128)(2,1)S(1)}, bf16[192,768]{1,0:T(8,128)(2,1)S(1)}, u32[]{:S(2)}, u32[]{:S(2)}) collective-permute-start(bf16[192,768]{1,0:T(8,128)(2,1)S(1)} %dynamic-slice_bitcast_fusion.2), channel_id=1, source_target_pairs={{0,16},{16,0},{1,17},{17,1},{2,18},{18,2},{3,19},{19,3},{4,20},{20... | collective-permute-start | bytes 884744 | tf_op jit(solution)/shard_map/ppermute | solution.py:21
  129.1 10.4 %collective-permute-start.13 = (bf16[256,768]{1,0:T(8,128)(2,1)}, bf16[256,768]{1,0:T(8,128)(2,1)S(1)}, u32[]{:S(2)}, u32[]{:S(2)}) collective-permute-start(bf16[256,768]{1,0:T(8,128)(2,1)} %get-tuple-element.179), channel_id=1, source_target_pairs={{0,16},{16,0},{1,17},{17,1},{2,18},{18,2},{3,19},{19,3},{4,20},{20... | collective-permute-start | bytes 1179656 | tf_op jit(solution)/shard_map/ppermute | solution.py:21
  138.2 469.7 %reduce-scatter.20.cloned.1.call-start = ((), (), s32[]{:S(2)}) async-start(), calls=%async_computation.10 | async-start | bytes 884736 | tf_op jit(solution)/shard_map/reduce_scatter | solution.py:372
  140.6 11.5 %collective-permute-start.14 = (bf16[256,768]{1,0:T(8,128)(2,1)S(1)}, bf16[256,768]{1,0:T(8,128)(2,1)S(1)}, u32[]{:S(2)}, u32[]{:S(2)}) collective-permute-start(bf16[256,768]{1,0:T(8,128)(2,1)S(1)} %add_convert_fusion.14), channel_id=1, source_target_pairs={{0,1},{1,0},{2,3},{3,2},{4,5},{5,4},{6,7},{7,6},{8,9},{9,8},{10,11... | collective-permute-start | bytes 1179656 | tf_op jit(solution)/shard_map/ppermute | solution.py:25
  174.7 37.7 %collective-permute-start.20 = (bf16[768,768]{1,0:T(8,128)(2,1)}, bf16[768,768]{1,0:T(8,128)(2,1)}, u32[]{:S(2)}, u32[]{:S(2)}) collective-permute-start(bf16[768,768]{1,0:T(8,128)(2,1)} %dynamic-slice_bitcast_fusion.1), channel_id=1, source_target_pairs={{0,16},{16,0},{1,17},{17,1},{2,18},{18,2},{3,19},{19,3},{4,20},{20... | collective-permute-start | bytes 3538952 | tf_op jit(solution)/shard_map/ppermute | solution.py:21
  175.0 11.6 %collective-permute-start.18 = (bf16[256,768]{1,0:T(8,128)(2,1)S(1)}, bf16[256,768]{1,0:T(8,128)(2,1)S(1)}, u32[]{:S(2)}, u32[]{:S(2)}) collective-permute-start(bf16[256,768]{1,0:T(8,128)(2,1)S(1)} %add_convert_fusion.13), channel_id=1, source_target_pairs={{0,1},{1,0},{2,3},{3,2},{4,5},{5,4},{6,7},{7,6},{8,9},{9,8},{10,11... | collective-permute-start | bytes 1179656 | tf_op jit(solution)/shard_map/ppermute | solution.py:25
  176.5 35.9 %collective-permute-start.17 = (bf16[256,768]{1,0:T(8,128)(2,1)S(1)}, bf16[256,768]{1,0:T(8,128)(2,1)}, u32[]{:S(2)}, u32[]{:S(2)}) collective-permute-start(bf16[256,768]{1,0:T(8,128)(2,1)S(1)} %add_convert_fusion.13), channel_id=1, source_target_pairs={{0,16},{16,0},{1,17},{17,1},{2,18},{18,2},{3,19},{19,3},{4,20},{20... | collective-permute-start | bytes 1179656 | tf_op jit(solution)/shard_map/ppermute | solution.py:21
  186.6 25.8 %collective-permute-start.19 = (bf16[256,768]{1,0:T(8,128)(2,1)S(1)}, bf16[256,768]{1,0:T(8,128)(2,1)}, u32[]{:S(2)}, u32[]{:S(2)}) collective-permute-start(bf16[256,768]{1,0:T(8,128)(2,1)S(1)} %collective-permute-done.18), channel_id=1, source_target_pairs={{0,16},{16,0},{1,17},{17,1},{2,18},{18,2},{3,19},{19,3},{4,20},{20... | collective-permute-start | bytes 1179656 | tf_op jit(solution)/shard_map/ppermute | solution.py:21
  191.0 35.0 %collective-permute-start.23 = (f32[768]{0:T(1024)S(1)}, f32[768]{0:T(1024)S(1)}, u32[]{:S(2)}, u32[]{:S(2)}) collective-permute-start(f32[768]{0:T(1024)S(1)} %get-tuple-element.122), channel_id=1, source_target_pairs={{0,16},{16,0},{1,17},{17,1},{2,18},{18,2},{3,19},{19,3},{4,20},{20... | collective-permute-start | bytes 9224 | tf_op jit(solution)/shard_map/ppermute | solution.py:21
  195.5 32.9 %collective-permute-start.24 = (f32[768]{0:T(1024)S(1)}, f32[768]{0:T(1024)S(1)}, u32[]{:S(2)}, u32[]{:S(2)}) collective-permute-start(f32[768]{0:T(1024)S(1)} %get-tuple-element.124), channel_id=1, source_target_pairs={{0,16},{16,0},{1,17},{17,1},{2,18},{18,2},{3,19},{19,3},{4,20},{20... | collective-permute-start | bytes 9224 | tf_op jit(solution)/shard_map/ppermute | solution.py:21
  212.4 18.3 %collective-permute-start.25 = (bf16[768,768]{1,0:T(8,128)(2,1)}, bf16[768,768]{1,0:T(8,128)(2,1)}, u32[]{:S(2)}, u32[]{:S(2)}) collective-permute-start(bf16[768,768]{1,0:T(8,128)(2,1)} %dynamic-slice_bitcast_fusion), channel_id=1, source_target_pairs={{0,16},{16,0},{1,17},{17,1},{2,18},{18,2},{3,19},{19,3},{4,20},{20... | collective-permute-start | bytes 3538952 | tf_op jit(solution)/shard_map/ppermute | solution.py:21
  234.9 7.6 collective-permute-start.49
  237.5 11.6 %collective-permute-start.28 = (bf16[256,768]{1,0:T(8,128)(2,1)S(1)}, bf16[256,768]{1,0:T(8,128)(2,1)S(1)}, u32[]{:S(2)}, u32[]{:S(2)}) collective-permute-start(bf16[256,768]{1,0:T(8,128)(2,1)S(1)} %add_convert_fusion.12), channel_id=1, source_target_pairs={{0,1},{1,0},{2,3},{3,2},{4,5},{5,4},{6,7},{7,6},{8,9},{9,8},{10,11... | collective-permute-start | bytes 1179656 | tf_op jit(solution)/shard_map/ppermute | solution.py:25
  250.5 10.8 %collective-permute-start.32 = (bf16[256,768]{1,0:T(8,128)(2,1)S(1)}, bf16[256,768]{1,0:T(8,128)(2,1)S(1)}, u32[]{:S(2)}, u32[]{:S(2)}) collective-permute-start(bf16[256,768]{1,0:T(8,128)(2,1)S(1)} %fusion.46), channel_id=1, source_target_pairs={{0,1},{1,0},{2,3},{3,2},{4,5},{5,4},{6,7},{7,6},{8,9},{9,8},{10,11... | collective-permute-start | bytes 1179656 | tf_op jit(solution)/shard_map/ppermute | solution.py:25
  252.3 9.0 collective-permute-start.31
  286.0 11.2 %collective-permute-start.38 = (bf16[256,768]{1,0:T(8,128)(2,1)S(1)}, bf16[256,768]{1,0:T(8,128)(2,1)S(1)}, u32[]{:S(2)}, u32[]{:S(2)}) collective-permute-start(bf16[256,768]{1,0:T(8,128)(2,1)S(1)} %add_convert_fusion.10), channel_id=1, source_target_pairs={{0,1},{1,0},{2,3},{3,2},{4,5},{5,4},{6,7},{7,6},{8,9},{9,8},{10,11... | collective-permute-start | bytes 1179656 | tf_op jit(solution)/shard_map/ppermute | solution.py:25
  298.6 12.1 %collective-permute-start.40 = (bf16[256,768]{1,0:T(8,128)(2,1)S(1)}, bf16[256,768]{1,0:T(8,128)(2,1)S(1)}, u32[]{:S(2)}, u32[]{:S(2)}) collective-permute-start(bf16[256,768]{1,0:T(8,128)(2,1)S(1)} %add_convert_fusion.9), channel_id=1, source_target_pairs={{0,1},{1,0},{2,3},{3,2},{4,5},{5,4},{6,7},{7,6},{8,9},{9,8},{10,11... | collective-permute-start | bytes 1179656 | tf_op jit(solution)/shard_map/ppermute | solution.py:25
  300.4 17.2 %collective-permute-start.51 = (bf16[256,768]{1,0:T(8,128)(2,1)}, bf16[256,768]{1,0:T(8,128)(2,1)}, u32[]{:S(2)}, u32[]{:S(2)}) collective-permute-start(bf16[256,768]{1,0:T(8,128)(2,1)} %get-tuple-element.240), channel_id=1, source_target_pairs={{0,1},{1,0},{2,3},{3,2},{4,5},{5,4},{6,7},{7,6},{8,9},{9,8},{10,11... | collective-permute-start | bytes 1179656 | tf_op jit(solution)/shard_map/ppermute | solution.py:25
  300.7 16.8 %collective-permute-start.39 = (bf16[256,768]{1,0:T(8,128)(2,1)S(1)}, bf16[256,768]{1,0:T(8,128)(2,1)S(1)}, u32[]{:S(2)}, u32[]{:S(2)}) collective-permute-start(bf16[256,768]{1,0:T(8,128)(2,1)S(1)} %add_convert_fusion.9), channel_id=1, source_target_pairs={{0,16},{16,0},{1,17},{17,1},{2,18},{18,2},{3,19},{19,3},{4,20},{20... | collective-permute-start | bytes 1179656 | tf_op jit(solution)/shard_map/ppermute | solution.py:21
  310.8 6.8 collective-permute-start.41
  310.8 24.5 %collective-permute-start.50 = (bf16[256,768]{1,0:T(8,128)(2,1)}, bf16[256,768]{1,0:T(8,128)(2,1)}, u32[]{:S(2)}, u32[]{:S(2)}) collective-permute-start(bf16[256,768]{1,0:T(8,128)(2,1)} %get-tuple-element.240), channel_id=1, source_target_pairs={{0,16},{16,0},{1,17},{17,1},{2,18},{18,2},{3,19},{19,3},{4,20},{20... | collective-permute-start | bytes 1179656 | tf_op jit(solution)/shard_map/ppermute | solution.py:21
  317.6 17.7 %collective-permute-start.52 = (bf16[256,768]{1,0:T(8,128)(2,1)}, bf16[256,768]{1,0:T(8,128)(2,1)}, u32[]{:S(2)}, u32[]{:S(2)}) collective-permute-start(bf16[256,768]{1,0:T(8,128)(2,1)} %collective-permute-done.51), channel_id=1, source_target_pairs={{0,16},{16,0},{1,17},{17,1},{2,18},{18,2},{3,19},{19,3},{4,20},{20... | collective-permute-start | bytes 1179656 | tf_op jit(solution)/shard_map/ppermute | solution.py:21
  333.5 9.7 %collective-permute-start.43 = (f32[2,2,2,256]{3,2,1,0:T(2,128)}, f32[2,2,2,256]{3,2,1,0:T(2,128)}, u32[]{:S(2)}, u32[]{:S(2)}) collective-permute-start(f32[2,2,2,256]{3,2,1,0:T(2,128)} %add.462), channel_id=1, source_target_pairs={{0,1},{1,0},{2,3},{3,2},{4,5},{5,4},{6,7},{7,6},{8,9},{9,8},{10,11... | collective-permute-start | bytes 24584 | tf_op jit(solution)/shard_map/ppermute | solution.py:25
  372.6 12.0 %collective-permute-start.57 = (bf16[256,768]{1,0:T(8,128)(2,1)S(1)}, bf16[256,768]{1,0:T(8,128)(2,1)S(1)}, u32[]{:S(2)}, u32[]{:S(2)}) collective-permute-start(bf16[256,768]{1,0:T(8,128)(2,1)S(1)} %add_convert_fusion.7), channel_id=1, source_target_pairs={{0,1},{1,0},{2,3},{3,2},{4,5},{5,4},{6,7},{7,6},{8,9},{9,8},{10,11... | collective-permute-start | bytes 1179656 | tf_op jit(solution)/shard_map/ppermute | solution.py:25
  373.0 12.8 %collective-permute-start.44 = (bf16[256,768]{1,0:T(8,128)(2,1)S(1)}, bf16[256,768]{1,0:T(8,128)(2,1)S(1)}, u32[]{:S(2)}, u32[]{:S(2)}) collective-permute-start(bf16[256,768]{1,0:T(8,128)(2,1)S(1)} %get-tuple-element.172), channel_id=1, source_target_pairs={{0,16},{16,0},{1,17},{17,1},{2,18},{18,2},{3,19},{19,3},{4,20},{20... | collective-permute-start | bytes 1179656 | tf_op jit(solution)/shard_map/ppermute | solution.py:21
  373.8 18.4 %collective-permute-start.46 = (bf16[256,768]{1,0:T(8,128)(2,1)S(1)}, bf16[256,768]{1,0:T(8,128)(2,1)S(1)}, u32[]{:S(2)}, u32[]{:S(2)}) collective-permute-start(bf16[256,768]{1,0:T(8,128)(2,1)S(1)} %add_convert_fusion.8), channel_id=1, source_target_pairs={{0,1},{1,0},{2,3},{3,2},{4,5},{5,4},{6,7},{7,6},{8,9},{9,8},{10,11... | collective-permute-start | bytes 1179656 | tf_op jit(solution)/shard_map/ppermute | solution.py:25
  393.6 10.3 %collective-permute-start.59 = (bf16[256,768]{1,0:T(8,128)(2,1)S(1)}, bf16[256,768]{1,0:T(8,128)(2,1)S(1)}, u32[]{:S(2)}, u32[]{:S(2)}) collective-permute-start(bf16[256,768]{1,0:T(8,128)(2,1)S(1)} %get-tuple-element.144), channel_id=1, source_target_pairs={{0,1},{1,0},{2,3},{3,2},{4,5},{5,4},{6,7},{7,6},{8,9},{9,8},{10,11... | collective-permute-start | bytes 1179656 | tf_op jit(solution)/shard_map/ppermute | solution.py:25
  394.0 9.9 %collective-permute-start.58 = (bf16[256,768]{1,0:T(8,128)(2,1)S(1)}, bf16[256,768]{1,0:T(8,128)(2,1)S(1)}, u32[]{:S(2)}, u32[]{:S(2)}) collective-permute-start(bf16[256,768]{1,0:T(8,128)(2,1)S(1)} %get-tuple-element.144), channel_id=1, source_target_pairs={{0,16},{16,0},{1,17},{17,1},{2,18},{18,2},{3,19},{19,3},{4,20},{20... | collective-permute-start | bytes 1179656 | tf_op jit(solution)/shard_map/ppermute | solution.py:21
  442.0 11.2 %collective-permute-start.65 = (bf16[256,768]{1,0:T(8,128)(2,1)S(1)}, bf16[256,768]{1,0:T(8,128)(2,1)S(1)}, u32[]{:S(2)}, u32[]{:S(2)}) collective-permute-start(bf16[256,768]{1,0:T(8,128)(2,1)S(1)} %add_convert_fusion.6), channel_id=1, source_target_pairs={{0,1},{1,0},{2,3},{3,2},{4,5},{5,4},{6,7},{7,6},{8,9},{9,8},{10,11... | collective-permute-start | bytes 1179656 | tf_op jit(solution)/shard_map/ppermute | solution.py:25
  455.5 10.3 %collective-permute-start.67 = (bf16[256,768]{1,0:T(8,128)(2,1)S(1)}, bf16[256,768]{1,0:T(8,128)(2,1)S(1)}, u32[]{:S(2)}, u32[]{:S(2)}) collective-permute-start(bf16[256,768]{1,0:T(8,128)(2,1)S(1)} %get-tuple-element.140), channel_id=1, source_target_pairs={{0,1},{1,0},{2,3},{3,2},{4,5},{5,4},{6,7},{7,6},{8,9},{9,8},{10,11... | collective-permute-start | bytes 1179656 | tf_op jit(solution)/shard_map/ppermute | solution.py:25
  455.8 10.0 %collective-permute-start.66 = (bf16[256,768]{1,0:T(8,128)(2,1)S(1)}, bf16[256,768]{1,0:T(8,128)(2,1)S(1)}, u32[]{:S(2)}, u32[]{:S(2)}) collective-permute-start(bf16[256,768]{1,0:T(8,128)(2,1)S(1)} %get-tuple-element.140), channel_id=1, source_target_pairs={{0,16},{16,0},{1,17},{17,1},{2,18},{18,2},{3,19},{19,3},{4,20},{20... | collective-permute-start | bytes 1179656 | tf_op jit(solution)/shard_map/ppermute | solution.py:21
  500.2 11.5 %collective-permute-start.73 = (bf16[256,768]{1,0:T(8,128)(2,1)S(1)}, bf16[256,768]{1,0:T(8,128)(2,1)S(1)}, u32[]{:S(2)}, u32[]{:S(2)}) collective-permute-start(bf16[256,768]{1,0:T(8,128)(2,1)S(1)} %add_convert_fusion.5), channel_id=1, source_target_pairs={{0,1},{1,0},{2,3},{3,2},{4,5},{5,4},{6,7},{7,6},{8,9},{9,8},{10,11... | collective-permute-start | bytes 1179656 | tf_op jit(solution)/shard_map/ppermute | solution.py:25
  514.0 10.6 %collective-permute-start.75 = (bf16[256,768]{1,0:T(8,128)(2,1)S(1)}, bf16[256,768]{1,0:T(8,128)(2,1)S(1)}, u32[]{:S(2)}, u32[]{:S(2)}) collective-permute-start(bf16[256,768]{1,0:T(8,128)(2,1)S(1)} %get-tuple-element.136), channel_id=1, source_target_pairs={{0,1},{1,0},{2,3},{3,2},{4,5},{5,4},{6,7},{7,6},{8,9},{9,8},{10,11... | collective-permute-start | bytes 1179656 | tf_op jit(solution)/shard_map/ppermute | solution.py:25
  514.4 10.3 %collective-permute-start.74 = (bf16[256,768]{1,0:T(8,128)(2,1)S(1)}, bf16[256,768]{1,0:T(8,128)(2,1)S(1)}, u32[]{:S(2)}, u32[]{:S(2)}) collective-permute-start(bf16[256,768]{1,0:T(8,128)(2,1)S(1)} %get-tuple-element.136), channel_id=1, source_target_pairs={{0,16},{16,0},{1,17},{17,1},{2,18},{18,2},{3,19},{19,3},{4,20},{20... | collective-permute-start | bytes 1179656 | tf_op jit(solution)/shard_map/ppermute | solution.py:21
  533.2 28.9 %collective-permute-start.90 = (bf16[192,768]{1,0:T(8,128)(2,1)}, bf16[192,768]{1,0:T(8,128)(2,1)}, u32[]{:S(2)}, u32[]{:S(2)}) collective-permute-start(bf16[192,768]{1,0:T(8,128)(2,1)} %get-tuple-element.271), channel_id=1, source_target_pairs={{0,16},{16,0},{1,17},{17,1},{2,18},{18,2},{3,19},{19,3},{4,20},{20... | collective-permute-start | bytes 884744 | tf_op jit(solution)/shard_map/ppermute | solution.py:21
  564.0 46.1 %reduce-scatter.18.cloned.1.call-start = ((), (), s32[]{:S(2)}) async-start(), calls=%async_computation.9 | async-start | bytes 2654208 | tf_op jit(solution)/shard_map/reduce_scatter | solution.py:372
  566.4 88.2 %reduce-scatter.26.cloned.1.call-start = ((), (), s32[]{:S(2)}) async-start(), calls=%async_computation.13 | async-start | bytes 3538944 | tf_op jit(solution)/shard_map/reduce_scatter | solution.py:372
  578.3 122.1 %reduce-scatter.22.cloned.1.call-start = ((), (), s32[]{:S(2)}) async-start(), calls=%async_computation.11 | async-start | bytes 3538944 | tf_op jit(solution)/shard_map/reduce_scatter | solution.py:372
  588.0 234.3 %reduce-scatter.28.cloned.1.call-start = ((), (), s32[]{:S(2)}) async-start(), calls=%async_computation.19 | async-start | bytes 417792
  592.9 11.5 %collective-permute-start.81 = (bf16[256,768]{1,0:T(8,128)(2,1)S(1)}, bf16[256,768]{1,0:T(8,128)(2,1)S(1)}, u32[]{:S(2)}, u32[]{:S(2)}) collective-permute-start(bf16[256,768]{1,0:T(8,128)(2,1)S(1)} %add_convert_fusion.4), channel_id=1, source_target_pairs={{0,1},{1,0},{2,3},{3,2},{4,5},{5,4},{6,7},{7,6},{8,9},{9,8},{10,11... | collective-permute-start | bytes 1179656 | tf_op jit(solution)/shard_map/ppermute | solution.py:25
  607.8 237.2 %reduce-scatter.32.cloned.1.call-start = ((), (), s32[]{:S(2)}) async-start(), calls=%async_computation.21 | async-start | bytes 491520
  609.8 261.8 %reduce-scatter.30.cloned.1.call-start = ((), (), s32[]{:S(2)}) async-start(), calls=%async_computation.20 | async-start | bytes 1228800
  612.4 289.3 %reduce-scatter.34.cloned.1.call-start = ((), (), s32[]{:S(2)}) async-start(), calls=%async_computation.22 | async-start | bytes 1474560
  612.5 44.7 %collective-permute-start.29 = (bf16[256,768]{1,0:T(8,128)(2,1)S(1)}, bf16[256,768]{1,0:T(8,128)(2,1)}, u32[]{:S(2)}, u32[]{:S(2)}) collective-permute-start(bf16[256,768]{1,0:T(8,128)(2,1)S(1)} %get-tuple-element.151), channel_id=1, source_target_pairs={{0,0},{1,1},{16,2},{17,3},{4,4},{5,5},{20,6},{21,7},{8,8},{9,9},{2... | collective-permute-start | bytes 1179656 | tf_op jit(solution)/shard_map/ppermute | solution.py:296
  614.0 43.2 %collective-permute-start.30 = (bf16[256,768]{1,0:T(8,128)(2,1)S(1)}, bf16[256,768]{1,0:T(8,128)(2,1)}, u32[]{:S(2)}, u32[]{:S(2)}) collective-permute-start(bf16[256,768]{1,0:T(8,128)(2,1)S(1)} %get-tuple-element.151), channel_id=1, source_target_pairs={{2,0},{3,1},{18,2},{19,3},{6,4},{7,5},{22,6},{23,7},{10,8},{11,9},... | collective-permute-start | bytes 1179656 | tf_op jit(solution)/shard_map/ppermute | solution.py:296
  615.3 41.9 %collective-permute-start.47 = (bf16[256,768]{1,0:T(8,128)(2,1)}, bf16[256,768]{1,0:T(8,128)(2,1)}, u32[]{:S(2)}, u32[]{:S(2)}) collective-permute-start(bf16[256,768]{1,0:T(8,128)(2,1)} %get-tuple-element.188), channel_id=1, source_target_pairs={{0,16},{1,17},{16,18},{17,19},{4,20},{5,21},{20,22},{21,23},{8,24}... | collective-permute-start | bytes 1179656 | tf_op jit(solution)/shard_map/ppermute | solution.py:296
  620.3 36.9 %collective-permute-start.48 = (bf16[256,768]{1,0:T(8,128)(2,1)}, bf16[256,768]{1,0:T(8,128)(2,1)}, u32[]{:S(2)}, u32[]{:S(2)}) collective-permute-start(bf16[256,768]{1,0:T(8,128)(2,1)} %get-tuple-element.188), channel_id=1, source_target_pairs={{2,16},{3,17},{18,18},{19,19},{6,20},{7,21},{22,22},{23,23},{10,24... | collective-permute-start | bytes 1179656 | tf_op jit(solution)/shard_map/ppermute | solution.py:296
  657.1 274.8 %reduce-scatter.24.cloned.1.call-start = ((), (), s32[]{:S(2)}) async-start(), calls=%async_computation.12 | async-start | bytes 1474560 | tf_op jit(solution)/shard_map/reduce_scatter | solution.py:375
  659.7 165.9 %collective-permute-start.84 = (bf16[256,768]{1,0:T(8,128)(2,1)S(1)}, bf16[256,768]{1,0:T(8,128)(2,1)}, u32[]{:S(2)}, u32[]{:S(2)}) collective-permute-start(bf16[256,768]{1,0:T(8,128)(2,1)S(1)} %copy-done.46), channel_id=1, source_target_pairs={{0,16},{1,17},{16,18},{17,19},{4,20},{5,21},{20,22},{21,23},{8,24}... | collective-permute-start | bytes 1179656 | tf_op jit(solution)/shard_map/ppermute | solution.py:296
  662.4 163.2 %collective-permute-start.85 = (bf16[256,768]{1,0:T(8,128)(2,1)S(1)}, bf16[256,768]{1,0:T(8,128)(2,1)}, u32[]{:S(2)}, u32[]{:S(2)}) collective-permute-start(bf16[256,768]{1,0:T(8,128)(2,1)S(1)} %copy-done.46), channel_id=1, source_target_pairs={{2,16},{3,17},{18,18},{19,19},{6,20},{7,21},{22,22},{23,23},{10,24... | collective-permute-start | bytes 1179656 | tf_op jit(solution)/shard_map/ppermute | solution.py:296
  705.2 120.4 %collective-permute-start.82 = (bf16[256,768]{1,0:T(8,128)(2,1)}, bf16[256,768]{1,0:T(8,128)(2,1)S(1)}, u32[]{:S(2)}, u32[]{:S(2)}) collective-permute-start(bf16[256,768]{1,0:T(8,128)(2,1)} %fusion.59), channel_id=1, source_target_pairs={{0,0},{1,1},{16,2},{17,3},{4,4},{5,5},{20,6},{21,7},{8,8},{9,9},{2... | collective-permute-start | bytes 1179656 | tf_op jit(solution)/shard_map/ppermute | solution.py:296
  706.9 118.7 %collective-permute-start.83 = (bf16[256,768]{1,0:T(8,128)(2,1)}, bf16[256,768]{1,0:T(8,128)(2,1)S(1)}, u32[]{:S(2)}, u32[]{:S(2)}) collective-permute-start(bf16[256,768]{1,0:T(8,128)(2,1)} %fusion.59), channel_id=1, source_target_pairs={{2,0},{3,1},{18,2},{19,3},{6,4},{7,5},{22,6},{23,7},{10,8},{11,9},... | collective-permute-start | bytes 1179656 | tf_op jit(solution)/shard_map/ppermute | solution.py:296
  (271 other events, 3336.1 us)
Sparse Core Ops, SparseCore 0:
  32.5 31.2 all-gather.16
  65.4 39.2 all-gather.18
  106.2 29.5 all-gather.22
  137.1 35.1 all-gather.20
  173.7 36.1 all-gather.24
  564.2 15.2 reduce-scatter.19
  581.8 28.2 reduce-scatter.17
  612.3 42.2 reduce-scatter.25
  657.0 39.0 reduce-scatter.21
  700.6 121.5 reduce-scatter.27
  825.2 19.6 reduce-scatter.31
  847.1 24.3 reduce-scatter.29
  874.0 27.7 reduce-scatter.33
  904.1 27.8 reduce-scatter.23

commit v2 on v1

v2 whole, which is shorter than its diff:
```python
from functools import partial

import jax
import jax.numpy as jnp
from jax import lax
from jax.experimental import pallas as pl
from jax.experimental.pallas import tpu as pltpu
from jax.sharding import PartitionSpec as P

D = 768
HEAD_DIM = 64
FF = 3072
MICRO = 2
LANES = 4
EPS = 1e-05
SCALE = HEAD_DIM ** (-0.5)
LOG2E = 1.4426950408889634
SQRT_HALF = 0.7071067811865476
INV_SQRT_2PI = 0.3989422804014327
BOTH = ("section", "mp")
Y_PAIRS = [[0, 2], [1, 3]]
QKV = 3 * D // LANES
UNITS = FF // LANES
TAIL = 16
F32 = jnp.float32
BF16 = jnp.bfloat16

VMEM = pl.BlockSpec(memory_space=pltpu.VMEM)
ANY = pl.BlockSpec(memory_space=pl.ANY)
PARAMS = pltpu.CompilerParams(vmem_limit_bytes=48 * 1024 * 1024)


def call(name, body, outs, ins, scratch=(), after=(), cost=None):
    count = len(ins)

    def kernel(*refs):
        body(*refs[:count], *refs[count + len(after) :])

    return pl.pallas_call(
        kernel,
        out_shape=tuple(jax.ShapeDtypeStruct(shape, kind) for shape, kind in outs),
        in_specs=[VMEM] * count + [ANY] * len(after),
        out_specs=(VMEM,) * len(outs),
        scratch_shapes=list(scratch),
        compiler_params=PARAMS,
        name=name,
        cost_estimate=cost,
    )(*ins, *after)


def work(flops, size):
    return pl.CostEstimate(flops=int(flops), bytes_accessed=int(size), transcendentals=0)


def nn(a, b):
    return jnp.dot(a, b, preferred_element_type=F32)


def nt(a, b):
    return lax.dot_general(a, b, (((1,), (1,)), ((), ())), preferred_element_type=F32)


def tn(a, b):
    return lax.dot_general(a, b, (((0,), (0,)), ((), ())), preferred_element_type=F32)


def to_rows(*columns):
    count = columns[0].shape[0]
    lane = lax.broadcasted_iota(jnp.int32, (count, 128), 1)
    tile = jnp.zeros((count, 128), F32)
    for place, column in enumerate(columns):
        tile = jnp.where(lane == place, column, tile)
    return tile.T[:8]


def to_columns(rows):
    return jnp.concatenate([rows, jnp.zeros((120, rows.shape[1]), F32)], axis=0).T


def split_three(values):
    high = values.astype(BF16)
    rest = values - high.astype(F32)
    middle = rest.astype(BF16)
    return high, middle, (rest - middle.astype(F32)).astype(BF16)


def encode(rows):
    return jnp.concatenate(split_three(rows), axis=1)


def decode(tail):
    tail = tail.astype(F32)
    count = tail.shape[1] // 3
    return tail[:, :count] + tail[:, count : 2 * count] + tail[:, 2 * count :]


def decode_vectors(tail):
    tail = tail.astype(F32)
    return jnp.concatenate(
        [jnp.sum(tail[0:3], axis=0, keepdims=True), jnp.sum(tail[3:6], axis=0, keepdims=True)],
        axis=0,
    )


def encode_vectors(first, second):
    return jnp.concatenate(
        [*split_three(first), *split_three(second), jnp.zeros((2, first.shape[1]), BF16)], axis=0
    )


def split_norm(values):
    mean = jnp.mean(values, axis=-1, keepdims=True)
    spread = jnp.mean(values * values, axis=-1, keepdims=True) - mean * mean
    scaled = lax.rsqrt(spread + EPS)
    return (values - mean) * scaled, scaled


def norm_back(values, gain, upstream):
    normal, scaled = split_norm(values)
    inner = upstream * gain
    one = jnp.mean(inner, axis=-1, keepdims=True)
    two = jnp.mean(inner * normal, axis=-1, keepdims=True)
    back = scaled * (inner - one - normal * two)
    return (
        back,
        jnp.sum(upstream * normal, axis=0, keepdims=True),
        jnp.sum(upstream, axis=0, keepdims=True),
    )


def vector_rows(first, second):
    return jnp.concatenate([first, second, jnp.zeros((6, first.shape[1]), F32)], axis=0)


def folded_vectors(mat, gain, bias):
    rows = jnp.concatenate(
        [*split_three(gain), *split_three(bias), jnp.zeros((10, gain.shape[1]), BF16)], axis=0
    )
    folded = nt(rows, mat)
    return encode_vectors(
        jnp.sum(folded[0:3], axis=0, keepdims=True), jnp.sum(folded[3:6], axis=0, keepdims=True)
    )


def core_swap(x):
    return lax.ppermute(x, "section", [(0, 1), (1, 0)])


def x_swap(x):
    return lax.ppermute(x, "mp", [(i, i ^ 1) for i in range(LANES)])


def y_swap(x):
    return lax.ppermute(x, "mp", [(i, i ^ 2) for i in range(LANES)])


def gather_rows(own):
    far = x_swap(own)
    return own, core_swap(own), far, core_swap(far)


def pair_sum_body(first, second, out):
    rows = out.shape[0] - TAIL
    out[:rows] = (first[:rows].astype(F32) + second[:rows].astype(F32)).astype(BF16)
    half = rows + TAIL // 2
    out[rows:half] = encode(decode(first[rows:half]) + decode(second[rows:half]))
    folded = decode_vectors(first[half:]) + decode_vectors(second[half:])
    out[half:] = encode_vectors(folded[0:1], folded[1:2])


def settle(own, mate, far, far_mate):
    got = core_swap(far_mate)
    if own.shape[0] % 256:
        sent = call("pair_sum", pair_sum_body, [(far.shape, BF16)], [far, got])[0]
    else:
        sent = (far.astype(F32) + got.astype(F32)).astype(BF16)
    return own, core_swap(mate), x_swap(sent)


def project_body(first, second, mat, out):
    size = first.shape[0]
    for place, piece in enumerate((first, second)):
        out[place * size : (place + 1) * size, :] = nn(piece[...], mat[:, :QKV]).astype(BF16)


def project(first, second, mat):
    count = 2 * first.shape[0]
    return call(
        "project",
        project_body,
        [((count, QKV), BF16)],
        [first, second, mat],
        cost=work(2 * count * D * QKV, 2 * count * (D + QKV) + 2 * D * D),
    )[0]


def split_heads(source, target, first, start, head_count):
    size = source.shape[0]
    for head in range(head_count):
        lanes = slice(first + head * HEAD_DIM, first + (head + 1) * HEAD_DIM)
        target[head, start : start + size, :] = source[:, lanes]


def attend_body(
    q_start, q_ref, near, far, labels, mat, gain, bias, o_ref, p_one, p_two, sum_ref, ks, vs
):
    head_count = QKV // (3 * HEAD_DIM)
    width = head_count * HEAD_DIM
    half = near.shape[0]
    for start, ref in ((0, near), (half, far)):
        split_heads(ref, ks, width, start, head_count)
        split_heads(ref, vs, 2 * width, start, head_count)
    out_mat = mat[:, QKV:]
    folded = folded_vectors(out_mat, gain[...], bias[...])
    size = half // 2
    key_labels = labels[0:1, :]
    for place, p_ref in enumerate((p_one, p_two)):
        rows = slice(place * size, (place + 1) * size)
        first = q_start + place * size
        allowed = to_columns(labels[:, first : first + size])[:, 0:1] == key_labels
        outs = []
        sums = []
        for head in range(head_count):
            query = q_ref[rows, head * HEAD_DIM : (head + 1) * HEAD_DIM]
            scores = jnp.where(allowed, nt(query, ks[head]), -1e30)
            peak = jnp.max(scores, axis=-1, keepdims=True)
            terms = jnp.exp2((scores - peak) * (SCALE * LOG2E))
            total = jnp.sum(terms, axis=-1, keepdims=True)
            outs.append(nn(terms.astype(BF16), vs[head]) / total)
            sums.append(peak * (SCALE * LOG2E) + jnp.log(total) * LOG2E)
        out = jnp.concatenate(outs, axis=1)
        o_ref[rows, :] = out
        lane = lax.broadcasted_iota(jnp.int32, (size, 128), 1)
        tile = jnp.zeros((size, 128), F32)
        for spot, column in enumerate(sums):
            tile = jnp.where(lane == spot, column, tile)
        sum_ref[rows, :] = tile
        p_ref[:size] = nt((out * gain[...]).astype(BF16), out_mat).astype(BF16)
        stats = to_rows(
            jnp.sum(out, axis=-1, keepdims=True), jnp.sum(out * out, axis=-1, keepdims=True)
        )
        p_ref[size : size + TAIL // 2] = encode(stats)
        p_ref[size + TAIL // 2 :] = folded


def attend(q_start, queries, near, far, labels, mat, gain, bias, after=()):
    count, keys = queries.shape[0], 2 * near.shape[0]
    heads = QKV // (3 * HEAD_DIM)
    width = heads * HEAD_DIM
    by_head = pltpu.VMEM((heads, keys, HEAD_DIM), BF16)
    payload = ((count // 2 + TAIL, D), BF16)
    return call(
        "attend",
        partial(attend_body, q_start),
        [((count, width), F32), payload, payload, ((count, 128), F32)],
        [queries, near, far, labels, mat, gain, bias],
        [by_head, by_head],
        after,
        work(2 * count * (2 * keys * width * 4 + width * D), 4 * count * D),
    )


def attend_back_body(
    near, far, do_near, do_far, sum_near, sum_far, labels, near_out, far_out,
    qs, ks, vs, grads, dqs, dks, dvs, sums,
):
    head_count = QKV // (3 * HEAD_DIM)
    width = head_count * HEAD_DIM
    half = near.shape[0]
    for start, ref, grad in ((0, near, do_near), (half, far, do_far)):
        split_heads(ref, qs, 0, start, head_count)
        split_heads(ref, ks, width, start, head_count)
        split_heads(ref, vs, 2 * width, start, head_count)
        split_heads(grad, grads, 0, start, head_count)
    sums[:half] = sum_near[...]
    sums[half:] = sum_far[...]
    dks[...] = jnp.zeros_like(dks)
    dvs[...] = jnp.zeros_like(dvs)
    key_labels = labels[0:1, :]
    size = half // 2

    def block(index, carry):
        rows = pl.ds(pl.multiple_of(index * size, size), size)
        allowed = to_columns(labels[:, rows])[:, 0:1] == key_labels
        for head in range(head_count):
            query, grad = qs[head, rows, :], grads[head, rows, :]
            scores = jnp.where(allowed, nt(query, ks[head]), -1e30)
            prob = jnp.exp2(scores * (SCALE * LOG2E) - sums[rows, head : head + 1])
            prob_grad = nt(grad, vs[head])
            delta = jnp.sum(prob * prob_grad, axis=-1, keepdims=True)
            score_grad = (prob * (prob_grad - delta)).astype(BF16)
            dqs[head, rows, :] = nn(score_grad, ks[head]) * SCALE
            dks[head] += tn(query, score_grad)
            dvs[head] += tn(grad, prob.astype(BF16))
        return carry

    lax.fori_loop(0, 4, block, 0)
    for start, out in ((0, near_out), (half, far_out)):
        rows = slice(start, start + half)
        heads = range(head_count)
        out[...] = jnp.concatenate(
            [dqs[head, rows, :].astype(BF16) for head in heads]
            + [(dks[head, :, rows].T * SCALE).astype(BF16) for head in heads]
            + [dvs[head, :, rows].T.astype(BF16) for head in heads],
            axis=1,
        )


def attend_back(near, far, do_near, do_far, sum_near, sum_far, labels, after=()):
    half, width = do_near.shape
    keys = 2 * half
    heads = width // HEAD_DIM
    by_head = pltpu.VMEM((heads, keys, HEAD_DIM), BF16)
    turned = pltpu.VMEM((heads, HEAD_DIM, keys), F32)
    return call(
        "attend_back",
        attend_back_body,
        [(near.shape, BF16)] * 2,
        [near, far, do_near, do_far, sum_near, sum_far, labels],
        [by_head] * 4
        + [pltpu.VMEM((heads, keys, HEAD_DIM), F32), turned, turned, pltpu.VMEM((keys, 128), F32)],
        after,
        work(2 * keys * keys * width * 5 * 3, 8 * keys * D),
    )


def gelu_parts(x):
    spread = 0.5 + 0.5 * lax.erf(x * SQRT_HALF)
    return x * spread, spread


def feed_body(with_back, *refs):
    if with_back:
        one, two, back_one, back_two, up, down, gain, bias, f_ref, p_one, p_two, s_one, s_two = refs
    else:
        one, two, up, down, gain, bias, f_ref, p_one, p_two = refs
        back_one = back_two = s_one = s_two = None
    size = one.shape[0]
    folded = folded_vectors(down[...], gain[...], bias[...])
    for place, (piece, p_ref, back, s_ref) in enumerate(
        ((one, p_one, back_one, s_one), (two, p_two, back_two, s_two))
    ):
        rows = slice(place * size, (place + 1) * size)
        pre = nn(piece[...], up[...])
        f_ref[rows, :] = pre
        act, _ = gelu_parts(pre)
        p_ref[:size] = nt((act * gain[...]).astype(BF16), down[...]).astype(BF16)
        columns = [
            jnp.sum(act, axis=-1, keepdims=True),
            jnp.sum(act * act, axis=-1, keepdims=True),
        ]
        p_ref[size : size + TAIL // 2] = encode(to_rows(*columns))
        p_ref[size + TAIL // 2 :] = folded
        if with_back:
            inner = nn(back[...], down[...]) * gain[...]
            columns.append(jnp.sum(inner, axis=-1, keepdims=True))
            columns.append(jnp.sum(inner * act, axis=-1, keepdims=True))
            s_ref[...] = to_rows(*columns)


def feed(pieces, backs, up, down, gain, bias, after=()):
    size = pieces[0].shape[0]
    outs = [((2 * size, UNITS), F32)] + [((size + TAIL, D), BF16)] * 2
    if backs:
        outs += [((8, size), F32)] * 2
    return call(
        "feed",
        partial(feed_body, bool(backs)),
        outs,
        [*pieces, *backs, up, down, gain, bias],
        after=after,
        cost=work(2 * 2 * size * D * UNITS * 4, 8 * size * D * 4),
    )


def feed_back_body(with_stats, *refs):
    if with_stats:
        one, two, s_one, s_two, *refs = refs
    else:
        one, two, *refs = refs
        s_one = s_two = None
    f_ref, gain, bias, up, down, df_ref, n_ref, p_one, p_two, vec_ref = refs
    size = p_one.shape[0]
    gain_grad = jnp.zeros((1, UNITS), F32)
    bias_grad = jnp.zeros((1, UNITS), F32)
    for place, (piece, s_ref, p_ref) in enumerate(((one, s_one, p_one), (two, s_two, p_two))):
        rows = slice(place * size, (place + 1) * size)
        upstream = nn(piece[:size], down[...])
        pre = f_ref[rows, :]
        stats = s_ref[...] if with_stats else decode(piece[size : size + TAIL // 2])
        columns = to_columns(stats)
        mean, scaled, first, second = (columns[:, i : i + 1] for i in range(4))
        act, spread = gelu_parts(pre)
        normal = (act - mean) * scaled
        act_grad = scaled * (upstream * gain[...] - first - normal * second)
        slope = spread + pre * (jnp.exp(-0.5 * pre * pre) * INV_SQRT_2PI)
        pre_grad = (act_grad * slope).astype(BF16)
        df_ref[rows, :] = pre_grad
        n_ref[rows, :] = (normal * gain[...] + bias[...]).astype(BF16)
        p_ref[...] = nt(pre_grad, up[...]).astype(BF16)
        gain_grad += jnp.sum(upstream * normal, axis=0, keepdims=True)
        bias_grad += jnp.sum(upstream, axis=0, keepdims=True)
    vec_ref[...] = vector_rows(gain_grad, bias_grad)


def feed_back(pieces, stats, pre, gain, bias, up, down, after=()):
    count = pre.shape[0]
    size = count // 2
    return call(
        "feed_back",
        partial(feed_back_body, bool(stats)),
        [((count, UNITS), BF16)] * 2 + [((size, D), BF16)] * 2 + [((8, UNITS), F32)],
        [*pieces, *stats, pre, gain, bias, up, down],
        after=after,
        cost=work(2 * count * D * UNITS * 4, 8 * count * D),
    )


def grads_body(pieces, halves, size, *refs):
    out = refs[-1]
    place = 0
    column = 0
    for left_count, right_count in zip(pieces, halves):
        left = refs[place : place + left_count]
        right = refs[place + left_count : place + left_count + right_count]
        place += left_count + right_count
        width = right[0].shape[1]
        per = left_count // right_count
        total = None
        for index, piece in enumerate(left):
            start = (index % per) * size
            term = tn(piece[:size], right[index // per][start : start + size, :])
            total = term if total is None else total + term
        out[:, column : column + width] = total.astype(BF16)
        column += width


def grads_of(*pairs, after=()):
    pieces = tuple(len(left) for left, _ in pairs)
    halves = tuple(len(right) for _, right in pairs)
    size = pairs[0][1][0].shape[0] // 2
    args = [item for left, right in pairs for item in (*left, *right)]
    width = sum(right[0].shape[1] for _, right in pairs)
    return call(
        "grads",
        partial(grads_body, pieces, halves, size),
        [((D, width), BF16)],
        args,
        after=after,
        cost=work(2 * 4 * size * D * width, 8 * size * (D + width)),
    )[0]


def inner_back_body(one, two, o_ref, gain, bias, mat, do_ref, u_ref, vec_ref):
    size = o_ref.shape[0] // 2
    gain_grad = jnp.zeros((1, o_ref.shape[1]), F32)
    bias_grad = jnp.zeros((1, o_ref.shape[1]), F32)
    out_mat = mat[:, QKV:]
    for place, piece in enumerate((one, two)):
        rows = slice(place * size, (place + 1) * size)
        upstream = nn(piece[:size], out_mat)
        columns = to_columns(decode(piece[size : size + TAIL // 2]))
        mean, scaled, first, second = (columns[:, i : i + 1] for i in range(4))
        normal = (o_ref[rows, :] - mean) * scaled
        back = scaled * (upstream * gain[...] - first - normal * second)
        do_ref[rows, :] = back.astype(BF16)
        u_ref[rows, :] = (normal * gain[...] + bias[...]).astype(BF16)
        gain_grad += jnp.sum(upstream * normal, axis=0, keepdims=True)
        bias_grad += jnp.sum(upstream, axis=0, keepdims=True)
    vec_ref[...] = vector_rows(gain_grad, bias_grad)


def inner_back(pieces, out, gain, bias, mat, after=()):
    count, width = out.shape
    return call(
        "inner_back",
        inner_back_body,
        [((count, width), BF16)] * 2 + [((8, width), F32)],
        [*pieces, out, gain, bias, mat],
        after=after,
        cost=work(2 * count * D * width, 4 * count * D),
    )


def unproject_body(rows, mat, p_one, p_two):
    size = p_one.shape[0]
    for place, p_ref in enumerate((p_one, p_two)):
        p_ref[...] = nt(rows[place * size : (place + 1) * size], mat[:, :QKV]).astype(BF16)


def unproject(rows, mat, after=()):
    count = rows.shape[0]
    return call(
        "unproject",
        unproject_body,
        [((count // 2, D), BF16)] * 2,
        [rows, mat],
        after=after,
        cost=work(2 * count * D * QKV, 4 * count * D),
    )


def branch_of(own, mate, far, feature_count):
    rows = own.shape[0] - TAIL
    half = rows + TAIL // 2
    pieces = (own, mate, far)
    product = sum(piece[:rows].astype(F32) for piece in pieces)
    stats = sum(decode(piece[rows:half]) for piece in pieces) / feature_count
    folded = sum(decode_vectors(piece[half:]) for piece in pieces)
    mean = stats[0:1]
    scaled = lax.rsqrt(stats[1:2] - mean * mean + EPS)
    kept = jnp.concatenate([mean, scaled, jnp.zeros((6, rows), F32)], axis=0)
    columns = to_columns(kept)
    branch = columns[:, 1:2] * (product - columns[:, 0:1] * folded[0:1])
    return branch, folded[1:2], folded[0:1], kept


def enter_body(x_ref, gain, bias, h_ref):
    normal, _ = split_norm(x_ref[...].astype(F32))
    h_ref[...] = (normal * gain[...] + bias[...]).astype(BF16)


def enter(rows, gain, bias):
    return call("enter", enter_body, [(rows.shape, BF16)], [rows, gain, bias])[0]


def after_attend_body(x_ref, own, mate, far, gain, bias, x2_ref, z_ref, h_ref, fold_ref, kept_ref):
    branch, shift, folded, kept = branch_of(own, mate, far, D)
    mid = x_ref[...].astype(F32) + branch + shift
    x2_ref[...] = mid
    z_ref[...] = branch
    normal, _ = split_norm(mid)
    h_ref[...] = (normal * gain[...] + bias[...]).astype(BF16)
    fold_ref[...] = jnp.broadcast_to(folded, fold_ref.shape)
    kept_ref[...] = kept


def after_attend(x, pieces, gain, bias):
    rows = x.shape[0]
    return call(
        "after_attend",
        after_attend_body,
        [((rows, D), F32), ((rows, D), F32), ((rows, D), BF16), ((8, D), F32), ((8, rows), F32)],
        [x, *pieces, gain, bias],
    )


def mask_column(labels, rows):
    return (to_columns(labels[:, :rows])[:, 0:1] >= 0).astype(F32)


def after_feed_body(x2, own, mate, far, labels, gain, bias, y_ref, z_ref, h_ref, fold_ref, kept_ref):
    branch, shift, folded, kept = branch_of(own, mate, far, FF)
    out = (mask_column(labels, x2.shape[0]) * (x2[...] + branch + shift)).astype(BF16)
    y_ref[...] = out
    z_ref[...] = branch
    normal, _ = split_norm(out.astype(F32))
    h_ref[...] = (normal * gain[...] + bias[...]).astype(BF16)
    fold_ref[...] = jnp.broadcast_to(folded, fold_ref.shape)
    kept_ref[...] = kept


def after_feed(x2, pieces, labels, gain, bias):
    rows = x2.shape[0]
    return call(
        "after_feed",
        after_feed_body,
        [((rows, D), BF16), ((rows, D), F32), ((rows, D), BF16), ((8, D), F32), ((8, rows), F32)],
        [x2, *pieces, labels, gain, bias],
    )


def finish_feed_body(x2, own, mate, far, labels, y_ref):
    branch, shift, _, _ = branch_of(own, mate, far, FF)
    y_ref[...] = (mask_column(labels, x2.shape[0]) * (x2[...] + branch + shift)).astype(BF16)


def finish_feed(x2, pieces, labels):
    return call("finish_feed", finish_feed_body, [(x2.shape, BF16)], [x2, *pieces, labels])[0]


def payload_of(grad, branch, folded, kept, feature_count):
    sent = grad.astype(BF16)
    wide = sent.astype(F32)
    means = to_rows(
        jnp.sum(wide * folded, axis=-1, keepdims=True),
        jnp.sum(wide * branch, axis=-1, keepdims=True),
    )
    stats = jnp.concatenate([kept[0:2], means[0:2] / feature_count, kept[4:8]], axis=0)
    tail = jnp.concatenate([encode(stats), jnp.zeros((TAIL // 2, D), BF16)], axis=0)
    return jnp.concatenate([sent, tail], axis=0)


def feed_norm_back_body(
    own, mate, far, g_ref, labels, x2, gain, branch, folded, kept, dx_ref, out_ref, vec_ref
):
    upstream = own[...].astype(F32) + mate[...].astype(F32) + far[...].astype(F32)
    back, gain_grad, bias_grad = norm_back(x2[...], gain[...], upstream)
    total = mask_column(labels, x2.shape[0]) * g_ref[...].astype(F32) + back
    dx_ref[...] = total
    out_ref[...] = payload_of(total, branch[...], folded[0:1], kept[...], D)
    vec_ref[...] = vector_rows(gain_grad, bias_grad)


def feed_norm_back(pieces, grad, labels, x2, gain, branch, folded, kept):
    rows = x2.shape[0]
    return call(
        "feed_norm_back",
        feed_norm_back_body,
        [((rows, D), F32), ((rows + TAIL, D), BF16), ((8, D), F32)],
        [*pieces, grad, labels, x2, gain, branch, folded, kept],
    )


def first_norm_back_body(has_next, *refs):
    own, mate, far, dx2, x_ref, gain, *refs = refs
    upstream = own[...].astype(F32) + mate[...].astype(F32) + far[...].astype(F32)
    back, gain_grad, bias_grad = norm_back(x_ref[...].astype(F32), gain[...], upstream)
    total = (dx2[...] + back).astype(BF16)
    if has_next:
        labels, branch, folded, kept, g_ref, vec_ref, out_ref = refs
        masked = mask_column(labels, dx2.shape[0]) * total.astype(F32)
        out_ref[...] = payload_of(masked, branch[...], folded[0:1], kept[...], FF)
    else:
        g_ref, vec_ref = refs
    g_ref[...] = total
    vec_ref[...] = vector_rows(gain_grad, bias_grad)


def first_norm_back(pieces, dx2, x, gain, following=()):
    rows = x.shape[0]
    outs = [((rows, D), BF16), ((8, D), F32)]
    if following:
        outs.append(((rows + TAIL, D), BF16))
    return call(
        "first_norm_back",
        partial(first_norm_back_body, bool(following)),
        outs,
        [*pieces, dx2, x, gain, *following],
    )


def dp_scatter(parts):
    count = parts.shape[0]
    if count > 4:
        return lax.psum_scatter(parts, "dp", scatter_dimension=0, tiled=False)
    place = lax.axis_index("dp")
    total = lax.dynamic_index_in_dim(parts, place, 0, keepdims=False).astype(F32)
    for step in range(1, count):
        sent = lax.dynamic_index_in_dim(parts, (place + step) % count, 0, keepdims=False)
        got = lax.ppermute(sent, "dp", [(i, (i + step) % count) for i in range(count)])
        total += got.astype(F32)
    return total


def on_device(
    inputs,
    cotangent,
    doc_ids,
    norm_gain,
    norm_bias,
    w_query,
    w_key,
    w_value,
    inner_gain,
    inner_bias,
    w_output,
    feed_gain,
    feed_bias,
    w_up,
    middle_gain,
    middle_bias,
    w_down,
):
    core = lax.axis_index("section")
    lane = lax.axis_index("mp")
    lane_x = lane % 2
    lane_y = lane // 2
    count = lax.axis_size("dp")
    slice_len = inputs.shape[0] // MICRO
    rank = 2 * core + lane_x
    crossing = [(s * 4 + r, s * 4 + (r ^ 2)) for s in range(2) for r in range(4) if s == r // 2]
    returning = [(s * 4 + r, s * 4 + (r ^ 2)) for s in range(2) for r in range(4) if s != r // 2]

    def by_core(first, second):
        return jnp.where(core == 0, first, second)

    def rows_of(array, micro_index):
        return lax.dynamic_slice_in_dim(array, micro_index * slice_len, slice_len, 0)

    def own_slice(array):
        sent = lax.ppermute(rows_of(array, 1 - lane_y), BOTH, crossing)
        return jnp.where(core == lane_y, rows_of(array, lane_y), sent)

    def placed(pairs):
        stacked = jnp.stack([jnp.stack(pair) for pair in pairs], axis=1)
        sent = lax.ppermute(stacked, BOTH, returning)
        micros = jnp.stack(
            [jnp.where(lane_y == 0, stacked, sent), jnp.where(lane_y == 0, sent, stacked)], axis=2
        )
        other = core_swap(lax.dynamic_index_in_dim(micros, 1 - core, 0, keepdims=False))
        kept = lax.dynamic_index_in_dim(micros, core, 0, keepdims=False)
        held = jnp.where(core == lane_y, kept, other)
        return held.reshape(len(pairs), 1, MICRO * slice_len, D)

    label_grid = lax.dynamic_index_in_dim(
        doc_ids.reshape(LANES, MICRO, slice_len), lane_y, 1, keepdims=False
    )
    order = (rank, 2 * (1 - core) + lane_x, rank ^ 1, 2 * (1 - core) + (1 - lane_x))
    labels = jnp.concatenate(
        [lax.dynamic_index_in_dim(label_grid, item, 0, keepdims=False) for item in order]
    )
    labels = jnp.broadcast_to(labels.astype(F32)[None], (8, LANES * slice_len))

    first_block = jnp.concatenate([w_query[0], w_key[0], w_value[0], w_output[0].T], axis=1)
    up_block, down_block = w_up[0], w_down[0].T

    def fetch(block, layer):
        whole = lax.all_gather(block, "dp", axis=0, tiled=True)
        across = lax.ppermute(
            whole, BOTH, [(layer * 4 + r, (r // 2) * 4 + (r ^ 2)) for r in range(LANES)]
        )
        beside = lax.ppermute(
            whole, BOTH, [(layer * 4 + r, (r // 2) * 4 + r) for r in range(LANES)]
        )
        return jnp.where(core == lane_y, beside, across)

    lower_first = fetch(first_block, 0)
    lower_up, lower_down = fetch(up_block, 0), fetch(down_block, 0)
    upper_first = fetch(first_block, 1)
    upper_up, upper_down = fetch(up_block, 1), fetch(down_block, 1)

    outer_own = jnp.concatenate([norm_gain, norm_bias, feed_gain, feed_bias], axis=0)
    outer_other = core_swap(outer_own)
    split_own = jnp.concatenate([inner_gain, inner_bias, middle_gain, middle_bias], axis=1)
    split_far = y_swap(split_own)
    split_kept = jnp.where(lane_y == core, split_own, split_far)
    split_other = core_swap(jnp.where(lane_y == core, split_far, split_own))

    def small_of(outer, split):
        width = D // LANES
        return (
            [outer[i : i + 1] for i in range(4)],
            [
                split[:, :width],
                split[:, width : 2 * width],
                split[:, 2 * width : 2 * width + UNITS],
                split[:, 2 * width + UNITS :],
            ],
        )

    lower_outer, lower_split = small_of(
        by_core(outer_own, outer_other), by_core(split_kept, split_other)
    )
    upper_outer, upper_split = small_of(
        by_core(outer_other, outer_own), by_core(split_other, split_kept)
    )

    def attention(x, h, first, outer, split):
        pieces = gather_rows(h)
        near = project(pieces[0], pieces[1], first)
        far = project(pieces[2], pieces[3], first)
        half = 2 * slice_len
        o_far, p_far, p_far_mate, sum_far = attend(
            half, far, near, far, labels, first, split[0], split[1]
        )
        o_near, p_own, p_mate, sum_near = attend(
            0, near, near, far, labels, first, split[0], split[1], after=[p_far]
        )
        terms = settle(p_own, p_mate, p_far, p_far_mate)
        x2, branch, h2, folded, kept = after_attend(x, terms, outer[2], outer[3])
        state = (x, pieces, near, far, o_near, o_far, sum_near, sum_far, x2, branch, folded, kept)
        return x2, h2, state

    def attention_back(grad, sums, state, first, outer, split, following, after=()):
        x, pieces, near, far, o_near, o_far, sum_near, sum_far, x2, branch, folded, kept = state
        dx2, sent, feed_vec = feed_norm_back(
            sums, grad, labels, x2, outer[2], branch, folded, kept
        )
        backs = gather_rows(sent)
        do_near, u_near, vec_near = inner_back(backs[:2], o_near, split[0], split[1], first)
        do_far, u_far, vec_far = inner_back(backs[2:], o_far, split[0], split[1], first)
        dq_near, dq_far = attend_back(
            near, far, do_near, do_far, sum_near, sum_far, labels, after=after
        )
        p_far, p_far_mate = unproject(dq_far, first)
        p_own, p_mate = unproject(dq_near, first, after=[p_far])
        terms = settle(p_own, p_mate, p_far, p_far_mate)
        mat_grad = grads_of((pieces, (dq_near, dq_far)), (backs, (u_near, u_far)), after=[p_far])
        result = first_norm_back(terms, dx2, x, outer[0], following)
        return result, mat_grad, vec_near + vec_far, feed_vec

    lower_in = own_slice(inputs)
    upstream = own_slice(cotangent)
    masked = jnp.where(
        jnp.broadcast_to(labels[0, :slice_len, None], upstream.shape) >= 0,
        upstream,
        jnp.zeros_like(upstream),
    )
    top = gather_rows(masked)

    h = enter(lower_in, lower_outer[0], lower_outer[1])
    x2, h2, lower_state = attention(lower_in, h, lower_first, lower_outer, lower_split)
    lower_pieces = gather_rows(h2)
    f_near, p_own, p_mate = feed(lower_pieces[:2], (), lower_up, lower_down, *lower_split[2:])
    f_far, p_far, p_far_mate = feed(lower_pieces[2:], (), lower_up, lower_down, *lower_split[2:])
    lower_pre = (f_near, f_far)
    terms = settle(p_own, p_mate, p_far, p_far_mate)
    lower_out, lower_branch, h, lower_folded, lower_kept = after_feed(
        x2, terms, labels, upper_outer[0], upper_outer[1]
    )
    x2, h2, upper_state = attention(lower_out, h, upper_first, upper_outer, upper_split)
    upper_pieces = gather_rows(h2)
    f_near, p_own, p_mate, s_own, s_mate = feed(
        upper_pieces[:2], top[:2], upper_up, upper_down, *upper_split[2:]
    )
    f_far, p_far, p_far_mate, s_far, s_far_mate = feed(
        upper_pieces[2:], top[2:], upper_up, upper_down, *upper_split[2:]
    )
    upper_pre = (f_near, f_far)

    near_stats, far_stats = jnp.stack([s_own, s_mate]), jnp.stack([s_far, s_far_mate])
    stats = jnp.stack([near_stats, far_stats])
    got = core_swap(stats)
    stats = stats + jnp.stack([got[:, 1], got[:, 0]], axis=1)
    got = x_swap(stats)
    stats = (stats + jnp.stack([got[1], got[0]])) / FF
    mean = stats[:, :, 0:1]
    scaled = lax.rsqrt(stats[:, :, 1:2] - mean * mean + EPS)
    second = scaled * (stats[:, :, 3:4] - mean * stats[:, :, 2:3])
    stats = jnp.concatenate(
        [mean, scaled, stats[:, :, 2:3], second, jnp.zeros_like(stats[:, :, 4:])], axis=2
    )

    def feed_backward(pieces, rows, stat_pieces, pre, up, down, split):
        near_stats = [stat_pieces[0, 0], stat_pieces[0, 1]] if stat_pieces is not None else []
        far_stats = [stat_pieces[1, 0], stat_pieces[1, 1]] if stat_pieces is not None else []
        df_far, n_far, p_far, p_far_mate, vec_far = feed_back(
            pieces[2:], far_stats, pre[1], split[2], split[3], up, down
        )
        df_near, n_near, p_own, p_mate, vec_near = feed_back(
            pieces[:2], near_stats, pre[0], split[2], split[3], up, down, after=[p_far]
        )
        terms = settle(p_own, p_mate, p_far, p_far_mate)
        mat_grad = grads_of((rows, (df_near, df_far)), (pieces, (n_near, n_far)), after=[p_far])
        return terms, mat_grad, vec_near + vec_far

    sums, upper_feed_grad, upper_middle = feed_backward(
        top, upper_pieces, stats, upper_pre, upper_up, upper_down, upper_split
    )
    following = (labels, lower_branch, lower_folded, lower_kept)
    (upper_grad, upper_norm, sent), upper_first_grad, upper_inner, upper_feed = attention_back(
        upstream, sums, upper_state, upper_first, upper_outer, upper_split, following
    )
    upper_out = finish_feed(x2, settle(p_own, p_mate, p_far, p_far_mate), labels)

    backs = gather_rows(sent)
    sums, lower_feed_grad, lower_middle = feed_backward(
        backs, lower_pieces, None, lower_pre, lower_up, lower_down, lower_split
    )
    (lower_grad, lower_norm), lower_first_grad, lower_inner, lower_feed = attention_back(
        upper_grad, sums, lower_state, lower_first, lower_outer, lower_split, ()
    )

    layer_outputs, upper_grad_held = placed([(lower_out, upper_out), (upper_grad, upper_grad)])
    lower_grad_held = placed([(lower_grad, lower_grad)])[0]
    input_grads = by_core(lower_grad_held, upper_grad_held)

    def collect(grad):
        parts = grad.reshape(count, 2, D // count // 2, -1)
        kept = lax.dynamic_index_in_dim(parts, core, 1, keepdims=False)
        got = core_swap(lax.dynamic_index_in_dim(parts, 1 - core, 1, keepdims=False))
        both = jnp.stack([by_core(kept, got), by_core(got, kept)])
        line = lax.psum_scatter(
            both, "mp", scatter_dimension=0, axis_index_groups=Y_PAIRS, tiled=False
        )
        return lax.psum_scatter(line, "dp", scatter_dimension=0, tiled=False)

    upper_sum = jnp.concatenate([collect(upper_first_grad), collect(upper_feed_grad)], axis=1)
    lower_sum = jnp.concatenate([collect(lower_first_grad), collect(lower_feed_grad)], axis=1)
    sum_kept = by_core(lower_sum, upper_sum)
    sum_got = core_swap(by_core(upper_sum, lower_sum))
    summed = jnp.concatenate(
        [by_core(sum_kept, sum_got), by_core(sum_got, sum_kept)], axis=0
    ).astype(F32)
    width = D // LANES
    grad_query, grad_key, grad_value, grad_output, grad_up, grad_down = jnp.split(
        summed, [width, 2 * width, 3 * width, D, D + UNITS], axis=1
    )

    outer = jnp.concatenate([lower_norm[:2], lower_feed[:2], upper_norm[:2], upper_feed[:2]])
    split = jnp.stack(
        [
            jnp.concatenate([lower_inner[:2], lower_middle[:2]], axis=1),
            jnp.concatenate([upper_inner[:2], upper_middle[:2]], axis=1),
        ]
    )
    packed = jnp.concatenate([outer.reshape(-1), split.reshape(-1)])
    packed += y_swap(packed)
    outer = packed[: 8 * D].reshape(8, D)
    split = packed[8 * D :].reshape(2, 2, -1)
    outer += core_swap(outer)
    outer += x_swap(outer)

    def by_dest(items):
        return [item.reshape(-1, count, item.shape[-1] // count) for item in items]

    outer, inner, middle = by_dest([outer, split[:, :, :width], split[:, :, width:]])
    sizes = [item.shape[0] * item.shape[2] for item in (outer, inner, middle)]
    packed = jnp.concatenate(
        [item.transpose(1, 0, 2).reshape(count, -1) for item in (outer, inner, middle)], axis=1
    )
    packed = dp_scatter(packed)
    outer = packed[: sizes[0]].reshape(2, 4, LANES, -1)
    outer = lax.dynamic_index_in_dim(outer, core, 0, keepdims=False)
    outer = lax.dynamic_index_in_dim(outer, lane, 1, keepdims=False)
    split = packed[sizes[0] :]
    split = jnp.where(core == lane_y, split, core_swap(split))
    inner = lax.dynamic_index_in_dim(
        split[: sizes[1]].reshape(2, 2, -1), core, 0, keepdims=False
    )
    middle = lax.dynamic_index_in_dim(
        split[sizes[1] :].reshape(2, 2, -1), core, 0, keepdims=False
    )
    return (
        layer_outputs,
        input_grads,
        outer[0][None],
        outer[1][None],
        grad_query[None],
        grad_key[None],
        grad_value[None],
        inner[0][None],
        inner[1][None],
        grad_output.T[None],
        outer[2][None],
        outer[3][None],
        grad_up[None],
        middle[0][None],
        middle[1][None],
        grad_down.T[None],
    )


def solution(mesh):
    placed = (
        P(("dp", "mp"), None),
        P(("dp", "mp"), None),
        P("dp"),
        P("section", None),
        P("section", None),
        P("section", "dp", "mp"),
        P("section", "dp", "mp"),
        P("section", "dp", "mp"),
        P("section", "mp"),
        P("section", "mp"),
        P("section", "mp", "dp"),
        P("section", None),
        P("section", None),
        P("section", "dp", "mp"),
        P("section", "mp"),
        P("section", "mp"),
        P("section", "mp", "dp"),
    )
    return jax.shard_map(
        on_device,
        mesh=mesh,
        in_specs=placed,
        out_specs=(
            P("section", ("dp", "mp"), None),
            P("section", ("dp", "mp"), None),
            P("section", ("dp", "mp")),
            P("section", ("dp", "mp")),
            P("section", "dp", "mp"),
            P("section", "dp", "mp"),
            P("section", "dp", "mp"),
            P("section", ("mp", "dp")),
            P("section", ("mp", "dp")),
            P("section", "mp", "dp"),
            P("section", ("dp", "mp")),
            P("section", ("dp", "mp")),
            P("section", "dp", "mp"),
            P("section", ("mp", "dp")),
            P("section", ("mp", "dp")),
            P("section", "mp", "dp"),
        ),
        check_vma=False,
    )
```

time: 951 us -> 691 us (0.73)
  waiting for transfers between devices: 472 us -> 321 us
  matrix products: 124 us -> 0 us
  Pallas kernels: 0 us -> 123 us
  blocking collectives: 104 us -> 0 us
  other arithmetic: 86.8 us -> 42.1 us
  starting transfers between devices: 59.8 us -> 87.9 us
  local copies, waits for them, and re-layouts: 74.3 us -> 87.5 us
    unnamed x18 -> x11, waiting for transfers between devices: 181 us -> 1.52 us
    dot_general x36 -> x0, matrix products: 124 us -> none  [the longest x8 41.2 us: dot_plain(): return jnp.dot(first_mat, second_mat, preferred_element_type=jnp.float32)]
    pallas_call x0 -> x43, Pallas kernels: none -> 123 us  [call(): pl.pallas_call(kernel, out_shape=tuple((jax.ShapeDtypeStruct(shape, kind)...]
    all_gather x7 -> x0, blocking collectives: 82 us -> none  [the longest x2 52.2 us: fetch(): whole = lax.all_gather(block, 'dp', axis=axis, tiled=True)]
    ppermute x10 -> x21, waiting for transfers between devices: 3.23 us -> 61.2 us  [the longest x2 44.8 us: placed(): sent = lax.ppermute(stacked, BOTH, returning)]
    reduce_scatter x1 -> x4, waiting for transfers between devices: 27.9 us -> 77.6 us  [collect(): return lax.psum_scatter(line, 'dp', scatter_dimension=0, tiled=False)]
    convert_element_type x23 -> x5, other arithmetic: 32.6 us -> 1.45 us  [the longest x4 1.44 us: settle(): sent = (far.astype(F32) + got.astype(F32)).astype(BF16)]
    reduce_scatter x4, waiting for transfers between devices: 30.8 us -> 0.02 us  [collect(): lax.psum_scatter(both, 'mp', scatter_dimension=0, axis_index_groups=Y_PAI...]
  transfers between devices with their start and end apart: 109 -> 94, of which waited for: 57 -> 37; matrix products, arithmetic and copies ran while one was open for 18% -> 11% of each run, Pallas kernels for 0% -> 13%
where the time goes in v2:
time: 691 us; the launch traced here: 679 us
  waiting for transfers between devices  321 us (46%)
  Pallas kernels  123 us (18%)
  starting transfers between devices  87.9 us (13%)
  local copies, waits for them, and re-layouts  87.5 us (13%)
  other arithmetic  42.1 us (6%)
  between operations  17.3 us (3%)
    ppermute x18, waiting for transfers between devices, x_swap(): return lax.ppermute(x, 'mp', [(i, i ^ 1) for i in range(LANES)])  133 us
    pallas_call x43, Pallas kernels, call(): pl.pallas_call(kernel, out_shape=tuple((jax.ShapeDtypeStruct(shape, kind)...  123 us
    reduce_scatter x4, waiting for transfers between devices, collect(): return lax.psum_scatter(line, 'dp', scatter_dimension=0, tiled=False)  77.6 us
    ppermute x2, waiting for transfers between devices, placed(): sent = lax.ppermute(stacked, BOTH, returning)  44.8 us
    unnamed x413, local copies, waits for them, and re-layouts  43.3 us
    all_gather x3, waiting for transfers between devices, fetch(): whole = lax.all_gather(block, 'dp', axis=0, tiled=True)  39.7 us
    ppermute x18, starting transfers between devices, x_swap(): return lax.ppermute(x, 'mp', [(i, i ^ 1) for i in range(LANES)])  26.6 us
    dynamic_slice x8, local copies, waits for them, and re-layouts, collect(): kept = lax.dynamic_index_in_dim(parts, core, 1, keepdims=False)  20.4 us
  transfers between devices with their start and end apart: 94, of which 37 were waited for; matrix products, arithmetic and copies ran while one was open for 11% of the time, Pallas kernels for 13%

profile of v2, /device:TPU:0, one launch (start us, length us, event | category | flops | bytes accessed | tf_op | source)
XLA Modules:
  0.0 679.2 jit_solution(10268644507788686555)
XLA Ops:
  11.8 3.0 collective-permute-start.7
  18.1 25.5 %all-gather.5.cloned.1.call-done = bf16[768,768]{1,0:T(8,128)(2,1)} async-done(((bf16[192,768]{1,0:T(8,128)(2,1)}), bf16[768,768]{1,0:T(8,128)(2,1)}) %all-gather.5.cloned.1.call-update) | async-done | bytes 1179664 | tf_op jit(solution)/shard_map/all_gather | solution.py:719
  43.5 3.4 collective-permute-start.4
  51.1 6.2 collective-permute-done.5.refs_0_.refs_2_
  57.3 3.6 collective-permute-done.4
  62.7 5.0 attend.4
  69.2 4.3 attend.5
  75.8 5.2 collective-permute-start.16
  81.0 10.6 %collective-permute-start.15 = (bf16[768,768]{1,0:T(8,128)(2,1)}, bf16[768,768]{1,0:T(8,128)(2,1)}, u32[]{:S(2)}, u32[]{:S(2)}) collective-permute-start(bf16[768,768]{1,0:T(8,128)(2,1)} %all-gather.7.cloned.1.call-done), channel_id=1, source_target_pairs={{0,0},{1,1},{2,18},{3,19},{4,4},{5,5},{6,22},{7,23},{8,8},{9,9},{1... | collective-permute-start | bytes 3538952 | tf_op jit(solution)/shard_map/ppermute | solution.py:723
  91.6 14.2 %all-gather.9.cloned.1.call-done = bf16[1,768,768]{2,1,0:T(8,128)(2,1)} async-done(((bf16[1,192,768]{2,1,0:T(8,128)(2,1)}), bf16[1,768,768]{2,1,0:T(8,128)(2,1)}) %all-gather.9.cloned.1.call-update) | async-done | bytes 1179664 | tf_op jit(solution)/shard_map/all_gather | solution.py:719
  105.8 3.4 collective-permute-start.14
  115.7 6.6 collective-permute-done.11.refs_3_
  126.6 6.3 collective-permute-done.18.refs_0_.refs_2_
  142.3 2.7 collective-permute-start.17
  146.7 10.1 %collective-permute-done.21.refs_3_ = bf16[272,768]{1,0:T(8,128)(2,1)S(1)} collective-permute-done((bf16[272,768]{1,0:T(8,128)(2,1)S(1)}, bf16[272,768]{1,0:T(8,128)(2,1)S(1)}, u32[]{:S(2)}, u32[]{:S(2)}) %collective-permute-start.21) | collective-permute-done | bytes 417824 | tf_op jit(solution)/shard_map/ppermute | solution.py:150
  160.6 8.7 %collective-permute-done.25.refs_0_.refs_2_ = bf16[256,768]{1,0:T(8,128)(2,1)S(1)} collective-permute-done((bf16[256,768]{1,0:T(8,128)(2,1)S(1)}, bf16[256,768]{1,0:T(8,128)(2,1)S(1)}, u32[]{:S(2)}, u32[]{:S(2)}) %collective-permute-start.25) | collective-permute-done | bytes 393248 | tf_op jit(solution)/shard_map/ppermute | solution.py:150
  171.9 4.3 attend.6
  177.8 14.2 %attend.7 = (f32[512,192]{1,0:T(8,128)S(1)}, bf16[272,768]{1,0:T(8,128)(2,1)S(1)}, bf16[272,768]{1,0:T(8,128)(2,1)S(1)}, f32[512,128]{1,0:T(8,128)S(1)}) custom-call(bf16[512,576]{1,0:T(8,128)(2,1)S(1)} %project.6.refs_1_.refs_0_, bf16[512,576]{1,0:T(8,128)(2,1)S(1)} %project.6.refs_1_.refs_0_, bf16[512,576]{1,0:T(8,128)(2,1)S(1)} %project.7.refs_0_.refs_2_.refs_1_, ...), custom_call_target="tpu_custom_call" | custom-call | flops 1761607680 | bytes 1572864 | tf_op jit(solution)/shard_map/attend/pallas_call | solution.py:39
  192.6 2.3 collective-permute-start.31
  198.6 5.0 collective-permute-done.31
  206.6 2.8 collective-permute-done.29.refs_3_
  211.7 9.6 %collective-permute-done.40.refs_2_.refs_0_.refs_8_ = bf16[256,768]{1,0:T(8,128)(2,1)S(1)} collective-permute-done((bf16[256,768]{1,0:T(8,128)(2,1)S(1)}, bf16[256,768]{1,0:T(8,128)(2,1)S(1)}, u32[]{:S(2)}, u32[]{:S(2)}) %collective-permute-start.40) | collective-permute-done | bytes 393248 | tf_op jit(solution)/shard_map/ppermute | solution.py:150
  223.6 3.4 collective-permute-start.41
  226.9 5.5 collective-permute-done.38.refs_0_.refs_2_
  232.6 3.7 feed.6
  237.2 3.7 feed.7
  245.3 2.4 collective-permute-done.45
  257.1 4.0 feed_back.4
  263.5 4.0 feed_back.5
  270.8 10.0 %collective-permute-done.48.refs_2_ = bf16[256,768]{1,0:T(8,128)(2,1)S(1)} collective-permute-done((bf16[256,768]{1,0:T(8,128)(2,1)S(1)}, bf16[256,768]{1,0:T(8,128)(2,1)S(1)}, u32[]{:S(2)}, u32[]{:S(2)}) %collective-permute-start.48) | collective-permute-done | bytes 393248 | tf_op jit(solution)/shard_map/ppermute | solution.py:150
  280.8 2.3 feed_norm_back.2
  286.1 10.0 %collective-permute-done.50.refs_0_.refs_8_ = bf16[272,768]{1,0:T(8,128)(2,1)} collective-permute-done((bf16[272,768]{1,0:T(8,128)(2,1)}, bf16[272,768]{1,0:T(8,128)(2,1)}, u32[]{:S(2)}, u32[]{:S(2)}) %collective-permute-start.50) | collective-permute-done | bytes 417824 | tf_op jit(solution)/shard_map/ppermute | solution.py:150
  302.5 13.3 %attend_back.2 = (bf16[512,576]{1,0:T(8,128)(2,1)S(1)}, bf16[512,576]{1,0:T(8,128)(2,1)S(1)}) custom-call(bf16[512,576]{1,0:T(8,128)(2,1)S(1)} %copy-done.72, bf16[512,576]{1,0:T(8,128)(2,1)S(1)} %copy-done.74, bf16[512,192]{1,0:T(8,128)(2,1)S(1)} %get-tuple-element.155.refs_2_, bf16[512,192]{1,0:T(8,128)(2,1)S(1)} %get-tuple-element.157.refs_3_, ...), custom_call_target="tpu_custom_call" | custom-call | flops 6039797760 | bytes 6291456 | tf_op jit(solution)/shard_map/attend_back/pallas_call | solution.py:39
  317.5 4.5 grads.6
  322.0 2.5 constant_dynamic-slice_fusion.5
  325.1 5.3 grads.7
  330.4 3.2 constant_dynamic-slice_fusion.4
  341.7 2.7 copy.86
  344.4 2.7 copy.87
  353.0 9.9 %collective-permute-done.54.refs_2_ = bf16[256,768]{1,0:T(8,128)(2,1)S(1)} collective-permute-done((bf16[256,768]{1,0:T(8,128)(2,1)S(1)}, bf16[256,768]{1,0:T(8,128)(2,1)S(1)}, u32[]{:S(2)}, u32[]{:S(2)}) %collective-permute-start.54) | collective-permute-done | bytes 393248 | tf_op jit(solution)/shard_map/ppermute | solution.py:150
  366.0 2.5 pad_maximum_fusion.1
  368.6 7.5 %collective-permute-done.58.refs_0_.refs_8_ = bf16[272,768]{1,0:T(8,128)(2,1)} collective-permute-done((bf16[272,768]{1,0:T(8,128)(2,1)S(1)}, bf16[272,768]{1,0:T(8,128)(2,1)}, u32[]{:S(2)}, u32[]{:S(2)}) %collective-permute-start.58) | collective-permute-done | bytes 417824 | tf_op jit(solution)/shard_map/ppermute | solution.py:150
  381.2 4.0 feed_back.6
  386.2 3.9 feed_back.7
  392.1 9.8 %collective-permute-done.62.refs_2_ = bf16[256,768]{1,0:T(8,128)(2,1)S(1)} collective-permute-done((bf16[256,768]{1,0:T(8,128)(2,1)S(1)}, bf16[256,768]{1,0:T(8,128)(2,1)S(1)}, u32[]{:S(2)}, u32[]{:S(2)}) %collective-permute-start.62) | collective-permute-done | bytes 393248 | tf_op jit(solution)/shard_map/ppermute | solution.py:150
  404.6 9.6 %collective-permute-done.64.refs_0_.refs_8_ = bf16[272,768]{1,0:T(8,128)(2,1)S(1)} collective-permute-done((bf16[272,768]{1,0:T(8,128)(2,1)S(1)}, bf16[272,768]{1,0:T(8,128)(2,1)S(1)}, u32[]{:S(2)}, u32[]{:S(2)}) %collective-permute-start.64) | collective-permute-done | bytes 417824 | tf_op jit(solution)/shard_map/ppermute | solution.py:150
  416.7 13.5 %attend_back.3 = (bf16[512,576]{1,0:T(8,128)(2,1)S(1)}, bf16[512,576]{1,0:T(8,128)(2,1)S(1)}) custom-call(bf16[512,576]{1,0:T(8,128)(2,1)S(1)} %copy-done.70, bf16[512,576]{1,0:T(8,128)(2,1)S(1)} %copy-done.68, bf16[512,192]{1,0:T(8,128)(2,1)S(1)} %get-tuple-element.183.refs_2_, bf16[512,192]{1,0:T(8,128)(2,1)S(1)} %get-tuple-element.185.refs_3_, ...), custom_call_target="tpu_custom_call" | custom-call | flops 6039797760 | bytes 6291456 | tf_op jit(solution)/shard_map/attend_back/pallas_call | solution.py:39
  431.6 3.0 grads.4
  434.6 2.5 constant_dynamic-slice_fusion.7
  437.3 5.4 grads.5
  449.2 3.2 constant_dynamic-slice_fusion.6
  452.8 2.7 copy.80
  455.6 2.5 copy.81
  460.2 2.5 pad_maximum_fusion
  469.2 10.5 %collective-permute-done.43.refs_3_ = bf16[272,768]{1,0:T(8,128)(2,1)} collective-permute-done((bf16[272,768]{1,0:T(8,128)(2,1)}, bf16[272,768]{1,0:T(8,128)(2,1)}, u32[]{:S(2)}, u32[]{:S(2)}) %collective-permute-start.43) | collective-permute-done | bytes 417824 | tf_op jit(solution)/shard_map/ppermute | solution.py:150
  489.4 44.7 %collective-permute-done.55 = bf16[2,2,256,768]{3,2,0,1:T(8,128)(2,1)} collective-permute-done((bf16[2,2,256,768]{3,2,0,1:T(8,128)(2,1)}, bf16[2,2,256,768]{3,2,0,1:T(8,128)(2,1)}, u32[]{:S(2)}, u32[]{:S(2)}) %collective-permute-start.55) | collective-permute-done | bytes 1572896 | tf_op jit(solution)/shard_map/ppermute | solution.py:697
  549.5 7.1 %collective-permute-done.68.refs_2_ = bf16[256,768]{1,0:T(8,128)(2,1)S(1)} collective-permute-done((bf16[256,768]{1,0:T(8,128)(2,1)S(1)}, bf16[256,768]{1,0:T(8,128)(2,1)S(1)}, u32[]{:S(2)}, u32[]{:S(2)}) %collective-permute-start.68) | collective-permute-done | bytes 393248 | tf_op jit(solution)/shard_map/ppermute | solution.py:150
  558.4 4.0 collective-permute-done.71
  569.5 2.4 collective-permute-start.76
  573.8 3.8 collective-permute-done.75
  581.6 16.2 %reduce-scatter.23.cloned.1.call-done = bf16[1,96,1536]{1,2,0:T(8,128)(2,1)} async-done(((bf16[4,96,1536]{1,2,0:T(8,128)(2,1)}), bf16[1,96,1536]{1,2,0:T(8,128)(2,1)}) %reduce-scatter.23.cloned.1.call-update) | async-done | bytes 294928 | tf_op jit(solution)/shard_map/reduce_scatter | solution.py:877
  597.8 24.4 %reduce-scatter.11.cloned.1.call-done = bf16[1,96,768]{1,2,0:T(8,128)(2,1)} async-done(((bf16[4,96,768]{1,2,0:T(8,128)(2,1)}), bf16[1,96,768]{1,2,0:T(8,128)(2,1)}) %reduce-scatter.11.cloned.1.call-update) | async-done | bytes 147472 | tf_op jit(solution)/shard_map/reduce_scatter | solution.py:877
  622.2 36.9 %reduce-scatter.15.cloned.1.call-done = bf16[1,96,1536]{1,2,0:T(8,128)(2,1)} async-done(((bf16[4,96,1536]{1,2,0:T(8,128)(2,1)}), bf16[1,96,1536]{1,2,0:T(8,128)(2,1)}) %reduce-scatter.15.cloned.1.call-update) | async-done | bytes 294928 | tf_op jit(solution)/shard_map/reduce_scatter | solution.py:877
  662.9 2.9 fusion.11
  (717 shorter events, 186.6 us)
Async XLA Ops:
  7.2 36.3 %all-gather.5.cloned.1.call-start = ((), (), s32[]{:S(2)}) async-start(), calls=%async_computation.8 | async-start | bytes 1474560 | tf_op jit(solution)/shard_map/all_gather | solution.py:719
  10.2 65.6 %all-gather.7.cloned.1.call-start = ((), (), s32[]{:S(2)}) async-start(), calls=%async_computation.9 | async-start | bytes 1474560 | tf_op jit(solution)/shard_map/all_gather | solution.py:719
  11.0 94.9 %all-gather.9.cloned.1.call-start = ((), (), s32[]{:S(2)}) async-start(), calls=%async_computation.18 | async-start | bytes 1474560 | tf_op jit(solution)/shard_map/all_gather | solution.py:719
  15.6 33.3 %collective-permute-start.1 = (f32[4,768]{1,0:T(4,128)S(1)}, f32[4,768]{1,0:T(4,128)S(1)}, u32[]{:S(2)}, u32[]{:S(2)}) collective-permute-start(f32[4,768]{1,0:T(4,128)S(1)} %pad_maximum_fusion.12), channel_id=1, source_target_pairs={{0,16},{16,0},{1,17},{17,1},{2,18},{18,2},{3,19},{19,3},{4,20},{20... | collective-permute-start | bytes 36872 | tf_op jit(solution)/shard_map/ppermute | solution.py:146
  15.7 33.3 %collective-permute-start = (bf16[256,768]{1,0:T(8,128)(2,1)S(1)}, bf16[256,768]{1,0:T(8,128)(2,1)S(1)}, u32[]{:S(2)}, u32[]{:S(2)}) collective-permute-start(bf16[256,768]{1,0:T(8,128)(2,1)S(1)} %constant_dynamic-slice_fusion.16), channel_id=1, source_target_pairs={{0,2},{1,3},{18,16},{19,17},{4,6},{5,7},{22,20},{23,21},{8,10},{9,... | collective-permute-start | bytes 1179656 | tf_op jit(solution)/shard_map/ppermute | solution.py:692
  17.7 445.1 %reduce-scatter.17.cloned.1.call-start = ((), (), s32[]{:S(2)}) async-start(), calls=%async_computation.14 | async-start | bytes 2359296 | tf_op jit(solution)/shard_map/reduce_scatter | solution.py:874
  18.0 33.0 %collective-permute-start.8 = (f32[1,1920]{1,0:T(1,128)S(1)}, f32[1,1920]{1,0:T(1,128)S(1)}, u32[]{:S(2)}, u32[]{:S(2)}) collective-permute-start(f32[1,1920]{1,0:T(1,128)S(1)} %broadcast_select_fusion.11), channel_id=1, source_target_pairs={{0,16},{16,0},{1,17},{17,1},{2,18},{18,2},{3,19},{19,3},{4,20},{20... | collective-permute-start | bytes 23048 | tf_op jit(solution)/shard_map/ppermute | solution.py:146
  43.5 17.4 %collective-permute-start.4 = (bf16[768,768]{1,0:T(8,128)(2,1)}, bf16[768,768]{1,0:T(8,128)(2,1)S(1)}, u32[]{:S(2)}, u32[]{:S(2)}) collective-permute-start(bf16[768,768]{1,0:T(8,128)(2,1)} %all-gather.5.cloned.1.call-done), channel_id=1, source_target_pairs={{0,2},{1,3},{2,16},{3,17},{4,6},{5,7},{6,20},{7,21},{8,10},{9,11},... | collective-permute-start | bytes 3538952 | tf_op jit(solution)/shard_map/ppermute | solution.py:720
  47.0 14.0 %collective-permute-start.3 = (bf16[768,768]{1,0:T(8,128)(2,1)}, bf16[768,768]{1,0:T(8,128)(2,1)S(1)}, u32[]{:S(2)}, u32[]{:S(2)}) collective-permute-start(bf16[768,768]{1,0:T(8,128)(2,1)} %all-gather.5.cloned.1.call-done), channel_id=1, source_target_pairs={{0,0},{1,1},{2,18},{3,19},{4,4},{5,5},{6,22},{7,23},{8,8},{9,9},{1... | collective-permute-start | bytes 3538952 | tf_op jit(solution)/shard_map/ppermute | solution.py:723
  49.4 7.8 %collective-permute-start.5 = (bf16[256,768]{1,0:T(8,128)(2,1)S(1)}, bf16[256,768]{1,0:T(8,128)(2,1)S(1)}, u32[]{:S(2)}, u32[]{:S(2)}) collective-permute-start(bf16[256,768]{1,0:T(8,128)(2,1)S(1)} %enter.1.refs_0_), channel_id=1, source_target_pairs={{0,1},{1,0},{2,3},{3,2},{4,5},{5,4},{6,7},{7,6},{8,9},{9,8},{10,11... | collective-permute-start | bytes 1179656 | tf_op jit(solution)/shard_map/ppermute | solution.py:150
  51.0 10.9 %collective-permute-start.2 = (bf16[256,768]{1,0:T(8,128)(2,1)S(1)}, bf16[256,768]{1,0:T(8,128)(2,1)S(1)}, u32[]{:S(2)}, u32[]{:S(2)}) collective-permute-start(bf16[256,768]{1,0:T(8,128)(2,1)S(1)} %enter.1.refs_0_), channel_id=1, source_target_pairs={{0,16},{16,0},{1,17},{17,1},{2,18},{18,2},{3,19},{19,3},{4,20},{20... | collective-permute-start | bytes 1179656 | tf_op jit(solution)/shard_map/ppermute | solution.py:146
  68.6 40.7 %collective-permute-start.10 = (bf16[272,768]{1,0:T(8,128)(2,1)}, bf16[272,768]{1,0:T(8,128)(2,1)}, u32[]{:S(2)}, u32[]{:S(2)}) collective-permute-start(bf16[272,768]{1,0:T(8,128)(2,1)} %get-tuple-element.121), channel_id=1, source_target_pairs={{0,16},{16,0},{1,17},{17,1},{2,18},{18,2},{3,19},{19,3},{4,20},{20... | collective-permute-start | bytes 1253384 | tf_op jit(solution)/shard_map/ppermute | solution.py:146
  75.8 37.7 %collective-permute-start.9 = (bf16[272,768]{1,0:T(8,128)(2,1)S(1)}, bf16[272,768]{1,0:T(8,128)(2,1)S(1)}, u32[]{:S(2)}, u32[]{:S(2)}) collective-permute-start(bf16[272,768]{1,0:T(8,128)(2,1)S(1)} %get-tuple-element.120), channel_id=1, source_target_pairs={{0,16},{16,0},{1,17},{17,1},{2,18},{18,2},{3,19},{19,3},{4,20},{20... | collective-permute-start | bytes 1253384 | tf_op jit(solution)/shard_map/ppermute | solution.py:146
  75.8 57.1 %collective-permute-start.16 = (bf16[768,768]{1,0:T(8,128)(2,1)}, bf16[768,768]{1,0:T(8,128)(2,1)}, u32[]{:S(2)}, u32[]{:S(2)}) collective-permute-start(bf16[768,768]{1,0:T(8,128)(2,1)} %all-gather.7.cloned.1.call-done), channel_id=1, source_target_pairs={{0,2},{1,3},{2,16},{3,17},{4,6},{5,7},{6,20},{7,21},{8,10},{9,11},... | collective-permute-start | bytes 3538952 | tf_op jit(solution)/shard_map/ppermute | solution.py:720
  81.0 51.9 %collective-permute-start.15 = (bf16[768,768]{1,0:T(8,128)(2,1)}, bf16[768,768]{1,0:T(8,128)(2,1)}, u32[]{:S(2)}, u32[]{:S(2)}) collective-permute-start(bf16[768,768]{1,0:T(8,128)(2,1)} %all-gather.7.cloned.1.call-done), channel_id=1, source_target_pairs={{0,0},{1,1},{2,18},{3,19},{4,4},{5,5},{6,22},{7,23},{8,8},{9,9},{1... | collective-permute-start | bytes 3538952 | tf_op jit(solution)/shard_map/ppermute | solution.py:723
  105.8 28.6 %collective-permute-start.14 = (bf16[768,768]{1,0:T(8,128)(2,1)}, bf16[768,768]{1,0:T(8,128)(2,1)S(1)}, u32[]{:S(2)}, u32[]{:S(2)}) collective-permute-start(bf16[768,768]{1,0:T(8,128)(2,1)} %bitcast.217), channel_id=1, source_target_pairs={{0,2},{1,3},{2,16},{3,17},{4,6},{5,7},{6,20},{7,21},{8,10},{9,11},... | collective-permute-start | bytes 3538952 | tf_op jit(solution)/shard_map/ppermute | solution.py:720
  109.3 25.2 %collective-permute-start.13 = (bf16[768,768]{1,0:T(8,128)(2,1)}, bf16[768,768]{1,0:T(8,128)(2,1)S(1)}, u32[]{:S(2)}, u32[]{:S(2)}) collective-permute-start(bf16[768,768]{1,0:T(8,128)(2,1)} %bitcast.218), channel_id=1, source_target_pairs={{0,0},{1,1},{2,18},{3,19},{4,4},{5,5},{6,22},{7,23},{8,8},{9,9},{1... | collective-permute-start | bytes 3538952 | tf_op jit(solution)/shard_map/ppermute | solution.py:723
  114.2 8.0 %collective-permute-start.11 = (bf16[272,768]{1,0:T(8,128)(2,1)S(1)}, bf16[272,768]{1,0:T(8,128)(2,1)S(1)}, u32[]{:S(2)}, u32[]{:S(2)}) collective-permute-start(bf16[272,768]{1,0:T(8,128)(2,1)S(1)} %pair_sum.4), channel_id=1, source_target_pairs={{0,1},{1,0},{2,3},{3,2},{4,5},{5,4},{6,7},{7,6},{8,9},{9,8},{10,11... | collective-permute-start | bytes 1253384 | tf_op jit(solution)/shard_map/ppermute | solution.py:150
  125.0 7.8 %collective-permute-start.18 = (bf16[256,768]{1,0:T(8,128)(2,1)S(1)}, bf16[256,768]{1,0:T(8,128)(2,1)S(1)}, u32[]{:S(2)}, u32[]{:S(2)}) collective-permute-start(bf16[256,768]{1,0:T(8,128)(2,1)S(1)} %get-tuple-element.123.refs_0_), channel_id=1, source_target_pairs={{0,1},{1,0},{2,3},{3,2},{4,5},{5,4},{6,7},{7,6},{8,9},{9,8},{10,11... | collective-permute-start | bytes 1179656 | tf_op jit(solution)/shard_map/ppermute | solution.py:150
  138.3 31.1 %collective-permute-start.24 = (bf16[768,768]{1,0:T(8,128)(2,1)S(1)}, bf16[768,768]{1,0:T(8,128)(2,1)S(1)}, u32[]{:S(2)}, u32[]{:S(2)}) collective-permute-start(bf16[768,768]{1,0:T(8,128)(2,1)S(1)} %copy-done.202), channel_id=1, source_target_pairs={{16,2},{17,3},{18,16},{19,17},{20,6},{21,7},{22,20},{23,21},{24,10... | collective-permute-start | bytes 3538952 | tf_op jit(solution)/shard_map/ppermute | solution.py:720
  139.0 30.4 %collective-permute-start.23 = (bf16[768,768]{1,0:T(8,128)(2,1)S(1)}, bf16[768,768]{1,0:T(8,128)(2,1)S(1)}, u32[]{:S(2)}, u32[]{:S(2)}) collective-permute-start(bf16[768,768]{1,0:T(8,128)(2,1)S(1)} %copy-done.202), channel_id=1, source_target_pairs={{16,0},{17,1},{18,18},{19,19},{20,4},{21,5},{22,22},{23,23},{24,8}... | collective-permute-start | bytes 3538952 | tf_op jit(solution)/shard_map/ppermute | solution.py:723
  145.1 11.6 %collective-permute-start.21 = (bf16[272,768]{1,0:T(8,128)(2,1)S(1)}, bf16[272,768]{1,0:T(8,128)(2,1)S(1)}, u32[]{:S(2)}, u32[]{:S(2)}) collective-permute-start(bf16[272,768]{1,0:T(8,128)(2,1)S(1)} %pair_sum.5), channel_id=1, source_target_pairs={{0,1},{1,0},{2,3},{3,2},{4,5},{5,4},{6,7},{7,6},{8,9},{9,8},{10,11... | collective-permute-start | bytes 1253384 | tf_op jit(solution)/shard_map/ppermute | solution.py:150
  159.1 10.2 %collective-permute-start.25 = (bf16[256,768]{1,0:T(8,128)(2,1)S(1)}, bf16[256,768]{1,0:T(8,128)(2,1)S(1)}, u32[]{:S(2)}, u32[]{:S(2)}) collective-permute-start(bf16[256,768]{1,0:T(8,128)(2,1)S(1)} %get-tuple-element.129.refs_0_), channel_id=1, source_target_pairs={{0,1},{1,0},{2,3},{3,2},{4,5},{5,4},{6,7},{7,6},{8,9},{9,8},{10,11... | collective-permute-start | bytes 1179656 | tf_op jit(solution)/shard_map/ppermute | solution.py:150
  160.6 9.0 %collective-permute-start.22 = (bf16[256,768]{1,0:T(8,128)(2,1)S(1)}, bf16[256,768]{1,0:T(8,128)(2,1)S(1)}, u32[]{:S(2)}, u32[]{:S(2)}) collective-permute-start(bf16[256,768]{1,0:T(8,128)(2,1)S(1)} %get-tuple-element.129.refs_0_), channel_id=1, source_target_pairs={{0,16},{16,0},{1,17},{17,1},{2,18},{18,2},{3,19},{19,3},{4,20},{20... | collective-permute-start | bytes 1179656 | tf_op jit(solution)/shard_map/ppermute | solution.py:146
  177.6 19.3 %collective-permute-start.28 = (bf16[272,768]{1,0:T(8,128)(2,1)S(1)}, bf16[272,768]{1,0:T(8,128)(2,1)S(1)}, u32[]{:S(2)}, u32[]{:S(2)}) collective-permute-start(bf16[272,768]{1,0:T(8,128)(2,1)S(1)} %get-tuple-element.133), channel_id=1, source_target_pairs={{0,16},{16,0},{1,17},{17,1},{2,18},{18,2},{3,19},{19,3},{4,20},{20... | collective-permute-start | bytes 1253384 | tf_op jit(solution)/shard_map/ppermute | solution.py:146
  192.1 12.2 %collective-permute-start.27 = (bf16[272,768]{1,0:T(8,128)(2,1)S(1)}, bf16[272,768]{1,0:T(8,128)(2,1)S(1)}, u32[]{:S(2)}, u32[]{:S(2)}) collective-permute-start(bf16[272,768]{1,0:T(8,128)(2,1)S(1)} %get-tuple-element.132), channel_id=1, source_target_pairs={{0,16},{16,0},{1,17},{17,1},{2,18},{18,2},{3,19},{19,3},{4,20},{20... | collective-permute-start | bytes 1253384 | tf_op jit(solution)/shard_map/ppermute | solution.py:146
  192.6 11.0 %collective-permute-start.31 = (bf16[256,768]{1,0:T(8,128)(2,1)S(1)}, bf16[256,768]{1,0:T(8,128)(2,1)S(1)}, u32[]{:S(2)}, u32[]{:S(2)}) collective-permute-start(bf16[256,768]{1,0:T(8,128)(2,1)S(1)} %constant_dynamic-slice_fusion.11), channel_id=1, source_target_pairs={{0,2},{1,3},{18,16},{19,17},{4,6},{5,7},{22,20},{23,21},{8,10},{9,... | collective-permute-start | bytes 1179656 | tf_op jit(solution)/shard_map/ppermute | solution.py:692
  194.9 27.9 %collective-permute-start.36 = (bf16[768,768]{1,0:T(8,128)(2,1)S(1)}, bf16[768,768]{1,0:T(8,128)(2,1)S(1)}, u32[]{:S(2)}, u32[]{:S(2)}) collective-permute-start(bf16[768,768]{1,0:T(8,128)(2,1)S(1)} %copy-done.200), channel_id=1, source_target_pairs={{16,2},{17,3},{18,16},{19,17},{20,6},{21,7},{22,20},{23,21},{24,10... | collective-permute-start | bytes 3538952 | tf_op jit(solution)/shard_map/ppermute | solution.py:720
  195.6 27.3 %collective-permute-start.35 = (bf16[768,768]{1,0:T(8,128)(2,1)S(1)}, bf16[768,768]{1,0:T(8,128)(2,1)S(1)}, u32[]{:S(2)}, u32[]{:S(2)}) collective-permute-start(bf16[768,768]{1,0:T(8,128)(2,1)S(1)} %copy-done.200), channel_id=1, source_target_pairs={{16,0},{17,1},{18,18},{19,19},{20,4},{21,5},{22,22},{23,23},{24,8}... | collective-permute-start | bytes 3538952 | tf_op jit(solution)/shard_map/ppermute | solution.py:723
  197.1 12.4 %collective-permute-start.29 = (bf16[272,768]{1,0:T(8,128)(2,1)S(1)}, bf16[272,768]{1,0:T(8,128)(2,1)S(1)}, u32[]{:S(2)}, u32[]{:S(2)}) collective-permute-start(bf16[272,768]{1,0:T(8,128)(2,1)S(1)} %pair_sum.6), channel_id=1, source_target_pairs={{0,1},{1,0},{2,3},{3,2},{4,5},{5,4},{6,7},{7,6},{8,9},{9,8},{10,11... | collective-permute-start | bytes 1253384 | tf_op jit(solution)/shard_map/ppermute | solution.py:150
  203.6 19.9 %collective-permute-start.34 = (bf16[768,768]{1,0:T(8,128)(2,1)S(1)}, bf16[768,768]{1,0:T(8,128)(2,1)S(1)}, u32[]{:S(2)}, u32[]{:S(2)}) collective-permute-start(bf16[768,768]{1,0:T(8,128)(2,1)S(1)} %bitcast.219), channel_id=1, source_target_pairs={{16,2},{17,3},{18,16},{19,17},{20,6},{21,7},{22,20},{23,21},{24,10... | collective-permute-start | bytes 3538952 | tf_op jit(solution)/shard_map/ppermute | solution.py:720
  204.4 28.1 %collective-permute-start.33 = (bf16[768,768]{1,0:T(8,128)(2,1)S(1)}, bf16[768,768]{1,0:T(8,128)(2,1)S(1)}, u32[]{:S(2)}, u32[]{:S(2)}) collective-permute-start(bf16[768,768]{1,0:T(8,128)(2,1)S(1)} %bitcast.220), channel_id=1, source_target_pairs={{16,0},{17,1},{18,18},{19,19},{20,4},{21,5},{22,22},{23,23},{24,8}... | collective-permute-start | bytes 3538952 | tf_op jit(solution)/shard_map/ppermute | solution.py:723
  209.4 11.9 %collective-permute-start.40 = (bf16[256,768]{1,0:T(8,128)(2,1)S(1)}, bf16[256,768]{1,0:T(8,128)(2,1)S(1)}, u32[]{:S(2)}, u32[]{:S(2)}) collective-permute-start(bf16[256,768]{1,0:T(8,128)(2,1)S(1)} %get-tuple-element.274.refs_2_.refs_0_.refs_6_), channel_id=1, source_target_pairs={{0,1},{1,0},{2,3},{3,2},{4,5},{5,4},{6,7},{7,6},{8,9},{9,8},{10,11... | collective-permute-start | bytes 1179656 | tf_op jit(solution)/shard_map/ppermute | solution.py:150
  221.3 11.1 %collective-permute-start.38 = (bf16[256,768]{1,0:T(8,128)(2,1)S(1)}, bf16[256,768]{1,0:T(8,128)(2,1)S(1)}, u32[]{:S(2)}, u32[]{:S(2)}) collective-permute-start(bf16[256,768]{1,0:T(8,128)(2,1)S(1)} %get-tuple-element.135.refs_0_), channel_id=1, source_target_pairs={{0,1},{1,0},{2,3},{3,2},{4,5},{5,4},{6,7},{7,6},{8,9},{9,8},{10,11... | collective-permute-start | bytes 1179656 | tf_op jit(solution)/shard_map/ppermute | solution.py:150
  222.8 9.8 %collective-permute-start.32 = (bf16[256,768]{1,0:T(8,128)(2,1)S(1)}, bf16[256,768]{1,0:T(8,128)(2,1)S(1)}, u32[]{:S(2)}, u32[]{:S(2)}) collective-permute-start(bf16[256,768]{1,0:T(8,128)(2,1)S(1)} %get-tuple-element.274.refs_2_.refs_0_.refs_6_), channel_id=1, source_target_pairs={{0,16},{16,0},{1,17},{17,1},{2,18},{18,2},{3,19},{19,3},{4,20},{20... | collective-permute-start | bytes 1179656 | tf_op jit(solution)/shard_map/ppermute | solution.py:146
  222.9 9.7 %collective-permute-start.30 = (bf16[256,768]{1,0:T(8,128)(2,1)S(1)}, bf16[256,768]{1,0:T(8,128)(2,1)S(1)}, u32[]{:S(2)}, u32[]{:S(2)}) collective-permute-start(bf16[256,768]{1,0:T(8,128)(2,1)S(1)} %get-tuple-element.135.refs_0_), channel_id=1, source_target_pairs={{0,16},{16,0},{1,17},{17,1},{2,18},{18,2},{3,19},{19,3},{4,20},{20... | collective-permute-start | bytes 1179656 | tf_op jit(solution)/shard_map/ppermute | solution.py:146
  223.6 13.5 %collective-permute-start.41 = (bf16[256,768]{1,0:T(8,128)(2,1)S(1)}, bf16[256,768]{1,0:T(8,128)(2,1)S(1)}, u32[]{:S(2)}, u32[]{:S(2)}) collective-permute-start(bf16[256,768]{1,0:T(8,128)(2,1)S(1)} %collective-permute-done.40.refs_2_.refs_0_.refs_8_), channel_id=1, source_target_pairs={{0,16},{16,0},{1,17},{17,1},{2,18},{18,2},{3,19},{19,3},{4,20},{20... | collective-permute-start | bytes 1179656 | tf_op jit(solution)/shard_map/ppermute | solution.py:146
  269.3 11.5 %collective-permute-start.48 = (bf16[256,768]{1,0:T(8,128)(2,1)S(1)}, bf16[256,768]{1,0:T(8,128)(2,1)S(1)}, u32[]{:S(2)}, u32[]{:S(2)}) collective-permute-start(bf16[256,768]{1,0:T(8,128)(2,1)S(1)} %add_convert_fusion.3), channel_id=1, source_target_pairs={{0,1},{1,0},{2,3},{3,2},{4,5},{5,4},{6,7},{7,6},{8,9},{9,8},{10,11... | collective-permute-start | bytes 1179656 | tf_op jit(solution)/shard_map/ppermute | solution.py:150
  284.6 11.5 %collective-permute-start.50 = (bf16[272,768]{1,0:T(8,128)(2,1)}, bf16[272,768]{1,0:T(8,128)(2,1)}, u32[]{:S(2)}, u32[]{:S(2)}) collective-permute-start(bf16[272,768]{1,0:T(8,128)(2,1)} %get-tuple-element.153.refs_0_.refs_6_), channel_id=1, source_target_pairs={{0,1},{1,0},{2,3},{3,2},{4,5},{5,4},{6,7},{7,6},{8,9},{9,8},{10,11... | collective-permute-start | bytes 1253384 | tf_op jit(solution)/shard_map/ppermute | solution.py:150
  286.1 10.0 %collective-permute-start.49 = (bf16[272,768]{1,0:T(8,128)(2,1)}, bf16[272,768]{1,0:T(8,128)(2,1)}, u32[]{:S(2)}, u32[]{:S(2)}) collective-permute-start(bf16[272,768]{1,0:T(8,128)(2,1)} %get-tuple-element.153.refs_0_.refs_6_), channel_id=1, source_target_pairs={{0,16},{16,0},{1,17},{17,1},{2,18},{18,2},{3,19},{19,3},{4,20},{20... | collective-permute-start | bytes 1253384 | tf_op jit(solution)/shard_map/ppermute | solution.py:146
  324.5 11.4 %collective-permute-start.79 = (bf16[4,96,768]{2,1,0:T(8,128)(2,1)}, bf16[4,96,768]{2,1,0:T(8,128)(2,1)}, u32[]{:S(2)}, u32[]{:S(2)}) collective-permute-start(bf16[4,96,768]{2,1,0:T(8,128)(2,1)} %get-tuple-element.305), channel_id=1, source_target_pairs={{0,16},{16,0},{1,17},{17,1},{2,18},{18,2},{3,19},{19,3},{4,20},{20... | collective-permute-start | bytes 1769480 | tf_op jit(solution)/shard_map/ppermute | solution.py:146
  333.6 10.8 %collective-permute-start.80 = (bf16[4,96,1536]{2,1,0:T(8,128)(2,1)}, bf16[4,96,1536]{2,1,0:T(8,128)(2,1)}, u32[]{:S(2)}, u32[]{:S(2)}) collective-permute-start(bf16[4,96,1536]{2,1,0:T(8,128)(2,1)} %get-tuple-element.287), channel_id=1, source_target_pairs={{0,16},{16,0},{1,17},{17,1},{2,18},{18,2},{3,19},{19,3},{4,20},{20... | collective-permute-start | bytes 3538952 | tf_op jit(solution)/shard_map/ppermute | solution.py:146
  341.1 127.8 %reduce-scatter.21.cloned.1.call-start = ((), (), s32[]{:S(2)}) async-start(), calls=%async_computation.16 | async-start | bytes 4718592 | tf_op jit(solution)/shard_map/reduce_scatter | solution.py:874
  341.1 9.0 %collective-permute-start.53 = (bf16[256,768]{1,0:T(8,128)(2,1)}, bf16[256,768]{1,0:T(8,128)(2,1)}, u32[]{:S(2)}, u32[]{:S(2)}) collective-permute-start(bf16[256,768]{1,0:T(8,128)(2,1)} %copy-done.162), channel_id=1, source_target_pairs={{0,16},{16,0},{1,17},{17,1},{2,18},{18,2},{3,19},{19,3},{4,20},{20... | collective-permute-start | bytes 1179656 | tf_op jit(solution)/shard_map/ppermute | solution.py:146
  351.3 11.5 %collective-permute-start.54 = (bf16[256,768]{1,0:T(8,128)(2,1)S(1)}, bf16[256,768]{1,0:T(8,128)(2,1)S(1)}, u32[]{:S(2)}, u32[]{:S(2)}) collective-permute-start(bf16[256,768]{1,0:T(8,128)(2,1)S(1)} %add_convert_fusion.2), channel_id=1, source_target_pairs={{0,1},{1,0},{2,3},{3,2},{4,5},{5,4},{6,7},{7,6},{8,9},{9,8},{10,11... | collective-permute-start | bytes 1179656 | tf_op jit(solution)/shard_map/ppermute | solution.py:150
  364.7 11.4 %collective-permute-start.58 = (bf16[272,768]{1,0:T(8,128)(2,1)S(1)}, bf16[272,768]{1,0:T(8,128)(2,1)}, u32[]{:S(2)}, u32[]{:S(2)}) collective-permute-start(bf16[272,768]{1,0:T(8,128)(2,1)S(1)} %get-tuple-element.171.refs_0_.refs_6_), channel_id=1, source_target_pairs={{0,1},{1,0},{2,3},{3,2},{4,5},{5,4},{6,7},{7,6},{8,9},{9,8},{10,11... | collective-permute-start | bytes 1253384 | tf_op jit(solution)/shard_map/ppermute | solution.py:150
  368.5 120.8 %reduce-scatter.9.cloned.1.call-start = ((), (), s32[]{:S(2)}) async-start(), calls=%async_computation.10 | async-start | bytes 2359296 | tf_op jit(solution)/shard_map/reduce_scatter | solution.py:874
  376.1 10.1 %collective-permute-start.57 = (bf16[272,768]{1,0:T(8,128)(2,1)S(1)}, bf16[272,768]{1,0:T(8,128)(2,1)S(1)}, u32[]{:S(2)}, u32[]{:S(2)}) collective-permute-start(bf16[272,768]{1,0:T(8,128)(2,1)S(1)} %get-tuple-element.171.refs_0_.refs_6_), channel_id=1, source_target_pairs={{0,16},{16,0},{1,17},{17,1},{2,18},{18,2},{3,19},{19,3},{4,20},{20... | collective-permute-start | bytes 1253384 | tf_op jit(solution)/shard_map/ppermute | solution.py:146
  390.7 11.2 %collective-permute-start.62 = (bf16[256,768]{1,0:T(8,128)(2,1)S(1)}, bf16[256,768]{1,0:T(8,128)(2,1)S(1)}, u32[]{:S(2)}, u32[]{:S(2)}) collective-permute-start(bf16[256,768]{1,0:T(8,128)(2,1)S(1)} %add_convert_fusion.1), channel_id=1, source_target_pairs={{0,1},{1,0},{2,3},{3,2},{4,5},{5,4},{6,7},{7,6},{8,9},{9,8},{10,11... | collective-permute-start | bytes 1179656 | tf_op jit(solution)/shard_map/ppermute | solution.py:150
  403.1 11.0 %collective-permute-start.64 = (bf16[272,768]{1,0:T(8,128)(2,1)S(1)}, bf16[272,768]{1,0:T(8,128)(2,1)S(1)}, u32[]{:S(2)}, u32[]{:S(2)}) collective-permute-start(bf16[272,768]{1,0:T(8,128)(2,1)S(1)} %get-tuple-element.181.refs_0_.refs_6_), channel_id=1, source_target_pairs={{0,1},{1,0},{2,3},{3,2},{4,5},{5,4},{6,7},{7,6},{8,9},{9,8},{10,11... | collective-permute-start | bytes 1253384 | tf_op jit(solution)/shard_map/ppermute | solution.py:150
  404.6 9.6 %collective-permute-start.63 = (bf16[272,768]{1,0:T(8,128)(2,1)S(1)}, bf16[272,768]{1,0:T(8,128)(2,1)S(1)}, u32[]{:S(2)}, u32[]{:S(2)}) collective-permute-start(bf16[272,768]{1,0:T(8,128)(2,1)S(1)} %get-tuple-element.181.refs_0_.refs_6_), channel_id=1, source_target_pairs={{0,16},{16,0},{1,17},{17,1},{2,18},{18,2},{3,19},{19,3},{4,20},{20... | collective-permute-start | bytes 1253384 | tf_op jit(solution)/shard_map/ppermute | solution.py:146
  437.1 7.0 %collective-permute-start.77 = (bf16[4,96,768]{2,1,0:T(8,128)(2,1)}, bf16[4,96,768]{2,1,0:T(8,128)(2,1)}, u32[]{:S(2)}, u32[]{:S(2)}) collective-permute-start(bf16[4,96,768]{2,1,0:T(8,128)(2,1)} %get-tuple-element.303), channel_id=1, source_target_pairs={{0,16},{16,0},{1,17},{17,1},{2,18},{18,2},{3,19},{19,3},{4,20},{20... | collective-permute-start | bytes 1769480 | tf_op jit(solution)/shard_map/ppermute | solution.py:146
  449.2 97.5 %reduce-scatter.13.cloned.1.call-start = ((), (), s32[]{:S(2)}) async-start(), calls=%async_computation.12 | async-start | bytes 4718592 | tf_op jit(solution)/shard_map/reduce_scatter | solution.py:874
  462.7 118.8 %reduce-scatter.19.cloned.1.call-start = ((), (), s32[]{:S(2)}) async-start(), calls=%async_computation.15 | async-start | bytes 983040 | tf_op jit(solution)/shard_map/reduce_scatter | solution.py:877
  463.5 134.3 %reduce-scatter.23.cloned.1.call-start = ((), (), s32[]{:S(2)}) async-start(), calls=%async_computation.17 | async-start | bytes 1966080 | tf_op jit(solution)/shard_map/reduce_scatter | solution.py:877
  467.5 12.2 %collective-permute-start.43 = (bf16[272,768]{1,0:T(8,128)(2,1)}, bf16[272,768]{1,0:T(8,128)(2,1)}, u32[]{:S(2)}, u32[]{:S(2)}) collective-permute-start(bf16[272,768]{1,0:T(8,128)(2,1)} %pair_sum.7), channel_id=1, source_target_pairs={{0,1},{1,0},{2,3},{3,2},{4,5},{5,4},{6,7},{7,6},{8,9},{9,8},{10,11... | collective-permute-start | bytes 1253384 | tf_op jit(solution)/shard_map/ppermute | solution.py:150
  468.9 153.3 %reduce-scatter.11.cloned.1.call-start = ((), (), s32[]{:S(2)}) async-start(), calls=%async_computation.11 | async-start | bytes 983040 | tf_op jit(solution)/shard_map/reduce_scatter | solution.py:877
  485.2 48.8 %collective-permute-start.55 = (bf16[2,2,256,768]{3,2,0,1:T(8,128)(2,1)}, bf16[2,2,256,768]{3,2,0,1:T(8,128)(2,1)}, u32[]{:S(2)}, u32[]{:S(2)}) collective-permute-start(bf16[2,2,256,768]{3,2,0,1:T(8,128)(2,1)} %pad_maximum_fusion.2), channel_id=1, source_target_pairs={{2,0},{3,1},{16,18},{17,19},{6,4},{7,5},{20,22},{21,23},{10,8},{11... | collective-permute-start | bytes 4718600 | tf_op jit(solution)/shard_map/ppermute | solution.py:697
  489.3 169.8 %reduce-scatter.15.cloned.1.call-start = ((), (), s32[]{:S(2)}) async-start(), calls=%async_computation.13 | async-start | bytes 1966080 | tf_op jit(solution)/shard_map/reduce_scatter | solution.py:877
  536.1 8.9 %collective-permute-start.67 = (bf16[256,768]{1,0:T(8,128)(2,1)S(1)}, bf16[256,768]{1,0:T(8,128)(2,1)S(1)}, u32[]{:S(2)}, u32[]{:S(2)}) collective-permute-start(bf16[256,768]{1,0:T(8,128)(2,1)S(1)} %copy-done.161), channel_id=1, source_target_pairs={{0,16},{16,0},{1,17},{17,1},{2,18},{18,2},{3,19},{19,3},{4,20},{20... | collective-permute-start | bytes 1179656 | tf_op jit(solution)/shard_map/ppermute | solution.py:146
  538.9 33.6 %collective-permute-start.56 = (bf16[2,2,256,768]{3,2,1,0:T(8,128)(2,1)}, bf16[2,2,256,768]{3,2,1,0:T(8,128)(2,1)}, u32[]{:S(2)}, u32[]{:S(2)}) collective-permute-start(bf16[2,2,256,768]{3,2,1,0:T(8,128)(2,1)} %bitcast.173), channel_id=1, source_target_pairs={{0,16},{16,0},{1,17},{17,1},{2,18},{18,2},{3,19},{19,3},{4,20},{20... | collective-permute-start | bytes 4718600 | tf_op jit(solution)/shard_map/ppermute | solution.py:146
  545.1 11.6 %collective-permute-start.68 = (bf16[256,768]{1,0:T(8,128)(2,1)S(1)}, bf16[256,768]{1,0:T(8,128)(2,1)S(1)}, u32[]{:S(2)}, u32[]{:S(2)}) collective-permute-start(bf16[256,768]{1,0:T(8,128)(2,1)S(1)} %add_convert_fusion), channel_id=1, source_target_pairs={{0,1},{1,0},{2,3},{3,2},{4,5},{5,4},{6,7},{7,6},{8,9},{9,8},{10,11... | collective-permute-start | bytes 1179656 | tf_op jit(solution)/shard_map/ppermute | solution.py:150
  565.2 14.0 %collective-permute-start.69 = (bf16[2,1,256,768]{3,2,0,1:T(8,128)(2,1)S(1)}, bf16[2,1,256,768]{3,2,0,1:T(8,128)(2,1)}, u32[]{:S(2)}, u32[]{:S(2)}) collective-permute-start(bf16[2,1,256,768]{3,2,0,1:T(8,128)(2,1)S(1)} %maximum_bitcast_fusion.2), channel_id=1, source_target_pairs={{2,0},{3,1},{16,18},{17,19},{6,4},{7,5},{20,22},{21,23},{10,8},{11... | collective-permute-start | bytes 2359304 | tf_op jit(solution)/shard_map/ppermute | solution.py:697
  581.5 81.3 %collective-permute-start.70 = (bf16[1,2,256,768]{3,2,1,0:T(8,128)(2,1)}, bf16[1,2,256,768]{3,2,1,0:T(8,128)(2,1)}, u32[]{:S(2)}, u32[]{:S(2)}) collective-permute-start(bf16[1,2,256,768]{3,2,1,0:T(8,128)(2,1)} %fusion.7), channel_id=1, source_target_pairs={{0,16},{16,0},{1,17},{17,1},{2,18},{18,2},{3,19},{19,3},{4,20},{20... | collective-permute-start | bytes 2359304 | tf_op jit(solution)/shard_map/ppermute | solution.py:146
  (233 other events, 1988.8 us)
Sparse Core Ops, SparseCore 0:
  10.3 33.1 all-gather.4
  45.1 29.5 all-gather.6
  76.3 29.5 all-gather.8
  341.2 23.9 reduce-scatter.16
  368.7 42.0 reduce-scatter.20
  449.3 23.7 reduce-scatter.8
  475.4 56.5 reduce-scatter.12
  534.3 25.7 reduce-scatter.18
  562.4 35.3 reduce-scatter.22
  600.0 22.2 reduce-scatter.10
  624.5 34.5 reduce-scatter.14

commit v3 on v2

--- a/solution.py
+++ b/solution.py
@@ -26,8 +26,9 @@
 BF16 = jnp.bfloat16
 
 VMEM = pl.BlockSpec(memory_space=pltpu.VMEM)
+SMEM = pl.BlockSpec(memory_space=pltpu.SMEM)
 ANY = pl.BlockSpec(memory_space=pl.ANY)
-PARAMS = pltpu.CompilerParams(vmem_limit_bytes=48 * 1024 * 1024)
+PARAMS = pltpu.CompilerParams(vmem_limit_bytes=16 * 1024 * 1024)
 
 
 def call(name, body, outs, ins, scratch=(), after=(), cost=None):
@@ -39,7 +40,7 @@
     return pl.pallas_call(
         kernel,
         out_shape=tuple(jax.ShapeDtypeStruct(shape, kind) for shape, kind in outs),
-        in_specs=[VMEM] * count + [ANY] * len(after),
+        in_specs=[SMEM if item.ndim == 1 else VMEM for item in ins] + [ANY] * len(after),
         out_specs=(VMEM,) * len(outs),
         scratch_shapes=list(scratch),
         compiler_params=PARAMS,
@@ -168,12 +169,14 @@
     out[half:] = encode_vectors(folded[0:1], folded[1:2])
 
 
-def settle(own, mate, far, far_mate):
+def pair_add_body(first, second, out):
+    out[...] = (first[...].astype(F32) + second[...].astype(F32)).astype(BF16)
+
+
+def settle(own, mate, far, far_mate, after=()):
+    body = pair_sum_body if own.shape[0] % 256 else pair_add_body
     got = core_swap(far_mate)
-    if own.shape[0] % 256:
-        sent = call("pair_sum", pair_sum_body, [(far.shape, BF16)], [far, got])[0]
-    else:
-        sent = (far.astype(F32) + got.astype(F32)).astype(BF16)
+    sent = call("pair_sum", body, [(far.shape, BF16)], [far, got], after=after)[0]
     return own, core_swap(mate), x_swap(sent)
 
 
@@ -331,15 +334,14 @@
 
 def feed_body(with_back, *refs):
     if with_back:
-        one, two, back_one, back_two, up, down, gain, bias, f_ref, p_one, p_two, s_one, s_two = refs
+        one, two, back_one, back_two, mat, gain, bias, f_ref, p_one, p_two, s_ref = refs
     else:
-        one, two, up, down, gain, bias, f_ref, p_one, p_two = refs
-        back_one = back_two = s_one = s_two = None
+        one, two, mat, gain, bias, f_ref, p_one, p_two = refs
+        back_one = back_two = s_ref = None
     size = one.shape[0]
+    up, down = mat.at[:, :UNITS], mat.at[:, UNITS:]
     folded = folded_vectors(down[...], gain[...], bias[...])
-    for place, (piece, p_ref, back, s_ref) in enumerate(
-        ((one, p_one, back_one, s_one), (two, p_two, back_two, s_two))
-    ):
+    for place, (piece, p_ref, back) in enumerate(((one, p_one, back_one), (two, p_two, back_two))):
         rows = slice(place * size, (place + 1) * size)
         pre = nn(piece[...], up[...])
         f_ref[rows, :] = pre
@@ -355,39 +357,44 @@
             inner = nn(back[...], down[...]) * gain[...]
             columns.append(jnp.sum(inner, axis=-1, keepdims=True))
             columns.append(jnp.sum(inner * act, axis=-1, keepdims=True))
-            s_ref[...] = to_rows(*columns)
-
-
-def feed(pieces, backs, up, down, gain, bias, after=()):
+            s_ref[8 * place : 8 * place + 8, :] = to_rows(*columns)
+
+
+def feed(pieces, backs, mat, gain, bias, after=()):
     size = pieces[0].shape[0]
     outs = [((2 * size, UNITS), F32)] + [((size + TAIL, D), BF16)] * 2
     if backs:
-        outs += [((8, size), F32)] * 2
+        outs += [((16, size), F32)]
     return call(
         "feed",
         partial(feed_body, bool(backs)),
         outs,
-        [*pieces, *backs, up, down, gain, bias],
+        [*pieces, *backs, mat, gain, bias],
         after=after,
         cost=work(2 * 2 * size * D * UNITS * 4, 8 * size * D * 4),
     )
 
 
-def feed_back_body(with_stats, *refs):
-    if with_stats:
-        one, two, s_one, s_two, *refs = refs
+def feed_back_body(first_piece, *refs):
+    if first_piece is not None:
+        one, two, s_ref, *refs = refs
     else:
         one, two, *refs = refs
-        s_one = s_two = None
-    f_ref, gain, bias, up, down, df_ref, n_ref, p_one, p_two, vec_ref = refs
+        s_ref = None
+    f_ref, gain, bias, mat, df_ref, n_ref, p_one, p_two, vec_ref = refs
+    up, down = mat.at[:, :UNITS], mat.at[:, UNITS:]
     size = p_one.shape[0]
     gain_grad = jnp.zeros((1, UNITS), F32)
     bias_grad = jnp.zeros((1, UNITS), F32)
-    for place, (piece, s_ref, p_ref) in enumerate(((one, s_one, p_one), (two, s_two, p_two))):
+    for place, (piece, p_ref) in enumerate(((one, p_one), (two, p_two))):
         rows = slice(place * size, (place + 1) * size)
         upstream = nn(piece[:size], down[...])
         pre = f_ref[rows, :]
-        stats = s_ref[...] if with_stats else decode(piece[size : size + TAIL // 2])
+        if first_piece is not None:
+            start = 8 * (first_piece + place)
+            stats = s_ref[start : start + 8, :]
+        else:
+            stats = decode(piece[size : size + TAIL // 2])
         columns = to_columns(stats)
         mean, scaled, first, second = (columns[:, i : i + 1] for i in range(4))
         act, spread = gelu_parts(pre)
@@ -403,21 +410,50 @@
     vec_ref[...] = vector_rows(gain_grad, bias_grad)
 
 
-def feed_back(pieces, stats, pre, gain, bias, up, down, after=()):
+def feed_back(pieces, stats, first_piece, pre, gain, bias, mat, after=()):
     count = pre.shape[0]
     size = count // 2
     return call(
         "feed_back",
-        partial(feed_back_body, bool(stats)),
+        partial(feed_back_body, first_piece if stats else None),
         [((count, UNITS), BF16)] * 2 + [((size, D), BF16)] * 2 + [((8, UNITS), F32)],
-        [*pieces, *stats, pre, gain, bias, up, down],
+        [*pieces, *stats, pre, gain, bias, mat],
         after=after,
         cost=work(2 * count * D * UNITS * 4, 8 * count * D),
     )
 
 
+def stats_pack_body(near, far, out):
+    out[:16] = near[...]
+    out[16:] = far[...]
+
+
+def stats_near_body(stats, got, out):
+    for place in range(4):
+        other = 8 * (place ^ 1)
+        out[8 * place : 8 * place + 8] = stats[8 * place : 8 * place + 8] + got[other : other + 8]
+
+
+def stats_far_body(stats, got, out):
+    for place in range(4):
+        other = 8 * (place ^ 2)
+        rows = slice(8 * place, 8 * place + 8)
+        total = (stats[rows] + got[other : other + 8]) * (1.0 / FF)
+        mean, one = total[0:1], total[2:3]
+        scaled = lax.rsqrt(total[1:2] - mean * mean + EPS)
+        two = scaled * (total[3:4] - mean * one)
+        out[rows] = jnp.concatenate([mean, scaled, one, two, total[4:8]], axis=0)
+
+
+def group_stats(near, far):
+    shape = [((32, near.shape[1]), F32)]
+    stats = call("stats_pack", stats_pack_body, shape, [near, far])[0]
+    stats = call("stats_near", stats_near_body, shape, [stats, core_swap(stats)])[0]
+    return call("stats_far", stats_far_body, shape, [stats, x_swap(stats)])[0]
+
+
 def grads_body(pieces, halves, size, *refs):
-    out = refs[-1]
+    *refs, out = refs
     place = 0
     column = 0
     for left_count, right_count in zip(pieces, halves):
@@ -535,13 +571,14 @@
     kept_ref[...] = kept
 
 
-def after_attend(x, pieces, gain, bias):
+def after_attend(x, pieces, gain, bias, after=()):
     rows = x.shape[0]
     return call(
         "after_attend",
         after_attend_body,
         [((rows, D), F32), ((rows, D), F32), ((rows, D), BF16), ((8, D), F32), ((8, rows), F32)],
         [x, *pieces, gain, bias],
+        after=after,
     )
 
 
@@ -560,13 +597,14 @@
     kept_ref[...] = kept
 
 
-def after_feed(x2, pieces, labels, gain, bias):
+def after_feed(x2, pieces, labels, gain, bias, after=()):
     rows = x2.shape[0]
     return call(
         "after_feed",
         after_feed_body,
         [((rows, D), BF16), ((rows, D), F32), ((rows, D), BF16), ((8, D), F32), ((8, rows), F32)],
         [x2, *pieces, labels, gain, bias],
+        after=after,
     )
 
 
@@ -602,13 +640,14 @@
     vec_ref[...] = vector_rows(gain_grad, bias_grad)
 
 
-def feed_norm_back(pieces, grad, labels, x2, gain, branch, folded, kept):
+def feed_norm_back(pieces, grad, labels, x2, gain, branch, folded, kept, after=()):
     rows = x2.shape[0]
     return call(
         "feed_norm_back",
         feed_norm_back_body,
         [((rows, D), F32), ((rows + TAIL, D), BF16), ((8, D), F32)],
         [*pieces, grad, labels, x2, gain, branch, folded, kept],
+        after=after,
     )
 
 
@@ -627,7 +666,7 @@
     vec_ref[...] = vector_rows(gain_grad, bias_grad)
 
 
-def first_norm_back(pieces, dx2, x, gain, following=()):
+def first_norm_back(pieces, dx2, x, gain, following=(), after=()):
     rows = x.shape[0]
     outs = [((rows, D), BF16), ((8, D), F32)]
     if following:
@@ -637,20 +676,227 @@
         partial(first_norm_back_body, bool(following)),
         outs,
         [*pieces, dx2, x, gain, *following],
-    )
-
-
-def dp_scatter(parts):
-    count = parts.shape[0]
-    if count > 4:
-        return lax.psum_scatter(parts, "dp", scatter_dimension=0, tiled=False)
-    place = lax.axis_index("dp")
-    total = lax.dynamic_index_in_dim(parts, place, 0, keepdims=False).astype(F32)
-    for step in range(1, count):
-        sent = lax.dynamic_index_in_dim(parts, (place + step) % count, 0, keepdims=False)
-        got = lax.ppermute(sent, "dp", [(i, (i + step) % count) for i in range(count)])
-        total += got.astype(F32)
-    return total
+        after=after,
+    )
+
+
+def first_block_body(query, key, value, output, out):
+    width = query.shape[1]
+    for place, ref in enumerate((query, key, value)):
+        out[:, place * width : (place + 1) * width] = ref[...]
+    out[:, 3 * width :] = output[...].T
+
+
+def first_block(query, key, value, output):
+    rows = query.shape[0]
+    return call("first_block", first_block_body, [((rows, D), BF16)], [query, key, value, output])[0]
+
+
+def second_block_body(up, down, out):
+    out[:, :UNITS] = up[...]
+    out[:, UNITS:] = down[...].T
+
+
+def second_block(up, down, after=()):
+    rows = up.shape[0]
+    return call(
+        "second_block", second_block_body, [((rows, 2 * UNITS), BF16)], [up, down], after=after
+    )[0]
+
+
+def mask_body(rows, labels, out):
+    out[...] = (mask_column(labels, rows.shape[0]) * rows[...].astype(F32)).astype(BF16)
+
+
+def mask_rows(rows, labels):
+    return call("mask_rows", mask_body, [(rows.shape, BF16)], [rows, labels])[0]
+
+
+def pack_body(*refs):
+    *items, out = refs
+    size = items[0].shape[0]
+    for place, item in enumerate(items):
+        out[place * size : (place + 1) * size, :] = item[...]
+
+
+def pack(items):
+    rows, width = items[0].shape
+    return call("pack", pack_body, [((len(items) * rows, width), BF16)], list(items))[0]
+
+
+def unpack_body(flags, own, sent, got_own, got_sent, y_ref, g_ref):
+    size = y_ref.shape[0] // 2
+    width = y_ref.shape[1]
+    here = jnp.full((1, width), flags[0], jnp.int32) == 1
+    rows = pl.ds(pl.multiple_of(flags[2] * size, size), size)
+    first = pl.ds(pl.multiple_of(flags[3] * size, size), size)
+    second = pl.ds(pl.multiple_of((1 - flags[3]) * size, size), size)
+    last = slice(2 * size, 3 * size)
+    y_ref[first, :] = jnp.where(here, own[rows, :], got_own[rows, :])
+    y_ref[second, :] = jnp.where(here, sent[rows, :], got_sent[rows, :])
+    g_ref[first, :] = jnp.where(here, own[last, :], got_own[last, :])
+    g_ref[second, :] = jnp.where(here, sent[last, :], got_sent[last, :])
+
+
+def unpack(flags, own, sent, got_own, got_sent):
+    rows = 2 * own.shape[0] // 3
+    return call(
+        "unpack",
+        unpack_body,
+        [((rows, own.shape[1]), BF16)] * 2,
+        [flags, own, sent, got_own, got_sent],
+    )
+
+
+def share_body(count, flags, block, across, own, *sent):
+    size = own.shape[0]
+    for step, out in enumerate((own, *sent)):
+        rows = pl.ds(pl.multiple_of((flags[1] ^ step) * size, size), size)
+        out[...] = (block[rows, :].astype(F32) + across[rows, :].astype(F32)).astype(BF16)
+
+
+def share(flags, block, across, count, after=()):
+    rows, width = block.shape
+    return call(
+        "share",
+        partial(share_body, count),
+        [((rows // count, width), BF16)] * count,
+        [flags, block, across],
+        after=after,
+    )
+
+
+def total_body(*refs):
+    *parts, out = refs
+    out[...] = sum(part[...].astype(F32) for part in parts).astype(out.dtype)
+
+
+def total_of(parts, kind=BF16):
+    return call("total", total_body, [(parts[0].shape, kind)], list(parts))[0]
+
+
+def final_first_body(flags, lower, upper, q_ref, k_ref, v_ref, o_ref):
+    width = q_ref.shape[1]
+    first = jnp.full((1, D), flags[2], jnp.int32) == 0
+    total = jnp.where(first, lower[...].astype(F32), upper[...].astype(F32))
+    for place, ref in enumerate((q_ref, k_ref, v_ref)):
+        ref[...] = total[:, place * width : (place + 1) * width]
+    o_ref[...] = total[:, 3 * width :].T
+
+
+def final_first(flags, lower, upper):
+    rows, width = lower.shape[0], D // LANES
+    return call(
+        "final_first",
+        final_first_body,
+        [((rows, width), F32)] * 3 + [((width, rows), F32)],
+        [flags, lower, upper],
+    )
+
+
+def final_second_body(flags, lower, upper, up_ref, down_ref):
+    first = jnp.full((1, 2 * UNITS), flags[2], jnp.int32) == 0
+    total = jnp.where(first, lower[...].astype(F32), upper[...].astype(F32))
+    up_ref[...] = total[:, :UNITS]
+    down_ref[...] = total[:, UNITS:].T
+
+
+def final_second(flags, lower, upper):
+    rows = lower.shape[0]
+    return call(
+        "final_second",
+        final_second_body,
+        [((rows, UNITS), F32), ((UNITS, rows), F32)],
+        [flags, lower, upper],
+    )
+
+
+def merge_body(flags, one, two, upper, out):
+    size, width = one.shape
+    first = jnp.full((1, width), flags[2], jnp.int32) == 0
+    for place, ref in enumerate((one, two)):
+        rows = slice(place * size, (place + 1) * size)
+        out[rows] = jnp.where(first, ref[...], upper[rows])
+
+
+def merge(flags, one, two, upper):
+    return call("merge", merge_body, [(upper.shape, BF16)], [flags, one, two, upper])[0]
+
+
+def vectors_body(*refs):
+    *items, out = refs
+    out[...] = jnp.zeros_like(out)
+    for place, item in enumerate(items):
+        out[2 * place : 2 * place + 2, : item.shape[1]] = item[0:2, :]
+
+
+def vectors_of(items):
+    return call("vectors", vectors_body, [((2 * len(items), D), F32)], list(items))[0]
+
+
+def ranks_body(flags, own, got, out):
+    here = jnp.full((1, D), flags[0], jnp.int32) == 1
+    out[0:8] = own[0:8] + got[0:8]
+    out[8:] = jnp.where(here, own[8:], got[8:])
+
+
+def outer_body(own, got, out):
+    out[0:8] = own[0:8] + got[...]
+    out[8:] = own[8:]
+
+
+def first_rows_body(own, out):
+    out[...] = own[0:8]
+
+
+def line_up_body(count, flags, *refs):
+    *pieces, out = refs
+    size = pieces[0].shape[0]
+    for step, piece in enumerate(pieces):
+        rows = pl.ds(pl.multiple_of((flags[1] ^ step) * size, size), size)
+        out[rows, :] = piece[...]
+
+
+def line_up(flags, pieces, after=()):
+    count, (size, width) = len(pieces), pieces[0].shape
+    return call(
+        "line_up",
+        partial(line_up_body, count),
+        [((count * size, width), BF16)],
+        [flags, *pieces],
+        after=after,
+    )[0]
+
+
+def pick_body(flags, beside, across, out):
+    near = jnp.full((1, out.shape[1]), flags[0], jnp.int32) == 1
+    out[...] = jnp.where(near, beside[...], across[...])
+
+
+def pick(flags, beside, across, after=()):
+    return call(
+        "pick", pick_body, [(beside.shape, BF16)], [flags, beside, across], after=after
+    )[0]
+
+
+def assemble_body(count, flags, *refs):
+    beside, across, out = refs[:count], refs[count:-1], refs[-1]
+    size = beside[0].shape[0]
+    width = out.shape[1]
+    near = jnp.full((1, width), flags[0], jnp.int32) == 1
+    for step in range(count):
+        rows = pl.ds(pl.multiple_of((flags[1] ^ step) * size, size), size)
+        out[rows, :] = jnp.where(near, beside[step][...], across[step][...])
+
+
+def assemble(flags, beside, across):
+    count, (size, width) = len(beside), beside[0].shape
+    return call(
+        "assemble",
+        partial(assemble_body, count),
+        [((count * size, width), BF16)],
+        [flags, *beside, *across],
+    )[0]
 
 
 def on_device(
@@ -692,16 +938,15 @@
         sent = lax.ppermute(rows_of(array, 1 - lane_y), BOTH, crossing)
         return jnp.where(core == lane_y, rows_of(array, lane_y), sent)
 
-    def placed(pairs):
-        stacked = jnp.stack([jnp.stack(pair) for pair in pairs], axis=1)
-        sent = lax.ppermute(stacked, BOTH, returning)
-        micros = jnp.stack(
-            [jnp.where(lane_y == 0, stacked, sent), jnp.where(lane_y == 0, sent, stacked)], axis=2
-        )
-        other = core_swap(lax.dynamic_index_in_dim(micros, 1 - core, 0, keepdims=False))
-        kept = lax.dynamic_index_in_dim(micros, core, 0, keepdims=False)
-        held = jnp.where(core == lane_y, kept, other)
-        return held.reshape(len(pairs), 1, MICRO * slice_len, D)
+    def placed(array, layer):
+        return [
+            lax.ppermute(
+                array,
+                BOTH,
+                [(s * 4 + 2 * m + x, layer * 4 + 2 * s + x) for s in range(2) for x in range(2)],
+            )
+            for m in range(MICRO)
+        ]
 
     label_grid = lax.dynamic_index_in_dim(
         doc_ids.reshape(LANES, MICRO, slice_len), lane_y, 1, keepdims=False
@@ -712,23 +957,52 @@
     )
     labels = jnp.broadcast_to(labels.astype(F32)[None], (8, LANES * slice_len))
 
-    first_block = jnp.concatenate([w_query[0], w_key[0], w_value[0], w_output[0].T], axis=1)
-    up_block, down_block = w_up[0], w_down[0].T
-
-    def fetch(block, layer):
-        whole = lax.all_gather(block, "dp", axis=0, tiled=True)
-        across = lax.ppermute(
-            whole, BOTH, [(layer * 4 + r, (r // 2) * 4 + (r ^ 2)) for r in range(LANES)]
-        )
-        beside = lax.ppermute(
-            whole, BOTH, [(layer * 4 + r, (r // 2) * 4 + r) for r in range(LANES)]
-        )
-        return jnp.where(core == lane_y, beside, across)
-
-    lower_first = fetch(first_block, 0)
-    lower_up, lower_down = fetch(up_block, 0), fetch(down_block, 0)
-    upper_first = fetch(first_block, 1)
-    upper_up, upper_down = fetch(up_block, 1), fetch(down_block, 1)
+    place = lax.axis_index("dp")
+    flags = jnp.stack([core == lane_y, place, core, lane_y]).astype(jnp.int32)
+
+    def line_pairs(step):
+        return [
+            ((r // 2 * count + i) * LANES + r, (r // 2 * count + (i ^ step)) * LANES + r)
+            for i in range(count)
+            for r in range(LANES)
+        ]
+
+    def along_line(block, step):
+        return lax.ppermute(block, ("section", "dp", "mp"), line_pairs(step))
+
+    def line_pieces(block, layer):
+        if count != 4:
+            block = lax.all_gather(block, "dp", axis=0, tiled=True)
+        block = lax.ppermute(
+            block, BOTH, [(layer * LANES + r, (r // 2) * LANES + r) for r in range(LANES)]
+        )
+        if count != 4:
+            return [block]
+        return [block] + [along_line(block, step) for step in range(1, count)]
+
+    def fetched(pieces, hook=()):
+        whole = line_up(flags, pieces, after=hook) if len(pieces) > 1 else pieces[0]
+        across = lax.ppermute(whole, BOTH, crossing)
+        return whole, across
+
+    first = first_block(w_query[0], w_key[0], w_value[0], w_output[0])
+    pieces = line_pieces(first, 0)
+    across = [lax.ppermute(piece, BOTH, crossing) for piece in pieces]
+    if count == 4:
+        lower_first = assemble(flags, pieces, across)
+    else:
+        lower_first = pick(flags, pieces[0], across[0])
+    second = second_block(w_up[0], w_down[0], after=[lower_first])
+    lower_second_whole, lower_second_across = fetched(line_pieces(second, 0))
+    lower_second = pick(flags, lower_second_whole, lower_second_across)
+    upper_first_whole, upper_first_across = fetched(
+        line_pieces(first, 1), [lower_second_whole]
+    )
+    upper_first = pick(flags, upper_first_whole, upper_first_across)
+    upper_second_whole, upper_second_across = fetched(
+        line_pieces(second, 1), [upper_first_whole]
+    )
+    upper_second = pick(flags, upper_second_whole, upper_second_across)
 
     outer_own = jnp.concatenate([norm_gain, norm_bias, feed_gain, feed_bias], axis=0)
     outer_other = core_swap(outer_own)
@@ -756,7 +1030,7 @@
         by_core(outer_other, outer_own), by_core(split_other, split_kept)
     )
 
-    def attention(x, h, first, outer, split):
+    def attention(x, h, first, outer, split, hooks):
         pieces = gather_rows(h)
         near = project(pieces[0], pieces[1], first)
         far = project(pieces[2], pieces[3], first)
@@ -767,178 +1041,222 @@
         o_near, p_own, p_mate, sum_near = attend(
             0, near, near, far, labels, first, split[0], split[1], after=[p_far]
         )
-        terms = settle(p_own, p_mate, p_far, p_far_mate)
-        x2, branch, h2, folded, kept = after_attend(x, terms, outer[2], outer[3])
+        terms = settle(p_own, p_mate, p_far, p_far_mate, after=hooks[0])
+        x2, branch, h2, folded, kept = after_attend(x, terms, outer[2], outer[3], after=hooks[1])
         state = (x, pieces, near, far, o_near, o_far, sum_near, sum_far, x2, branch, folded, kept)
         return x2, h2, state
 
-    def attention_back(grad, sums, state, first, outer, split, following, after=()):
+    def attention_back(grad, sums, state, first, outer, split, following, hooks):
         x, pieces, near, far, o_near, o_far, sum_near, sum_far, x2, branch, folded, kept = state
         dx2, sent, feed_vec = feed_norm_back(
-            sums, grad, labels, x2, outer[2], branch, folded, kept
+            sums, grad, labels, x2, outer[2], branch, folded, kept, after=hooks[0]
         )
         backs = gather_rows(sent)
-        do_near, u_near, vec_near = inner_back(backs[:2], o_near, split[0], split[1], first)
-        do_far, u_far, vec_far = inner_back(backs[2:], o_far, split[0], split[1], first)
+        do_near, u_near, vec_near = inner_back(
+            backs[:2], o_near, split[0], split[1], first, after=hooks[1]
+        )
+        do_far, u_far, vec_far = inner_back(
+            backs[2:], o_far, split[0], split[1], first, after=hooks[2]
+        )
         dq_near, dq_far = attend_back(
-            near, far, do_near, do_far, sum_near, sum_far, labels, after=after
+            near, far, do_near, do_far, sum_near, sum_far, labels, after=hooks[3]
         )
         p_far, p_far_mate = unproject(dq_far, first)
         p_own, p_mate = unproject(dq_near, first, after=[p_far])
         terms = settle(p_own, p_mate, p_far, p_far_mate)
-        mat_grad = grads_of((pieces, (dq_near, dq_far)), (backs, (u_near, u_far)), after=[p_far])
-        result = first_norm_back(terms, dx2, x, outer[0], following)
+        mat_grad = grads_of(
+            (pieces, (dq_near, dq_far)), (backs, (u_near, u_far)), after=[p_far]
+        )
+        result = first_norm_back(terms, dx2, x, outer[0], following, after=hooks[4](mat_grad))
         return result, mat_grad, vec_near + vec_far, feed_vec
 
+    def reduce_blocks(block, after=()):
+        across = lax.ppermute(block, BOTH, returning)
+        if count != 4:
+            total = total_of([block, across])
+            return [lax.psum_scatter(total, "dp", scatter_dimension=0, tiled=True)]
+        return share(flags, block, across, count, after)
+
+    def reduce_line(parts, layer):
+        if count == 4:
+            parts = [parts[0]] + [
+                along_line(part, step) for step, part in enumerate(parts) if step > 0
+            ]
+            parts = [total_of(parts)]
+        return lax.ppermute(
+            parts[0], BOTH, [((r // 2) * LANES + r, layer * LANES + r) for r in range(LANES)]
+        )
+
     lower_in = own_slice(inputs)
+
     upstream = own_slice(cotangent)
-    masked = jnp.where(
-        jnp.broadcast_to(labels[0, :slice_len, None], upstream.shape) >= 0,
-        upstream,
-        jnp.zeros_like(upstream),
-    )
-    top = gather_rows(masked)
+    top = gather_rows(mask_rows(upstream, labels))
 
     h = enter(lower_in, lower_outer[0], lower_outer[1])
-    x2, h2, lower_state = attention(lower_in, h, lower_first, lower_outer, lower_split)
+    x2, h2, lower_state = attention(
+        lower_in,
+        h,
+        lower_first,
+        lower_outer,
+        lower_split,
+        ([lower_second_whole, top[3]], [upper_first_whole]),
+    )
     lower_pieces = gather_rows(h2)
-    f_near, p_own, p_mate = feed(lower_pieces[:2], (), lower_up, lower_down, *lower_split[2:])
-    f_far, p_far, p_far_mate = feed(lower_pieces[2:], (), lower_up, lower_down, *lower_split[2:])
+    f_near, p_own, p_mate = feed(lower_pieces[:2], (), lower_second, *lower_split[2:])
+    f_far, p_far, p_far_mate = feed(lower_pieces[2:], (), lower_second, *lower_split[2:])
     lower_pre = (f_near, f_far)
     terms = settle(p_own, p_mate, p_far, p_far_mate)
     lower_out, lower_branch, h, lower_folded, lower_kept = after_feed(
-        x2, terms, labels, upper_outer[0], upper_outer[1]
-    )
-    x2, h2, upper_state = attention(lower_out, h, upper_first, upper_outer, upper_split)
+        x2,
+        terms,
+        labels,
+        upper_outer[0],
+        upper_outer[1],
+        after=[upper_first_across, upper_second_whole],
+    )
+    x2, h2, upper_state = attention(
+        lower_out, h, upper_first, upper_outer, upper_split, ((), [upper_second_across])
+    )
     upper_pieces = gather_rows(h2)
-    f_near, p_own, p_mate, s_own, s_mate = feed(
-        upper_pieces[:2], top[:2], upper_up, upper_down, *upper_split[2:]
-    )
-    f_far, p_far, p_far_mate, s_far, s_far_mate = feed(
-        upper_pieces[2:], top[2:], upper_up, upper_down, *upper_split[2:]
+    f_near, p_own, p_mate, near_stats = feed(
+        upper_pieces[:2], top[:2], upper_second, *upper_split[2:]
+    )
+    f_far, p_far, p_far_mate, far_stats = feed(
+        upper_pieces[2:], top[2:], upper_second, *upper_split[2:]
     )
     upper_pre = (f_near, f_far)
 
-    near_stats, far_stats = jnp.stack([s_own, s_mate]), jnp.stack([s_far, s_far_mate])
-    stats = jnp.stack([near_stats, far_stats])
-    got = core_swap(stats)
-    stats = stats + jnp.stack([got[:, 1], got[:, 0]], axis=1)
-    got = x_swap(stats)
-    stats = (stats + jnp.stack([got[1], got[0]])) / FF
-    mean = stats[:, :, 0:1]
-    scaled = lax.rsqrt(stats[:, :, 1:2] - mean * mean + EPS)
-    second = scaled * (stats[:, :, 3:4] - mean * stats[:, :, 2:3])
-    stats = jnp.concatenate(
-        [mean, scaled, stats[:, :, 2:3], second, jnp.zeros_like(stats[:, :, 4:])], axis=2
-    )
-
-    def feed_backward(pieces, rows, stat_pieces, pre, up, down, split):
-        near_stats = [stat_pieces[0, 0], stat_pieces[0, 1]] if stat_pieces is not None else []
-        far_stats = [stat_pieces[1, 0], stat_pieces[1, 1]] if stat_pieces is not None else []
+    stats = group_stats(near_stats, far_stats)
+
+    def feed_backward(pieces, rows, stats, pre, second, split, hooks):
         df_far, n_far, p_far, p_far_mate, vec_far = feed_back(
-            pieces[2:], far_stats, pre[1], split[2], split[3], up, down
+            pieces[2:], stats, 2, pre[1], split[2], split[3], second, after=hooks[0]
         )
         df_near, n_near, p_own, p_mate, vec_near = feed_back(
-            pieces[:2], near_stats, pre[0], split[2], split[3], up, down, after=[p_far]
+            pieces[:2], stats, 0, pre[0], split[2], split[3], second, after=[p_far, *hooks[1]]
         )
         terms = settle(p_own, p_mate, p_far, p_far_mate)
-        mat_grad = grads_of((rows, (df_near, df_far)), (pieces, (n_near, n_far)), after=[p_far])
+        mat_grad = grads_of(
+            (rows, (df_near, df_far)), (pieces, (n_near, n_far)), after=[p_far, p_own]
+        )
         return terms, mat_grad, vec_near + vec_far
 
-    sums, upper_feed_grad, upper_middle = feed_backward(
-        top, upper_pieces, stats, upper_pre, upper_up, upper_down, upper_split
-    )
+    sums, block, upper_middle = feed_backward(
+        top, upper_pieces, [stats], upper_pre, upper_second, upper_split, ((), ())
+    )
+    upper_second_parts = reduce_blocks(block)
+    sent = call(
+        "pair_sum", pair_sum_body, [(p_far.shape, BF16)], [p_far, core_swap(p_far_mate)]
+    )[0]
+    upper_out = finish_feed(x2, (p_own, core_swap(p_mate), x_swap(sent)), labels)
     following = (labels, lower_branch, lower_folded, lower_kept)
-    (upper_grad, upper_norm, sent), upper_first_grad, upper_inner, upper_feed = attention_back(
-        upstream, sums, upper_state, upper_first, upper_outer, upper_split, following
-    )
-    upper_out = finish_feed(x2, settle(p_own, p_mate, p_far, p_far_mate), labels)
+    (upper_grad, upper_norm, sent), block, upper_inner, upper_feed = attention_back(
+        upstream,
+        sums,
+        upper_state,
+        upper_first,
+        upper_outer,
+        upper_split,
+        following,
+        ([block], (), (), [upper_second_parts[0], sent], lambda item: [item, upper_out]),
+    )
+    upper_second_sum = reduce_line(upper_second_parts, 1)
+    upper_first_parts = reduce_blocks(block)
 
     backs = gather_rows(sent)
-    sums, lower_feed_grad, lower_middle = feed_backward(
-        backs, lower_pieces, None, lower_pre, lower_up, lower_down, lower_split
-    )
-    (lower_grad, lower_norm), lower_first_grad, lower_inner, lower_feed = attention_back(
-        upper_grad, sums, lower_state, lower_first, lower_outer, lower_split, ()
-    )
-
-    layer_outputs, upper_grad_held = placed([(lower_out, upper_out), (upper_grad, upper_grad)])
-    lower_grad_held = placed([(lower_grad, lower_grad)])[0]
-    input_grads = by_core(lower_grad_held, upper_grad_held)
-
-    def collect(grad):
-        parts = grad.reshape(count, 2, D // count // 2, -1)
-        kept = lax.dynamic_index_in_dim(parts, core, 1, keepdims=False)
-        got = core_swap(lax.dynamic_index_in_dim(parts, 1 - core, 1, keepdims=False))
-        both = jnp.stack([by_core(kept, got), by_core(got, kept)])
-        line = lax.psum_scatter(
-            both, "mp", scatter_dimension=0, axis_index_groups=Y_PAIRS, tiled=False
-        )
-        return lax.psum_scatter(line, "dp", scatter_dimension=0, tiled=False)
-
-    upper_sum = jnp.concatenate([collect(upper_first_grad), collect(upper_feed_grad)], axis=1)
-    lower_sum = jnp.concatenate([collect(lower_first_grad), collect(lower_feed_grad)], axis=1)
-    sum_kept = by_core(lower_sum, upper_sum)
-    sum_got = core_swap(by_core(upper_sum, lower_sum))
-    summed = jnp.concatenate(
-        [by_core(sum_kept, sum_got), by_core(sum_got, sum_kept)], axis=0
-    ).astype(F32)
+    own = pack([lower_out, upper_out, upper_grad])
+    swapped = lax.ppermute(own, BOTH, returning)
+    inward = [((r // 2) * LANES + r, (1 - r // 2) * LANES + r) for r in range(LANES)]
+    layer_outputs, upper_held = unpack(
+        flags, own, swapped, lax.ppermute(own, BOTH, inward), lax.ppermute(swapped, BOTH, inward)
+    )
+    sums, block, lower_middle = feed_backward(
+        backs,
+        lower_pieces,
+        (),
+        lower_pre,
+        lower_second,
+        lower_split,
+        ([own], [upper_first_parts[0], upper_second_sum]),
+    )
+    upper_first_sum = reduce_line(upper_first_parts, 1)
+    lower_second_parts = reduce_blocks(block)
+    lower_second_sum = reduce_line(lower_second_parts, 0)
+    last_parts = []
+
+    def reduced(item):
+        last_parts.extend(reduce_blocks(item))
+        return last_parts
+
+    (lower_grad, lower_norm), _, lower_inner, lower_feed = attention_back(
+        upper_grad,
+        sums,
+        lower_state,
+        lower_first,
+        lower_outer,
+        lower_split,
+        (),
+        (
+            [block, swapped],
+            (),
+            (),
+            [lower_second_parts[0], upper_first_sum, layer_outputs],
+            lambda item: [reduced(item)[0], lower_second_sum],
+        ),
+    )
+    input_grads = merge(flags, *placed(lower_grad, 0), upper_held)
+    grad_query, grad_key, grad_value, grad_output = final_first(
+        flags, reduce_line(last_parts, 0), upper_first_sum
+    )
+    grad_up, grad_down = final_second(flags, lower_second_sum, upper_second_sum)
+
+    vectors = vectors_of(
+        [lower_norm, lower_feed, upper_norm, upper_feed, lower_middle, upper_middle]
+        + [lower_inner, upper_inner]
+    )
+    shape = [(vectors.shape, F32)]
+    vectors = total_of([vectors, y_swap(vectors)], F32)
+    vectors = call("ranks", ranks_body, shape, [flags, vectors, core_swap(vectors)])[0]
+    outer = call("first_rows", first_rows_body, [((8, D), F32)], [vectors])[0]
+    vectors = call("outer", outer_body, shape, [vectors, x_swap(outer)])[0]
+    if count == 4:
+        vectors = total_of(
+            [vectors]
+            + [
+                lax.ppermute(vectors, "dp", [(i, i ^ step) for i in range(count)])
+                for step in range(1, count)
+            ],
+            F32,
+        )
+    else:
+        vectors = lax.psum(vectors, "dp")
+
+    def part(rows, start, size):
+        rows = lax.dynamic_slice(rows, (core * rows.shape[0] // 2, start), (rows.shape[0] // 2, size))
+        return [rows[i : i + 1] for i in range(rows.shape[0])]
+
     width = D // LANES
-    grad_query, grad_key, grad_value, grad_output, grad_up, grad_down = jnp.split(
-        summed, [width, 2 * width, 3 * width, D, D + UNITS], axis=1
-    )
-
-    outer = jnp.concatenate([lower_norm[:2], lower_feed[:2], upper_norm[:2], upper_feed[:2]])
-    split = jnp.stack(
-        [
-            jnp.concatenate([lower_inner[:2], lower_middle[:2]], axis=1),
-            jnp.concatenate([upper_inner[:2], upper_middle[:2]], axis=1),
-        ]
-    )
-    packed = jnp.concatenate([outer.reshape(-1), split.reshape(-1)])
-    packed += y_swap(packed)
-    outer = packed[: 8 * D].reshape(8, D)
-    split = packed[8 * D :].reshape(2, 2, -1)
-    outer += core_swap(outer)
-    outer += x_swap(outer)
-
-    def by_dest(items):
-        return [item.reshape(-1, count, item.shape[-1] // count) for item in items]
-
-    outer, inner, middle = by_dest([outer, split[:, :, :width], split[:, :, width:]])
-    sizes = [item.shape[0] * item.shape[2] for item in (outer, inner, middle)]
-    packed = jnp.concatenate(
-        [item.transpose(1, 0, 2).reshape(count, -1) for item in (outer, inner, middle)], axis=1
-    )
-    packed = dp_scatter(packed)
-    outer = packed[: sizes[0]].reshape(2, 4, LANES, -1)
-    outer = lax.dynamic_index_in_dim(outer, core, 0, keepdims=False)
-    outer = lax.dynamic_index_in_dim(outer, lane, 1, keepdims=False)
-    split = packed[sizes[0] :]
-    split = jnp.where(core == lane_y, split, core_swap(split))
-    inner = lax.dynamic_index_in_dim(
-        split[: sizes[1]].reshape(2, 2, -1), core, 0, keepdims=False
-    )
-    middle = lax.dynamic_index_in_dim(
-        split[sizes[1] :].reshape(2, 2, -1), core, 0, keepdims=False
-    )
+    size = D // count // LANES
+    outer = part(vectors[:8], (place * LANES + lane) * size, size)
+    middle = part(vectors[8:12], place * (UNITS // count), UNITS // count)
+    inner = part(vectors[12:], place * (width // count), width // count)
     return (
-        layer_outputs,
-        input_grads,
-        outer[0][None],
-        outer[1][None],
+        layer_outputs[None],
+        input_grads[None],
+        outer[0],
+        outer[1],
         grad_query[None],
         grad_key[None],
         grad_value[None],
-        inner[0][None],
-        inner[1][None],
-        grad_output.T[None],
-        outer[2][None],
-        outer[3][None],
+        inner[0],
+        inner[1],
+        grad_output[None],
+        outer[2],
+        outer[3],
         grad_up[None],
-        middle[0][None],
-        middle[1][None],
-        grad_down.T[None],
+        middle[0],
+        middle[1],
+        grad_down[None],
     )
 
 

time: 691 us -> 518 us (0.75)
  waiting for transfers between devices: 321 us -> 196 us
  starting transfers between devices: 87.9 us -> 178 us
  local copies, waits for them, and re-layouts: 87.5 us -> 20.5 us
  other arithmetic: 42.1 us -> 4.16 us
  Pallas kernels: 123 us -> 107 us
  between operations: 17.3 us -> 2.72 us
    ppermute x17 -> x51, starting transfers between devices: 39.7 us -> 140 us  [the longest x24 99.6 us: along_line(): return lax.ppermute(block, ('section', 'dp', 'mp'), line_pairs(step))]
    reduce_scatter x8 -> x0, waiting for transfers between devices: 77.6 us -> none  [the longest x4 77.6 us: collect(): return lax.psum_scatter(line, 'dp', scatter_dimension=0, tiled=False)]
    all_gather x3 -> x0, waiting for transfers between devices: 39.7 us -> none  [fetch(): whole = lax.all_gather(block, 'dp', axis=0, tiled=True)]
    ppermute x17 -> x51, waiting for transfers between devices: 52.3 us -> 87.4 us  [the longest x24 72.4 us: along_line(): return lax.ppermute(block, ('section', 'dp', 'mp'), line_pairs(step))]
    ppermute x18, waiting for transfers between devices: 133 us -> 100 us  [x_swap(): return lax.ppermute(x, 'mp', [(i, i ^ 1) for i in range(LANES)])]
    unnamed x413 -> x46, local copies, waits for them, and re-layouts: 43.3 us -> 13.3 us
    dynamic_slice x11 -> x2, local copies, waits for them, and re-layouts: 21.8 us -> 0.16 us  [part(): lax.dynamic_slice(rows, (core * rows.shape[0] // 2, start), (rows.shape[0...]
    another operation x20 -> x1, other arithmetic: 21.6 us -> 0.08 us  [on_device(): flags = jnp.stack([core == lane_y, place, core, lane_y]).astype(jnp.int32)]
  transfers between devices with their start and end apart: 94 -> 109, of which waited for: 37 -> 34; matrix products, arithmetic and copies ran while one was open for 11% -> 3% of each run, Pallas kernels for 13% -> 12%
where the time goes in v3:
time: 518 us; the launch traced here: 509 us
  waiting for transfers between devices  196 us (38%)
  starting transfers between devices  178 us (34%)
  Pallas kernels  107 us (21%)
  local copies, waits for them, and re-layouts  20.5 us (4%)
    pallas_call x79, Pallas kernels, call(): pl.pallas_call(kernel, out_shape=tuple((jax.ShapeDtypeStruct(shape, kind)...  107 us
    ppermute x18, waiting for transfers between devices, x_swap(): return lax.ppermute(x, 'mp', [(i, i ^ 1) for i in range(LANES)])  100 us
    ppermute x24, starting transfers between devices, along_line(): return lax.ppermute(block, ('section', 'dp', 'mp'), line_pairs(step))  99.6 us
    ppermute x24, waiting for transfers between devices, along_line(): return lax.ppermute(block, ('section', 'dp', 'mp'), line_pairs(step))  72.4 us
    ppermute x18, starting transfers between devices, x_swap(): return lax.ppermute(x, 'mp', [(i, i ^ 1) for i in range(LANES)])  26.3 us
    unnamed x46, local copies, waits for them, and re-layouts  13.3 us
  transfers between devices with their start and end apart: 109, of which 34 were waited for; matrix products, arithmetic and copies ran while one was open for 3% of the time, Pallas kernels for 12%

profile of v3, /device:TPU:0, one launch (start us, length us, event | category | flops | bytes accessed | tf_op | source)
XLA Modules:
  0.0 509.1 jit_solution(15800736143012480033)
XLA Ops:
  5.1 4.9 collective-permute-start.4
  10.0 4.5 collective-permute-start.5
  21.8 4.1 collective-permute-done.5.refs_3_
  39.6 2.7 collective-permute-start.13
  49.4 4.6 collective-permute-start.18
  54.0 3.0 collective-permute-start.19
  57.0 3.4 collective-permute-start.20
  62.7 3.2 collective-permute-done.18.refs_2_
  67.2 12.1 %collective-permute-done.19.refs_3_ = bf16[192,1536]{1,0:T(8,128)(2,1)S(1)} collective-permute-done((bf16[192,1536]{1,0:T(8,128)(2,1)S(1)}, bf16[192,1536]{1,0:T(8,128)(2,1)S(1)}, u32[]{:S(2)}, u32[]{:S(2)}) %collective-permute-start.19) | collective-permute-done | bytes 589856 | tf_op jit(solution)/shard_map/ppermute | solution.py:971
  83.1 4.0 collective-permute-done.11.refs_0_.refs_2_
  90.8 4.2 attend.4
  95.3 3.9 collective-permute-done.22.refs_2_.refs_0_.refs_8_
  99.2 3.4 collective-permute-start.26
  102.5 3.7 collective-permute-start.27
  106.3 4.2 attend.5
  112.3 3.2 collective-permute-start.28
  116.8 6.0 %collective-permute-done.28.refs_4_ = bf16[192,768]{1,0:T(8,128)(2,1)S(1)} collective-permute-done((bf16[192,768]{1,0:T(8,128)(2,1)S(1)}, bf16[192,768]{1,0:T(8,128)(2,1)S(1)}, u32[]{:S(2)}, u32[]{:S(2)}) %collective-permute-start.28) | collective-permute-done | bytes 294944 | tf_op jit(solution)/shard_map/ppermute | solution.py:971
  125.1 9.2 %collective-permute-done.32.refs_0_.refs_2_ = bf16[256,768]{1,0:T(8,128)(2,1)S(1)} collective-permute-done((bf16[256,768]{1,0:T(8,128)(2,1)S(1)}, bf16[256,768]{1,0:T(8,128)(2,1)S(1)}, u32[]{:S(2)}, u32[]{:S(2)}) %collective-permute-start.32) | collective-permute-done | bytes 393248 | tf_op jit(solution)/shard_map/ppermute | solution.py:151
  134.4 3.4 collective-permute-start.38
  140.1 4.4 collective-permute-start.40
  149.2 13.9 %collective-permute-done.39.refs_3_ = bf16[192,1536]{1,0:T(8,128)(2,1)S(1)} collective-permute-done((bf16[192,1536]{1,0:T(8,128)(2,1)S(1)}, bf16[192,1536]{1,0:T(8,128)(2,1)S(1)}, u32[]{:S(2)}, u32[]{:S(2)}) %collective-permute-start.39) | collective-permute-done | bytes 589856 | tf_op jit(solution)/shard_map/ppermute | solution.py:971
  169.4 10.5 %collective-permute-done.35.refs_3_ = bf16[272,768]{1,0:T(8,128)(2,1)S(1)} collective-permute-done((bf16[272,768]{1,0:T(8,128)(2,1)S(1)}, bf16[272,768]{1,0:T(8,128)(2,1)S(1)}, u32[]{:S(2)}, u32[]{:S(2)}) %collective-permute-start.35) | collective-permute-done | bytes 417824 | tf_op jit(solution)/shard_map/ppermute | solution.py:151
  182.3 9.2 %collective-permute-done.42.refs_0_.refs_2_ = bf16[256,768]{1,0:T(8,128)(2,1)S(1)} collective-permute-done((bf16[256,768]{1,0:T(8,128)(2,1)S(1)}, bf16[256,768]{1,0:T(8,128)(2,1)S(1)}, u32[]{:S(2)}, u32[]{:S(2)}) %collective-permute-start.42) | collective-permute-done | bytes 393248 | tf_op jit(solution)/shard_map/ppermute | solution.py:151
  194.0 4.2 attend.6
  198.6 4.4 attend.7
  205.0 10.4 %collective-permute-done.46.refs_3_ = bf16[272,768]{1,0:T(8,128)(2,1)S(1)} collective-permute-done((bf16[272,768]{1,0:T(8,128)(2,1)S(1)}, bf16[272,768]{1,0:T(8,128)(2,1)S(1)}, u32[]{:S(2)}, u32[]{:S(2)}) %collective-permute-start.46) | collective-permute-done | bytes 417824 | tf_op jit(solution)/shard_map/ppermute | solution.py:151
  218.2 8.5 %collective-permute-done.51.refs_0_.refs_2_ = bf16[256,768]{1,0:T(8,128)(2,1)S(1)} collective-permute-done((bf16[256,768]{1,0:T(8,128)(2,1)S(1)}, bf16[256,768]{1,0:T(8,128)(2,1)S(1)}, u32[]{:S(2)}, u32[]{:S(2)}) %collective-permute-start.51) | collective-permute-done | bytes 393248 | tf_op jit(solution)/shard_map/ppermute | solution.py:151
  227.5 2.6 feed.6
  230.1 2.6 feed.7
  235.6 2.4 collective-permute-done.56.refs_1_
  238.1 2.3 feed_back.4
  240.4 2.4 feed_back.5
  242.8 3.1 grads.4.refs_10_.refs_1_
  250.7 9.7 %collective-permute-done.59.refs_2_ = bf16[256,768]{1,0:T(8,128)(2,1)S(1)} collective-permute-done((bf16[256,768]{1,0:T(8,128)(2,1)S(1)}, bf16[256,768]{1,0:T(8,128)(2,1)S(1)}, u32[]{:S(2)}, u32[]{:S(2)}) %collective-permute-start.59) | collective-permute-done | bytes 393248 | tf_op jit(solution)/shard_map/ppermute | solution.py:151
  263.5 8.8 %collective-permute-done.61.refs_0_.refs_8_ = bf16[272,768]{1,0:T(8,128)(2,1)S(1)} collective-permute-done((bf16[272,768]{1,0:T(8,128)(2,1)S(1)}, bf16[272,768]{1,0:T(8,128)(2,1)S(1)}, u32[]{:S(2)}, u32[]{:S(2)}) %collective-permute-start.61) | collective-permute-done | bytes 417824 | tf_op jit(solution)/shard_map/ppermute | solution.py:151
  277.8 13.1 %attend_back.2 = (bf16[512,576]{1,0:T(8,128)(2,1)S(1)}, bf16[512,576]{1,0:T(8,128)(2,1)S(1)}) custom-call(bf16[512,576]{1,0:T(8,128)(2,1)S(1)} %project.6.refs_1_.refs_0_, bf16[512,576]{1,0:T(8,128)(2,1)S(1)} %project.7.refs_0_.refs_2_.refs_1_, bf16[512,192]{1,0:T(8,128)(2,1)S(1)} %get-tuple-element.179.refs_2_, ...), custom_call_target="tpu_custom_call" | custom-call | flops 6039797760 | bytes 6291456 | tf_op jit(solution)/shard_map/attend_back/pallas_call | solution.py:40
  298.6 8.8 %collective-permute-start.74 = (bf16[192,1536]{1,0:T(8,128)(2,1)S(1)}, bf16[192,1536]{1,0:T(8,128)(2,1)S(1)}, u32[]{:S(2)}, u32[]{:S(2)}) collective-permute-start(bf16[192,1536]{1,0:T(8,128)(2,1)S(1)} %get-tuple-element.204), channel_id=1, source_target_pairs={{0,4},{1,5},{18,22},{19,23},{4,0},{5,1},{22,18},{23,19},{8,12},{9,... | collective-permute-start | bytes 1769480 | tf_op jit(solution)/shard_map/ppermute | solution.py:971
  307.4 6.0 %collective-permute-start.75 = (bf16[192,1536]{1,0:T(8,128)(2,1)S(1)}, bf16[192,1536]{1,0:T(8,128)(2,1)S(1)}, u32[]{:S(2)}, u32[]{:S(2)}) collective-permute-start(bf16[192,1536]{1,0:T(8,128)(2,1)S(1)} %get-tuple-element.205), channel_id=1, source_target_pairs={{0,8},{1,9},{18,26},{19,27},{4,12},{5,13},{22,30},{23,31},{8,0},{9... | collective-permute-start | bytes 1769480 | tf_op jit(solution)/shard_map/ppermute | solution.py:971
  313.4 4.6 collective-permute-start.76
  321.2 6.5 %collective-permute-done.71.refs_0_.refs_8_ = bf16[272,768]{1,0:T(8,128)(2,1)S(1)} collective-permute-done((bf16[272,768]{1,0:T(8,128)(2,1)S(1)}, bf16[272,768]{1,0:T(8,128)(2,1)S(1)}, u32[]{:S(2)}, u32[]{:S(2)}) %collective-permute-start.71) | collective-permute-done | bytes 417824 | tf_op jit(solution)/shard_map/ppermute | solution.py:151
  327.7 6.2 %collective-permute-done.75.refs_2_ = bf16[192,1536]{1,0:T(8,128)(2,1)S(1)} collective-permute-done((bf16[192,1536]{1,0:T(8,128)(2,1)S(1)}, bf16[192,1536]{1,0:T(8,128)(2,1)S(1)}, u32[]{:S(2)}, u32[]{:S(2)}) %collective-permute-start.75) | collective-permute-done | bytes 589856 | tf_op jit(solution)/shard_map/ppermute | solution.py:971
  337.8 2.4 feed_back.6
  340.3 2.4 feed_back.7
  342.7 2.7 grads.6.refs_10_.refs_1_
  347.5 8.8 %collective-permute-start.85 = (bf16[192,768]{1,0:T(8,128)(2,1)S(1)}, bf16[192,768]{1,0:T(8,128)(2,1)S(1)}, u32[]{:S(2)}, u32[]{:S(2)}) collective-permute-start(bf16[192,768]{1,0:T(8,128)(2,1)S(1)} %get-tuple-element.225), channel_id=1, source_target_pairs={{0,4},{1,5},{18,22},{19,23},{4,0},{5,1},{22,18},{23,19},{8,12},{9,... | collective-permute-start | bytes 884744 | tf_op jit(solution)/shard_map/ppermute | solution.py:971
  358.0 3.0 collective-permute-done.85.refs_1_
  363.7 5.0 collective-permute-start.86
  368.7 3.6 collective-permute-start.87
  373.4 6.4 %collective-permute-done.86.refs_2_ = bf16[192,768]{1,0:T(8,128)(2,1)S(1)} collective-permute-done((bf16[192,768]{1,0:T(8,128)(2,1)S(1)}, bf16[192,768]{1,0:T(8,128)(2,1)S(1)}, u32[]{:S(2)}, u32[]{:S(2)}) %collective-permute-start.86) | collective-permute-done | bytes 294944 | tf_op jit(solution)/shard_map/ppermute | solution.py:971
  381.2 6.5 %collective-permute-done.82.refs_0_.refs_8_ = bf16[272,768]{1,0:T(8,128)(2,1)S(1)} collective-permute-done((bf16[272,768]{1,0:T(8,128)(2,1)S(1)}, bf16[272,768]{1,0:T(8,128)(2,1)S(1)}, u32[]{:S(2)}, u32[]{:S(2)}) %collective-permute-start.82) | collective-permute-done | bytes 417824 | tf_op jit(solution)/shard_map/ppermute | solution.py:151
  387.9 2.4 collective-permute-start.88
  394.5 13.1 %attend_back.3 = (bf16[512,576]{1,0:T(8,128)(2,1)S(1)}, bf16[512,576]{1,0:T(8,128)(2,1)S(1)}) custom-call(bf16[512,576]{1,0:T(8,128)(2,1)S(1)} %project.4.refs_1_.refs_0_, bf16[512,576]{1,0:T(8,128)(2,1)S(1)} %project.5.refs_0_.refs_2_.refs_1_, bf16[512,192]{1,0:T(8,128)(2,1)S(1)} %get-tuple-element.219.refs_2_, ...), custom_call_target="tpu_custom_call" | custom-call | flops 6039797760 | bytes 6291456 | tf_op jit(solution)/shard_map/attend_back/pallas_call | solution.py:40
  413.5 4.8 collective-permute-start.94
  418.3 3.4 collective-permute-start.95
  421.8 5.5 %collective-permute-done.93.refs_1_ = bf16[192,1536]{1,0:T(8,128)(2,1)S(1)} collective-permute-done((bf16[192,1536]{1,0:T(8,128)(2,1)S(1)}, bf16[192,1536]{1,0:T(8,128)(2,1)S(1)}, u32[]{:S(2)}, u32[]{:S(2)}) %collective-permute-start.93) | collective-permute-done | bytes 589856 | tf_op jit(solution)/shard_map/ppermute | solution.py:971
  427.2 11.6 %collective-permute-done.94.refs_2_ = bf16[192,1536]{1,0:T(8,128)(2,1)S(1)} collective-permute-done((bf16[192,1536]{1,0:T(8,128)(2,1)S(1)}, bf16[192,1536]{1,0:T(8,128)(2,1)S(1)}, u32[]{:S(2)}, u32[]{:S(2)}) %collective-permute-start.94) | collective-permute-done | bytes 589856 | tf_op jit(solution)/shard_map/ppermute | solution.py:971
  444.4 8.3 %collective-permute-done.91.refs_2_ = bf16[256,768]{1,0:T(8,128)(2,1)S(1)} collective-permute-done((bf16[256,768]{1,0:T(8,128)(2,1)S(1)}, bf16[256,768]{1,0:T(8,128)(2,1)S(1)}, u32[]{:S(2)}, u32[]{:S(2)}) %collective-permute-start.91) | collective-permute-done | bytes 393248 | tf_op jit(solution)/shard_map/ppermute | solution.py:151
  454.3 4.1 collective-permute-done.99.refs_1_
  464.1 6.9 %collective-permute-start.102 = (f32[16,768]{1,0:T(8,128)S(1)}, f32[16,768]{1,0:T(8,128)S(1)}, u32[]{:S(2)}, u32[]{:S(2)}) collective-permute-start(f32[16,768]{1,0:T(8,128)S(1)} %outer.1.refs_0_), channel_id=1, source_target_pairs={{0,4},{4,0},{8,12},{12,8},{1,5},{5,1},{9,13},{13,9},{2,6},{6,2},{1... | collective-permute-start | bytes 147464 | tf_op jit(solution)/shard_map/ppermute | solution.py:1226
  472.9 4.8 collective-permute-start.106
  477.7 3.4 collective-permute-start.107
  481.2 2.4 collective-permute-start.104
  486.3 7.9 %collective-permute-done.103.refs_2_ = f32[16,768]{1,0:T(8,128)S(1)} collective-permute-done((f32[16,768]{1,0:T(8,128)S(1)}, f32[16,768]{1,0:T(8,128)S(1)}, u32[]{:S(2)}, u32[]{:S(2)}) %collective-permute-start.103) | collective-permute-done | bytes 49184 | tf_op jit(solution)/shard_map/ppermute | solution.py:1226
  500.5 5.2 %collective-permute-done.98.refs_2_ = bf16[256,768]{1,0:T(8,128)(2,1)S(1)} collective-permute-done((bf16[256,768]{1,0:T(8,128)(2,1)}, bf16[256,768]{1,0:T(8,128)(2,1)S(1)}, u32[]{:S(2)}, u32[]{:S(2)}) %collective-permute-start.98) | collective-permute-done | bytes 393248 | tf_op jit(solution)/shard_map/ppermute | solution.py:943
  (309 shorter events, 149.6 us)
Async XLA Ops:
  5.1 15.4 %collective-permute-start.4 = (bf16[192,768]{1,0:T(8,128)(2,1)S(1)}, bf16[192,768]{1,0:T(8,128)(2,1)S(1)}, u32[]{:S(2)}, u32[]{:S(2)}) collective-permute-start(bf16[192,768]{1,0:T(8,128)(2,1)S(1)} %collective-permute-done.3.refs_1_), channel_id=1, source_target_pairs={{0,4},{1,5},{18,22},{19,23},{4,0},{5,1},{22,18},{23,19},{8,12},{9,... | collective-permute-start | bytes 884744 | tf_op jit(solution)/shard_map/ppermute | solution.py:971
  10.0 15.8 %collective-permute-start.5 = (bf16[192,768]{1,0:T(8,128)(2,1)S(1)}, bf16[192,768]{1,0:T(8,128)(2,1)S(1)}, u32[]{:S(2)}, u32[]{:S(2)}) collective-permute-start(bf16[192,768]{1,0:T(8,128)(2,1)S(1)} %collective-permute-done.3.refs_1_), channel_id=1, source_target_pairs={{0,8},{1,9},{18,26},{19,27},{4,12},{5,13},{22,30},{23,31},{8,0},{9... | collective-permute-start | bytes 884744 | tf_op jit(solution)/shard_map/ppermute | solution.py:971
  14.5 12.6 %collective-permute-start.6 = (bf16[192,768]{1,0:T(8,128)(2,1)S(1)}, bf16[192,768]{1,0:T(8,128)(2,1)S(1)}, u32[]{:S(2)}, u32[]{:S(2)}) collective-permute-start(bf16[192,768]{1,0:T(8,128)(2,1)S(1)} %collective-permute-done.3.refs_1_), channel_id=1, source_target_pairs={{0,12},{1,13},{18,30},{19,31},{4,8},{5,9},{22,26},{23,27},{8,4},{9... | collective-permute-start | bytes 884744 | tf_op jit(solution)/shard_map/ppermute | solution.py:971
  16.4 82.7 %collective-permute-start.25 = (bf16[192,768]{1,0:T(8,128)(2,1)S(1)}, bf16[192,768]{1,0:T(8,128)(2,1)S(1)}, u32[]{:S(2)}, u32[]{:S(2)}) collective-permute-start(bf16[192,768]{1,0:T(8,128)(2,1)S(1)} %first_block.1), channel_id=1, source_target_pairs={{16,0},{17,1},{18,18},{19,19},{20,4},{21,5},{22,22},{23,23},{24,8}... | collective-permute-start | bytes 884744 | tf_op jit(solution)/shard_map/ppermute | solution.py:976
  19.1 16.2 %collective-permute-start.7 = (bf16[192,768]{1,0:T(8,128)(2,1)S(1)}, bf16[192,768]{1,0:T(8,128)(2,1)S(1)}, u32[]{:S(2)}, u32[]{:S(2)}) collective-permute-start(bf16[192,768]{1,0:T(8,128)(2,1)S(1)} %collective-permute-done.3.refs_1_), channel_id=1, source_target_pairs={{0,2},{1,3},{18,16},{19,17},{4,6},{5,7},{22,20},{23,21},{8,10},{9,... | collective-permute-start | bytes 884744 | tf_op jit(solution)/shard_map/ppermute | solution.py:990
  20.4 17.7 %collective-permute-start.8 = (bf16[192,768]{1,0:T(8,128)(2,1)S(1)}, bf16[192,768]{1,0:T(8,128)(2,1)S(1)}, u32[]{:S(2)}, u32[]{:S(2)}) collective-permute-start(bf16[192,768]{1,0:T(8,128)(2,1)S(1)} %collective-permute-done.4.refs_2_), channel_id=1, source_target_pairs={{0,2},{1,3},{18,16},{19,17},{4,6},{5,7},{22,20},{23,21},{8,10},{9,... | collective-permute-start | bytes 884744 | tf_op jit(solution)/shard_map/ppermute | solution.py:990
  25.9 13.0 %collective-permute-start.9 = (bf16[192,768]{1,0:T(8,128)(2,1)S(1)}, bf16[192,768]{1,0:T(8,128)(2,1)S(1)}, u32[]{:S(2)}, u32[]{:S(2)}) collective-permute-start(bf16[192,768]{1,0:T(8,128)(2,1)S(1)} %collective-permute-done.5.refs_3_), channel_id=1, source_target_pairs={{0,2},{1,3},{18,16},{19,17},{4,6},{5,7},{22,20},{23,21},{8,10},{9,... | collective-permute-start | bytes 884744 | tf_op jit(solution)/shard_map/ppermute | solution.py:990
  27.2 15.1 %collective-permute-start.10 = (bf16[192,768]{1,0:T(8,128)(2,1)S(1)}, bf16[192,768]{1,0:T(8,128)(2,1)S(1)}, u32[]{:S(2)}, u32[]{:S(2)}) collective-permute-start(bf16[192,768]{1,0:T(8,128)(2,1)S(1)} %collective-permute-done.6.refs_4_), channel_id=1, source_target_pairs={{0,2},{1,3},{18,16},{19,17},{4,6},{5,7},{22,20},{23,21},{8,10},{9,... | collective-permute-start | bytes 884744 | tf_op jit(solution)/shard_map/ppermute | solution.py:990
  36.1 25.1 %collective-permute-start = (bf16[256,768]{1,0:T(8,128)(2,1)}, bf16[256,768]{1,0:T(8,128)(2,1)}, u32[]{:S(2)}, u32[]{:S(2)}) collective-permute-start(bf16[256,768]{1,0:T(8,128)(2,1)} %constant_dynamic-slice_fusion.5), channel_id=1, source_target_pairs={{0,2},{1,3},{18,16},{19,17},{4,6},{5,7},{22,20},{23,21},{8,10},{9,... | collective-permute-start | bytes 1179656 | tf_op jit(solution)/shard_map/ppermute | solution.py:938
  38.8 18.1 %collective-permute-start.1 = (f32[4,768]{1,0:T(4,128)}, f32[4,768]{1,0:T(4,128)}, u32[]{:S(2)}, u32[]{:S(2)}) collective-permute-start(f32[4,768]{1,0:T(4,128)} %pad_maximum_fusion), channel_id=1, source_target_pairs={{0,16},{16,0},{1,17},{17,1},{2,18},{18,2},{3,19},{19,3},{4,20},{20... | collective-permute-start | bytes 36872 | tf_op jit(solution)/shard_map/ppermute | solution.py:147
  49.4 16.5 %collective-permute-start.18 = (bf16[192,1536]{1,0:T(8,128)(2,1)S(1)}, bf16[192,1536]{1,0:T(8,128)(2,1)S(1)}, u32[]{:S(2)}, u32[]{:S(2)}) collective-permute-start(bf16[192,1536]{1,0:T(8,128)(2,1)S(1)} %collective-permute-done.17.refs_1_), channel_id=1, source_target_pairs={{0,4},{1,5},{18,22},{19,23},{4,0},{5,1},{22,18},{23,19},{8,12},{9,... | collective-permute-start | bytes 1769480 | tf_op jit(solution)/shard_map/ppermute | solution.py:971
  54.0 25.4 %collective-permute-start.19 = (bf16[192,1536]{1,0:T(8,128)(2,1)S(1)}, bf16[192,1536]{1,0:T(8,128)(2,1)S(1)}, u32[]{:S(2)}, u32[]{:S(2)}) collective-permute-start(bf16[192,1536]{1,0:T(8,128)(2,1)S(1)} %collective-permute-done.17.refs_1_), channel_id=1, source_target_pairs={{0,8},{1,9},{18,26},{19,27},{4,12},{5,13},{22,30},{23,31},{8,0},{9... | collective-permute-start | bytes 1769480 | tf_op jit(solution)/shard_map/ppermute | solution.py:971
  57.0 23.9 %collective-permute-start.20 = (bf16[192,1536]{1,0:T(8,128)(2,1)S(1)}, bf16[192,1536]{1,0:T(8,128)(2,1)S(1)}, u32[]{:S(2)}, u32[]{:S(2)}) collective-permute-start(bf16[192,1536]{1,0:T(8,128)(2,1)S(1)} %collective-permute-done.17.refs_1_), channel_id=1, source_target_pairs={{0,12},{1,13},{18,30},{19,31},{4,8},{5,9},{22,26},{23,27},{8,4},{9... | collective-permute-start | bytes 1769480 | tf_op jit(solution)/shard_map/ppermute | solution.py:971
  61.2 21.8 %collective-permute-start.14 = (f32[1,1920]{1,0:T(1,128)S(1)}, f32[1,1920]{1,0:T(1,128)S(1)}, u32[]{:S(2)}, u32[]{:S(2)}) collective-permute-start(f32[1,1920]{1,0:T(1,128)S(1)} %broadcast_select_fusion), channel_id=1, source_target_pairs={{0,16},{16,0},{1,17},{17,1},{2,18},{18,2},{3,19},{19,3},{4,20},{20... | collective-permute-start | bytes 23048 | tf_op jit(solution)/shard_map/ppermute | solution.py:147
  65.9 21.2 %collective-permute-start.21 = (bf16[256,768]{1,0:T(8,128)(2,1)S(1)}, bf16[256,768]{1,0:T(8,128)(2,1)S(1)}, u32[]{:S(2)}, u32[]{:S(2)}) collective-permute-start(bf16[256,768]{1,0:T(8,128)(2,1)S(1)} %copy-done.16), channel_id=1, source_target_pairs={{0,2},{1,3},{18,16},{19,17},{4,6},{5,7},{22,20},{23,21},{8,10},{9,... | collective-permute-start | bytes 1179656 | tf_op jit(solution)/shard_map/ppermute | solution.py:938
  81.6 62.9 %collective-permute-start.30 = (bf16[768,1536]{1,0:T(8,128)(2,1)S(1)}, bf16[768,1536]{1,0:T(8,128)(2,1)S(1)}, u32[]{:S(2)}, u32[]{:S(2)}) collective-permute-start(bf16[768,1536]{1,0:T(8,128)(2,1)S(1)} %line_up.3.refs_2_.refs_5_.refs_1_), channel_id=1, source_target_pairs={{0,2},{1,3},{18,16},{19,17},{4,6},{5,7},{22,20},{23,21},{8,10},{9,... | collective-permute-start | bytes 7077896 | tf_op jit(solution)/shard_map/ppermute | solution.py:985
  87.6 11.6 %collective-permute-start.22 = (bf16[256,768]{1,0:T(8,128)(2,1)S(1)}, bf16[256,768]{1,0:T(8,128)(2,1)S(1)}, u32[]{:S(2)}, u32[]{:S(2)}) collective-permute-start(bf16[256,768]{1,0:T(8,128)(2,1)S(1)} %mask_rows.1.refs_2_.refs_0_.refs_6_), channel_id=1, source_target_pairs={{0,1},{1,0},{2,3},{3,2},{4,5},{5,4},{6,7},{7,6},{8,9},{9,8},{10,11... | collective-permute-start | bytes 1179656 | tf_op jit(solution)/shard_map/ppermute | solution.py:151
  95.0 15.6 %collective-permute-start.16 = (bf16[272,768]{1,0:T(8,128)(2,1)S(1)}, bf16[272,768]{1,0:T(8,128)(2,1)S(1)}, u32[]{:S(2)}, u32[]{:S(2)}) collective-permute-start(bf16[272,768]{1,0:T(8,128)(2,1)S(1)} %get-tuple-element.143), channel_id=1, source_target_pairs={{0,16},{16,0},{1,17},{17,1},{2,18},{18,2},{3,19},{19,3},{4,20},{20... | collective-permute-start | bytes 1253384 | tf_op jit(solution)/shard_map/ppermute | solution.py:147
  99.1 11.3 %collective-permute-start.23 = (bf16[256,768]{1,0:T(8,128)(2,1)S(1)}, bf16[256,768]{1,0:T(8,128)(2,1)S(1)}, u32[]{:S(2)}, u32[]{:S(2)}) collective-permute-start(bf16[256,768]{1,0:T(8,128)(2,1)S(1)} %collective-permute-done.22.refs_2_.refs_0_.refs_8_), channel_id=1, source_target_pairs={{0,16},{16,0},{1,17},{17,1},{2,18},{18,2},{3,19},{19,3},{4,20},{20... | collective-permute-start | bytes 1179656 | tf_op jit(solution)/shard_map/ppermute | solution.py:147
  99.2 13.2 %collective-permute-start.26 = (bf16[192,768]{1,0:T(8,128)(2,1)S(1)}, bf16[192,768]{1,0:T(8,128)(2,1)S(1)}, u32[]{:S(2)}, u32[]{:S(2)}) collective-permute-start(bf16[192,768]{1,0:T(8,128)(2,1)S(1)} %collective-permute-done.25.refs_1_), channel_id=1, source_target_pairs={{0,4},{1,5},{18,22},{19,23},{4,0},{5,1},{22,18},{23,19},{8,12},{9,... | collective-permute-start | bytes 884744 | tf_op jit(solution)/shard_map/ppermute | solution.py:971
  102.5 13.0 %collective-permute-start.27 = (bf16[192,768]{1,0:T(8,128)(2,1)S(1)}, bf16[192,768]{1,0:T(8,128)(2,1)S(1)}, u32[]{:S(2)}, u32[]{:S(2)}) collective-permute-start(bf16[192,768]{1,0:T(8,128)(2,1)S(1)} %collective-permute-done.25.refs_1_), channel_id=1, source_target_pairs={{0,8},{1,9},{18,26},{19,27},{4,12},{5,13},{22,30},{23,31},{8,0},{9... | collective-permute-start | bytes 884744 | tf_op jit(solution)/shard_map/ppermute | solution.py:971
  110.5 13.0 %collective-permute-start.15 = (bf16[272,768]{1,0:T(8,128)(2,1)S(1)}, bf16[272,768]{1,0:T(8,128)(2,1)S(1)}, u32[]{:S(2)}, u32[]{:S(2)}) collective-permute-start(bf16[272,768]{1,0:T(8,128)(2,1)S(1)} %get-tuple-element.142), channel_id=1, source_target_pairs={{0,16},{16,0},{1,17},{17,1},{2,18},{18,2},{3,19},{19,3},{4,20},{20... | collective-permute-start | bytes 1253384 | tf_op jit(solution)/shard_map/ppermute | solution.py:147
  110.7 12.7 %collective-permute-start.24 = (bf16[272,768]{1,0:T(8,128)(2,1)S(1)}, bf16[272,768]{1,0:T(8,128)(2,1)S(1)}, u32[]{:S(2)}, u32[]{:S(2)}) collective-permute-start(bf16[272,768]{1,0:T(8,128)(2,1)S(1)} %pair_sum.8), channel_id=1, source_target_pairs={{0,1},{1,0},{2,3},{3,2},{4,5},{5,4},{6,7},{7,6},{8,9},{9,8},{10,11... | collective-permute-start | bytes 1253384 | tf_op jit(solution)/shard_map/ppermute | solution.py:151
  115.5 18.8 %collective-permute-start.37 = (bf16[192,1536]{1,0:T(8,128)(2,1)S(1)}, bf16[192,1536]{1,0:T(8,128)(2,1)S(1)}, u32[]{:S(2)}, u32[]{:S(2)}) collective-permute-start(bf16[192,1536]{1,0:T(8,128)(2,1)S(1)} %second_block.1), channel_id=1, source_target_pairs={{16,0},{17,1},{18,18},{19,19},{20,4},{21,5},{22,22},{23,23},{24,8}... | collective-permute-start | bytes 1769480 | tf_op jit(solution)/shard_map/ppermute | solution.py:976
  134.4 12.3 %collective-permute-start.33 = (bf16[256,768]{1,0:T(8,128)(2,1)S(1)}, bf16[256,768]{1,0:T(8,128)(2,1)S(1)}, u32[]{:S(2)}, u32[]{:S(2)}) collective-permute-start(bf16[256,768]{1,0:T(8,128)(2,1)S(1)} %collective-permute-done.32.refs_0_.refs_2_), channel_id=1, source_target_pairs={{0,16},{16,0},{1,17},{17,1},{2,18},{18,2},{3,19},{19,3},{4,20},{20... | collective-permute-start | bytes 1179656 | tf_op jit(solution)/shard_map/ppermute | solution.py:147
  134.4 14.6 %collective-permute-start.38 = (bf16[192,1536]{1,0:T(8,128)(2,1)S(1)}, bf16[192,1536]{1,0:T(8,128)(2,1)S(1)}, u32[]{:S(2)}, u32[]{:S(2)}) collective-permute-start(bf16[192,1536]{1,0:T(8,128)(2,1)S(1)} %collective-permute-done.37.refs_1_), channel_id=1, source_target_pairs={{0,4},{1,5},{18,22},{19,23},{4,0},{5,1},{22,18},{23,19},{8,12},{9,... | collective-permute-start | bytes 1769480 | tf_op jit(solution)/shard_map/ppermute | solution.py:971
  137.7 25.4 %collective-permute-start.39 = (bf16[192,1536]{1,0:T(8,128)(2,1)S(1)}, bf16[192,1536]{1,0:T(8,128)(2,1)S(1)}, u32[]{:S(2)}, u32[]{:S(2)}) collective-permute-start(bf16[192,1536]{1,0:T(8,128)(2,1)S(1)} %collective-permute-done.37.refs_1_), channel_id=1, source_target_pairs={{0,8},{1,9},{18,26},{19,27},{4,12},{5,13},{22,30},{23,31},{8,0},{9... | collective-permute-start | bytes 1769480 | tf_op jit(solution)/shard_map/ppermute | solution.py:971
  140.1 23.0 %collective-permute-start.40 = (bf16[192,1536]{1,0:T(8,128)(2,1)S(1)}, bf16[192,1536]{1,0:T(8,128)(2,1)S(1)}, u32[]{:S(2)}, u32[]{:S(2)}) collective-permute-start(bf16[192,1536]{1,0:T(8,128)(2,1)S(1)} %collective-permute-done.37.refs_1_), channel_id=1, source_target_pairs={{0,12},{1,13},{18,30},{19,31},{4,8},{5,9},{22,26},{23,27},{8,4},{9... | collective-permute-start | bytes 1769480 | tf_op jit(solution)/shard_map/ppermute | solution.py:971
  144.5 24.9 %collective-permute-start.36 = (bf16[768,768]{1,0:T(8,128)(2,1)S(1)}, bf16[768,768]{1,0:T(8,128)(2,1)S(1)}, u32[]{:S(2)}, u32[]{:S(2)}) collective-permute-start(bf16[768,768]{1,0:T(8,128)(2,1)S(1)} %line_up.4.refs_6_.refs_5_.refs_1_), channel_id=1, source_target_pairs={{0,2},{1,3},{18,16},{19,17},{4,6},{5,7},{22,20},{23,21},{8,10},{9,... | collective-permute-start | bytes 3538952 | tf_op jit(solution)/shard_map/ppermute | solution.py:985
  146.7 19.0 %collective-permute-start.29 = (bf16[256,768]{1,0:T(8,128)(2,1)S(1)}, bf16[256,768]{1,0:T(8,128)(2,1)S(1)}, u32[]{:S(2)}, u32[]{:S(2)}) collective-permute-start(bf16[256,768]{1,0:T(8,128)(2,1)S(1)} %get-tuple-element.145.refs_0_), channel_id=1, source_target_pairs={{0,16},{16,0},{1,17},{17,1},{2,18},{18,2},{3,19},{19,3},{4,20},{20... | collective-permute-start | bytes 1179656 | tf_op jit(solution)/shard_map/ppermute | solution.py:147
  149.0 18.7 %collective-permute-start.34 = (bf16[272,768]{1,0:T(8,128)(2,1)S(1)}, bf16[272,768]{1,0:T(8,128)(2,1)S(1)}, u32[]{:S(2)}, u32[]{:S(2)}) collective-permute-start(bf16[272,768]{1,0:T(8,128)(2,1)S(1)} %get-tuple-element.149), channel_id=1, source_target_pairs={{0,16},{16,0},{1,17},{17,1},{2,18},{18,2},{3,19},{19,3},{4,20},{20... | collective-permute-start | bytes 1253384 | tf_op jit(solution)/shard_map/ppermute | solution.py:147
  163.8 41.2 %collective-permute-start.47 = (bf16[768,1536]{1,0:T(8,128)(2,1)S(1)}, bf16[768,1536]{1,0:T(8,128)(2,1)S(1)}, u32[]{:S(2)}, u32[]{:S(2)}) collective-permute-start(bf16[768,1536]{1,0:T(8,128)(2,1)S(1)} %line_up.5.refs_8_.refs_1_), channel_id=1, source_target_pairs={{0,2},{1,3},{18,16},{19,17},{4,6},{5,7},{22,20},{23,21},{8,10},{9,... | collective-permute-start | bytes 7077896 | tf_op jit(solution)/shard_map/ppermute | solution.py:985
  167.8 12.1 %collective-permute-start.35 = (bf16[272,768]{1,0:T(8,128)(2,1)S(1)}, bf16[272,768]{1,0:T(8,128)(2,1)S(1)}, u32[]{:S(2)}, u32[]{:S(2)}) collective-permute-start(bf16[272,768]{1,0:T(8,128)(2,1)S(1)} %pair_sum.9), channel_id=1, source_target_pairs={{0,1},{1,0},{2,3},{3,2},{4,5},{5,4},{6,7},{7,6},{8,9},{9,8},{10,11... | collective-permute-start | bytes 1253384 | tf_op jit(solution)/shard_map/ppermute | solution.py:151
  203.4 11.9 %collective-permute-start.46 = (bf16[272,768]{1,0:T(8,128)(2,1)S(1)}, bf16[272,768]{1,0:T(8,128)(2,1)S(1)}, u32[]{:S(2)}, u32[]{:S(2)}) collective-permute-start(bf16[272,768]{1,0:T(8,128)(2,1)S(1)} %pair_sum.10), channel_id=1, source_target_pairs={{0,1},{1,0},{2,3},{3,2},{4,5},{5,4},{6,7},{7,6},{8,9},{9,8},{10,11... | collective-permute-start | bytes 1253384 | tf_op jit(solution)/shard_map/ppermute | solution.py:151
  245.9 30.7 %collective-permute-start.63 = (bf16[768,1536]{1,0:T(8,128)(2,1)S(1)}, bf16[768,1536]{1,0:T(8,128)(2,1)S(1)}, u32[]{:S(2)}, u32[]{:S(2)}) collective-permute-start(bf16[768,1536]{1,0:T(8,128)(2,1)S(1)} %grads.4.refs_10_.refs_1_), channel_id=1, source_target_pairs={{2,0},{3,1},{16,18},{17,19},{6,4},{7,5},{20,22},{21,23},{10,8},{11... | collective-permute-start | bytes 7077896 | tf_op jit(solution)/shard_map/ppermute | solution.py:1074
  292.2 15.1 %collective-permute-start.54 = (bf16[272,768]{1,0:T(8,128)(2,1)S(1)}, bf16[272,768]{1,0:T(8,128)(2,1)S(1)}, u32[]{:S(2)}, u32[]{:S(2)}) collective-permute-start(bf16[272,768]{1,0:T(8,128)(2,1)S(1)} %pair_sum.11.refs_8_), channel_id=1, source_target_pairs={{0,1},{1,0},{2,3},{3,2},{4,5},{5,4},{6,7},{7,6},{8,9},{9,8},{10,11... | collective-permute-start | bytes 1253384 | tf_op jit(solution)/shard_map/ppermute | solution.py:151
  294.6 18.8 %collective-permute-start.64 = (bf16[256,768]{1,0:T(8,128)(2,1)S(1)}, bf16[256,768]{1,0:T(8,128)(2,1)S(1)}, u32[]{:S(2)}, u32[]{:S(2)}) collective-permute-start(bf16[256,768]{1,0:T(8,128)(2,1)S(1)} %get-tuple-element.189), channel_id=1, source_target_pairs={{0,16},{16,0},{1,17},{17,1},{2,18},{18,2},{3,19},{19,3},{4,20},{20... | collective-permute-start | bytes 1179656 | tf_op jit(solution)/shard_map/ppermute | solution.py:147
  294.7 23.8 %collective-permute-start.66 = (bf16[256,768]{1,0:T(8,128)(2,1)S(1)}, bf16[256,768]{1,0:T(8,128)(2,1)S(1)}, u32[]{:S(2)}, u32[]{:S(2)}) collective-permute-start(bf16[256,768]{1,0:T(8,128)(2,1)S(1)} %pair_sum.13), channel_id=1, source_target_pairs={{0,1},{1,0},{2,3},{3,2},{4,5},{5,4},{6,7},{7,6},{8,9},{9,8},{10,11... | collective-permute-start | bytes 1179656 | tf_op jit(solution)/shard_map/ppermute | solution.py:151
  297.3 39.7 %collective-permute-start.73 = (bf16[768,768]{1,0:T(8,128)(2,1)S(1)}, bf16[768,768]{1,0:T(8,128)(2,1)S(1)}, u32[]{:S(2)}, u32[]{:S(2)}) collective-permute-start(bf16[768,768]{1,0:T(8,128)(2,1)S(1)} %grads.5.refs_10_.refs_1_), channel_id=1, source_target_pairs={{2,0},{3,1},{16,18},{17,19},{6,4},{7,5},{20,22},{21,23},{10,8},{11... | collective-permute-start | bytes 3538952 | tf_op jit(solution)/shard_map/ppermute | solution.py:1074
  298.6 29.2 %collective-permute-start.74 = (bf16[192,1536]{1,0:T(8,128)(2,1)S(1)}, bf16[192,1536]{1,0:T(8,128)(2,1)S(1)}, u32[]{:S(2)}, u32[]{:S(2)}) collective-permute-start(bf16[192,1536]{1,0:T(8,128)(2,1)S(1)} %get-tuple-element.204), channel_id=1, source_target_pairs={{0,4},{1,5},{18,22},{19,23},{4,0},{5,1},{22,18},{23,19},{8,12},{9,... | collective-permute-start | bytes 1769480 | tf_op jit(solution)/shard_map/ppermute | solution.py:971
  307.4 26.5 %collective-permute-start.75 = (bf16[192,1536]{1,0:T(8,128)(2,1)S(1)}, bf16[192,1536]{1,0:T(8,128)(2,1)S(1)}, u32[]{:S(2)}, u32[]{:S(2)}) collective-permute-start(bf16[192,1536]{1,0:T(8,128)(2,1)S(1)} %get-tuple-element.205), channel_id=1, source_target_pairs={{0,8},{1,9},{18,26},{19,27},{4,12},{5,13},{22,30},{23,31},{8,0},{9... | collective-permute-start | bytes 1769480 | tf_op jit(solution)/shard_map/ppermute | solution.py:971
  313.4 20.5 %collective-permute-start.76 = (bf16[192,1536]{1,0:T(8,128)(2,1)S(1)}, bf16[192,1536]{1,0:T(8,128)(2,1)S(1)}, u32[]{:S(2)}, u32[]{:S(2)}) collective-permute-start(bf16[192,1536]{1,0:T(8,128)(2,1)S(1)} %get-tuple-element.206), channel_id=1, source_target_pairs={{0,12},{1,13},{18,30},{19,31},{4,8},{5,9},{22,26},{23,27},{8,4},{9... | collective-permute-start | bytes 1769480 | tf_op jit(solution)/shard_map/ppermute | solution.py:971
  335.7 26.7 %collective-permute-start.67 = (bf16[768,768]{1,0:T(8,128)(2,1)S(1)}, bf16[768,768]{1,0:T(8,128)(2,1)S(1)}, u32[]{:S(2)}, u32[]{:S(2)}) collective-permute-start(bf16[768,768]{1,0:T(8,128)(2,1)S(1)} %pack.1.refs_1_.refs_6_), channel_id=1, source_target_pairs={{2,0},{3,1},{16,18},{17,19},{6,4},{7,5},{20,22},{21,23},{10,8},{11... | collective-permute-start | bytes 3538952 | tf_op jit(solution)/shard_map/ppermute | solution.py:1168
  345.4 48.0 %collective-permute-start.84 = (bf16[768,1536]{1,0:T(8,128)(2,1)S(1)}, bf16[768,1536]{1,0:T(8,128)(2,1)S(1)}, u32[]{:S(2)}, u32[]{:S(2)}) collective-permute-start(bf16[768,1536]{1,0:T(8,128)(2,1)S(1)} %grads.6.refs_10_.refs_1_), channel_id=1, source_target_pairs={{2,0},{3,1},{16,18},{17,19},{6,4},{7,5},{20,22},{21,23},{10,8},{11... | collective-permute-start | bytes 7077896 | tf_op jit(solution)/shard_map/ppermute | solution.py:1074
  347.4 16.3 %collective-permute-start.78 = (bf16[256,768]{1,0:T(8,128)(2,1)S(1)}, bf16[256,768]{1,0:T(8,128)(2,1)S(1)}, u32[]{:S(2)}, u32[]{:S(2)}) collective-permute-start(bf16[256,768]{1,0:T(8,128)(2,1)S(1)} %get-tuple-element.208), channel_id=1, source_target_pairs={{0,16},{16,0},{1,17},{17,1},{2,18},{18,2},{3,19},{19,3},{4,20},{20... | collective-permute-start | bytes 1179656 | tf_op jit(solution)/shard_map/ppermute | solution.py:147
  347.5 13.5 %collective-permute-start.85 = (bf16[192,768]{1,0:T(8,128)(2,1)S(1)}, bf16[192,768]{1,0:T(8,128)(2,1)S(1)}, u32[]{:S(2)}, u32[]{:S(2)}) collective-permute-start(bf16[192,768]{1,0:T(8,128)(2,1)S(1)} %get-tuple-element.225), channel_id=1, source_target_pairs={{0,4},{1,5},{18,22},{19,23},{4,0},{5,1},{22,18},{23,19},{8,12},{9,... | collective-permute-start | bytes 884744 | tf_op jit(solution)/shard_map/ppermute | solution.py:971
  356.4 12.3 %collective-permute-start.80 = (bf16[256,768]{1,0:T(8,128)(2,1)S(1)}, bf16[256,768]{1,0:T(8,128)(2,1)S(1)}, u32[]{:S(2)}, u32[]{:S(2)}) collective-permute-start(bf16[256,768]{1,0:T(8,128)(2,1)S(1)} %pair_sum.14), channel_id=1, source_target_pairs={{0,1},{1,0},{2,3},{3,2},{4,5},{5,4},{6,7},{7,6},{8,9},{9,8},{10,11... | collective-permute-start | bytes 1179656 | tf_op jit(solution)/shard_map/ppermute | solution.py:151
  361.0 30.0 %collective-permute-start.68 = (bf16[768,768]{1,0:T(8,128)(2,1)S(1)}, bf16[768,768]{1,0:T(8,128)(2,1)S(1)}, u32[]{:S(2)}, u32[]{:S(2)}) collective-permute-start(bf16[768,768]{1,0:T(8,128)(2,1)S(1)} %pack.1.refs_1_.refs_6_), channel_id=1, source_target_pairs={{0,16},{1,17},{18,2},{19,3},{4,20},{5,21},{22,6},{23,7},{8,24},{9,... | collective-permute-start | bytes 3538952 | tf_op jit(solution)/shard_map/ppermute | solution.py:1171
  362.4 28.7 %collective-permute-start.69 = (bf16[768,768]{1,0:T(8,128)(2,1)S(1)}, bf16[768,768]{1,0:T(8,128)(2,1)S(1)}, u32[]{:S(2)}, u32[]{:S(2)}) collective-permute-start(bf16[768,768]{1,0:T(8,128)(2,1)S(1)} %collective-permute-done.67.refs_2_.refs_11_), channel_id=1, source_target_pairs={{0,16},{1,17},{18,2},{19,3},{4,20},{5,21},{22,6},{23,7},{8,24},{9,... | collective-permute-start | bytes 3538952 | tf_op jit(solution)/shard_map/ppermute | solution.py:1171
  363.7 16.0 %collective-permute-start.86 = (bf16[192,768]{1,0:T(8,128)(2,1)S(1)}, bf16[192,768]{1,0:T(8,128)(2,1)S(1)}, u32[]{:S(2)}, u32[]{:S(2)}) collective-permute-start(bf16[192,768]{1,0:T(8,128)(2,1)S(1)} %get-tuple-element.226), channel_id=1, source_target_pairs={{0,8},{1,9},{18,26},{19,27},{4,12},{5,13},{22,30},{23,31},{8,0},{9... | collective-permute-start | bytes 884744 | tf_op jit(solution)/shard_map/ppermute | solution.py:971
  368.7 12.5 %collective-permute-start.87 = (bf16[192,768]{1,0:T(8,128)(2,1)S(1)}, bf16[192,768]{1,0:T(8,128)(2,1)S(1)}, u32[]{:S(2)}, u32[]{:S(2)}) collective-permute-start(bf16[192,768]{1,0:T(8,128)(2,1)S(1)} %get-tuple-element.227), channel_id=1, source_target_pairs={{0,12},{1,13},{18,30},{19,31},{4,8},{5,9},{22,26},{23,27},{8,4},{9... | collective-permute-start | bytes 884744 | tf_op jit(solution)/shard_map/ppermute | solution.py:971
  410.3 32.5 %collective-permute-start.92 = (bf16[768,768]{1,0:T(8,128)(2,1)S(1)}, bf16[768,768]{1,0:T(8,128)(2,1)S(1)}, u32[]{:S(2)}, u32[]{:S(2)}) collective-permute-start(bf16[768,768]{1,0:T(8,128)(2,1)S(1)} %grads.7.refs_1_), channel_id=1, source_target_pairs={{2,0},{3,1},{16,18},{17,19},{6,4},{7,5},{20,22},{21,23},{10,8},{11... | collective-permute-start | bytes 3538952 | tf_op jit(solution)/shard_map/ppermute | solution.py:1074
  411.6 15.7 %collective-permute-start.93 = (bf16[192,1536]{1,0:T(8,128)(2,1)S(1)}, bf16[192,1536]{1,0:T(8,128)(2,1)S(1)}, u32[]{:S(2)}, u32[]{:S(2)}) collective-permute-start(bf16[192,1536]{1,0:T(8,128)(2,1)S(1)} %get-tuple-element.238), channel_id=1, source_target_pairs={{0,4},{1,5},{18,22},{19,23},{4,0},{5,1},{22,18},{23,19},{8,12},{9,... | collective-permute-start | bytes 1769480 | tf_op jit(solution)/shard_map/ppermute | solution.py:971
  413.5 25.4 %collective-permute-start.94 = (bf16[192,1536]{1,0:T(8,128)(2,1)S(1)}, bf16[192,1536]{1,0:T(8,128)(2,1)S(1)}, u32[]{:S(2)}, u32[]{:S(2)}) collective-permute-start(bf16[192,1536]{1,0:T(8,128)(2,1)S(1)} %get-tuple-element.239), channel_id=1, source_target_pairs={{0,8},{1,9},{18,26},{19,27},{4,12},{5,13},{22,30},{23,31},{8,0},{9... | collective-permute-start | bytes 1769480 | tf_op jit(solution)/shard_map/ppermute | solution.py:971
  418.3 20.5 %collective-permute-start.95 = (bf16[192,1536]{1,0:T(8,128)(2,1)S(1)}, bf16[192,1536]{1,0:T(8,128)(2,1)S(1)}, u32[]{:S(2)}, u32[]{:S(2)}) collective-permute-start(bf16[192,1536]{1,0:T(8,128)(2,1)S(1)} %get-tuple-element.240), channel_id=1, source_target_pairs={{0,12},{1,13},{18,30},{19,31},{4,8},{5,9},{22,26},{23,27},{8,4},{9... | collective-permute-start | bytes 1769480 | tf_op jit(solution)/shard_map/ppermute | solution.py:971
  421.7 19.3 %collective-permute-start.90 = (bf16[256,768]{1,0:T(8,128)(2,1)S(1)}, bf16[256,768]{1,0:T(8,128)(2,1)S(1)}, u32[]{:S(2)}, u32[]{:S(2)}) collective-permute-start(bf16[256,768]{1,0:T(8,128)(2,1)S(1)} %get-tuple-element.233), channel_id=1, source_target_pairs={{0,16},{16,0},{1,17},{17,1},{2,18},{18,2},{3,19},{19,3},{4,20},{20... | collective-permute-start | bytes 1179656 | tf_op jit(solution)/shard_map/ppermute | solution.py:147
  439.2 13.5 %collective-permute-start.96 = (bf16[192,1536]{1,0:T(8,128)(2,1)S(1)}, bf16[192,1536]{1,0:T(8,128)(2,1)S(1)}, u32[]{:S(2)}, u32[]{:S(2)}) collective-permute-start(bf16[192,1536]{1,0:T(8,128)(2,1)S(1)} %total.8), channel_id=1, source_target_pairs={{0,0},{1,1},{18,2},{19,3},{4,4},{5,5},{22,6},{23,7},{8,8},{9,9},{2... | collective-permute-start | bytes 1769480 | tf_op jit(solution)/shard_map/ppermute | solution.py:1086
  441.1 11.6 %collective-permute-start.91 = (bf16[256,768]{1,0:T(8,128)(2,1)S(1)}, bf16[256,768]{1,0:T(8,128)(2,1)S(1)}, u32[]{:S(2)}, u32[]{:S(2)}) collective-permute-start(bf16[256,768]{1,0:T(8,128)(2,1)S(1)} %pair_sum.15), channel_id=1, source_target_pairs={{0,1},{1,0},{2,3},{3,2},{4,5},{5,4},{6,7},{7,6},{8,9},{9,8},{10,11... | collective-permute-start | bytes 1179656 | tf_op jit(solution)/shard_map/ppermute | solution.py:151
  464.1 17.1 %collective-permute-start.102 = (f32[16,768]{1,0:T(8,128)S(1)}, f32[16,768]{1,0:T(8,128)S(1)}, u32[]{:S(2)}, u32[]{:S(2)}) collective-permute-start(f32[16,768]{1,0:T(8,128)S(1)} %outer.1.refs_0_), channel_id=1, source_target_pairs={{0,4},{4,0},{8,12},{12,8},{1,5},{5,1},{9,13},{13,9},{2,6},{6,2},{1... | collective-permute-start | bytes 147464 | tf_op jit(solution)/shard_map/ppermute | solution.py:1226
  471.0 26.3 %collective-permute-start.105 = (bf16[192,768]{1,0:T(8,128)(2,1)}, bf16[192,768]{1,0:T(8,128)(2,1)}, u32[]{:S(2)}, u32[]{:S(2)}) collective-permute-start(bf16[192,768]{1,0:T(8,128)(2,1)} %get-tuple-element.255), channel_id=1, source_target_pairs={{0,4},{1,5},{18,22},{19,23},{4,0},{5,1},{22,18},{23,19},{8,12},{9,... | collective-permute-start | bytes 884744 | tf_op jit(solution)/shard_map/ppermute | solution.py:971
  472.9 24.4 %collective-permute-start.106 = (bf16[192,768]{1,0:T(8,128)(2,1)}, bf16[192,768]{1,0:T(8,128)(2,1)}, u32[]{:S(2)}, u32[]{:S(2)}) collective-permute-start(bf16[192,768]{1,0:T(8,128)(2,1)} %get-tuple-element.256), channel_id=1, source_target_pairs={{0,8},{1,9},{18,26},{19,27},{4,12},{5,13},{22,30},{23,31},{8,0},{9... | collective-permute-start | bytes 884744 | tf_op jit(solution)/shard_map/ppermute | solution.py:971
  477.7 19.6 %collective-permute-start.107 = (bf16[192,768]{1,0:T(8,128)(2,1)}, bf16[192,768]{1,0:T(8,128)(2,1)}, u32[]{:S(2)}, u32[]{:S(2)}) collective-permute-start(bf16[192,768]{1,0:T(8,128)(2,1)} %get-tuple-element.257), channel_id=1, source_target_pairs={{0,12},{1,13},{18,30},{19,31},{4,8},{5,9},{22,26},{23,27},{8,4},{9... | collective-permute-start | bytes 884744 | tf_op jit(solution)/shard_map/ppermute | solution.py:971
  481.1 13.0 %collective-permute-start.103 = (f32[16,768]{1,0:T(8,128)S(1)}, f32[16,768]{1,0:T(8,128)S(1)}, u32[]{:S(2)}, u32[]{:S(2)}) collective-permute-start(f32[16,768]{1,0:T(8,128)S(1)} %outer.1.refs_0_), channel_id=1, source_target_pairs={{0,8},{4,12},{8,0},{12,4},{1,9},{5,13},{9,1},{13,5},{2,10},{6,14},... | collective-permute-start | bytes 147464 | tf_op jit(solution)/shard_map/ppermute | solution.py:1226
  481.2 14.6 %collective-permute-start.104 = (f32[16,768]{1,0:T(8,128)S(1)}, f32[16,768]{1,0:T(8,128)S(1)}, u32[]{:S(2)}, u32[]{:S(2)}) collective-permute-start(f32[16,768]{1,0:T(8,128)S(1)} %outer.1.refs_0_), channel_id=1, source_target_pairs={{0,12},{4,8},{8,4},{12,0},{1,13},{5,9},{9,5},{13,1},{2,14},{6,10},... | collective-permute-start | bytes 147464 | tf_op jit(solution)/shard_map/ppermute | solution.py:1226
  (67 other events, 398.8 us)

commit v4 on v3

--- a/solution.py
+++ b/solution.py
@@ -28,6 +28,7 @@
 VMEM = pl.BlockSpec(memory_space=pltpu.VMEM)
 SMEM = pl.BlockSpec(memory_space=pltpu.SMEM)
 ANY = pl.BlockSpec(memory_space=pl.ANY)
+HBM = pl.BlockSpec(memory_space=pltpu.HBM)
 PARAMS = pltpu.CompilerParams(vmem_limit_bytes=16 * 1024 * 1024)
 
 
@@ -45,7 +46,7 @@
         scratch_shapes=list(scratch),
         compiler_params=PARAMS,
         name=name,
-        cost_estimate=cost,
+        cost_estimate=cost or work(1, 1),
     )(*ins, *after)
 
 
@@ -173,10 +174,13 @@
     out[...] = (first[...].astype(F32) + second[...].astype(F32)).astype(BF16)
 
 
-def settle(own, mate, far, far_mate, after=()):
-    body = pair_sum_body if own.shape[0] % 256 else pair_add_body
-    got = core_swap(far_mate)
-    sent = call("pair_sum", body, [(far.shape, BF16)], [far, got], after=after)[0]
+def pair_sum(far, far_mate):
+    body = pair_sum_body if far.shape[0] % 256 else pair_add_body
+    return call("pair_sum", body, [(far.shape, BF16)], [far, core_swap(far_mate)])[0]
+
+
+def settle(own, mate, far, far_mate):
+    sent = pair_sum(far, far_mate)
     return own, core_swap(mate), x_swap(sent)
 
 
@@ -193,7 +197,6 @@
         project_body,
         [((count, QKV), BF16)],
         [first, second, mat],
-        cost=work(2 * count * D * QKV, 2 * count * (D + QKV) + 2 * D * D),
     )[0]
 
 
@@ -259,7 +262,7 @@
         [queries, near, far, labels, mat, gain, bias],
         [by_head, by_head],
         after,
-        work(2 * count * (2 * keys * width * 4 + width * D), 4 * count * D),
+        work(4e9, 1),
     )
 
 
@@ -323,7 +326,7 @@
         [by_head] * 4
         + [pltpu.VMEM((heads, keys, HEAD_DIM), F32), turned, turned, pltpu.VMEM((keys, 128), F32)],
         after,
-        work(2 * keys * keys * width * 5 * 3, 8 * keys * D),
+        work(1.4e10, 1),
     )
 
 
@@ -371,7 +374,6 @@
         outs,
         [*pieces, *backs, mat, gain, bias],
         after=after,
-        cost=work(2 * 2 * size * D * UNITS * 4, 8 * size * D * 4),
     )
 
 
@@ -419,7 +421,6 @@
         [((count, UNITS), BF16)] * 2 + [((size, D), BF16)] * 2 + [((8, UNITS), F32)],
         [*pieces, *stats, pre, gain, bias, mat],
         after=after,
-        cost=work(2 * count * D * UNITS * 4, 8 * count * D),
     )
 
 
@@ -483,7 +484,6 @@
         [((D, width), BF16)],
         args,
         after=after,
-        cost=work(2 * 4 * size * D * width, 8 * size * (D + width)),
     )[0]
 
 
@@ -514,25 +514,29 @@
         [((count, width), BF16)] * 2 + [((8, width), F32)],
         [*pieces, out, gain, bias, mat],
         after=after,
-        cost=work(2 * count * D * width, 4 * count * D),
-    )
-
-
-def unproject_body(rows, mat, p_one, p_two):
+    )
+
+
+def unproject_body(rows, mat, one, two, gain, bias, p_one, p_two, vec_ref):
     size = p_one.shape[0]
-    for place, p_ref in enumerate((p_one, p_two)):
-        p_ref[...] = nt(rows[place * size : (place + 1) * size], mat[:, :QKV]).astype(BF16)
-
-
-def unproject(rows, mat, after=()):
+    gain_grad = jnp.zeros((1, D), F32)
+    bias_grad = jnp.zeros((1, D), F32)
+    for place, (piece, p_ref) in enumerate(((one, p_one), (two, p_two))):
+        term = nt(rows[place * size : (place + 1) * size], mat[:, :QKV])
+        p_ref[...] = term.astype(BF16)
+        gain_grad += jnp.sum(term * (piece[...].astype(F32) - bias[...]), axis=0, keepdims=True)
+        bias_grad += jnp.sum(term, axis=0, keepdims=True)
+    vec_ref[...] = vector_rows(gain_grad / gain[...], bias_grad)
+
+
+def unproject(rows, mat, pieces, gain, bias, after=()):
     count = rows.shape[0]
     return call(
         "unproject",
         unproject_body,
-        [((count // 2, D), BF16)] * 2,
-        [rows, mat],
+        [((count // 2, D), BF16)] * 2 + [((8, D), F32)],
+        [rows, mat, *pieces, gain, bias],
         after=after,
-        cost=work(2 * count * D * QKV, 4 * count * D),
     )
 
 
@@ -551,15 +555,6 @@
     return branch, folded[1:2], folded[0:1], kept
 
 
-def enter_body(x_ref, gain, bias, h_ref):
-    normal, _ = split_norm(x_ref[...].astype(F32))
-    h_ref[...] = (normal * gain[...] + bias[...]).astype(BF16)
-
-
-def enter(rows, gain, bias):
-    return call("enter", enter_body, [(rows.shape, BF16)], [rows, gain, bias])[0]
-
-
 def after_attend_body(x_ref, own, mate, far, gain, bias, x2_ref, z_ref, h_ref, fold_ref, kept_ref):
     branch, shift, folded, kept = branch_of(own, mate, far, D)
     mid = x_ref[...].astype(F32) + branch + shift
@@ -654,21 +649,20 @@
 def first_norm_back_body(has_next, *refs):
     own, mate, far, dx2, x_ref, gain, *refs = refs
     upstream = own[...].astype(F32) + mate[...].astype(F32) + far[...].astype(F32)
-    back, gain_grad, bias_grad = norm_back(x_ref[...].astype(F32), gain[...], upstream)
+    back, _, _ = norm_back(x_ref[...].astype(F32), gain[...], upstream)
     total = (dx2[...] + back).astype(BF16)
     if has_next:
-        labels, branch, folded, kept, g_ref, vec_ref, out_ref = refs
+        labels, branch, folded, kept, g_ref, out_ref = refs
         masked = mask_column(labels, dx2.shape[0]) * total.astype(F32)
         out_ref[...] = payload_of(masked, branch[...], folded[0:1], kept[...], FF)
     else:
-        g_ref, vec_ref = refs
+        (g_ref,) = refs
     g_ref[...] = total
-    vec_ref[...] = vector_rows(gain_grad, bias_grad)
 
 
 def first_norm_back(pieces, dx2, x, gain, following=(), after=()):
     rows = x.shape[0]
-    outs = [((rows, D), BF16), ((8, D), F32)]
+    outs = [((rows, D), BF16)]
     if following:
         outs.append(((rows + TAIL, D), BF16))
     return call(
@@ -680,36 +674,87 @@
     )
 
 
-def first_block_body(query, key, value, output, out):
+def fetch_all(refs, held, sems):
+    copies = [
+        pltpu.make_async_copy(ref, spot, sems.at[place])
+        for place, (ref, spot) in enumerate(zip(refs, held))
+    ]
+    for copy in copies:
+        copy.start()
+    for copy in copies:
+        copy.wait()
+
+
+def first_block_body(query, key, value, output, down, out, down_out, *scratch):
+    *held, sems = scratch
+    fetch_all((query, key, value, output, down), held, sems)
     width = query.shape[1]
-    for place, ref in enumerate((query, key, value)):
+    for place, ref in enumerate(held[:3]):
         out[:, place * width : (place + 1) * width] = ref[...]
-    out[:, 3 * width :] = output[...].T
-
-
-def first_block(query, key, value, output):
-    rows = query.shape[0]
-    return call("first_block", first_block_body, [((rows, D), BF16)], [query, key, value, output])[0]
-
-
-def second_block_body(up, down, out):
-    out[:, :UNITS] = up[...]
-    out[:, UNITS:] = down[...].T
-
-
-def second_block(up, down, after=()):
-    rows = up.shape[0]
-    return call(
-        "second_block", second_block_body, [((rows, 2 * UNITS), BF16)], [up, down], after=after
-    )[0]
-
-
-def mask_body(rows, labels, out):
-    out[...] = (mask_column(labels, rows.shape[0]) * rows[...].astype(F32)).astype(BF16)
-
-
-def mask_rows(rows, labels):
-    return call("mask_rows", mask_body, [(rows.shape, BF16)], [rows, labels])[0]
+    out[:, 3 * width :] = held[3][...].T
+    down_out[...] = held[4][...].T
+
+
+def first_block(*blocks):
+    rows = blocks[0].shape[0]
+    return pl.pallas_call(
+        first_block_body,
+        out_shape=(
+            jax.ShapeDtypeStruct((rows, D), BF16),
+            jax.ShapeDtypeStruct(blocks[4].shape[::-1], BF16),
+        ),
+        in_specs=[HBM] * 5,
+        out_specs=(VMEM, VMEM),
+        scratch_shapes=[pltpu.VMEM(block.shape, BF16) for block in blocks]
+        + [pltpu.SemaphoreType.DMA((5,))],
+        compiler_params=PARAMS,
+        name="first_block",
+    )(*blocks)
+
+
+def beside_body(one, two, out):
+    width = one.shape[1]
+    out[:, :width] = one[...]
+    out[:, width:] = two[...]
+
+
+def beside(one, two, after=()):
+    rows, width = one.shape
+    return call("beside", beside_body, [((rows, 2 * width), BF16)], [one, two], after=after)[0]
+
+
+def entry_body(flags, inputs, cotangent, out):
+    size = inputs.shape[0] // 2
+    rows = pl.ds(pl.multiple_of((1 - flags[3]) * size, size), size)
+    out[:size] = inputs[rows, :]
+    out[size:] = cotangent[rows, :]
+
+
+def entry(flags, inputs, cotangent):
+    return call("entry", entry_body, [(inputs.shape, BF16)], [flags, inputs, cotangent])[0]
+
+
+def enter_body(flags, inputs, cotangent, got, labels, gain, bias, x_ref, g_ref, top_ref, h_ref):
+    size, width = x_ref.shape
+    here = jnp.full((1, width), flags[0], jnp.int32) == 1
+    rows = pl.ds(pl.multiple_of(flags[3] * size, size), size)
+    own = jnp.where(here, inputs[rows, :], got[:size])
+    grad = jnp.where(here, cotangent[rows, :], got[size:])
+    x_ref[...] = own
+    g_ref[...] = grad
+    top_ref[...] = (mask_column(labels, size) * grad.astype(F32)).astype(BF16)
+    normal, _ = split_norm(own.astype(F32))
+    h_ref[...] = (normal * gain[...] + bias[...]).astype(BF16)
+
+
+def enter(flags, inputs, cotangent, got, labels, gain, bias):
+    rows = inputs.shape[0] // 2
+    return call(
+        "enter",
+        enter_body,
+        [((rows, D), BF16)] * 4,
+        [flags, inputs, cotangent, got, labels, gain, bias],
+    )
 
 
 def pack_body(*refs):
@@ -748,21 +793,36 @@
     )
 
 
-def share_body(count, flags, block, across, own, *sent):
-    size = own.shape[0]
-    for step, out in enumerate((own, *sent)):
+def halve_body(flags, block, across, kept, sent):
+    size = kept.shape[0] // 2
+    for place, (out, step) in enumerate(((kept, 0), (kept, 2), (sent, 1), (sent, 3))):
         rows = pl.ds(pl.multiple_of((flags[1] ^ step) * size, size), size)
-        out[...] = (block[rows, :].astype(F32) + across[rows, :].astype(F32)).astype(BF16)
-
-
-def share(flags, block, across, count, after=()):
+        spot = slice((place % 2) * size, (place % 2 + 1) * size)
+        out[spot] = (block[rows, :].astype(F32) + across[rows, :].astype(F32)).astype(BF16)
+
+
+def halve(flags, block, across, after=()):
     rows, width = block.shape
     return call(
-        "share",
-        partial(share_body, count),
-        [((rows // count, width), BF16)] * count,
+        "halve",
+        halve_body,
+        [((rows // 2, width), BF16)] * 2,
         [flags, block, across],
         after=after,
+    )
+
+
+def quarter_body(kept, got, own, sent):
+    size = own.shape[0]
+    for place, out in enumerate((own, sent)):
+        rows = slice(place * size, (place + 1) * size)
+        out[...] = (kept[rows].astype(F32) + got[rows].astype(F32)).astype(BF16)
+
+
+def quarter(kept, got, after=()):
+    rows, width = kept.shape
+    return call(
+        "quarter", quarter_body, [((rows // 2, width), BF16)] * 2, [kept, got], after=after
     )
 
 
@@ -771,8 +831,8 @@
     out[...] = sum(part[...].astype(F32) for part in parts).astype(out.dtype)
 
 
-def total_of(parts, kind=BF16):
-    return call("total", total_body, [(parts[0].shape, kind)], list(parts))[0]
+def total_of(parts, kind=BF16, after=()):
+    return call("total", total_body, [(parts[0].shape, kind)], list(parts), after=after)[0]
 
 
 def final_first_body(flags, lower, upper, q_ref, k_ref, v_ref, o_ref):
@@ -849,34 +909,35 @@
     out[...] = own[0:8]
 
 
-def line_up_body(count, flags, *refs):
-    *pieces, out = refs
-    size = pieces[0].shape[0]
-    for step, piece in enumerate(pieces):
-        rows = pl.ds(pl.multiple_of((flags[1] ^ step) * size, size), size)
-        out[rows, :] = piece[...]
-
-
-def line_up(flags, pieces, after=()):
-    count, (size, width) = len(pieces), pieces[0].shape
-    return call(
-        "line_up",
-        partial(line_up_body, count),
-        [((count * size, width), BF16)],
-        [flags, *pieces],
-        after=after,
+def choose_body(flags, one, two, out):
+    first = jnp.full((1, out.shape[1]), flags[2], jnp.int32) == 0
+    out[...] = jnp.where(first, one[...], two[...])
+
+
+def choose(flags, one, two, after=()):
+    return call("choose", choose_body, [(one.shape, one.dtype)], [flags, one, two], after=after)[0]
+
+
+def join_body(flags, own, got, out):
+    half = own.shape[1]
+    first = jnp.full((1, half), flags[2], jnp.int32) == 0
+    out[:, :half] = jnp.where(first, own[...], got[...])
+    out[:, half:] = jnp.where(first, got[...], own[...])
+
+
+def join(flags, own, got, after=()):
+    rows, half = own.shape
+    return call(
+        "join", join_body, [((rows, 2 * half), BF16)], [flags, own, got], after=after
     )[0]
 
 
-def pick_body(flags, beside, across, out):
-    near = jnp.full((1, out.shape[1]), flags[0], jnp.int32) == 1
-    out[...] = jnp.where(near, beside[...], across[...])
-
-
-def pick(flags, beside, across, after=()):
-    return call(
-        "pick", pick_body, [(beside.shape, BF16)], [flags, beside, across], after=after
-    )[0]
+def hold_body(ref, out):
+    out[...] = ref[...]
+
+
+def hold(x, after):
+    return call("hold", hold_body, [(x.shape, x.dtype)], [x], after=after)[0]
 
 
 def assemble_body(count, flags, *refs):
@@ -889,13 +950,54 @@
         out[rows, :] = jnp.where(near, beside[step][...], across[step][...])
 
 
-def assemble(flags, beside, across):
+def assemble(flags, beside, across, after=()):
     count, (size, width) = len(beside), beside[0].shape
     return call(
         "assemble",
         partial(assemble_body, count),
         [((count * size, width), BF16)],
         [flags, *beside, *across],
+        after=after,
+    )[0]
+
+
+def upper_block_body(flags, up, first, down, out):
+    width = up.shape[1]
+    lower = jnp.full((1, width), flags[2], jnp.int32) == 0
+    out[:, :width] = jnp.where(lower, up[...], first[...])
+    out[:, width:] = down[...]
+
+
+def upper_block(flags, up, first, down, after):
+    rows, width = up.shape
+    return call(
+        "upper_block",
+        upper_block_body,
+        [((rows, 2 * width), BF16)],
+        [flags, up, first, down],
+        after=after,
+    )[0]
+
+
+def halves_body(ref, one, two):
+    width = one.shape[1]
+    one[...] = ref[:, :width]
+    two[...] = ref[:, width:]
+
+
+def halves_of(x, after):
+    rows, width = x.shape
+    return call("halves", halves_body, [((rows, width // 2), x.dtype)] * 2, [x], after=after)
+
+
+def pick_body(flags, beside, across, out):
+    near = jnp.full((1, out.shape[1]), flags[0], jnp.int32) == 1
+    out[...] = jnp.where(near, beside[...], across[...])
+
+
+def pick(flags, beside, across, after=()):
+    return call(
+        "pick", pick_body, [(beside.shape, BF16)], [flags, beside, across], after=after
     )[0]
 
 
@@ -931,13 +1033,6 @@
     def by_core(first, second):
         return jnp.where(core == 0, first, second)
 
-    def rows_of(array, micro_index):
-        return lax.dynamic_slice_in_dim(array, micro_index * slice_len, slice_len, 0)
-
-    def own_slice(array):
-        sent = lax.ppermute(rows_of(array, 1 - lane_y), BOTH, crossing)
-        return jnp.where(core == lane_y, rows_of(array, lane_y), sent)
-
     def placed(array, layer):
         return [
             lax.ppermute(
@@ -970,39 +1065,22 @@
     def along_line(block, step):
         return lax.ppermute(block, ("section", "dp", "mp"), line_pairs(step))
 
-    def line_pieces(block, layer):
-        if count != 4:
-            block = lax.all_gather(block, "dp", axis=0, tiled=True)
-        block = lax.ppermute(
-            block, BOTH, [(layer * LANES + r, (r // 2) * LANES + r) for r in range(LANES)]
-        )
-        if count != 4:
-            return [block]
-        return [block] + [along_line(block, step) for step in range(1, count)]
-
-    def fetched(pieces, hook=()):
-        whole = line_up(flags, pieces, after=hook) if len(pieces) > 1 else pieces[0]
-        across = lax.ppermute(whole, BOTH, crossing)
-        return whole, across
-
-    first = first_block(w_query[0], w_key[0], w_value[0], w_output[0])
-    pieces = line_pieces(first, 0)
-    across = [lax.ppermute(piece, BOTH, crossing) for piece in pieces]
-    if count == 4:
-        lower_first = assemble(flags, pieces, across)
-    else:
-        lower_first = pick(flags, pieces[0], across[0])
-    second = second_block(w_up[0], w_down[0], after=[lower_first])
-    lower_second_whole, lower_second_across = fetched(line_pieces(second, 0))
-    lower_second = pick(flags, lower_second_whole, lower_second_across)
-    upper_first_whole, upper_first_across = fetched(
-        line_pieces(first, 1), [lower_second_whole]
-    )
-    upper_first = pick(flags, upper_first_whole, upper_first_across)
-    upper_second_whole, upper_second_across = fetched(
-        line_pieces(second, 1), [upper_first_whole]
-    )
-    upper_second = pick(flags, upper_second_whole, upper_second_across)
+    first, down_block = first_block(w_query[0], w_key[0], w_value[0], w_output[0], w_down[0])
+    up_block = w_up[0]
+    to_second, to_first = [(r, LANES + r) for r in range(LANES)], [(LANES + r, r) for r in range(LANES)]
+    inner_ranks = [((1 - r // 2) * LANES + r, (r // 2) * LANES + r) for r in range(LANES)]
+
+    def along_dp(block):
+        return lax.all_gather(block, "dp", axis=0, tiled=True)
+
+    def fetched(line, hook=()):
+        whole = join(flags, line, lax.ppermute(line, BOTH, inner_ranks), after=hook)
+        return whole, lax.ppermute(whole, BOTH, crossing)
+
+    def rank_of(line, source):
+        return lax.ppermute(
+            line, BOTH, [(source * LANES + r, (r // 2) * LANES + r) for r in range(LANES)]
+        )
 
     outer_own = jnp.concatenate([norm_gain, norm_bias, feed_gain, feed_bias], axis=0)
     outer_other = core_swap(outer_own)
@@ -1030,96 +1108,137 @@
         by_core(outer_other, outer_own), by_core(split_other, split_kept)
     )
 
-    def attention(x, h, first, outer, split, hooks):
-        pieces = gather_rows(h)
-        near = project(pieces[0], pieces[1], first)
+    def gather_around(own, near_of, far=None, after=()):
+        if far is None:
+            far = x_swap(own)
+        mate = core_swap(own)
+        near = near_of([own, mate])
+        far = hold(far, after=[near[0], *after])
+        return (own, mate, far, core_swap(far)), near
+
+    def attention(x, h, first, outer, split, hooks, far=None):
+        pieces, (near,) = gather_around(h, lambda rows: [project(*rows, first)], far)
         far = project(pieces[2], pieces[3], first)
         half = 2 * slice_len
         o_far, p_far, p_far_mate, sum_far = attend(
             half, far, near, far, labels, first, split[0], split[1]
         )
+        sent = pair_sum(p_far, p_far_mate)
         o_near, p_own, p_mate, sum_near = attend(
-            0, near, near, far, labels, first, split[0], split[1], after=[p_far]
-        )
-        terms = settle(p_own, p_mate, p_far, p_far_mate, after=hooks[0])
+            0, near, near, far, labels, first, split[0], split[1], after=[sent, *hooks[0]]
+        )
+        arrived = hold(x_swap(sent), after=[p_own])
+        terms = (p_own, core_swap(p_mate), arrived)
         x2, branch, h2, folded, kept = after_attend(x, terms, outer[2], outer[3], after=hooks[1])
-        state = (x, pieces, near, far, o_near, o_far, sum_near, sum_far, x2, branch, folded, kept)
-        return x2, h2, state
+        state = (pieces, near, far, o_near, o_far, sum_near, sum_far, x, x2, branch, folded, kept)
+        return x2, h2, state, arrived
 
     def attention_back(grad, sums, state, first, outer, split, following, hooks):
-        x, pieces, near, far, o_near, o_far, sum_near, sum_far, x2, branch, folded, kept = state
+        pieces, near, far, o_near, o_far, sum_near, sum_far, x, x2, branch, folded, kept = state
         dx2, sent, feed_vec = feed_norm_back(
             sums, grad, labels, x2, outer[2], branch, folded, kept, after=hooks[0]
         )
-        backs = gather_rows(sent)
-        do_near, u_near, vec_near = inner_back(
-            backs[:2], o_near, split[0], split[1], first, after=hooks[1]
-        )
-        do_far, u_far, vec_far = inner_back(
-            backs[2:], o_far, split[0], split[1], first, after=hooks[2]
-        )
+        block = hooks[3](sent)
+        backs, (do_near, u_near, vec_near) = gather_around(
+            sent, lambda rows: inner_back(rows, o_near, split[0], split[1], first), after=block
+        )
+        do_far, u_far, vec_far = inner_back(backs[2:], o_far, split[0], split[1], first)
         dq_near, dq_far = attend_back(
-            near, far, do_near, do_far, sum_near, sum_far, labels, after=hooks[3]
-        )
-        p_far, p_far_mate = unproject(dq_far, first)
-        p_own, p_mate = unproject(dq_near, first, after=[p_far])
-        terms = settle(p_own, p_mate, p_far, p_far_mate)
+            near, far, do_near, do_far, sum_near, sum_far, labels, after=hooks[1]
+        )
+        p_far, p_far_mate, norm_far = unproject(
+            dq_far, first, pieces[2:], outer[0], outer[1], after=hooks[4]
+        )
+        sent = pair_sum(p_far, p_far_mate)
+        p_own, p_mate, norm_near = unproject(
+            dq_near, first, pieces[:2], outer[0], outer[1], after=[sent]
+        )
         mat_grad = grads_of(
-            (pieces, (dq_near, dq_far)), (backs, (u_near, u_far)), after=[p_far]
-        )
-        result = first_norm_back(terms, dx2, x, outer[0], following, after=hooks[4](mat_grad))
-        return result, mat_grad, vec_near + vec_far, feed_vec
-
-    def reduce_blocks(block, after=()):
+            (pieces, (dq_near, dq_far)), (backs, (u_near, u_far)), after=[sent]
+        )
+        terms = (p_own, core_swap(p_mate), hold(x_swap(sent), after=[p_own, mat_grad]))
+        result = first_norm_back(
+            terms, dx2, x, outer[0], following, after=hooks[2](mat_grad, dq_far)
+        )
+        return result, vec_near + vec_far, feed_vec, norm_near + norm_far
+
+    def reduce_across(block):
         across = lax.ppermute(block, BOTH, returning)
         if count != 4:
             total = total_of([block, across])
             return [lax.psum_scatter(total, "dp", scatter_dimension=0, tiled=True)]
-        return share(flags, block, across, count, after)
-
-    def reduce_line(parts, layer):
-        if count == 4:
-            parts = [parts[0]] + [
-                along_line(part, step) for step, part in enumerate(parts) if step > 0
-            ]
-            parts = [total_of(parts)]
+        return block, across
+
+    def reduce_near(pair, after=()):
+        if count != 4:
+            return pair
+        kept, sent = halve(flags, *pair, after)
+        return kept, along_line(sent, 1)
+
+    def reduce_far(pair, after=()):
+        if count != 4:
+            return pair
+        kept, sent = quarter(*pair, after)
+        return kept, along_line(sent, 2)
+
+    def reduce_end(pair, layer, after=()):
+        total = total_of(pair, after=after) if count == 4 else pair[0]
         return lax.ppermute(
-            parts[0], BOTH, [((r // 2) * LANES + r, layer * LANES + r) for r in range(LANES)]
-        )
-
-    lower_in = own_slice(inputs)
-
-    upstream = own_slice(cotangent)
-    top = gather_rows(mask_rows(upstream, labels))
-
-    h = enter(lower_in, lower_outer[0], lower_outer[1])
-    x2, h2, lower_state = attention(
-        lower_in,
-        h,
-        lower_first,
-        lower_outer,
-        lower_split,
-        ([lower_second_whole, top[3]], [upper_first_whole]),
-    )
-    lower_pieces = gather_rows(h2)
-    f_near, p_own, p_mate = feed(lower_pieces[:2], (), lower_second, *lower_split[2:])
+            total, BOTH, [((r // 2) * LANES + r, layer * LANES + r) for r in range(LANES)]
+        )
+
+    got = lax.ppermute(entry(flags, inputs, cotangent), BOTH, crossing)
+    lower_in, upstream, masked, h = enter(
+        flags, inputs, cotangent, got, labels, lower_outer[0], lower_outer[1]
+    )
+    far = x_swap(h)
+    moved = rank_of(first, 0)
+    if count == 4:
+        pieces = [moved] + [along_line(moved, step) for step in range(1, count)]
+        lower_first = assemble(
+            flags, pieces, [lax.ppermute(piece, BOTH, crossing) for piece in pieces], after=[far]
+        )
+    else:
+        pieces = [along_dp(moved)]
+        lower_first = pick(flags, pieces[0], lax.ppermute(pieces[0], BOTH, crossing))
+    lower_second_line = along_dp(
+        choose(
+            flags, up_block, lax.ppermute(down_block, BOTH, to_second), after=[pieces[-1]]
+        )
+    )
+    upper_line = along_dp(
+        upper_block(
+            flags, lax.ppermute(up_block, BOTH, to_first), first, down_block, [pieces[-1]]
+        )
+    )
+    top = gather_rows(masked)
+    x2, h2, lower_state, arrived = attention(
+        lower_in, h, lower_first, lower_outer, lower_split, ([top[3]], ()), far
+    )
+    lower_second = pick(flags, *fetched(hold(lower_second_line, after=[arrived])))
+    lower_pieces, (f_near, p_own, p_mate) = gather_around(
+        h2, lambda rows: feed(rows, (), lower_second, *lower_split[2:])
+    )
     f_far, p_far, p_far_mate = feed(lower_pieces[2:], (), lower_second, *lower_split[2:])
     lower_pre = (f_near, f_far)
+    upper_left, upper_right = halves_of(upper_line, [f_far])
+    upper_first_whole = rank_of(upper_left, 1)
+    upper_first_across = lax.ppermute(upper_first_whole, BOTH, crossing)
+    upper_first = pick(flags, upper_first_whole, upper_first_across)
     terms = settle(p_own, p_mate, p_far, p_far_mate)
     lower_out, lower_branch, h, lower_folded, lower_kept = after_feed(
-        x2,
-        terms,
-        labels,
-        upper_outer[0],
-        upper_outer[1],
-        after=[upper_first_across, upper_second_whole],
-    )
-    x2, h2, upper_state = attention(
-        lower_out, h, upper_first, upper_outer, upper_split, ((), [upper_second_across])
-    )
-    upper_pieces = gather_rows(h2)
-    f_near, p_own, p_mate, near_stats = feed(
-        upper_pieces[:2], top[:2], upper_second, *upper_split[2:]
+        x2, terms, labels, upper_outer[0], upper_outer[1]
+    )
+    upper_second_whole = beside(
+        rank_of(upper_left, 0), rank_of(upper_right, 1), after=[lower_out]
+    )
+    upper_second_across = lax.ppermute(upper_second_whole, BOTH, crossing)
+    upper_second = pick(flags, upper_second_whole, upper_second_across)
+    x2, h2, upper_state, _ = attention(
+        lower_out, h, upper_first, upper_outer, upper_split, ((), [upper_second])
+    )
+    upper_pieces, (f_near, p_own, p_mate, near_stats) = gather_around(
+        h2, lambda rows: feed(rows, top[:2], upper_second, *upper_split[2:])
     )
     f_far, p_far, p_far_mate, far_stats = feed(
         upper_pieces[2:], top[2:], upper_second, *upper_split[2:]
@@ -1127,30 +1246,32 @@
     upper_pre = (f_near, f_far)
 
     stats = group_stats(near_stats, far_stats)
-
-    def feed_backward(pieces, rows, stats, pre, second, split, hooks):
-        df_far, n_far, p_far, p_far_mate, vec_far = feed_back(
-            pieces[2:], stats, 2, pre[1], split[2], split[3], second, after=hooks[0]
-        )
-        df_near, n_near, p_own, p_mate, vec_near = feed_back(
-            pieces[:2], stats, 0, pre[0], split[2], split[3], second, after=[p_far, *hooks[1]]
-        )
-        terms = settle(p_own, p_mate, p_far, p_far_mate)
-        mat_grad = grads_of(
-            (rows, (df_near, df_far)), (pieces, (n_near, n_far)), after=[p_far, p_own]
-        )
-        return terms, mat_grad, vec_near + vec_far
-
-    sums, block, upper_middle = feed_backward(
-        top, upper_pieces, [stats], upper_pre, upper_second, upper_split, ((), ())
-    )
-    upper_second_parts = reduce_blocks(block)
-    sent = call(
-        "pair_sum", pair_sum_body, [(p_far.shape, BF16)], [p_far, core_swap(p_far_mate)]
-    )[0]
-    upper_out = finish_feed(x2, (p_own, core_swap(p_mate), x_swap(sent)), labels)
+    df_far, n_far, q_far, q_far_mate, vec_far = feed_back(
+        top[2:], [stats], 2, upper_pre[1], *upper_split[2:], upper_second
+    )
+    sent = pair_sum(q_far, q_far_mate)
+    df_near, n_near, q_own, q_mate, vec_near = feed_back(
+        top[:2], [stats], 0, upper_pre[0], *upper_split[2:], upper_second, after=[sent]
+    )
+    upper_middle = vec_near + vec_far
+    sums = (q_own, core_swap(q_mate), hold(x_swap(sent), after=[q_own]))
+    ended = pair_sum(p_far, p_far_mate)
+    ended_far = hold(x_swap(ended), after=[ended])
     following = (labels, lower_branch, lower_folded, lower_kept)
-    (upper_grad, upper_norm, sent), block, upper_inner, upper_feed = attention_back(
+    pairs = {}
+
+    def upper_second_grads(after):
+        block = grads_of(
+            (upper_pieces, (df_near, df_far)), (top, (n_near, n_far)), after=[after]
+        )
+        pairs["second"] = reduce_near(reduce_across(block))
+        return [block]
+
+    def upper_hook(item, last):
+        pairs["upper"] = reduce_across(item)
+        return [item]
+
+    (upper_grad, sent), upper_inner, upper_feed, upper_norm = attention_back(
         upstream,
         sums,
         upper_state,
@@ -1158,37 +1279,53 @@
         upper_outer,
         upper_split,
         following,
-        ([block], (), (), [upper_second_parts[0], sent], lambda item: [item, upper_out]),
-    )
-    upper_second_sum = reduce_line(upper_second_parts, 1)
-    upper_first_parts = reduce_blocks(block)
-
-    backs = gather_rows(sent)
+        ((), [ended], upper_hook, upper_second_grads, [ended_far]),
+    )
+
+    upper_out = finish_feed(x2, (p_own, core_swap(p_mate), ended_far), labels)
     own = pack([lower_out, upper_out, upper_grad])
     swapped = lax.ppermute(own, BOTH, returning)
+    upper_second_pair = reduce_far(pairs["second"], [own])
+    backs, (df_near, n_near, q_own, q_mate, vec_near) = gather_around(
+        sent,
+        lambda rows: feed_back(
+            rows, (), 0, lower_pre[0], *lower_split[2:], lower_second, after=[own]
+        ),
+    )
+    upper_first_pair = reduce_near(pairs["upper"])
+    df_far, n_far, q_far, q_far_mate, vec_far = feed_back(
+        backs[2:],
+        (),
+        2,
+        lower_pre[1],
+        *lower_split[2:],
+        lower_second,
+        after=[own, upper_first_pair[0], upper_second_pair[0]],
+    )
+    lower_middle = vec_near + vec_far
+    sent = pair_sum(q_far, q_far_mate)
+    sums = (q_own, core_swap(q_mate), x_swap(sent))
+
+    def lower_second_grads(after):
+        block = grads_of(
+            (lower_pieces, (df_near, df_far)), (backs, (n_near, n_far)), after=[after]
+        )
+        pairs["second"] = reduce_near(reduce_across(block))
+        pairs["sum"] = reduce_end(upper_second_pair, 1, after=[block])
+        pairs["first"] = reduce_far(upper_first_pair, after=[block])
+        return [block]
+
     inward = [((r // 2) * LANES + r, (1 - r // 2) * LANES + r) for r in range(LANES)]
     layer_outputs, upper_held = unpack(
         flags, own, swapped, lax.ppermute(own, BOTH, inward), lax.ppermute(swapped, BOTH, inward)
     )
-    sums, block, lower_middle = feed_backward(
-        backs,
-        lower_pieces,
-        (),
-        lower_pre,
-        lower_second,
-        lower_split,
-        ([own], [upper_first_parts[0], upper_second_sum]),
-    )
-    upper_first_sum = reduce_line(upper_first_parts, 1)
-    lower_second_parts = reduce_blocks(block)
-    lower_second_sum = reduce_line(lower_second_parts, 0)
-    last_parts = []
-
-    def reduced(item):
-        last_parts.extend(reduce_blocks(item))
-        return last_parts
-
-    (lower_grad, lower_norm), _, lower_inner, lower_feed = attention_back(
+
+    def lower_hook(item, last):
+        pairs["lower"] = reduce_across(item)
+        pairs["second"] = reduce_far(pairs["second"], after=[item])
+        return [item]
+
+    (lower_grad,), lower_inner, lower_feed, lower_norm = attention_back(
         upper_grad,
         sums,
         lower_state,
@@ -1196,20 +1333,11 @@
         lower_outer,
         lower_split,
         (),
-        (
-            [block, swapped],
-            (),
-            (),
-            [lower_second_parts[0], upper_first_sum, layer_outputs],
-            lambda item: [reduced(item)[0], lower_second_sum],
-        ),
-    )
-    input_grads = merge(flags, *placed(lower_grad, 0), upper_held)
-    grad_query, grad_key, grad_value, grad_output = final_first(
-        flags, reduce_line(last_parts, 0), upper_first_sum
-    )
-    grad_up, grad_down = final_second(flags, lower_second_sum, upper_second_sum)
-
+        ((), [layer_outputs], lower_hook, lower_second_grads, ()),
+    )
+    upper_second_sum = pairs["sum"]
+    upper_first_sum = reduce_end(pairs["first"], 1)
+    lower_second_pair = pairs["second"]
     vectors = vectors_of(
         [lower_norm, lower_feed, upper_norm, upper_feed, lower_middle, upper_middle]
         + [lower_inner, upper_inner]
@@ -1219,17 +1347,22 @@
     vectors = call("ranks", ranks_body, shape, [flags, vectors, core_swap(vectors)])[0]
     outer = call("first_rows", first_rows_body, [((8, D), F32)], [vectors])[0]
     vectors = call("outer", outer_body, shape, [vectors, x_swap(outer)])[0]
+    lower_held = placed(lower_grad, 0)
+    lower_first_pair = reduce_near(pairs["lower"], after=[vectors])
     if count == 4:
-        vectors = total_of(
-            [vectors]
-            + [
-                lax.ppermute(vectors, "dp", [(i, i ^ step) for i in range(count)])
-                for step in range(1, count)
-            ],
-            F32,
-        )
+        for step in (1, 2):
+            got = lax.ppermute(vectors, "dp", [(i, i ^ step) for i in range(count)])
+            vectors = total_of([vectors, got], F32)
+            if step == 1:
+                lower_first_pair = reduce_far(lower_first_pair, after=[vectors, *lower_held])
     else:
         vectors = lax.psum(vectors, "dp")
+    lower_second_sum = reduce_end(lower_second_pair, 0)
+    input_grads = merge(flags, *lower_held, upper_held)
+    grad_query, grad_key, grad_value, grad_output = final_first(
+        flags, reduce_end(lower_first_pair, 0), upper_first_sum
+    )
+    grad_up, grad_down = final_second(flags, lower_second_sum, upper_second_sum)
 
     def part(rows, start, size):
         rows = lax.dynamic_slice(rows, (core * rows.shape[0] // 2, start), (rows.shape[0] // 2, size))

time: 518 us -> 460 us (0.89)
  starting transfers between devices: 178 us -> 123 us
  waiting for transfers between devices: 196 us -> 164 us
  local copies, waits for them, and re-layouts: 20.5 us -> 34.9 us
  between operations: 2.72 us -> 16.7 us
  Pallas kernels: 107 us -> 115 us
    ppermute x24 -> x11, waiting for transfers between devices: 72.4 us -> 2.12 us  [along_line(): return lax.ppermute(block, ('section', 'dp', 'mp'), line_pairs(step))]
    ppermute x24 -> x11, starting transfers between devices: 99.6 us -> 37.1 us  [along_line(): return lax.ppermute(block, ('section', 'dp', 'mp'), line_pairs(step))]
    ppermute x24 -> x25, waiting for transfers between devices: 9.84 us -> 42.4 us  [the longest x1 19.4 us: fetched(): return (whole, lax.ppermute(whole, BOTH, crossing))]
    ppermute x18, waiting for transfers between devices: 100 us -> 80.3 us  [x_swap(): return lax.ppermute(x, 'mp', [(i, i ^ 1) for i in range(LANES)])]
    unnamed x46 -> x248, local copies, waits for them, and re-layouts: 13.3 us -> 33.2 us
    ppermute x36, waiting for transfers between devices: 4.46 us -> 17.9 us  [core_swap(): return lax.ppermute(x, 'section', [(0, 1), (1, 0)])]
    all_gather x0 -> x2, waiting for transfers between devices: none -> 10.2 us  [along_dp(): return lax.all_gather(block, 'dp', axis=0, tiled=True)]
    pallas_call x79 -> x98, Pallas kernels: 107 us -> 114 us  [call(): pl.pallas_call(kernel, out_shape=tuple((jax.ShapeDtypeStruct(shape, kind)...]
  transfers between devices with their start and end apart: 109 -> 99, of which waited for: 34 -> 44; matrix products, arithmetic and copies ran while one was open for 3% -> 1% of each run, Pallas kernels for 12% -> 24%
where the time goes in v4:
time: 460 us; the launch traced here: 455 us
  waiting for transfers between devices  164 us (36%)
  starting transfers between devices  123 us (27%)
  Pallas kernels  115 us (25%)
  local copies, waits for them, and re-layouts  34.9 us (8%)
  between operations  16.7 us (4%)
    pallas_call x98, Pallas kernels, call(): pl.pallas_call(kernel, out_shape=tuple((jax.ShapeDtypeStruct(shape, kind)...  114 us
    ppermute x18, waiting for transfers between devices, x_swap(): return lax.ppermute(x, 'mp', [(i, i ^ 1) for i in range(LANES)])  80.3 us
    ppermute x11, starting transfers between devices, along_line(): return lax.ppermute(block, ('section', 'dp', 'mp'), line_pairs(step))  37.1 us
    unnamed x248, local copies, waits for them, and re-layouts  33.2 us
    ppermute x18, starting transfers between devices, x_swap(): return lax.ppermute(x, 'mp', [(i, i ^ 1) for i in range(LANES)])  26 us
    ppermute x1, waiting for transfers between devices, fetched(): return (whole, lax.ppermute(whole, BOTH, crossing))  19.4 us
    ppermute x36, waiting for transfers between devices, core_swap(): return lax.ppermute(x, 'section', [(0, 1), (1, 0)])  17.9 us
    ppermute x2, waiting for transfers between devices, on_device(): got = lax.ppermute(vectors, 'dp', [(i, i ^ step) for i in range(count)])  14.9 us
  transfers between devices with their start and end apart: 99, of which 44 were waited for; matrix products, arithmetic and copies ran while one was open for 1% of the time, Pallas kernels for 24%

profile of v4, /device:TPU:0, one launch (start us, length us, event | category | flops | bytes accessed | tf_op | source)
XLA Modules:
  0.0 455.2 jit_solution(13135926580757510193)
XLA Ops:
  10.4 5.9 %collective-permute-start = (bf16[512,768]{1,0:T(8,128)(2,1)S(1)}, bf16[512,768]{1,0:T(8,128)(2,1)}, u32[]{:S(2)}, u32[]{:S(2)}) collective-permute-start(bf16[512,768]{1,0:T(8,128)(2,1)S(1)} %entry.1), channel_id=1, source_target_pairs={{0,2},{1,3},{18,16},{19,17},{4,6},{5,7},{22,20},{23,21},{8,10},{9,... | collective-permute-start | bytes 2359304 | tf_op jit(solution)/shard_map/ppermute | solution.py:1190
  20.4 2.8 collective-permute-start.21
  23.3 4.3 collective-permute-start.4
  27.6 4.5 collective-permute-start.5
  32.1 1.9 collective-permute-start.6
  41.5 2.1 collective-permute-done.5.refs_3_
  43.6 2.1 collective-permute-start.9
  45.7 2.0 collective-permute-start.10
  53.3 6.7 %collective-permute-done.11.refs_9_.refs_0_ = bf16[256,768]{1,0:T(8,128)(2,1)S(1)} collective-permute-done((bf16[256,768]{1,0:T(8,128)(2,1)S(1)}, bf16[256,768]{1,0:T(8,128)(2,1)S(1)}, u32[]{:S(2)}, u32[]{:S(2)}) %collective-permute-start.11) | collective-permute-done | bytes 393248 | tf_op jit(solution)/shard_map/ppermute | solution.py:152
  68.9 4.2 attend.4
  74.6 3.2 collective-permute-done.16.refs_2_.refs_0_.refs_8_
  80.3 4.2 attend.5
  86.8 4.1 collective-permute-done.19.refs_0_
  90.9 3.9 all-gather.3.cloned.1.call-done.refs_0_
  98.9 3.2 collective-permute-done.30.refs_1_
  105.2 4.1 collective-permute-start.23
  109.3 1.7 collective-permute-done.18.refs_2_
  115.5 19.4 %collective-permute-done.23.refs_2_ = bf16[768,1536]{1,0:T(8,128)(2,1)S(1)} collective-permute-done((bf16[768,1536]{1,0:T(8,128)(2,1)S(1)}, bf16[768,1536]{1,0:T(8,128)(2,1)S(1)}, u32[]{:S(2)}, u32[]{:S(2)}) %collective-permute-start.23) | collective-permute-done | bytes 2359328 | tf_op jit(solution)/shard_map/ppermute | solution.py:1078
  135.8 1.9 feed.4
  141.5 1.9 feed.5
  147.6 6.3 %all-gather.5.cloned.1.call-done.refs_0_ = bf16[768,1536]{1,0:T(8,128)(2,1)} async-done(((bf16[192,1536]{1,0:T(8,128)(2,1)}), bf16[768,1536]{1,0:T(8,128)(2,1)}) %all-gather.5.cloned.1.call-update) | async-done | bytes 2359312 | tf_op jit(solution)/shard_map/all_gather | solution.py:1074
  162.1 2.1 collective-permute-start.32
  166.5 10.2 %collective-permute-done.28.refs_3_ = bf16[272,768]{1,0:T(8,128)(2,1)S(1)} collective-permute-done((bf16[272,768]{1,0:T(8,128)(2,1)S(1)}, bf16[272,768]{1,0:T(8,128)(2,1)S(1)}, u32[]{:S(2)}, u32[]{:S(2)}) %collective-permute-start.28) | collective-permute-done | bytes 417824 | tf_op jit(solution)/shard_map/ppermute | solution.py:152
  179.3 3.3 collective-permute-start.40
  184.2 5.0 %collective-permute-done.33.refs_0_ = bf16[256,768]{1,0:T(8,128)(2,1)S(1)} collective-permute-done((bf16[256,768]{1,0:T(8,128)(2,1)S(1)}, bf16[256,768]{1,0:T(8,128)(2,1)S(1)}, u32[]{:S(2)}, u32[]{:S(2)}) %collective-permute-start.33) | collective-permute-done | bytes 393248 | tf_op jit(solution)/shard_map/ppermute | solution.py:152
  191.7 4.2 attend.6
  199.5 4.2 attend.7
  204.3 4.4 collective-permute-done.40.refs_2_
  212.3 2.8 feed.6
  215.1 6.9 %collective-permute-done.44.refs_0_ = bf16[256,768]{1,0:T(8,128)(2,1)S(1)} collective-permute-done((bf16[256,768]{1,0:T(8,128)(2,1)S(1)}, bf16[256,768]{1,0:T(8,128)(2,1)S(1)}, u32[]{:S(2)}, u32[]{:S(2)}) %collective-permute-start.44) | collective-permute-done | bytes 393248 | tf_op jit(solution)/shard_map/ppermute | solution.py:152
  222.2 1.7 collective-permute-done.45.refs_1_.refs_3_
  223.9 2.6 feed.7
  229.2 2.5 collective-permute-done.49.refs_1_
  231.7 2.4 feed_back.4
  237.5 2.3 feed_back.5
  240.4 6.8 %collective-permute-done.52.refs_0_ = bf16[256,768]{1,0:T(8,128)(2,1)S(1)} collective-permute-done((bf16[256,768]{1,0:T(8,128)(2,1)S(1)}, bf16[256,768]{1,0:T(8,128)(2,1)S(1)}, u32[]{:S(2)}, u32[]{:S(2)}) %collective-permute-start.52) | collective-permute-done | bytes 393248 | tf_op jit(solution)/shard_map/ppermute | solution.py:152
  249.9 3.1 grads.4.refs_2_.refs_1_
  255.8 5.1 %collective-permute-done.54.refs_0_ = bf16[272,768]{1,0:T(8,128)(2,1)S(1)} collective-permute-done((bf16[272,768]{1,0:T(8,128)(2,1)S(1)}, bf16[272,768]{1,0:T(8,128)(2,1)S(1)}, u32[]{:S(2)}, u32[]{:S(2)}) %collective-permute-start.54) | collective-permute-done | bytes 417824 | tf_op jit(solution)/shard_map/ppermute | solution.py:152
  261.0 8.4 %collective-permute-done.47.refs_0_ = bf16[272,768]{1,0:T(8,128)(2,1)S(1)} collective-permute-done((bf16[272,768]{1,0:T(8,128)(2,1)S(1)}, bf16[272,768]{1,0:T(8,128)(2,1)S(1)}, u32[]{:S(2)}, u32[]{:S(2)}) %collective-permute-start.47) | collective-permute-done | bytes 417824 | tf_op jit(solution)/shard_map/ppermute | solution.py:152
  270.2 13.1 %attend_back.2 = (bf16[512,576]{1,0:T(8,128)(2,1)S(1)}, bf16[512,576]{1,0:T(8,128)(2,1)S(1)}) custom-call(bf16[512,576]{1,0:T(8,128)(2,1)S(1)} %project.6.refs_1_.refs_0_, bf16[512,576]{1,0:T(8,128)(2,1)S(1)} %project.7.refs_0_.refs_2_.refs_1_, bf16[512,192]{1,0:T(8,128)(2,1)S(1)} %get-tuple-element.194.refs_1_.refs_2_, ...), custom_call_target="tpu_custom_call" | custom-call | flops 14000000000 | bytes 1 | tf_op jit(solution)/shard_map/attend_back/pallas_call | solution.py:41
  288.4 1.9 grads.5.refs_2_.refs_10_.refs_1_
  292.7 2.1 collective-permute-start.68
  301.9 2.4 feed_back.6
  304.3 6.1 %collective-permute-done.64.refs_0_ = bf16[272,768]{1,0:T(8,128)(2,1)S(1)} collective-permute-done((bf16[272,768]{1,0:T(8,128)(2,1)S(1)}, bf16[272,768]{1,0:T(8,128)(2,1)S(1)}, u32[]{:S(2)}, u32[]{:S(2)}) %collective-permute-start.64) | collective-permute-done | bytes 417824 | tf_op jit(solution)/shard_map/ppermute | solution.py:152
  312.7 2.4 feed_back.7
  318.7 2.0 collective-permute-start.60
  322.4 6.2 %collective-permute-done.70.refs_2_ = bf16[256,768]{1,0:T(8,128)(2,1)S(1)} collective-permute-done((bf16[256,768]{1,0:T(8,128)(2,1)S(1)}, bf16[256,768]{1,0:T(8,128)(2,1)S(1)}, u32[]{:S(2)}, u32[]{:S(2)}) %collective-permute-start.70) | collective-permute-done | bytes 393248 | tf_op jit(solution)/shard_map/ppermute | solution.py:152
  331.4 2.7 grads.6.refs_2_.refs_1_
  336.4 5.5 %collective-permute-done.72.refs_0_ = bf16[272,768]{1,0:T(8,128)(2,1)S(1)} collective-permute-done((bf16[272,768]{1,0:T(8,128)(2,1)S(1)}, bf16[272,768]{1,0:T(8,128)(2,1)S(1)}, u32[]{:S(2)}, u32[]{:S(2)}) %collective-permute-start.72) | collective-permute-done | bytes 417824 | tf_op jit(solution)/shard_map/ppermute | solution.py:152
  345.3 13.1 %attend_back.3 = (bf16[512,576]{1,0:T(8,128)(2,1)S(1)}, bf16[512,576]{1,0:T(8,128)(2,1)S(1)}) custom-call(bf16[512,576]{1,0:T(8,128)(2,1)S(1)} %copy-done.31, bf16[512,576]{1,0:T(8,128)(2,1)S(1)} %copy-done.51, bf16[512,192]{1,0:T(8,128)(2,1)S(1)} %get-tuple-element.232.refs_1_.refs_2_, bf16[512,192]{1,0:T(8,128)(2,1)S(1)} %get-tuple-element.237.refs_3_, ...), custom_call_target="tpu_custom_call" | custom-call | flops 14000000000 | bytes 1 | tf_op jit(solution)/shard_map/attend_back/pallas_call | solution.py:41
  361.2 1.9 grads.7.refs_2_.refs_6_.refs_1_
  366.1 1.9 collective-permute-start.92
  371.6 2.5 collective-permute-start.88
  374.0 8.2 %collective-permute-done.79.refs_1_ = f32[16,768]{1,0:T(8,128)S(1)} collective-permute-done((f32[16,768]{1,0:T(8,128)S(1)}, f32[16,768]{1,0:T(8,128)S(1)}, u32[]{:S(2)}, u32[]{:S(2)}) %collective-permute-start.79) | collective-permute-done | bytes 49184 | tf_op jit(solution)/shard_map/ppermute | solution.py:156
  387.4 2.4 collective-permute-done.81.refs_1_
  390.6 2.1 collective-permute-start.85
  392.7 3.7 collective-permute-start.95
  396.8 3.3 collective-permute-start.93
  400.1 1.9 collective-permute-start.82
  401.9 12.5 %collective-permute-done.82.refs_1_ = f32[16,768]{1,0:T(8,128)S(1)} collective-permute-done((f32[16,768]{1,0:T(8,128)S(1)}, f32[16,768]{1,0:T(8,128)S(1)}, u32[]{:S(2)}, u32[]{:S(2)}) %collective-permute-start.82) | collective-permute-done | bytes 49184 | tf_op jit(solution)/shard_map/ppermute | solution.py:1354
  416.5 5.4 %collective-permute-start.89 = (bf16[192,768]{1,0:T(8,128)(2,1)}, bf16[192,768]{1,0:T(8,128)(2,1)}, u32[]{:S(2)}, u32[]{:S(2)}) collective-permute-start(bf16[192,768]{1,0:T(8,128)(2,1)} %get-tuple-element.270), channel_id=1, source_target_pairs={{0,8},{1,9},{18,26},{19,27},{4,12},{5,13},{22,30},{23,31},{8,0},{9... | collective-permute-start | bytes 884744 | tf_op jit(solution)/shard_map/ppermute | solution.py:1066
  421.9 2.1 collective-permute-done.78.refs_2_.refs_4_
  424.8 5.4 %collective-permute-start.86 = (bf16[192,768]{1,0:T(8,128)(2,1)}, bf16[192,768]{1,0:T(8,128)(2,1)}, u32[]{:S(2)}, u32[]{:S(2)}) collective-permute-start(bf16[192,768]{1,0:T(8,128)(2,1)} %get-tuple-element.267), channel_id=1, source_target_pairs={{0,8},{1,9},{18,26},{19,27},{4,12},{5,13},{22,30},{23,31},{8,0},{9... | collective-permute-start | bytes 884744 | tf_op jit(solution)/shard_map/ppermute | solution.py:1066
  436.9 2.5 collective-permute-done.83.refs_1_
  (511 shorter events, 156.9 us)
Async XLA Ops:
  7.2 87.7 %all-gather.3.cloned.1.call-start = ((), (), s32[]{:S(2)}) async-start(), calls=%async_computation | async-start | bytes 1474560 | tf_op jit(solution)/shard_map/all_gather | solution.py:1074
  10.4 23.7 %collective-permute-start = (bf16[512,768]{1,0:T(8,128)(2,1)S(1)}, bf16[512,768]{1,0:T(8,128)(2,1)}, u32[]{:S(2)}, u32[]{:S(2)}) collective-permute-start(bf16[512,768]{1,0:T(8,128)(2,1)S(1)} %entry.1), channel_id=1, source_target_pairs={{0,2},{1,3},{18,16},{19,17},{4,6},{5,7},{22,20},{23,21},{8,10},{9,... | collective-permute-start | bytes 2359304 | tf_op jit(solution)/shard_map/ppermute | solution.py:1190
  19.6 12.5 %collective-permute-start.1 = (f32[4,768]{1,0:T(4,128)S(1)}, f32[4,768]{1,0:T(4,128)S(1)}, u32[]{:S(2)}, u32[]{:S(2)}) collective-permute-start(f32[4,768]{1,0:T(4,128)S(1)} %pad_maximum_fusion), channel_id=1, source_target_pairs={{0,16},{16,0},{1,17},{17,1},{2,18},{18,2},{3,19},{19,3},{4,20},{20... | collective-permute-start | bytes 36872 | tf_op jit(solution)/shard_map/ppermute | solution.py:148
  19.9 7.8 %collective-permute-start.13 = (f32[1,1920]{1,0:T(1,128)S(1)}, f32[1,1920]{1,0:T(1,128)S(1)}, u32[]{:S(2)}, u32[]{:S(2)}) collective-permute-start(f32[1,1920]{1,0:T(1,128)S(1)} %concatenate.27), channel_id=1, source_target_pairs={{0,2},{1,3},{2,0},{3,1},{4,6},{5,7},{6,4},{7,5},{8,10},{9,11},{10,... | collective-permute-start | bytes 23048 | tf_op jit(solution)/shard_map/ppermute | solution.py:156
  20.4 27.4 %collective-permute-start.21 = (bf16[192,768]{1,0:T(8,128)(2,1)}, bf16[192,768]{1,0:T(8,128)(2,1)}, u32[]{:S(2)}, u32[]{:S(2)}) collective-permute-start(bf16[192,768]{1,0:T(8,128)(2,1)} %copy-done.78), channel_id=1, source_target_pairs={{0,16},{1,17},{2,18},{3,19},{4,20},{5,21},{6,22},{7,23},{8,24},{9,... | collective-permute-start | bytes 884744 | tf_op jit(solution)/shard_map/ppermute | solution.py:1206
  23.3 16.0 %collective-permute-start.4 = (bf16[192,768]{1,0:T(8,128)(2,1)S(1)}, bf16[192,768]{1,0:T(8,128)(2,1)S(1)}, u32[]{:S(2)}, u32[]{:S(2)}) collective-permute-start(bf16[192,768]{1,0:T(8,128)(2,1)S(1)} %collective-permute-done.3.refs_1_), channel_id=1, source_target_pairs={{0,4},{1,5},{18,22},{19,23},{4,0},{5,1},{22,18},{23,19},{8,12},{9,... | collective-permute-start | bytes 884744 | tf_op jit(solution)/shard_map/ppermute | solution.py:1066
  27.6 15.9 %collective-permute-start.5 = (bf16[192,768]{1,0:T(8,128)(2,1)S(1)}, bf16[192,768]{1,0:T(8,128)(2,1)}, u32[]{:S(2)}, u32[]{:S(2)}) collective-permute-start(bf16[192,768]{1,0:T(8,128)(2,1)S(1)} %collective-permute-done.3.refs_1_), channel_id=1, source_target_pairs={{0,8},{1,9},{18,26},{19,27},{4,12},{5,13},{22,30},{23,31},{8,0},{9... | collective-permute-start | bytes 884744 | tf_op jit(solution)/shard_map/ppermute | solution.py:1066
  32.1 13.6 %collective-permute-start.6 = (bf16[192,768]{1,0:T(8,128)(2,1)S(1)}, bf16[192,768]{1,0:T(8,128)(2,1)S(1)}, u32[]{:S(2)}, u32[]{:S(2)}) collective-permute-start(bf16[192,768]{1,0:T(8,128)(2,1)S(1)} %collective-permute-done.3.refs_1_), channel_id=1, source_target_pairs={{0,12},{1,13},{18,30},{19,31},{4,8},{5,9},{22,26},{23,27},{8,4},{9... | collective-permute-start | bytes 884744 | tf_op jit(solution)/shard_map/ppermute | solution.py:1066
  34.1 13.7 %collective-permute-start.7 = (bf16[192,768]{1,0:T(8,128)(2,1)S(1)}, bf16[192,768]{1,0:T(8,128)(2,1)S(1)}, u32[]{:S(2)}, u32[]{:S(2)}) collective-permute-start(bf16[192,768]{1,0:T(8,128)(2,1)S(1)} %collective-permute-done.3.refs_1_), channel_id=1, source_target_pairs={{0,2},{1,3},{18,16},{19,17},{4,6},{5,7},{22,20},{23,21},{8,10},{9,... | collective-permute-start | bytes 884744 | tf_op jit(solution)/shard_map/ppermute | solution.py:1199
  39.3 11.3 %collective-permute-start.8 = (bf16[192,768]{1,0:T(8,128)(2,1)S(1)}, bf16[192,768]{1,0:T(8,128)(2,1)S(1)}, u32[]{:S(2)}, u32[]{:S(2)}) collective-permute-start(bf16[192,768]{1,0:T(8,128)(2,1)S(1)} %collective-permute-done.4.refs_2_), channel_id=1, source_target_pairs={{0,2},{1,3},{18,16},{19,17},{4,6},{5,7},{22,20},{23,21},{8,10},{9,... | collective-permute-start | bytes 884744 | tf_op jit(solution)/shard_map/ppermute | solution.py:1199
  43.6 9.7 %collective-permute-start.9 = (bf16[192,768]{1,0:T(8,128)(2,1)}, bf16[192,768]{1,0:T(8,128)(2,1)}, u32[]{:S(2)}, u32[]{:S(2)}) collective-permute-start(bf16[192,768]{1,0:T(8,128)(2,1)} %collective-permute-done.5.refs_3_), channel_id=1, source_target_pairs={{0,2},{1,3},{18,16},{19,17},{4,6},{5,7},{22,20},{23,21},{8,10},{9,... | collective-permute-start | bytes 884744 | tf_op jit(solution)/shard_map/ppermute | solution.py:1199
  45.7 7.5 %collective-permute-start.10 = (bf16[192,768]{1,0:T(8,128)(2,1)S(1)}, bf16[192,768]{1,0:T(8,128)(2,1)}, u32[]{:S(2)}, u32[]{:S(2)}) collective-permute-start(bf16[192,768]{1,0:T(8,128)(2,1)S(1)} %collective-permute-done.6.refs_4_.refs_3_), channel_id=1, source_target_pairs={{0,2},{1,3},{18,16},{19,17},{4,6},{5,7},{22,20},{23,21},{8,10},{9,... | collective-permute-start | bytes 884744 | tf_op jit(solution)/shard_map/ppermute | solution.py:1199
  47.7 16.4 %collective-permute-start.2 = (bf16[256,768]{1,0:T(8,128)(2,1)S(1)}, bf16[256,768]{1,0:T(8,128)(2,1)S(1)}, u32[]{:S(2)}, u32[]{:S(2)}) collective-permute-start(bf16[256,768]{1,0:T(8,128)(2,1)S(1)} %get-tuple-element.150.refs_0_.refs_2_), channel_id=1, source_target_pairs={{0,16},{16,0},{1,17},{17,1},{2,18},{18,2},{3,19},{19,3},{4,20},{20... | collective-permute-start | bytes 1179656 | tf_op jit(solution)/shard_map/ppermute | solution.py:148
  48.5 11.5 %collective-permute-start.11 = (bf16[256,768]{1,0:T(8,128)(2,1)S(1)}, bf16[256,768]{1,0:T(8,128)(2,1)S(1)}, u32[]{:S(2)}, u32[]{:S(2)}) collective-permute-start(bf16[256,768]{1,0:T(8,128)(2,1)S(1)} %get-tuple-element.150.refs_0_.refs_2_), channel_id=1, source_target_pairs={{0,1},{1,0},{2,3},{3,2},{4,5},{5,4},{6,7},{7,6},{8,9},{9,8},{10,11... | collective-permute-start | bytes 1179656 | tf_op jit(solution)/shard_map/ppermute | solution.py:152
  51.3 14.2 %collective-permute-start.14 = (f32[1,1920]{1,0:T(1,128)}, f32[1,1920]{1,0:T(1,128)S(1)}, u32[]{:S(2)}, u32[]{:S(2)}) collective-permute-start(f32[1,1920]{1,0:T(1,128)} %broadcast_select_fusion), channel_id=1, source_target_pairs={{0,16},{16,0},{1,17},{17,1},{2,18},{18,2},{3,19},{19,3},{4,20},{20... | collective-permute-start | bytes 23048 | tf_op jit(solution)/shard_map/ppermute | solution.py:148
  65.1 88.9 %all-gather.5.cloned.1.call-start = ((), (), s32[]{:S(2)}) async-start(), calls=%async_computation.1 | async-start | bytes 2949120 | tf_op jit(solution)/shard_map/all_gather | solution.py:1074
  66.5 11.3 %collective-permute-start.16 = (bf16[256,768]{1,0:T(8,128)(2,1)S(1)}, bf16[256,768]{1,0:T(8,128)(2,1)S(1)}, u32[]{:S(2)}, u32[]{:S(2)}) collective-permute-start(bf16[256,768]{1,0:T(8,128)(2,1)S(1)} %get-tuple-element.154.refs_2_.refs_0_.refs_6_), channel_id=1, source_target_pairs={{0,1},{1,0},{2,3},{3,2},{4,5},{5,4},{6,7},{7,6},{8,9},{9,8},{10,11... | collective-permute-start | bytes 1179656 | tf_op jit(solution)/shard_map/ppermute | solution.py:152
  78.7 12.1 %collective-permute-start.19 = (bf16[272,768]{1,0:T(8,128)(2,1)S(1)}, bf16[272,768]{1,0:T(8,128)(2,1)S(1)}, u32[]{:S(2)}, u32[]{:S(2)}) collective-permute-start(bf16[272,768]{1,0:T(8,128)(2,1)S(1)} %pair_sum.8.refs_7_), channel_id=1, source_target_pairs={{0,1},{1,0},{2,3},{3,2},{4,5},{5,4},{6,7},{7,6},{8,9},{9,8},{10,11... | collective-permute-start | bytes 1253384 | tf_op jit(solution)/shard_map/ppermute | solution.py:152
  105.2 29.7 %collective-permute-start.23 = (bf16[768,1536]{1,0:T(8,128)(2,1)S(1)}, bf16[768,1536]{1,0:T(8,128)(2,1)S(1)}, u32[]{:S(2)}, u32[]{:S(2)}) collective-permute-start(bf16[768,1536]{1,0:T(8,128)(2,1)S(1)} %join.1.refs_1_), channel_id=1, source_target_pairs={{0,2},{1,3},{18,16},{19,17},{4,6},{5,7},{22,20},{23,21},{8,10},{9,... | collective-permute-start | bytes 7077896 | tf_op jit(solution)/shard_map/ppermute | solution.py:1078
  113.9 21.8 %collective-permute-start.20 = (bf16[256,768]{1,0:T(8,128)(2,1)S(1)}, bf16[256,768]{1,0:T(8,128)(2,1)S(1)}, u32[]{:S(2)}, u32[]{:S(2)}) collective-permute-start(bf16[256,768]{1,0:T(8,128)(2,1)S(1)} %get-tuple-element.158.refs_0_), channel_id=1, source_target_pairs={{0,16},{16,0},{1,17},{17,1},{2,18},{18,2},{3,19},{19,3},{4,20},{20... | collective-permute-start | bytes 1179656 | tf_op jit(solution)/shard_map/ppermute | solution.py:148
  114.0 24.4 %collective-permute-start.25 = (bf16[256,768]{1,0:T(8,128)(2,1)S(1)}, bf16[256,768]{1,0:T(8,128)(2,1)S(1)}, u32[]{:S(2)}, u32[]{:S(2)}) collective-permute-start(bf16[256,768]{1,0:T(8,128)(2,1)S(1)} %get-tuple-element.158.refs_0_), channel_id=1, source_target_pairs={{0,1},{1,0},{2,3},{3,2},{4,5},{5,4},{6,7},{7,6},{8,9},{9,8},{10,11... | collective-permute-start | bytes 1179656 | tf_op jit(solution)/shard_map/ppermute | solution.py:152
  158.6 20.5 %collective-permute-start.38 = (bf16[768,768]{1,0:T(8,128)(2,1)S(1)}, bf16[768,768]{1,0:T(8,128)(2,1)S(1)}, u32[]{:S(2)}, u32[]{:S(2)}) collective-permute-start(bf16[768,768]{1,0:T(8,128)(2,1)S(1)} %get-tuple-element.168), channel_id=1, source_target_pairs={{0,0},{1,1},{2,18},{3,19},{4,4},{5,5},{6,22},{7,23},{8,8},{9,9},{1... | collective-permute-start | bytes 3538952 | tf_op jit(solution)/shard_map/ppermute | solution.py:1081
  159.4 19.8 %collective-permute-start.39 = (bf16[768,768]{1,0:T(8,128)(2,1)S(1)}, bf16[768,768]{1,0:T(8,128)(2,1)S(1)}, u32[]{:S(2)}, u32[]{:S(2)}) collective-permute-start(bf16[768,768]{1,0:T(8,128)(2,1)S(1)} %get-tuple-element.173), channel_id=1, source_target_pairs={{16,0},{17,1},{18,18},{19,19},{20,4},{21,5},{22,22},{23,23},{24,8}... | collective-permute-start | bytes 3538952 | tf_op jit(solution)/shard_map/ppermute | solution.py:1081
  162.1 20.6 %collective-permute-start.32 = (bf16[768,768]{1,0:T(8,128)(2,1)S(1)}, bf16[768,768]{1,0:T(8,128)(2,1)S(1)}, u32[]{:S(2)}, u32[]{:S(2)}) collective-permute-start(bf16[768,768]{1,0:T(8,128)(2,1)S(1)} %collective-permute-done.31.refs_1_), channel_id=1, source_target_pairs={{0,2},{1,3},{18,16},{19,17},{4,6},{5,7},{22,20},{23,21},{8,10},{9,... | collective-permute-start | bytes 3538952 | tf_op jit(solution)/shard_map/ppermute | solution.py:1226
  164.9 11.7 %collective-permute-start.28 = (bf16[272,768]{1,0:T(8,128)(2,1)S(1)}, bf16[272,768]{1,0:T(8,128)(2,1)S(1)}, u32[]{:S(2)}, u32[]{:S(2)}) collective-permute-start(bf16[272,768]{1,0:T(8,128)(2,1)S(1)} %pair_sum.9), channel_id=1, source_target_pairs={{0,1},{1,0},{2,3},{3,2},{4,5},{5,4},{6,7},{7,6},{8,9},{9,8},{10,11... | collective-permute-start | bytes 1253384 | tf_op jit(solution)/shard_map/ppermute | solution.py:152
  177.6 11.5 %collective-permute-start.33 = (bf16[256,768]{1,0:T(8,128)(2,1)S(1)}, bf16[256,768]{1,0:T(8,128)(2,1)S(1)}, u32[]{:S(2)}, u32[]{:S(2)}) collective-permute-start(bf16[256,768]{1,0:T(8,128)(2,1)S(1)} %get-tuple-element.166.refs_0_.refs_2_), channel_id=1, source_target_pairs={{0,1},{1,0},{2,3},{3,2},{4,5},{5,4},{6,7},{7,6},{8,9},{9,8},{10,11... | collective-permute-start | bytes 1179656 | tf_op jit(solution)/shard_map/ppermute | solution.py:152
  179.3 29.4 %collective-permute-start.40 = (bf16[768,1536]{1,0:T(8,128)(2,1)S(1)}, bf16[768,1536]{1,0:T(8,128)(2,1)S(1)}, u32[]{:S(2)}, u32[]{:S(2)}) collective-permute-start(bf16[768,1536]{1,0:T(8,128)(2,1)S(1)} %beside.1.refs_1_), channel_id=1, source_target_pairs={{0,2},{1,3},{18,16},{19,17},{4,6},{5,7},{22,20},{23,21},{8,10},{9,... | collective-permute-start | bytes 7077896 | tf_op jit(solution)/shard_map/ppermute | solution.py:1235
  197.9 11.7 %collective-permute-start.37 = (bf16[272,768]{1,0:T(8,128)(2,1)S(1)}, bf16[272,768]{1,0:T(8,128)(2,1)S(1)}, u32[]{:S(2)}, u32[]{:S(2)}) collective-permute-start(bf16[272,768]{1,0:T(8,128)(2,1)S(1)} %pair_sum.10.refs_7_), channel_id=1, source_target_pairs={{0,1},{1,0},{2,3},{3,2},{4,5},{5,4},{6,7},{7,6},{8,9},{9,8},{10,11... | collective-permute-start | bytes 1253384 | tf_op jit(solution)/shard_map/ppermute | solution.py:152
  203.8 8.3 %collective-permute-start.42 = (bf16[256,768]{1,0:T(8,128)(2,1)S(1)}, bf16[256,768]{1,0:T(8,128)(2,1)S(1)}, u32[]{:S(2)}, u32[]{:S(2)}) collective-permute-start(bf16[256,768]{1,0:T(8,128)(2,1)S(1)} %copy-done.16), channel_id=1, source_target_pairs={{0,16},{16,0},{1,17},{17,1},{2,18},{18,2},{3,19},{19,3},{4,20},{20... | collective-permute-start | bytes 1179656 | tf_op jit(solution)/shard_map/ppermute | solution.py:148
  211.0 11.1 %collective-permute-start.44 = (bf16[256,768]{1,0:T(8,128)(2,1)S(1)}, bf16[256,768]{1,0:T(8,128)(2,1)S(1)}, u32[]{:S(2)}, u32[]{:S(2)}) collective-permute-start(bf16[256,768]{1,0:T(8,128)(2,1)S(1)} %get-tuple-element.175.refs_0_), channel_id=1, source_target_pairs={{0,1},{1,0},{2,3},{3,2},{4,5},{5,4},{6,7},{7,6},{8,9},{9,8},{10,11... | collective-permute-start | bytes 1179656 | tf_op jit(solution)/shard_map/ppermute | solution.py:152
  236.0 11.2 %collective-permute-start.52 = (bf16[256,768]{1,0:T(8,128)(2,1)S(1)}, bf16[256,768]{1,0:T(8,128)(2,1)S(1)}, u32[]{:S(2)}, u32[]{:S(2)}) collective-permute-start(bf16[256,768]{1,0:T(8,128)(2,1)S(1)} %pair_sum.12.refs_7_), channel_id=1, source_target_pairs={{0,1},{1,0},{2,3},{3,2},{4,5},{5,4},{6,7},{7,6},{8,9},{9,8},{10,11... | collective-permute-start | bytes 1179656 | tf_op jit(solution)/shard_map/ppermute | solution.py:152
  240.0 14.4 %collective-permute-start.46 = (bf16[272,768]{1,0:T(8,128)(2,1)S(1)}, bf16[272,768]{1,0:T(8,128)(2,1)S(1)}, u32[]{:S(2)}, u32[]{:S(2)}) collective-permute-start(bf16[272,768]{1,0:T(8,128)(2,1)S(1)} %get-tuple-element.180), channel_id=1, source_target_pairs={{0,16},{16,0},{1,17},{17,1},{2,18},{18,2},{3,19},{19,3},{4,20},{20... | collective-permute-start | bytes 1253384 | tf_op jit(solution)/shard_map/ppermute | solution.py:148
  248.4 12.5 %collective-permute-start.54 = (bf16[272,768]{1,0:T(8,128)(2,1)S(1)}, bf16[272,768]{1,0:T(8,128)(2,1)S(1)}, u32[]{:S(2)}, u32[]{:S(2)}) collective-permute-start(bf16[272,768]{1,0:T(8,128)(2,1)S(1)} %get-tuple-element.192.refs_0_.refs_12_.refs_6_), channel_id=1, source_target_pairs={{0,1},{1,0},{2,3},{3,2},{4,5},{5,4},{6,7},{7,6},{8,9},{9,8},{10,11... | collective-permute-start | bytes 1253384 | tf_op jit(solution)/shard_map/ppermute | solution.py:152
  253.0 38.6 %collective-permute-start.67 = (bf16[768,1536]{1,0:T(8,128)(2,1)S(1)}, bf16[768,1536]{1,0:T(8,128)(2,1)S(1)}, u32[]{:S(2)}, u32[]{:S(2)}) collective-permute-start(bf16[768,1536]{1,0:T(8,128)(2,1)S(1)} %grads.4.refs_2_.refs_1_), channel_id=1, source_target_pairs={{2,0},{3,1},{16,18},{17,19},{6,4},{7,5},{20,22},{21,23},{10,8},{11... | collective-permute-start | bytes 7077896 | tf_op jit(solution)/shard_map/ppermute | solution.py:1166
  254.5 14.9 %collective-permute-start.47 = (bf16[272,768]{1,0:T(8,128)(2,1)S(1)}, bf16[272,768]{1,0:T(8,128)(2,1)S(1)}, u32[]{:S(2)}, u32[]{:S(2)}) collective-permute-start(bf16[272,768]{1,0:T(8,128)(2,1)S(1)} %pair_sum.11.refs_1_.refs_7_), channel_id=1, source_target_pairs={{0,1},{1,0},{2,3},{3,2},{4,5},{5,4},{6,7},{7,6},{8,9},{9,8},{10,11... | collective-permute-start | bytes 1253384 | tf_op jit(solution)/shard_map/ppermute | solution.py:152
  261.0 8.5 %collective-permute-start.55 = (bf16[272,768]{1,0:T(8,128)(2,1)S(1)}, bf16[272,768]{1,0:T(8,128)(2,1)S(1)}, u32[]{:S(2)}, u32[]{:S(2)}) collective-permute-start(bf16[272,768]{1,0:T(8,128)(2,1)S(1)} %hold.23.refs_0_.refs_8_), channel_id=1, source_target_pairs={{0,16},{16,0},{1,17},{17,1},{2,18},{18,2},{3,19},{19,3},{4,20},{20... | collective-permute-start | bytes 1253384 | tf_op jit(solution)/shard_map/ppermute | solution.py:148
  286.0 11.2 %collective-permute-start.58 = (bf16[256,768]{1,0:T(8,128)(2,1)S(1)}, bf16[256,768]{1,0:T(8,128)(2,1)S(1)}, u32[]{:S(2)}, u32[]{:S(2)}) collective-permute-start(bf16[256,768]{1,0:T(8,128)(2,1)S(1)} %pair_sum.13.refs_6_.refs_12_), channel_id=1, source_target_pairs={{0,1},{1,0},{2,3},{3,2},{4,5},{5,4},{6,7},{7,6},{8,9},{9,8},{10,11... | collective-permute-start | bytes 1179656 | tf_op jit(solution)/shard_map/ppermute | solution.py:152
  288.3 8.9 %collective-permute-start.57 = (bf16[256,768]{1,0:T(8,128)(2,1)S(1)}, bf16[256,768]{1,0:T(8,128)(2,1)S(1)}, u32[]{:S(2)}, u32[]{:S(2)}) collective-permute-start(bf16[256,768]{1,0:T(8,128)(2,1)S(1)} %get-tuple-element.208), channel_id=1, source_target_pairs={{0,16},{16,0},{1,17},{17,1},{2,18},{18,2},{3,19},{19,3},{4,20},{20... | collective-permute-start | bytes 1179656 | tf_op jit(solution)/shard_map/ppermute | solution.py:148
  290.3 20.2 %collective-permute-start.66 = (bf16[768,768]{1,0:T(8,128)(2,1)S(1)}, bf16[768,768]{1,0:T(8,128)(2,1)S(1)}, u32[]{:S(2)}, u32[]{:S(2)}) collective-permute-start(bf16[768,768]{1,0:T(8,128)(2,1)S(1)} %grads.5.refs_2_.refs_10_.refs_1_), channel_id=1, source_target_pairs={{2,0},{3,1},{16,18},{17,19},{6,4},{7,5},{20,22},{21,23},{10,8},{11... | collective-permute-start | bytes 3538952 | tf_op jit(solution)/shard_map/ppermute | solution.py:1166
  292.7 18.6 %collective-permute-start.68 = (bf16[384,1536]{1,0:T(8,128)(2,1)S(1)}, bf16[384,1536]{1,0:T(8,128)(2,1)S(1)}, u32[]{:S(2)}, u32[]{:S(2)}) collective-permute-start(bf16[384,1536]{1,0:T(8,128)(2,1)S(1)} %get-tuple-element.223), channel_id=1, source_target_pairs={{0,4},{1,5},{18,22},{19,23},{4,0},{5,1},{22,18},{23,19},{8,12},{9,... | collective-permute-start | bytes 3538952 | tf_op jit(solution)/shard_map/ppermute | solution.py:1066
  298.3 12.1 %collective-permute-start.64 = (bf16[272,768]{1,0:T(8,128)(2,1)S(1)}, bf16[272,768]{1,0:T(8,128)(2,1)S(1)}, u32[]{:S(2)}, u32[]{:S(2)}) collective-permute-start(bf16[272,768]{1,0:T(8,128)(2,1)S(1)} %get-tuple-element.217.refs_0_.refs_6_), channel_id=1, source_target_pairs={{0,1},{1,0},{2,3},{3,2},{4,5},{5,4},{6,7},{7,6},{8,9},{9,8},{10,11... | collective-permute-start | bytes 1253384 | tf_op jit(solution)/shard_map/ppermute | solution.py:152
  300.5 20.6 %collective-permute-start.59 = (bf16[768,768]{1,0:T(8,128)(2,1)S(1)}, bf16[768,768]{1,0:T(8,128)(2,1)S(1)}, u32[]{:S(2)}, u32[]{:S(2)}) collective-permute-start(bf16[768,768]{1,0:T(8,128)(2,1)S(1)} %pack.1.refs_1_.refs_6_.refs_2_), channel_id=1, source_target_pairs={{2,0},{3,1},{16,18},{17,19},{6,4},{7,5},{20,22},{21,23},{10,8},{11... | collective-permute-start | bytes 3538952 | tf_op jit(solution)/shard_map/ppermute | solution.py:1287
  317.1 11.5 %collective-permute-start.70 = (bf16[256,768]{1,0:T(8,128)(2,1)S(1)}, bf16[256,768]{1,0:T(8,128)(2,1)S(1)}, u32[]{:S(2)}, u32[]{:S(2)}) collective-permute-start(bf16[256,768]{1,0:T(8,128)(2,1)S(1)} %pair_sum.14), channel_id=1, source_target_pairs={{0,1},{1,0},{2,3},{3,2},{4,5},{5,4},{6,7},{7,6},{8,9},{9,8},{10,11... | collective-permute-start | bytes 1179656 | tf_op jit(solution)/shard_map/ppermute | solution.py:152
  318.7 23.3 %collective-permute-start.60 = (bf16[768,768]{1,0:T(8,128)(2,1)S(1)}, bf16[768,768]{1,0:T(8,128)(2,1)S(1)}, u32[]{:S(2)}, u32[]{:S(2)}) collective-permute-start(bf16[768,768]{1,0:T(8,128)(2,1)S(1)} %pack.1.refs_1_.refs_6_.refs_2_), channel_id=1, source_target_pairs={{0,16},{1,17},{18,2},{19,3},{4,20},{5,21},{22,6},{23,7},{8,24},{9,... | collective-permute-start | bytes 3538952 | tf_op jit(solution)/shard_map/ppermute | solution.py:1320
  321.1 21.0 %collective-permute-start.61 = (bf16[768,768]{1,0:T(8,128)(2,1)S(1)}, bf16[768,768]{1,0:T(8,128)(2,1)S(1)}, u32[]{:S(2)}, u32[]{:S(2)}) collective-permute-start(bf16[768,768]{1,0:T(8,128)(2,1)S(1)} %collective-permute-done.59.refs_2_), channel_id=1, source_target_pairs={{0,16},{1,17},{18,2},{19,3},{4,20},{5,21},{22,6},{23,7},{8,24},{9,... | collective-permute-start | bytes 3538952 | tf_op jit(solution)/shard_map/ppermute | solution.py:1320
  329.8 12.1 %collective-permute-start.72 = (bf16[272,768]{1,0:T(8,128)(2,1)S(1)}, bf16[272,768]{1,0:T(8,128)(2,1)S(1)}, u32[]{:S(2)}, u32[]{:S(2)}) collective-permute-start(bf16[272,768]{1,0:T(8,128)(2,1)S(1)} %get-tuple-element.230.refs_0_.refs_12_.refs_6_), channel_id=1, source_target_pairs={{0,1},{1,0},{2,3},{3,2},{4,5},{5,4},{6,7},{7,6},{8,9},{9,8},{10,11... | collective-permute-start | bytes 1253384 | tf_op jit(solution)/shard_map/ppermute | solution.py:152
  334.2 30.7 %collective-permute-start.91 = (bf16[768,1536]{1,0:T(8,128)(2,1)S(1)}, bf16[768,1536]{1,0:T(8,128)(2,1)S(1)}, u32[]{:S(2)}, u32[]{:S(2)}) collective-permute-start(bf16[768,1536]{1,0:T(8,128)(2,1)S(1)} %grads.6.refs_2_.refs_1_), channel_id=1, source_target_pairs={{2,0},{3,1},{16,18},{17,19},{6,4},{7,5},{20,22},{21,23},{10,8},{11... | collective-permute-start | bytes 7077896 | tf_op jit(solution)/shard_map/ppermute | solution.py:1166
  363.1 26.7 %collective-permute-start.84 = (bf16[768,768]{1,0:T(8,128)(2,1)S(1)}, bf16[768,768]{1,0:T(8,128)(2,1)S(1)}, u32[]{:S(2)}, u32[]{:S(2)}) collective-permute-start(bf16[768,768]{1,0:T(8,128)(2,1)S(1)} %grads.7.refs_2_.refs_6_.refs_1_), channel_id=1, source_target_pairs={{2,0},{3,1},{16,18},{17,19},{6,4},{7,5},{20,22},{21,23},{10,8},{11... | collective-permute-start | bytes 3538952 | tf_op jit(solution)/shard_map/ppermute | solution.py:1166
  366.1 30.4 %collective-permute-start.92 = (bf16[384,1536]{1,0:T(8,128)(2,1)S(1)}, bf16[384,1536]{1,0:T(8,128)(2,1)S(1)}, u32[]{:S(2)}, u32[]{:S(2)}) collective-permute-start(bf16[384,1536]{1,0:T(8,128)(2,1)S(1)} %get-tuple-element.276), channel_id=1, source_target_pairs={{0,4},{1,5},{18,22},{19,23},{4,0},{5,1},{22,18},{23,19},{8,12},{9,... | collective-permute-start | bytes 3538952 | tf_op jit(solution)/shard_map/ppermute | solution.py:1066
  369.0 13.3 %collective-permute-start.79 = (f32[16,768]{1,0:T(8,128)S(1)}, f32[16,768]{1,0:T(8,128)S(1)}, u32[]{:S(2)}, u32[]{:S(2)}) collective-permute-start(f32[16,768]{1,0:T(8,128)S(1)} %vectors.1.refs_0_), channel_id=1, source_target_pairs={{0,2},{1,3},{2,0},{3,1},{4,6},{5,7},{6,4},{7,5},{8,10},{9,11},{10,... | collective-permute-start | bytes 147464 | tf_op jit(solution)/shard_map/ppermute | solution.py:156
  370.1 12.2 %collective-permute-start.76 = (bf16[256,768]{1,0:T(8,128)(2,1)S(1)}, bf16[256,768]{1,0:T(8,128)(2,1)S(1)}, u32[]{:S(2)}, u32[]{:S(2)}) collective-permute-start(bf16[256,768]{1,0:T(8,128)(2,1)S(1)} %pair_sum.15.refs_6_.refs_12_), channel_id=1, source_target_pairs={{0,1},{1,0},{2,3},{3,2},{4,5},{5,4},{6,7},{7,6},{8,9},{9,8},{10,11... | collective-permute-start | bytes 1179656 | tf_op jit(solution)/shard_map/ppermute | solution.py:152
  371.6 28.5 %collective-permute-start.88 = (bf16[384,768]{1,0:T(8,128)(2,1)S(1)}, bf16[384,768]{1,0:T(8,128)(2,1)S(1)}, u32[]{:S(2)}, u32[]{:S(2)}) collective-permute-start(bf16[384,768]{1,0:T(8,128)(2,1)S(1)} %get-tuple-element.268), channel_id=1, source_target_pairs={{0,4},{1,5},{18,22},{19,23},{4,0},{5,1},{22,18},{23,19},{8,12},{9,... | collective-permute-start | bytes 1769480 | tf_op jit(solution)/shard_map/ppermute | solution.py:1066
  384.6 31.9 %collective-permute-start.77 = (bf16[256,768]{1,0:T(8,128)(2,1)S(1)}, bf16[256,768]{1,0:T(8,128)(2,1)S(1)}, u32[]{:S(2)}, u32[]{:S(2)}) collective-permute-start(bf16[256,768]{1,0:T(8,128)(2,1)S(1)} %first_norm_back.3), channel_id=1, source_target_pairs={{0,0},{1,1},{16,2},{17,3},{4,4},{5,5},{20,6},{21,7},{8,8},{9,9},{2... | collective-permute-start | bytes 1179656 | tf_op jit(solution)/shard_map/ppermute | solution.py:1038
  390.6 33.4 %collective-permute-start.85 = (bf16[384,768]{1,0:T(8,128)(2,1)S(1)}, bf16[384,768]{1,0:T(8,128)(2,1)S(1)}, u32[]{:S(2)}, u32[]{:S(2)}) collective-permute-start(bf16[384,768]{1,0:T(8,128)(2,1)S(1)} %get-tuple-element.265), channel_id=1, source_target_pairs={{0,4},{1,5},{18,22},{19,23},{4,0},{5,1},{22,18},{23,19},{8,12},{9,... | collective-permute-start | bytes 1769480 | tf_op jit(solution)/shard_map/ppermute | solution.py:1066
  392.7 37.6 %collective-permute-start.95 = (bf16[192,1536]{1,0:T(8,128)(2,1)S(1)}, bf16[192,1536]{1,0:T(8,128)(2,1)S(1)}, u32[]{:S(2)}, u32[]{:S(2)}) collective-permute-start(bf16[192,1536]{1,0:T(8,128)(2,1)S(1)} %get-tuple-element.279), channel_id=1, source_target_pairs={{0,8},{1,9},{18,26},{19,27},{4,12},{5,13},{22,30},{23,31},{8,0},{9... | collective-permute-start | bytes 1769480 | tf_op jit(solution)/shard_map/ppermute | solution.py:1066
  396.8 35.9 %collective-permute-start.93 = (bf16[192,1536]{1,0:T(8,128)(2,1)S(1)}, bf16[192,1536]{1,0:T(8,128)(2,1)S(1)}, u32[]{:S(2)}, u32[]{:S(2)}) collective-permute-start(bf16[192,1536]{1,0:T(8,128)(2,1)S(1)} %get-tuple-element.278), channel_id=1, source_target_pairs={{0,8},{1,9},{18,26},{19,27},{4,12},{5,13},{22,30},{23,31},{8,0},{9... | collective-permute-start | bytes 1769480 | tf_op jit(solution)/shard_map/ppermute | solution.py:1066
  400.1 14.3 %collective-permute-start.82 = (f32[16,768]{1,0:T(8,128)S(1)}, f32[16,768]{1,0:T(8,128)S(1)}, u32[]{:S(2)}, u32[]{:S(2)}) collective-permute-start(f32[16,768]{1,0:T(8,128)S(1)} %outer.1.refs_0_.refs_3_), channel_id=1, source_target_pairs={{0,4},{4,0},{8,12},{12,8},{1,5},{5,1},{9,13},{13,9},{2,6},{6,2},{1... | collective-permute-start | bytes 147464 | tf_op jit(solution)/shard_map/ppermute | solution.py:1354
  414.4 9.7 %collective-permute-start.78 = (bf16[256,768]{1,0:T(8,128)(2,1)S(1)}, bf16[256,768]{1,0:T(8,128)(2,1)S(1)}, u32[]{:S(2)}, u32[]{:S(2)}) collective-permute-start(bf16[256,768]{1,0:T(8,128)(2,1)S(1)} %first_norm_back.3), channel_id=1, source_target_pairs={{2,0},{3,1},{18,2},{19,3},{6,4},{7,5},{22,6},{23,7},{10,8},{11,9},... | collective-permute-start | bytes 1179656 | tf_op jit(solution)/shard_map/ppermute | solution.py:1038
  416.5 17.1 %collective-permute-start.89 = (bf16[192,768]{1,0:T(8,128)(2,1)}, bf16[192,768]{1,0:T(8,128)(2,1)}, u32[]{:S(2)}, u32[]{:S(2)}) collective-permute-start(bf16[192,768]{1,0:T(8,128)(2,1)} %get-tuple-element.270), channel_id=1, source_target_pairs={{0,8},{1,9},{18,26},{19,27},{4,12},{5,13},{22,30},{23,31},{8,0},{9... | collective-permute-start | bytes 884744 | tf_op jit(solution)/shard_map/ppermute | solution.py:1066
  424.8 14.7 %collective-permute-start.86 = (bf16[192,768]{1,0:T(8,128)(2,1)}, bf16[192,768]{1,0:T(8,128)(2,1)}, u32[]{:S(2)}, u32[]{:S(2)}) collective-permute-start(bf16[192,768]{1,0:T(8,128)(2,1)} %get-tuple-element.267), channel_id=1, source_target_pairs={{0,8},{1,9},{18,26},{19,27},{4,12},{5,13},{22,30},{23,31},{8,0},{9... | collective-permute-start | bytes 884744 | tf_op jit(solution)/shard_map/ppermute | solution.py:1066
  430.2 9.1 %collective-permute-start.83 = (f32[16,768]{1,0:T(8,128)S(1)}, f32[16,768]{1,0:T(8,128)S(1)}, u32[]{:S(2)}, u32[]{:S(2)}) collective-permute-start(f32[16,768]{1,0:T(8,128)S(1)} %total.8.refs_0_.refs_2_), channel_id=1, source_target_pairs={{0,8},{4,12},{8,0},{12,4},{1,9},{5,13},{9,1},{13,5},{2,10},{6,14},... | collective-permute-start | bytes 147464 | tf_op jit(solution)/shard_map/ppermute | solution.py:1354
  431.3 14.2 %collective-permute-start.96 = (bf16[192,1536]{1,0:T(8,128)(2,1)}, bf16[192,1536]{1,0:T(8,128)(2,1)S(1)}, u32[]{:S(2)}, u32[]{:S(2)}) collective-permute-start(bf16[192,1536]{1,0:T(8,128)(2,1)} %total.13), channel_id=1, source_target_pairs={{0,16},{1,17},{18,18},{19,19},{4,20},{5,21},{22,22},{23,23},{8,24}... | collective-permute-start | bytes 1769480 | tf_op jit(solution)/shard_map/ppermute | solution.py:1186
  432.8 12.7 %collective-permute-start.94 = (bf16[192,1536]{1,0:T(8,128)(2,1)S(1)}, bf16[192,1536]{1,0:T(8,128)(2,1)S(1)}, u32[]{:S(2)}, u32[]{:S(2)}) collective-permute-start(bf16[192,1536]{1,0:T(8,128)(2,1)S(1)} %total.12), channel_id=1, source_target_pairs={{0,0},{1,1},{18,2},{19,3},{4,4},{5,5},{22,6},{23,7},{8,8},{9,9},{2... | collective-permute-start | bytes 1769480 | tf_op jit(solution)/shard_map/ppermute | solution.py:1186
  435.6 8.4 %collective-permute-start.90 = (bf16[192,768]{1,0:T(8,128)(2,1)S(1)}, bf16[192,768]{1,0:T(8,128)(2,1)S(1)}, u32[]{:S(2)}, u32[]{:S(2)}) collective-permute-start(bf16[192,768]{1,0:T(8,128)(2,1)S(1)} %total.11), channel_id=1, source_target_pairs={{0,16},{1,17},{18,18},{19,19},{4,20},{5,21},{22,22},{23,23},{8,24}... | collective-permute-start | bytes 884744 | tf_op jit(solution)/shard_map/ppermute | solution.py:1186
  (158 other events, 1013.0 us)
Sparse Core Ops, SparseCore 0:
  65.2 29.6 all-gather.2
  103.7 50.1 all-gather.4

commit v5 on v4

--- a/solution.py
+++ b/solution.py
@@ -174,8 +174,15 @@
     out[...] = (first[...].astype(F32) + second[...].astype(F32)).astype(BF16)
 
 
+def pair_ride_body(first, second, out):
+    rows = out.shape[0] - 32
+    out[:rows] = (first[:rows].astype(F32) + second[:rows].astype(F32)).astype(BF16)
+    total = decode_rows(first[rows : rows + 24]) + decode_rows(second[rows : rows + 24])
+    out[rows:] = jnp.concatenate([encode_rows(total), jnp.zeros((8, D), BF16)], axis=0)
+
+
 def pair_sum(far, far_mate):
-    body = pair_sum_body if far.shape[0] % 256 else pair_add_body
+    body = {0: pair_add_body, TAIL: pair_sum_body, 32: pair_ride_body}[far.shape[0] % 256]
     return call("pair_sum", body, [(far.shape, BF16)], [far, core_swap(far_mate)])[0]
 
 
@@ -517,25 +524,55 @@
     )
 
 
-def unproject_body(rows, mat, one, two, gain, bias, p_one, p_two, vec_ref):
-    size = p_one.shape[0]
+def encode_rows(values):
+    return jnp.concatenate(split_three(values), axis=0)
+
+
+def decode_rows(rows):
+    rows = rows.astype(F32)
+    count = rows.shape[0] // 3
+    return rows[:count] + rows[count : 2 * count] + rows[2 * count :]
+
+
+def unproject_body(riding, rows, mat, one, two, gain, bias, *refs):
+    if riding:
+        near, *others, p_one, p_two = refs
+        vec_ref = None
+    else:
+        others = []
+        near = None
+        p_one, p_two, vec_ref = refs
+    size = one.shape[0]
     gain_grad = jnp.zeros((1, D), F32)
     bias_grad = jnp.zeros((1, D), F32)
     for place, (piece, p_ref) in enumerate(((one, p_one), (two, p_two))):
         term = nt(rows[place * size : (place + 1) * size], mat[:, :QKV])
-        p_ref[...] = term.astype(BF16)
+        p_ref[:size] = term.astype(BF16)
         gain_grad += jnp.sum(term * (piece[...].astype(F32) - bias[...]), axis=0, keepdims=True)
         bias_grad += jnp.sum(term, axis=0, keepdims=True)
-    vec_ref[...] = vector_rows(gain_grad / gain[...], bias_grad)
-
-
-def unproject(rows, mat, pieces, gain, bias, after=()):
-    count = rows.shape[0]
+    gain_grad = gain_grad / gain[...]
+    if riding:
+        vectors = jnp.concatenate(
+            [gain_grad + near[0:1], bias_grad + near[1:2]] + [item[0:2, :] for item in others],
+            axis=0,
+        )
+        ride = jnp.concatenate([encode_rows(vectors), jnp.zeros((8, D), BF16)], axis=0)
+        p_one[size:] = ride
+        p_two[size:] = ride
+    else:
+        vec_ref[...] = vector_rows(gain_grad, bias_grad)
+
+
+def unproject(rows, mat, pieces, gain, bias, riding=(), after=()):
+    size = rows.shape[0] // 2
+    outs = [((size + 32 if riding else size, D), BF16)] * 2
+    if not riding:
+        outs.append(((8, D), F32))
     return call(
         "unproject",
-        unproject_body,
-        [((count // 2, D), BF16)] * 2 + [((8, D), F32)],
-        [rows, mat, *pieces, gain, bias],
+        partial(unproject_body, bool(riding)),
+        outs,
+        [rows, mat, *pieces, gain, bias, *riding],
         after=after,
     )
 
@@ -648,30 +685,40 @@
 
 def first_norm_back_body(has_next, *refs):
     own, mate, far, dx2, x_ref, gain, *refs = refs
-    upstream = own[...].astype(F32) + mate[...].astype(F32) + far[...].astype(F32)
+    rows = dx2.shape[0]
+    upstream = own[:rows].astype(F32) + mate[:rows].astype(F32) + far[:rows].astype(F32)
     back, _, _ = norm_back(x_ref[...].astype(F32), gain[...], upstream)
     total = (dx2[...] + back).astype(BF16)
     if has_next:
         labels, branch, folded, kept, g_ref, out_ref = refs
-        masked = mask_column(labels, dx2.shape[0]) * total.astype(F32)
+        masked = mask_column(labels, rows) * total.astype(F32)
         out_ref[...] = payload_of(masked, branch[...], folded[0:1], kept[...], FF)
     else:
-        (g_ref,) = refs
+        here, *items, g_ref, vec_ref = refs
+        spot = slice(rows, rows + 24)
+        vec_ref[...] = jnp.zeros_like(vec_ref)
+        vec_ref[0:8, :] = decode_rows(here[spot]) + decode_rows(far[spot])
+        for place, item in enumerate(items):
+            first = 8 + 2 * place
+            vec_ref[first : first + 2, : item.shape[1]] = item[0:2, :]
     g_ref[...] = total
 
 
-def first_norm_back(pieces, dx2, x, gain, following=(), after=()):
+def first_norm_back(pieces, dx2, x, gain, following=(), ending=(), after=()):
     rows = x.shape[0]
     outs = [((rows, D), BF16)]
-    if following:
-        outs.append(((rows + TAIL, D), BF16))
+    outs.append(((rows + TAIL, D), BF16) if following else ((16, D), F32))
     return call(
         "first_norm_back",
         partial(first_norm_back_body, bool(following)),
         outs,
-        [*pieces, dx2, x, gain, *following],
+        [*pieces, dx2, x, gain, *following, *ending],
         after=after,
     )
+
+
+def in_hbm(x):
+    return pltpu.with_memory_space_constraint(x, pltpu.HBM)
 
 
 def fetch_all(refs, held, sems):
@@ -685,31 +732,35 @@
         copy.wait()
 
 
-def first_block_body(query, key, value, output, down, out, down_out, *scratch):
+def first_block_body(
+    flags, query, key, value, output, down, up, out, down_out, swap_out, *scratch
+):
     *held, sems = scratch
-    fetch_all((query, key, value, output, down), held, sems)
+    fetch_all((query, key, value, output, down, up), held, sems)
     width = query.shape[1]
     for place, ref in enumerate(held[:3]):
         out[:, place * width : (place + 1) * width] = ref[...]
     out[:, 3 * width :] = held[3][...].T
     down_out[...] = held[4][...].T
-
-
-def first_block(*blocks):
-    rows = blocks[0].shape[0]
+    lower = jnp.full((1, D), flags[2], jnp.int32) == 0
+    swap_out[:, :D] = jnp.where(lower, down_out[...], held[5][...])
+    swap_out[:, D:] = out[:, : D // 2]
+
+
+def first_block(flags, *blocks):
     return pl.pallas_call(
         first_block_body,
-        out_shape=(
-            jax.ShapeDtypeStruct((rows, D), BF16),
-            jax.ShapeDtypeStruct(blocks[4].shape[::-1], BF16),
+        out_shape=tuple(
+            jax.ShapeDtypeStruct((blocks[0].shape[0], width), BF16)
+            for width in (D, D, 3 * D // 2)
         ),
-        in_specs=[HBM] * 5,
-        out_specs=(VMEM, VMEM),
+        in_specs=[SMEM] + [HBM] * 6,
+        out_specs=(VMEM,) * 3,
         scratch_shapes=[pltpu.VMEM(block.shape, BF16) for block in blocks]
-        + [pltpu.SemaphoreType.DMA((5,))],
+        + [pltpu.SemaphoreType.DMA((6,))],
         compiler_params=PARAMS,
         name="first_block",
-    )(*blocks)
+    )(flags, *map(in_hbm, blocks))
 
 
 def beside_body(one, two, out):
@@ -723,23 +774,53 @@
     return call("beside", beside_body, [((rows, 2 * width), BF16)], [one, two], after=after)[0]
 
 
-def entry_body(flags, inputs, cotangent, out):
-    size = inputs.shape[0] // 2
-    rows = pl.ds(pl.multiple_of((1 - flags[3]) * size, size), size)
-    out[:size] = inputs[rows, :]
-    out[size:] = cotangent[rows, :]
+def entry_body(flags, inputs, cotangent, out, far_out, own_in, own_grad, sems):
+    size = own_in.shape[0]
+
+    def rows_of(micro):
+        return pl.ds(pl.multiple_of(micro * size, size), size)
+
+    across, far, own = rows_of(1 - flags[3]), rows_of(flags[2]), rows_of(flags[3])
+    copies = [
+        pltpu.make_async_copy(source, target, sems.at[place])
+        for place, (source, target) in enumerate(
+            (
+                (inputs.at[across], out.at[:size]),
+                (cotangent.at[across], out.at[size:]),
+                (inputs.at[far], far_out.at[:size]),
+                (cotangent.at[far], far_out.at[size:]),
+                (inputs.at[own], own_in),
+                (cotangent.at[own], own_grad),
+            )
+        )
+    ]
+    for copy in copies:
+        copy.start()
+    for copy in copies:
+        copy.wait()
 
 
 def entry(flags, inputs, cotangent):
-    return call("entry", entry_body, [(inputs.shape, BF16)], [flags, inputs, cotangent])[0]
-
-
-def enter_body(flags, inputs, cotangent, got, labels, gain, bias, x_ref, g_ref, top_ref, h_ref):
+    rows = inputs.shape[0]
+    shapes = [rows, rows, rows // 2, rows // 2]
+    return pl.pallas_call(
+        entry_body,
+        out_shape=tuple(jax.ShapeDtypeStruct((count, D), BF16) for count in shapes),
+        in_specs=[SMEM, HBM, HBM],
+        out_specs=(VMEM,) * 4,
+        scratch_shapes=[pltpu.SemaphoreType.DMA((6,))],
+        compiler_params=PARAMS,
+        name="entry",
+    )(flags, in_hbm(inputs), in_hbm(cotangent))
+
+
+def enter_body(
+    flags, own_in, own_grad, got, labels, gain, bias, x_ref, g_ref, top_ref, h_ref
+):
     size, width = x_ref.shape
     here = jnp.full((1, width), flags[0], jnp.int32) == 1
-    rows = pl.ds(pl.multiple_of(flags[3] * size, size), size)
-    own = jnp.where(here, inputs[rows, :], got[:size])
-    grad = jnp.where(here, cotangent[rows, :], got[size:])
+    own = jnp.where(here, own_in[...], got[:size])
+    grad = jnp.where(here, own_grad[...], got[size:])
     x_ref[...] = own
     g_ref[...] = grad
     top_ref[...] = (mask_column(labels, size) * grad.astype(F32)).astype(BF16)
@@ -747,13 +828,27 @@
     h_ref[...] = (normal * gain[...] + bias[...]).astype(BF16)
 
 
-def enter(flags, inputs, cotangent, got, labels, gain, bias):
-    rows = inputs.shape[0] // 2
+def enter(flags, own_in, own_grad, got, labels, gain, bias):
     return call(
         "enter",
         enter_body,
-        [((rows, D), BF16)] * 4,
-        [flags, inputs, cotangent, got, labels, gain, bias],
+        [(own_in.shape, BF16)] * 4,
+        [flags, own_in, own_grad, got, labels, gain, bias],
+    )
+
+
+def enter_far_body(got, labels, gain, bias, top_ref, h_ref):
+    size = top_ref.shape[0]
+    mask = (to_columns(labels[:, 2 * size : 3 * size])[:, 0:1] >= 0).astype(F32)
+    top_ref[...] = (mask * got[size:].astype(F32)).astype(BF16)
+    normal, _ = split_norm(got[:size].astype(F32))
+    h_ref[...] = (normal * gain[...] + bias[...]).astype(BF16)
+
+
+def enter_far(got, labels, gain, bias):
+    rows = got.shape[0] // 2
+    return call(
+        "enter_far", enter_far_body, [((rows, D), BF16)] * 2, [got, labels, gain, bias]
     )
 
 
@@ -793,37 +888,73 @@
     )
 
 
-def halve_body(flags, block, across, kept, sent):
+def halve_body(with_vectors, flags, block, across, *refs):
+    if with_vectors:
+        vectors, got, kept, sent, vec_ref = refs
+        total = vectors[...] + got[...]
+        vec_ref[...] = total
+    else:
+        kept, sent = refs
     size = kept.shape[0] // 2
     for place, (out, step) in enumerate(((kept, 0), (kept, 2), (sent, 1), (sent, 3))):
         rows = pl.ds(pl.multiple_of((flags[1] ^ step) * size, size), size)
         spot = slice((place % 2) * size, (place % 2 + 1) * size)
         out[spot] = (block[rows, :].astype(F32) + across[rows, :].astype(F32)).astype(BF16)
-
-
-def halve(flags, block, across, after=()):
+    if with_vectors:
+        sent[2 * size :] = encode_rows(total)
+
+
+def halve(flags, block, across, vectors=(), after=()):
     rows, width = block.shape
+    outs = [((rows // 2, width), BF16)] * 2
+    if vectors:
+        outs = [outs[0], ((rows // 2 + 48, width), BF16), (vectors[0].shape, F32)]
     return call(
         "halve",
-        halve_body,
-        [((rows // 2, width), BF16)] * 2,
-        [flags, block, across],
+        partial(halve_body, bool(vectors)),
+        outs,
+        [flags, block, across, *vectors],
         after=after,
     )
 
 
-def quarter_body(kept, got, own, sent):
+def quarter_body(with_vectors, kept, got, *refs):
+    if with_vectors:
+        vectors, own, sent, vec_ref = refs
+    else:
+        own, sent = refs
     size = own.shape[0]
     for place, out in enumerate((own, sent)):
         rows = slice(place * size, (place + 1) * size)
-        out[...] = (kept[rows].astype(F32) + got[rows].astype(F32)).astype(BF16)
-
-
-def quarter(kept, got, after=()):
+        out[:size] = (kept[rows].astype(F32) + got[rows].astype(F32)).astype(BF16)
+    if with_vectors:
+        vec_ref[...] = vectors[...]
+        sent[size:] = encode_rows(vectors[...])
+
+
+def quarter(kept, got, vectors=(), after=()):
     rows, width = kept.shape
-    return call(
-        "quarter", quarter_body, [((rows // 2, width), BF16)] * 2, [kept, got], after=after
-    )
+    outs = [((rows // 2, width), BF16)] * 2
+    if vectors:
+        outs = [outs[0], ((rows // 2 + 48, width), BF16), (vectors[0].shape, F32)]
+    return call(
+        "quarter",
+        partial(quarter_body, bool(vectors)),
+        outs,
+        [kept, got, *vectors],
+        after=after,
+    )
+
+
+def last_body(kept, got, vectors, out, vec_ref):
+    size = kept.shape[0]
+    out[...] = (kept[...].astype(F32) + got[:size].astype(F32)).astype(BF16)
+    vec_ref[...] = vectors[...] + decode_rows(got[size:])
+
+
+def last_of(kept, got, vectors):
+    outs = [(kept.shape, BF16), (vectors.shape, F32)]
+    return call("last", last_body, outs, [kept, got, vectors])
 
 
 def total_body(*refs):
@@ -835,22 +966,24 @@
     return call("total", total_body, [(parts[0].shape, kind)], list(parts), after=after)[0]
 
 
-def final_first_body(flags, lower, upper, q_ref, k_ref, v_ref, o_ref):
+def final_first_body(flags, lower, upper, vec, vec_got, q_ref, k_ref, v_ref, o_ref, vec_ref):
     width = q_ref.shape[1]
     first = jnp.full((1, D), flags[2], jnp.int32) == 0
     total = jnp.where(first, lower[...].astype(F32), upper[...].astype(F32))
     for place, ref in enumerate((q_ref, k_ref, v_ref)):
         ref[...] = total[:, place * width : (place + 1) * width]
     o_ref[...] = total[:, 3 * width :].T
-
-
-def final_first(flags, lower, upper):
-    rows, width = lower.shape[0], D // LANES
+    here = jnp.full((1, D), flags[0], jnp.int32) == 1
+    vec_ref[...] = jnp.where(here, vec[...], vec_got[...])
+
+
+def final_first(flags, lower, upper, vec, vec_got):
+    rows, width = upper.shape[0], D // LANES
     return call(
         "final_first",
         final_first_body,
-        [((rows, width), F32)] * 3 + [((width, rows), F32)],
-        [flags, lower, upper],
+        [((rows, width), F32)] * 3 + [((width, rows), F32), ((16, D), F32)],
+        [flags, lower, upper, vec, vec_got],
     )
 
 
@@ -881,32 +1014,6 @@
 
 def merge(flags, one, two, upper):
     return call("merge", merge_body, [(upper.shape, BF16)], [flags, one, two, upper])[0]
-
-
-def vectors_body(*refs):
-    *items, out = refs
-    out[...] = jnp.zeros_like(out)
-    for place, item in enumerate(items):
-        out[2 * place : 2 * place + 2, : item.shape[1]] = item[0:2, :]
-
-
-def vectors_of(items):
-    return call("vectors", vectors_body, [((2 * len(items), D), F32)], list(items))[0]
-
-
-def ranks_body(flags, own, got, out):
-    here = jnp.full((1, D), flags[0], jnp.int32) == 1
-    out[0:8] = own[0:8] + got[0:8]
-    out[8:] = jnp.where(here, own[8:], got[8:])
-
-
-def outer_body(own, got, out):
-    out[0:8] = own[0:8] + got[...]
-    out[8:] = own[8:]
-
-
-def first_rows_body(own, out):
-    out[...] = own[0:8]
 
 
 def choose_body(flags, one, two, out):
@@ -961,33 +1068,48 @@
     )[0]
 
 
-def upper_block_body(flags, up, first, down, out):
+def early_block_body(flags, up, got, first, out):
     width = up.shape[1]
     lower = jnp.full((1, width), flags[2], jnp.int32) == 0
-    out[:, :width] = jnp.where(lower, up[...], first[...])
-    out[:, width:] = down[...]
-
-
-def upper_block(flags, up, first, down, after):
+    out[:, :width] = jnp.where(lower, up[...], got[:, :width])
+    half = first.shape[1] // 2
+    lower = jnp.full((1, half), flags[2], jnp.int32) == 0
+    out[:, width:] = jnp.where(lower, got[:, width:], first[:, half:])
+
+
+def early_block(flags, up, got, first, after=()):
     rows, width = up.shape
     return call(
-        "upper_block",
-        upper_block_body,
-        [((rows, 2 * width), BF16)],
-        [flags, up, first, down],
+        "early_block",
+        early_block_body,
+        [((rows, width + first.shape[1] // 2), BF16)],
+        [flags, up, got, first],
         after=after,
     )[0]
 
 
-def halves_body(ref, one, two):
+def late_block_body(flags, got, down, out):
+    width = down.shape[1]
+    lower = jnp.full((1, width), flags[2], jnp.int32) == 0
+    out[...] = jnp.where(lower, got[:, :width], down[...])
+
+
+def late_block(flags, got, down, after=()):
+    return call(
+        "late_block", late_block_body, [(down.shape, BF16)], [flags, got, down], after=after
+    )[0]
+
+
+def parts_body(ref, one, two):
     width = one.shape[1]
     one[...] = ref[:, :width]
     two[...] = ref[:, width:]
 
 
-def halves_of(x, after):
-    rows, width = x.shape
-    return call("halves", halves_body, [((rows, width // 2), x.dtype)] * 2, [x], after=after)
+def parts_of(x, width, after):
+    rows, whole = x.shape
+    shapes = [((rows, width), x.dtype), ((rows, whole - width), x.dtype)]
+    return call("parts", parts_body, shapes, [x], after=after)
 
 
 def pick_body(flags, beside, across, out):
@@ -1065,9 +1187,11 @@
     def along_line(block, step):
         return lax.ppermute(block, ("section", "dp", "mp"), line_pairs(step))
 
-    first, down_block = first_block(w_query[0], w_key[0], w_value[0], w_output[0], w_down[0])
+    first, down_block, swapped = first_block(
+        flags, w_query[0], w_key[0], w_value[0], w_output[0], w_down[0], w_up[0]
+    )
     up_block = w_up[0]
-    to_second, to_first = [(r, LANES + r) for r in range(LANES)], [(LANES + r, r) for r in range(LANES)]
+    to_first = [(LANES + r, r) for r in range(LANES)]
     inner_ranks = [((1 - r // 2) * LANES + r, (r // 2) * LANES + r) for r in range(LANES)]
 
     def along_dp(block):
@@ -1117,7 +1241,9 @@
         return (own, mate, far, core_swap(far)), near
 
     def attention(x, h, first, outer, split, hooks, far=None):
-        pieces, (near,) = gather_around(h, lambda rows: [project(*rows, first)], far)
+        pieces, (near,) = gather_around(
+            h, lambda rows: [project(*rows, first)], far, after=hooks[2]
+        )
         far = project(pieces[2], pieces[3], first)
         half = 2 * slice_len
         o_far, p_far, p_far_mate, sum_far = attend(
@@ -1125,8 +1251,9 @@
         )
         sent = pair_sum(p_far, p_far_mate)
         o_near, p_own, p_mate, sum_near = attend(
-            0, near, near, far, labels, first, split[0], split[1], after=[sent, *hooks[0]]
-        )
+            0, near, near, far, labels, first, split[0], split[1], after=[sent]
+        )
+        hooks[0](p_own)
         arrived = hold(x_swap(sent), after=[p_own])
         terms = (p_own, core_swap(p_mate), arrived)
         x2, branch, h2, folded, kept = after_attend(x, terms, outer[2], outer[3], after=hooks[1])
@@ -1146,21 +1273,34 @@
         dq_near, dq_far = attend_back(
             near, far, do_near, do_far, sum_near, sum_far, labels, after=hooks[1]
         )
-        p_far, p_far_mate, norm_far = unproject(
-            dq_far, first, pieces[2:], outer[0], outer[1], after=hooks[4]
-        )
-        sent = pair_sum(p_far, p_far_mate)
-        p_own, p_mate, norm_near = unproject(
-            dq_near, first, pieces[:2], outer[0], outer[1], after=[sent]
-        )
+        norm = (outer[0], outer[1])
+        if following:
+            p_far, p_far_mate, norm_far = unproject(
+                dq_far, first, pieces[2:], *norm, after=hooks[4](dq_far)
+            )
+            sent = pair_sum(p_far, p_far_mate)
+            p_own, p_mate, norm_near = unproject(
+                dq_near, first, pieces[:2], *norm, after=[sent, *hooks[5]()]
+            )
+            norm_vec = norm_near + norm_far
+            ending = ()
+        else:
+            p_own, p_mate, norm_near = unproject(
+                dq_near, first, pieces[:2], *norm, after=hooks[7]
+            )
+            riding = (norm_near, feed_vec, *hooks[4])
+            p_far, p_far_mate = unproject(dq_far, first, pieces[2:], *norm, riding=riding)
+            sent = pair_sum(p_far, p_far_mate)
+            norm_vec = None
+            ending = (sent, *hooks[5], vec_near + vec_far, hooks[6])
         mat_grad = grads_of(
             (pieces, (dq_near, dq_far)), (backs, (u_near, u_far)), after=[sent]
         )
         terms = (p_own, core_swap(p_mate), hold(x_swap(sent), after=[p_own, mat_grad]))
         result = first_norm_back(
-            terms, dx2, x, outer[0], following, after=hooks[2](mat_grad, dq_far)
-        )
-        return result, vec_near + vec_far, feed_vec, norm_near + norm_far
+            terms, dx2, x, outer[0], following, ending, after=hooks[2](mat_grad)
+        )
+        return result, vec_near + vec_far, feed_vec, norm_vec
 
     def reduce_across(block):
         across = lax.ppermute(block, BOTH, returning)
@@ -1172,13 +1312,13 @@
     def reduce_near(pair, after=()):
         if count != 4:
             return pair
-        kept, sent = halve(flags, *pair, after)
+        kept, sent = halve(flags, *pair, after=after)
         return kept, along_line(sent, 1)
 
     def reduce_far(pair, after=()):
         if count != 4:
             return pair
-        kept, sent = quarter(*pair, after)
+        kept, sent = quarter(*pair, after=after)
         return kept, along_line(sent, 2)
 
     def reduce_end(pair, layer, after=()):
@@ -1187,11 +1327,22 @@
             total, BOTH, [((r // 2) * LANES + r, layer * LANES + r) for r in range(LANES)]
         )
 
-    got = lax.ppermute(entry(flags, inputs, cotangent), BOTH, crossing)
+    sent, far_sent, own_in, own_grad = entry(flags, inputs, cotangent)
+    got = lax.ppermute(sent, BOTH, crossing)
+    far_got = lax.ppermute(
+        far_sent,
+        BOTH,
+        [
+            (s * LANES + r, s * LANES + (r ^ 1) if s == r // 2 else (r // 2) * LANES + (r ^ 3))
+            for s in range(2)
+            for r in range(LANES)
+        ],
+    )
     lower_in, upstream, masked, h = enter(
-        flags, inputs, cotangent, got, labels, lower_outer[0], lower_outer[1]
-    )
-    far = x_swap(h)
+        flags, own_in, own_grad, got, labels, lower_outer[0], lower_outer[1]
+    )
+    masked_far, far = enter_far(far_got, labels, lower_outer[0], lower_outer[1])
+    top = (masked, core_swap(masked), masked_far, core_swap(masked_far))
     moved = rank_of(first, 0)
     if count == 4:
         pieces = [moved] + [along_line(moved, step) for step in range(1, count)]
@@ -1201,41 +1352,41 @@
     else:
         pieces = [along_dp(moved)]
         lower_first = pick(flags, pieces[0], lax.ppermute(pieces[0], BOTH, crossing))
-    lower_second_line = along_dp(
-        choose(
-            flags, up_block, lax.ppermute(down_block, BOTH, to_second), after=[pieces[-1]]
-        )
-    )
-    upper_line = along_dp(
-        upper_block(
-            flags, lax.ppermute(up_block, BOTH, to_first), first, down_block, [pieces[-1]]
-        )
-    )
-    top = gather_rows(masked)
+    got = core_swap(swapped)
+    early_line = along_dp(early_block(flags, up_block, got, first, after=pieces[-1:]))
+    late_line = along_dp(late_block(flags, got, down_block))
+    coming = {}
+
+    def early_matrices(last):
+        coming["second"], coming["first"] = parts_of(early_line, UNITS, [last])
+
     x2, h2, lower_state, arrived = attention(
-        lower_in, h, lower_first, lower_outer, lower_split, ([top[3]], ()), far
-    )
-    lower_second = pick(flags, *fetched(hold(lower_second_line, after=[arrived])))
+        lower_in, h, lower_first, lower_outer, lower_split, (early_matrices, (), ()), far
+    )
+    lower_second_whole, lower_second_across = fetched(coming["second"])
+    lower_second = pick(flags, lower_second_whole, lower_second_across)
+    upper_first_whole, upper_first_across = fetched(coming["first"], [h2])
+    upper_first = pick(flags, upper_first_whole, upper_first_across)
     lower_pieces, (f_near, p_own, p_mate) = gather_around(
         h2, lambda rows: feed(rows, (), lower_second, *lower_split[2:])
     )
     f_far, p_far, p_far_mate = feed(lower_pieces[2:], (), lower_second, *lower_split[2:])
     lower_pre = (f_near, f_far)
-    upper_left, upper_right = halves_of(upper_line, [f_far])
-    upper_first_whole = rank_of(upper_left, 1)
-    upper_first_across = lax.ppermute(upper_first_whole, BOTH, crossing)
-    upper_first = pick(flags, upper_first_whole, upper_first_across)
-    terms = settle(p_own, p_mate, p_far, p_far_mate)
+    sent = pair_sum(p_far, p_far_mate)
+    upper_second_whole, upper_second_across = fetched(hold(late_line, after=[sent]))
+    upper_second = pick(flags, upper_second_whole, upper_second_across)
+    arrived = hold(x_swap(sent), after=[upper_second_whole])
+    terms = (p_own, core_swap(p_mate), arrived)
     lower_out, lower_branch, h, lower_folded, lower_kept = after_feed(
         x2, terms, labels, upper_outer[0], upper_outer[1]
     )
-    upper_second_whole = beside(
-        rank_of(upper_left, 0), rank_of(upper_right, 1), after=[lower_out]
-    )
-    upper_second_across = lax.ppermute(upper_second_whole, BOTH, crossing)
-    upper_second = pick(flags, upper_second_whole, upper_second_across)
     x2, h2, upper_state, _ = attention(
-        lower_out, h, upper_first, upper_outer, upper_split, ((), [upper_second])
+        lower_out,
+        h,
+        upper_first,
+        upper_outer,
+        upper_split,
+        (lambda last: None, (), [upper_second_whole]),
     )
     upper_pieces, (f_near, p_own, p_mate, near_stats) = gather_around(
         h2, lambda rows: feed(rows, top[:2], upper_second, *upper_split[2:])
@@ -1256,7 +1407,12 @@
     upper_middle = vec_near + vec_far
     sums = (q_own, core_swap(q_mate), hold(x_swap(sent), after=[q_own]))
     ended = pair_sum(p_far, p_far_mate)
-    ended_far = hold(x_swap(ended), after=[ended])
+    ended_far = []
+
+    def ended_hook(last):
+        ended_far.append(hold(x_swap(ended), after=[last]))
+        return ended_far
+
     following = (labels, lower_branch, lower_folded, lower_kept)
     pairs = {}
 
@@ -1267,7 +1423,7 @@
         pairs["second"] = reduce_near(reduce_across(block))
         return [block]
 
-    def upper_hook(item, last):
+    def upper_hook(item):
         pairs["upper"] = reduce_across(item)
         return [item]
 
@@ -1279,20 +1435,21 @@
         upper_outer,
         upper_split,
         following,
-        ((), [ended], upper_hook, upper_second_grads, [ended_far]),
-    )
-
-    upper_out = finish_feed(x2, (p_own, core_swap(p_mate), ended_far), labels)
+        ((), [ended], upper_hook, upper_second_grads, ended_hook, lambda: ()),
+    )
+
+    upper_out = finish_feed(x2, (p_own, core_swap(p_mate), ended_far[0]), labels)
     own = pack([lower_out, upper_out, upper_grad])
     swapped = lax.ppermute(own, BOTH, returning)
     upper_second_pair = reduce_far(pairs["second"], [own])
+    upper_first_pair = reduce_near(pairs["upper"])
     backs, (df_near, n_near, q_own, q_mate, vec_near) = gather_around(
         sent,
         lambda rows: feed_back(
             rows, (), 0, lower_pre[0], *lower_split[2:], lower_second, after=[own]
         ),
-    )
-    upper_first_pair = reduce_near(pairs["upper"])
+        after=upper_first_pair[:1],
+    )
     df_far, n_far, q_far, q_far_mate, vec_far = feed_back(
         backs[2:],
         (),
@@ -1300,7 +1457,7 @@
         lower_pre[1],
         *lower_split[2:],
         lower_second,
-        after=[own, upper_first_pair[0], upper_second_pair[0]],
+        after=[swapped, upper_second_pair[0]],
     )
     lower_middle = vec_near + vec_far
     sent = pair_sum(q_far, q_far_mate)
@@ -1310,22 +1467,24 @@
         block = grads_of(
             (lower_pieces, (df_near, df_far)), (backs, (n_near, n_far)), after=[after]
         )
-        pairs["second"] = reduce_near(reduce_across(block))
-        pairs["sum"] = reduce_end(upper_second_pair, 1, after=[block])
-        pairs["first"] = reduce_far(upper_first_pair, after=[block])
+        pairs["second"] = reduce_across(block)
         return [block]
+
+    upper_second_sum = reduce_end(upper_second_pair, 1, after=[q_far])
+    upper_first_pair = reduce_far(upper_first_pair, after=[q_far])
+    upper_first_sum = reduce_end(upper_first_pair, 1)
 
     inward = [((r // 2) * LANES + r, (1 - r // 2) * LANES + r) for r in range(LANES)]
     layer_outputs, upper_held = unpack(
         flags, own, swapped, lax.ppermute(own, BOTH, inward), lax.ppermute(swapped, BOTH, inward)
     )
 
-    def lower_hook(item, last):
+    def lower_hook(item):
         pairs["lower"] = reduce_across(item)
-        pairs["second"] = reduce_far(pairs["second"], after=[item])
-        return [item]
-
-    (lower_grad,), lower_inner, lower_feed, lower_norm = attention_back(
+        pairs["second"] = reduce_far(reduce_near(pairs["second"], after=[item]))
+        return [item, upper_first_sum, pairs["second"][0]]
+
+    (lower_grad, vectors), _, _, _ = attention_back(
         upper_grad,
         sums,
         lower_state,
@@ -1333,34 +1492,34 @@
         lower_outer,
         lower_split,
         (),
-        ((), [layer_outputs], lower_hook, lower_second_grads, ()),
-    )
-    upper_second_sum = pairs["sum"]
-    upper_first_sum = reduce_end(pairs["first"], 1)
+        (
+            [layer_outputs],
+            [upper_second_sum],
+            lower_hook,
+            lower_second_grads,
+            (upper_norm, upper_feed),
+            (lower_middle, upper_middle),
+            upper_inner,
+            [upper_first_pair[0]],
+        ),
+    )
     lower_second_pair = pairs["second"]
-    vectors = vectors_of(
-        [lower_norm, lower_feed, upper_norm, upper_feed, lower_middle, upper_middle]
-        + [lower_inner, upper_inner]
-    )
-    shape = [(vectors.shape, F32)]
-    vectors = total_of([vectors, y_swap(vectors)], F32)
-    vectors = call("ranks", ranks_body, shape, [flags, vectors, core_swap(vectors)])[0]
-    outer = call("first_rows", first_rows_body, [((8, D), F32)], [vectors])[0]
-    vectors = call("outer", outer_body, shape, [vectors, x_swap(outer)])[0]
     lower_held = placed(lower_grad, 0)
-    lower_first_pair = reduce_near(pairs["lower"], after=[vectors])
     if count == 4:
-        for step in (1, 2):
-            got = lax.ppermute(vectors, "dp", [(i, i ^ step) for i in range(count)])
-            vectors = total_of([vectors, got], F32)
-            if step == 1:
-                lower_first_pair = reduce_far(lower_first_pair, after=[vectors, *lower_held])
+        kept, got = reduce_near(pairs["lower"], after=[vectors])
+        vectors = total_of([vectors, y_swap(vectors)], F32)
+        vectors = total_of([vectors, along_line(vectors, 1)], F32)
+        kept, sent, vectors = quarter(kept, got, [vectors])
+        ended, vectors = last_of(kept, along_line(sent, 2), vectors)
     else:
-        vectors = lax.psum(vectors, "dp")
+        vectors = lax.psum(vectors + y_swap(vectors), "dp")
+        ended = pairs["lower"][0]
+    ended = lax.ppermute(ended, BOTH, [((r // 2) * LANES + r, r) for r in range(LANES)])
+    vectors_got = lax.ppermute(vectors, BOTH, inward)
     lower_second_sum = reduce_end(lower_second_pair, 0)
     input_grads = merge(flags, *lower_held, upper_held)
-    grad_query, grad_key, grad_value, grad_output = final_first(
-        flags, reduce_end(lower_first_pair, 0), upper_first_sum
+    grad_query, grad_key, grad_value, grad_output, vectors = final_first(
+        flags, ended, upper_first_sum, vectors, vectors_got
     )
     grad_up, grad_down = final_second(flags, lower_second_sum, upper_second_sum)
 

time: 460 us -> 444 us (0.965)
  waiting for transfers between devices: 164 us -> 145 us
  Pallas kernels: 115 us -> 121 us
    ppermute x11 -> x12, waiting for transfers between devices: 2.12 us -> 26.8 us  [along_line(): return lax.ppermute(block, ('section', 'dp', 'mp'), line_pairs(step))]
    ppermute x7 -> x4, waiting for transfers between devices: 22.5 us -> 0.01 us  [the longest x1 0.01 us: on_device(): got = lax.ppermute(sent, BOTH, crossing)]
    ppermute x18 -> x15, waiting for transfers between devices: 80.3 us -> 64.2 us  [x_swap(): return lax.ppermute(x, 'mp', [(i, i ^ 1) for i in range(LANES)])]
    ppermute x1 -> x3, starting transfers between devices: 4.05 us -> 16.5 us  [fetched(): return (whole, lax.ppermute(whole, BOTH, crossing))]
    ppermute x18 -> x15, starting transfers between devices: 26 us -> 13.9 us  [x_swap(): return lax.ppermute(x, 'mp', [(i, i ^ 1) for i in range(LANES)])]
    all_gather x2, waiting for transfers between devices: 10.2 us -> 0.01 us  [along_dp(): return lax.all_gather(block, 'dp', axis=0, tiled=True)]
    ppermute x4, waiting for transfers between devices: 0.01 us -> 5.63 us  [on_device(): lax.ppermute(piece, BOTH, crossing)]
    pallas_call x1 -> x2, Pallas kernels: 1.01 us -> 6.24 us  [the longest x1 3.33 us: entry(): pl.pallas_call(entry_body, out_shape=tuple((jax.ShapeDtypeStruct((count,...]
  transfers between devices with their start and end apart: 99 -> 94, of which waited for: 44 -> 40; matrix products, arithmetic and copies ran while one was open for 1% -> 1% of each run, Pallas kernels for 24% -> 24%
where the time goes in v5:
time: 444 us; the launch traced here: 440 us
  waiting for transfers between devices  145 us (33%)
  starting transfers between devices  122 us (27%)
  Pallas kernels  121 us (27%)
  local copies, waits for them, and re-layouts  33.7 us (8%)
  between operations  16.5 us (4%)
    pallas_call x95, Pallas kernels, call(): pl.pallas_call(kernel, out_shape=tuple((jax.ShapeDtypeStruct(shape, kind)...  115 us
    ppermute x15, waiting for transfers between devices, x_swap(): return lax.ppermute(x, 'mp', [(i, i ^ 1) for i in range(LANES)])  64.2 us
    ppermute x12, starting transfers between devices, along_line(): return lax.ppermute(block, ('section', 'dp', 'mp'), line_pairs(step))  40.5 us
    unnamed x198, local copies, waits for them, and re-layouts  31.5 us
    ppermute x12, waiting for transfers between devices, along_line(): return lax.ppermute(block, ('section', 'dp', 'mp'), line_pairs(step))  26.8 us
    ppermute x3, waiting for transfers between devices, fetched(): return (whole, lax.ppermute(whole, BOTH, crossing))  16.6 us
    ppermute x3, starting transfers between devices, fetched(): return (whole, lax.ppermute(whole, BOTH, crossing))  16.5 us
    ppermute x36, waiting for transfers between devices, core_swap(): return lax.ppermute(x, 'section', [(0, 1), (1, 0)])  15.5 us
  transfers between devices with their start and end apart: 94, of which 40 were waited for; matrix products, arithmetic and copies ran while one was open for 1% of the time, Pallas kernels for 24%

profile of v5, /device:TPU:0, one launch (start us, length us, event | category | flops | bytes accessed | tf_op | source)
XLA Modules:
  0.0 439.7 jit_solution(12952816033028134549)
XLA Ops:
  9.3 2.9 first_block.1
  14.3 3.3 entry.1
  17.6 6.0 %collective-permute-start = (bf16[512,768]{1,0:T(8,128)(2,1)}, bf16[512,768]{1,0:T(8,128)(2,1)S(1)}, u32[]{:S(2)}, u32[]{:S(2)}) collective-permute-start(bf16[512,768]{1,0:T(8,128)(2,1)} %get-tuple-element.163), channel_id=1, source_target_pairs={{0,2},{1,3},{18,16},{19,17},{4,6},{5,7},{22,20},{23,21},{8,10},{9,... | collective-permute-start | bytes 2359304 | tf_op jit(solution)/shard_map/ppermute | solution.py:1331
  23.8 5.5 %collective-permute-start.6 = (bf16[192,768]{1,0:T(8,128)(2,1)}, bf16[192,768]{1,0:T(8,128)(2,1)S(1)}, u32[]{:S(2)}, u32[]{:S(2)}) collective-permute-start(bf16[192,768]{1,0:T(8,128)(2,1)} %collective-permute-done.3.refs_1_), channel_id=1, source_target_pairs={{0,12},{1,13},{18,30},{19,31},{4,8},{5,9},{22,26},{23,27},{8,4},{9... | collective-permute-start | bytes 884744 | tf_op jit(solution)/shard_map/ppermute | solution.py:1188
  31.2 1.9 collective-permute-start.4
  34.5 5.7 %collective-permute-start.5 = (bf16[192,768]{1,0:T(8,128)(2,1)}, bf16[192,768]{1,0:T(8,128)(2,1)}, u32[]{:S(2)}, u32[]{:S(2)}) collective-permute-start(bf16[192,768]{1,0:T(8,128)(2,1)} %collective-permute-done.3.refs_1_), channel_id=1, source_target_pairs={{0,8},{1,9},{18,26},{19,27},{4,12},{5,13},{22,30},{23,31},{8,0},{9... | collective-permute-start | bytes 884744 | tf_op jit(solution)/shard_map/ppermute | solution.py:1188
  49.6 4.4 collective-permute-start.10
  59.0 2.5 collective-permute-done.8.refs_6_
  61.5 3.2 collective-permute-done.9.refs_7_
  69.4 4.2 attend.4
  77.1 4.2 attend.5
  88.4 3.4 collective-permute-done.20.refs_2_
  92.6 5.7 %collective-permute-start.21 = (bf16[768,1536]{1,0:T(8,128)(2,1)S(1)}, bf16[768,1536]{1,0:T(8,128)(2,1)}, u32[]{:S(2)}, u32[]{:S(2)}) collective-permute-start(bf16[768,1536]{1,0:T(8,128)(2,1)S(1)} %join.3.refs_1_), channel_id=1, source_target_pairs={{0,2},{1,3},{18,16},{19,17},{4,6},{5,7},{22,20},{23,21},{8,10},{9,... | collective-permute-start | bytes 7077896 | tf_op jit(solution)/shard_map/ppermute | solution.py:1202
  100.3 7.6 %collective-permute-done.17.refs_0_ = bf16[272,768]{1,0:T(8,128)(2,1)S(1)} collective-permute-done((bf16[272,768]{1,0:T(8,128)(2,1)}, bf16[272,768]{1,0:T(8,128)(2,1)S(1)}, u32[]{:S(2)}, u32[]{:S(2)}) %collective-permute-start.17) | collective-permute-done | bytes 417824 | tf_op jit(solution)/shard_map/ppermute | solution.py:152
  115.1 7.9 %collective-permute-done.21.refs_2_ = bf16[768,1536]{1,0:T(8,128)(2,1)} collective-permute-done((bf16[768,1536]{1,0:T(8,128)(2,1)S(1)}, bf16[768,1536]{1,0:T(8,128)(2,1)}, u32[]{:S(2)}, u32[]{:S(2)}) %collective-permute-start.21) | collective-permute-done | bytes 2359328 | tf_op jit(solution)/shard_map/ppermute | solution.py:1202
  124.7 1.9 pick.3.refs_2_.refs_5_
  143.3 6.1 %collective-permute-start.30 = (bf16[768,768]{1,0:T(8,128)(2,1)S(1)}, bf16[768,768]{1,0:T(8,128)(2,1)S(1)}, u32[]{:S(2)}, u32[]{:S(2)}) collective-permute-start(bf16[768,768]{1,0:T(8,128)(2,1)S(1)} %join.5.refs_1_), channel_id=1, source_target_pairs={{0,2},{1,3},{18,16},{19,17},{4,6},{5,7},{22,20},{23,21},{8,10},{9,... | collective-permute-start | bytes 3538952 | tf_op jit(solution)/shard_map/ppermute | solution.py:1202
  151.0 6.9 %collective-permute-done.26.refs_0_ = bf16[272,768]{1,0:T(8,128)(2,1)S(1)} collective-permute-done((bf16[272,768]{1,0:T(8,128)(2,1)S(1)}, bf16[272,768]{1,0:T(8,128)(2,1)S(1)}, u32[]{:S(2)}, u32[]{:S(2)}) %collective-permute-start.26) | collective-permute-done | bytes 417824 | tf_op jit(solution)/shard_map/ppermute | solution.py:152
  159.7 3.3 collective-permute-done.30.refs_2_
  164.5 5.9 %collective-permute-done.31.refs_0_ = bf16[256,768]{1,0:T(8,128)(2,1)S(1)} collective-permute-done((bf16[256,768]{1,0:T(8,128)(2,1)S(1)}, bf16[256,768]{1,0:T(8,128)(2,1)S(1)}, u32[]{:S(2)}, u32[]{:S(2)}) %collective-permute-start.31) | collective-permute-done | bytes 393248 | tf_op jit(solution)/shard_map/ppermute | solution.py:152
  170.5 4.7 %collective-permute-start.38 = (bf16[768,1536]{1,0:T(8,128)(2,1)S(1)}, bf16[768,1536]{1,0:T(8,128)(2,1)S(1)}, u32[]{:S(2)}, u32[]{:S(2)}) collective-permute-start(bf16[768,1536]{1,0:T(8,128)(2,1)S(1)} %join.4.refs_1_.refs_2_), channel_id=1, source_target_pairs={{0,2},{1,3},{18,16},{19,17},{4,6},{5,7},{22,20},{23,21},{8,10},{9,... | collective-permute-start | bytes 7077896 | tf_op jit(solution)/shard_map/ppermute | solution.py:1202
  176.1 4.2 attend.6
  183.1 4.2 attend.7
  187.9 6.1 %collective-permute-done.35.refs_0_ = bf16[272,768]{1,0:T(8,128)(2,1)S(1)} collective-permute-done((bf16[272,768]{1,0:T(8,128)(2,1)S(1)}, bf16[272,768]{1,0:T(8,128)(2,1)S(1)}, u32[]{:S(2)}, u32[]{:S(2)}) %collective-permute-start.35) | collective-permute-done | bytes 417824 | tf_op jit(solution)/shard_map/ppermute | solution.py:152
  195.9 5.3 %collective-permute-done.38.refs_2_ = bf16[768,1536]{1,0:T(8,128)(2,1)S(1)} collective-permute-done((bf16[768,1536]{1,0:T(8,128)(2,1)S(1)}, bf16[768,1536]{1,0:T(8,128)(2,1)S(1)}, u32[]{:S(2)}, u32[]{:S(2)}) %collective-permute-start.38) | collective-permute-done | bytes 2359328 | tf_op jit(solution)/shard_map/ppermute | solution.py:1202
  202.0 3.0 feed.6
  208.2 2.6 feed.7
  212.9 3.1 collective-permute-done.46.refs_1_
  216.1 2.4 feed_back.4
  221.2 2.4 feed_back.5
  223.7 7.9 %collective-permute-done.49.refs_0_ = bf16[256,768]{1,0:T(8,128)(2,1)S(1)} collective-permute-done((bf16[256,768]{1,0:T(8,128)(2,1)S(1)}, bf16[256,768]{1,0:T(8,128)(2,1)S(1)}, u32[]{:S(2)}, u32[]{:S(2)}) %collective-permute-start.49) | collective-permute-done | bytes 393248 | tf_op jit(solution)/shard_map/ppermute | solution.py:152
  233.8 2.8 grads.4.refs_2_.refs_1_
  237.5 7.4 %collective-permute-done.51.refs_0_ = bf16[272,768]{1,0:T(8,128)(2,1)S(1)} collective-permute-done((bf16[272,768]{1,0:T(8,128)(2,1)S(1)}, bf16[272,768]{1,0:T(8,128)(2,1)S(1)}, u32[]{:S(2)}, u32[]{:S(2)}) %collective-permute-start.51) | collective-permute-done | bytes 417824 | tf_op jit(solution)/shard_map/ppermute | solution.py:152
  248.0 13.1 %attend_back.2 = (bf16[512,576]{1,0:T(8,128)(2,1)S(1)}, bf16[512,576]{1,0:T(8,128)(2,1)S(1)}) custom-call(bf16[512,576]{1,0:T(8,128)(2,1)S(1)} %project.6.refs_1_.refs_0_, bf16[512,576]{1,0:T(8,128)(2,1)S(1)} %project.7.refs_0_.refs_2_.refs_1_, bf16[512,192]{1,0:T(8,128)(2,1)S(1)} %get-tuple-element.212.refs_1_.refs_2_, ...), custom_call_target="tpu_custom_call" | custom-call | flops 14000000000 | bytes 1 | tf_op jit(solution)/shard_map/attend_back/pallas_call | solution.py:41
  267.6 1.9 grads.5.refs_2_.refs_10_.refs_1_
  271.4 5.4 %collective-permute-done.55.refs_0_ = bf16[256,768]{1,0:T(8,128)(2,1)S(1)} collective-permute-done((bf16[256,768]{1,0:T(8,128)(2,1)S(1)}, bf16[256,768]{1,0:T(8,128)(2,1)S(1)}, u32[]{:S(2)}, u32[]{:S(2)}) %collective-permute-start.55) | collective-permute-done | bytes 393248 | tf_op jit(solution)/shard_map/ppermute | solution.py:152
  280.5 2.3 collective-permute-start.65
  284.6 2.4 feed_back.6
  287.0 2.3 collective-permute-done.62.refs_2_
  290.2 4.8 %collective-permute-done.61.refs_0_ = bf16[272,768]{1,0:T(8,128)(2,1)S(1)} collective-permute-done((bf16[272,768]{1,0:T(8,128)(2,1)S(1)}, bf16[272,768]{1,0:T(8,128)(2,1)S(1)}, u32[]{:S(2)}, u32[]{:S(2)}) %collective-permute-start.61) | collective-permute-done | bytes 417824 | tf_op jit(solution)/shard_map/ppermute | solution.py:152
  295.1 2.5 collective-permute-start.57
  297.5 4.5 %collective-permute-done.56.refs_2_.refs_6_ = bf16[768,768]{1,0:T(8,128)(2,1)S(1)} collective-permute-done((bf16[768,768]{1,0:T(8,128)(2,1)S(1)}, bf16[768,768]{1,0:T(8,128)(2,1)S(1)}, u32[]{:S(2)}, u32[]{:S(2)}) %collective-permute-start.56) | collective-permute-done | bytes 1179680 | tf_op jit(solution)/shard_map/ppermute | solution.py:1443
  304.8 2.4 feed_back.7
  310.4 2.1 collective-permute-start.71
  314.1 6.2 %collective-permute-done.67.refs_2_ = bf16[256,768]{1,0:T(8,128)(2,1)S(1)} collective-permute-done((bf16[256,768]{1,0:T(8,128)(2,1)S(1)}, bf16[256,768]{1,0:T(8,128)(2,1)S(1)}, u32[]{:S(2)}, u32[]{:S(2)}) %collective-permute-start.67) | collective-permute-done | bytes 393248 | tf_op jit(solution)/shard_map/ppermute | solution.py:152
  324.0 2.8 grads.6.refs_2_.refs_1_
  328.2 1.9 collective-permute-start.73
  330.3 2.1 collective-permute-start.72
  334.8 5.2 %collective-permute-done.73.refs_1_ = bf16[384,768]{1,0:T(8,128)(2,1)S(1)} collective-permute-done((bf16[384,768]{1,0:T(8,128)(2,1)S(1)}, bf16[384,768]{1,0:T(8,128)(2,1)S(1)}, u32[]{:S(2)}, u32[]{:S(2)}) %collective-permute-start.73) | collective-permute-done | bytes 589856 | tf_op jit(solution)/shard_map/ppermute | solution.py:1188
  341.6 13.1 %attend_back.3 = (bf16[512,576]{1,0:T(8,128)(2,1)S(1)}, bf16[512,576]{1,0:T(8,128)(2,1)S(1)}) custom-call(bf16[512,576]{1,0:T(8,128)(2,1)S(1)} %copy-done.26, bf16[512,576]{1,0:T(8,128)(2,1)S(1)} %copy-done.51, bf16[512,192]{1,0:T(8,128)(2,1)S(1)} %get-tuple-element.251.refs_1_.refs_2_, bf16[512,192]{1,0:T(8,128)(2,1)S(1)} %get-tuple-element.256.refs_3_, ...), custom_call_target="tpu_custom_call" | custom-call | flops 14000000000 | bytes 1 | tf_op jit(solution)/shard_map/attend_back/pallas_call | solution.py:41
  358.7 1.9 grads.7.refs_2_.refs_3_.refs_11_.refs_1_
  361.7 1.9 collective-permute-start.80
  364.9 3.3 collective-permute-start.77
  369.1 11.4 %collective-permute-done.77.refs_1_ = bf16[192,768]{1,0:T(8,128)(2,1)S(1)} collective-permute-done((bf16[192,768]{1,0:T(8,128)(2,1)S(1)}, bf16[192,768]{1,0:T(8,128)(2,1)S(1)}, u32[]{:S(2)}, u32[]{:S(2)}) %collective-permute-start.77) | collective-permute-done | bytes 294944 | tf_op jit(solution)/shard_map/ppermute | solution.py:1188
  386.1 3.2 collective-permute-start.84
  389.4 3.1 collective-permute-start.90
  392.6 4.1 collective-permute-done.85.refs_1_
  396.6 3.9 collective-permute-start.86
  400.6 3.1 collective-permute-done.86.refs_1_
  403.8 5.6 %collective-permute-start.87 = (bf16[240,768]{1,0:T(8,128)(2,1)S(1)}, bf16[240,768]{1,0:T(8,128)(2,1)S(1)}, u32[]{:S(2)}, u32[]{:S(2)}) collective-permute-start(bf16[240,768]{1,0:T(8,128)(2,1)S(1)} %get-tuple-element.294), channel_id=1, source_target_pairs={{0,8},{1,9},{18,26},{19,27},{4,12},{5,13},{22,30},{23,31},{8,0},{9... | collective-permute-start | bytes 1105928 | tf_op jit(solution)/shard_map/ppermute | solution.py:1188
  413.9 4.9 %collective-permute-done.87.refs_1_ = bf16[240,768]{1,0:T(8,128)(2,1)S(1)} collective-permute-done((bf16[240,768]{1,0:T(8,128)(2,1)S(1)}, bf16[240,768]{1,0:T(8,128)(2,1)S(1)}, u32[]{:S(2)}, u32[]{:S(2)}) %collective-permute-start.87) | collective-permute-done | bytes 368672 | tf_op jit(solution)/shard_map/ppermute | solution.py:1188
  419.6 3.7 collective-permute-start.88
  426.2 2.1 final_second.1
  429.4 2.0 final_first.1
  (448 shorter events, 145.4 us)
Async XLA Ops:
  7.2 77.2 %all-gather.3.cloned.1.call-start = ((), (), s32[]{:S(2)}) async-start(), calls=%async_computation | async-start | bytes 2211840 | tf_op jit(solution)/shard_map/all_gather | solution.py:1198
  12.9 10.8 %collective-permute-start.3 = (bf16[192,768]{1,0:T(8,128)(2,1)S(1)}, bf16[192,768]{1,0:T(8,128)(2,1)}, u32[]{:S(2)}, u32[]{:S(2)}) collective-permute-start(bf16[192,768]{1,0:T(8,128)(2,1)S(1)} %get-tuple-element.166.refs_3_), channel_id=1, source_target_pairs={{0,0},{1,1},{2,18},{3,19},{4,4},{5,5},{6,22},{7,23},{8,8},{9,9},{1... | collective-permute-start | bytes 884744 | tf_op jit(solution)/shard_map/ppermute | solution.py:1205
  17.6 26.9 %collective-permute-start = (bf16[512,768]{1,0:T(8,128)(2,1)}, bf16[512,768]{1,0:T(8,128)(2,1)S(1)}, u32[]{:S(2)}, u32[]{:S(2)}) collective-permute-start(bf16[512,768]{1,0:T(8,128)(2,1)} %get-tuple-element.163), channel_id=1, source_target_pairs={{0,2},{1,3},{18,16},{19,17},{4,6},{5,7},{22,20},{23,21},{8,10},{9,... | collective-permute-start | bytes 2359304 | tf_op jit(solution)/shard_map/ppermute | solution.py:1331
  23.7 7.6 %collective-permute-start.19 = (bf16[192,1152]{1,0:T(8,128)(2,1)}, bf16[192,1152]{1,0:T(8,128)(2,1)S(1)}, u32[]{:S(2)}, u32[]{:S(2)}) collective-permute-start(bf16[192,1152]{1,0:T(8,128)(2,1)} %get-tuple-element.175), channel_id=1, source_target_pairs={{0,16},{16,0},{1,17},{17,1},{2,18},{18,2},{3,19},{19,3},{4,20},{20... | collective-permute-start | bytes 1327112 | tf_op jit(solution)/shard_map/ppermute | solution.py:148
  23.8 10.7 %collective-permute-start.6 = (bf16[192,768]{1,0:T(8,128)(2,1)}, bf16[192,768]{1,0:T(8,128)(2,1)S(1)}, u32[]{:S(2)}, u32[]{:S(2)}) collective-permute-start(bf16[192,768]{1,0:T(8,128)(2,1)} %collective-permute-done.3.refs_1_), channel_id=1, source_target_pairs={{0,12},{1,13},{18,30},{19,31},{4,8},{5,9},{22,26},{23,27},{8,4},{9... | collective-permute-start | bytes 884744 | tf_op jit(solution)/shard_map/ppermute | solution.py:1188
  29.3 13.3 %collective-permute-start.1 = (f32[4,768]{1,0:T(4,128)S(1)}, f32[4,768]{1,0:T(4,128)S(1)}, u32[]{:S(2)}, u32[]{:S(2)}) collective-permute-start(f32[4,768]{1,0:T(4,128)S(1)} %pad_maximum_fusion), channel_id=1, source_target_pairs={{0,16},{16,0},{1,17},{17,1},{2,18},{18,2},{3,19},{19,3},{4,20},{20... | collective-permute-start | bytes 36872 | tf_op jit(solution)/shard_map/ppermute | solution.py:148
  29.4 27.8 %collective-permute-start.11 = (bf16[512,768]{1,0:T(8,128)(2,1)}, bf16[512,768]{1,0:T(8,128)(2,1)S(1)}, u32[]{:S(2)}, u32[]{:S(2)}) collective-permute-start(bf16[512,768]{1,0:T(8,128)(2,1)} %get-tuple-element.167), channel_id=1, source_target_pairs={{0,1},{1,0},{2,17},{3,16},{16,3},{17,2},{18,19},{19,18},{4,5},{5,4... | collective-permute-start | bytes 2359304 | tf_op jit(solution)/shard_map/ppermute | solution.py:1332
  31.2 22.8 %collective-permute-start.4 = (bf16[192,768]{1,0:T(8,128)(2,1)}, bf16[192,768]{1,0:T(8,128)(2,1)}, u32[]{:S(2)}, u32[]{:S(2)}) collective-permute-start(bf16[192,768]{1,0:T(8,128)(2,1)} %collective-permute-done.3.refs_1_), channel_id=1, source_target_pairs={{0,4},{1,5},{18,22},{19,23},{4,0},{5,1},{22,18},{23,19},{8,12},{9,... | collective-permute-start | bytes 884744 | tf_op jit(solution)/shard_map/ppermute | solution.py:1188
  34.5 20.9 %collective-permute-start.5 = (bf16[192,768]{1,0:T(8,128)(2,1)}, bf16[192,768]{1,0:T(8,128)(2,1)}, u32[]{:S(2)}, u32[]{:S(2)}) collective-permute-start(bf16[192,768]{1,0:T(8,128)(2,1)} %collective-permute-done.3.refs_1_), channel_id=1, source_target_pairs={{0,8},{1,9},{18,26},{19,27},{4,12},{5,13},{22,30},{23,31},{8,0},{9... | collective-permute-start | bytes 884744 | tf_op jit(solution)/shard_map/ppermute | solution.py:1188
  42.6 95.5 %all-gather.5.cloned.1.call-start = ((), (), s32[]{:S(2)}) async-start(), calls=%async_computation.1 | async-start | bytes 1474560 | tf_op jit(solution)/shard_map/all_gather | solution.py:1198
  42.6 14.5 %collective-permute-start.7 = (bf16[192,768]{1,0:T(8,128)(2,1)}, bf16[192,768]{1,0:T(8,128)(2,1)S(1)}, u32[]{:S(2)}, u32[]{:S(2)}) collective-permute-start(bf16[192,768]{1,0:T(8,128)(2,1)} %collective-permute-done.3.refs_1_), channel_id=1, source_target_pairs={{0,2},{1,3},{18,16},{19,17},{4,6},{5,7},{22,20},{23,21},{8,10},{9,... | collective-permute-start | bytes 884744 | tf_op jit(solution)/shard_map/ppermute | solution.py:1350
  49.6 15.0 %collective-permute-start.10 = (bf16[192,768]{1,0:T(8,128)(2,1)S(1)}, bf16[192,768]{1,0:T(8,128)(2,1)S(1)}, u32[]{:S(2)}, u32[]{:S(2)}) collective-permute-start(bf16[192,768]{1,0:T(8,128)(2,1)S(1)} %collective-permute-done.6.refs_4_), channel_id=1, source_target_pairs={{0,2},{1,3},{18,16},{19,17},{4,6},{5,7},{22,20},{23,21},{8,10},{9,... | collective-permute-start | bytes 884744 | tf_op jit(solution)/shard_map/ppermute | solution.py:1350
  55.4 9.3 %collective-permute-start.9 = (bf16[192,768]{1,0:T(8,128)(2,1)}, bf16[192,768]{1,0:T(8,128)(2,1)S(1)}, u32[]{:S(2)}, u32[]{:S(2)}) collective-permute-start(bf16[192,768]{1,0:T(8,128)(2,1)} %collective-permute-done.5.refs_3_), channel_id=1, source_target_pairs={{0,2},{1,3},{18,16},{19,17},{4,6},{5,7},{22,20},{23,21},{8,10},{9,... | collective-permute-start | bytes 884744 | tf_op jit(solution)/shard_map/ppermute | solution.py:1350
  57.1 8.8 %collective-permute-start.2 = (bf16[256,768]{1,0:T(8,128)(2,1)S(1)}, bf16[256,768]{1,0:T(8,128)(2,1)S(1)}, u32[]{:S(2)}, u32[]{:S(2)}) collective-permute-start(bf16[256,768]{1,0:T(8,128)(2,1)S(1)} %get-tuple-element.165.refs_0_.refs_2_), channel_id=1, source_target_pairs={{0,16},{16,0},{1,17},{17,1},{2,18},{18,2},{3,19},{19,3},{4,20},{20... | collective-permute-start | bytes 1179656 | tf_op jit(solution)/shard_map/ppermute | solution.py:148
  57.3 9.7 %collective-permute-start.14 = (f32[1,1920]{1,0:T(1,128)S(1)}, f32[1,1920]{1,0:T(1,128)S(1)}, u32[]{:S(2)}, u32[]{:S(2)}) collective-permute-start(f32[1,1920]{1,0:T(1,128)S(1)} %broadcast_select_fusion), channel_id=1, source_target_pairs={{0,16},{16,0},{1,17},{17,1},{2,18},{18,2},{3,19},{19,3},{4,20},{20... | collective-permute-start | bytes 23048 | tf_op jit(solution)/shard_map/ppermute | solution.py:148
  92.6 30.4 %collective-permute-start.21 = (bf16[768,1536]{1,0:T(8,128)(2,1)S(1)}, bf16[768,1536]{1,0:T(8,128)(2,1)}, u32[]{:S(2)}, u32[]{:S(2)}) collective-permute-start(bf16[768,1536]{1,0:T(8,128)(2,1)S(1)} %join.3.refs_1_), channel_id=1, source_target_pairs={{0,2},{1,3},{18,16},{19,17},{4,6},{5,7},{22,20},{23,21},{8,10},{9,... | collective-permute-start | bytes 7077896 | tf_op jit(solution)/shard_map/ppermute | solution.py:1202
  99.6 8.3 %collective-permute-start.17 = (bf16[272,768]{1,0:T(8,128)(2,1)}, bf16[272,768]{1,0:T(8,128)(2,1)S(1)}, u32[]{:S(2)}, u32[]{:S(2)}) collective-permute-start(bf16[272,768]{1,0:T(8,128)(2,1)} %copy-done.56), channel_id=1, source_target_pairs={{0,1},{1,0},{2,3},{3,2},{4,5},{5,4},{6,7},{7,6},{8,9},{9,8},{10,11... | collective-permute-start | bytes 1253384 | tf_op jit(solution)/shard_map/ppermute | solution.py:152
  100.3 8.7 %collective-permute-start.16 = (bf16[272,768]{1,0:T(8,128)(2,1)}, bf16[272,768]{1,0:T(8,128)(2,1)S(1)}, u32[]{:S(2)}, u32[]{:S(2)}) collective-permute-start(bf16[272,768]{1,0:T(8,128)(2,1)} %copy-done.80), channel_id=1, source_target_pairs={{0,16},{16,0},{1,17},{17,1},{2,18},{18,2},{3,19},{19,3},{4,20},{20... | collective-permute-start | bytes 1253384 | tf_op jit(solution)/shard_map/ppermute | solution.py:148
  114.4 12.1 %collective-permute-start.18 = (bf16[256,768]{1,0:T(8,128)(2,1)S(1)}, bf16[256,768]{1,0:T(8,128)(2,1)S(1)}, u32[]{:S(2)}, u32[]{:S(2)}) collective-permute-start(bf16[256,768]{1,0:T(8,128)(2,1)S(1)} %get-tuple-element.174.refs_0_.refs_3_), channel_id=1, source_target_pairs={{0,16},{16,0},{1,17},{17,1},{2,18},{18,2},{3,19},{19,3},{4,20},{20... | collective-permute-start | bytes 1179656 | tf_op jit(solution)/shard_map/ppermute | solution.py:148
  114.4 14.8 %collective-permute-start.23 = (bf16[256,768]{1,0:T(8,128)(2,1)S(1)}, bf16[256,768]{1,0:T(8,128)(2,1)S(1)}, u32[]{:S(2)}, u32[]{:S(2)}) collective-permute-start(bf16[256,768]{1,0:T(8,128)(2,1)S(1)} %get-tuple-element.174.refs_0_.refs_3_), channel_id=1, source_target_pairs={{0,1},{1,0},{2,3},{3,2},{4,5},{5,4},{6,7},{7,6},{8,9},{9,8},{10,11... | collective-permute-start | bytes 1179656 | tf_op jit(solution)/shard_map/ppermute | solution.py:152
  140.4 9.7 %collective-permute-start.27 = (bf16[768,768]{1,0:T(8,128)(2,1)S(1)}, bf16[768,768]{1,0:T(8,128)(2,1)S(1)}, u32[]{:S(2)}, u32[]{:S(2)}) collective-permute-start(bf16[768,768]{1,0:T(8,128)(2,1)S(1)} %hold.18.refs_1_), channel_id=1, source_target_pairs={{16,0},{17,1},{2,18},{3,19},{20,4},{21,5},{6,22},{7,23},{24,8},{25... | collective-permute-start | bytes 3538952 | tf_op jit(solution)/shard_map/ppermute | solution.py:1201
  143.3 19.7 %collective-permute-start.30 = (bf16[768,768]{1,0:T(8,128)(2,1)S(1)}, bf16[768,768]{1,0:T(8,128)(2,1)S(1)}, u32[]{:S(2)}, u32[]{:S(2)}) collective-permute-start(bf16[768,768]{1,0:T(8,128)(2,1)S(1)} %join.5.refs_1_), channel_id=1, source_target_pairs={{0,2},{1,3},{18,16},{19,17},{4,6},{5,7},{22,20},{23,21},{8,10},{9,... | collective-permute-start | bytes 3538952 | tf_op jit(solution)/shard_map/ppermute | solution.py:1202
  149.4 8.5 %collective-permute-start.26 = (bf16[272,768]{1,0:T(8,128)(2,1)S(1)}, bf16[272,768]{1,0:T(8,128)(2,1)S(1)}, u32[]{:S(2)}, u32[]{:S(2)}) collective-permute-start(bf16[272,768]{1,0:T(8,128)(2,1)S(1)} %copy-done.34), channel_id=1, source_target_pairs={{0,1},{1,0},{2,3},{3,2},{4,5},{5,4},{6,7},{7,6},{8,9},{9,8},{10,11... | collective-permute-start | bytes 1253384 | tf_op jit(solution)/shard_map/ppermute | solution.py:152
  150.1 7.8 %collective-permute-start.22 = (bf16[272,768]{1,0:T(8,128)(2,1)S(1)}, bf16[272,768]{1,0:T(8,128)(2,1)S(1)}, u32[]{:S(2)}, u32[]{:S(2)}) collective-permute-start(bf16[272,768]{1,0:T(8,128)(2,1)S(1)} %copy-done.79), channel_id=1, source_target_pairs={{0,16},{16,0},{1,17},{17,1},{2,18},{18,2},{3,19},{19,3},{4,20},{20... | collective-permute-start | bytes 1253384 | tf_op jit(solution)/shard_map/ppermute | solution.py:148
  158.9 11.5 %collective-permute-start.31 = (bf16[256,768]{1,0:T(8,128)(2,1)S(1)}, bf16[256,768]{1,0:T(8,128)(2,1)S(1)}, u32[]{:S(2)}, u32[]{:S(2)}) collective-permute-start(bf16[256,768]{1,0:T(8,128)(2,1)S(1)} %get-tuple-element.184.refs_0_.refs_2_), channel_id=1, source_target_pairs={{0,1},{1,0},{2,3},{3,2},{4,5},{5,4},{6,7},{7,6},{8,9},{9,8},{10,11... | collective-permute-start | bytes 1179656 | tf_op jit(solution)/shard_map/ppermute | solution.py:152
  170.5 30.7 %collective-permute-start.38 = (bf16[768,1536]{1,0:T(8,128)(2,1)S(1)}, bf16[768,1536]{1,0:T(8,128)(2,1)S(1)}, u32[]{:S(2)}, u32[]{:S(2)}) collective-permute-start(bf16[768,1536]{1,0:T(8,128)(2,1)S(1)} %join.4.refs_1_.refs_2_), channel_id=1, source_target_pairs={{0,2},{1,3},{18,16},{19,17},{4,6},{5,7},{22,20},{23,21},{8,10},{9,... | collective-permute-start | bytes 7077896 | tf_op jit(solution)/shard_map/ppermute | solution.py:1202
  182.3 11.7 %collective-permute-start.35 = (bf16[272,768]{1,0:T(8,128)(2,1)S(1)}, bf16[272,768]{1,0:T(8,128)(2,1)S(1)}, u32[]{:S(2)}, u32[]{:S(2)}) collective-permute-start(bf16[272,768]{1,0:T(8,128)(2,1)S(1)} %pair_sum.10.refs_7_), channel_id=1, source_target_pairs={{0,1},{1,0},{2,3},{3,2},{4,5},{5,4},{6,7},{7,6},{8,9},{9,8},{10,11... | collective-permute-start | bytes 1253384 | tf_op jit(solution)/shard_map/ppermute | solution.py:152
  187.5 14.5 %collective-permute-start.37 = (bf16[256,768]{1,0:T(8,128)(2,1)S(1)}, bf16[256,768]{1,0:T(8,128)(2,1)S(1)}, u32[]{:S(2)}, u32[]{:S(2)}) collective-permute-start(bf16[256,768]{1,0:T(8,128)(2,1)S(1)} %copy-done.18), channel_id=1, source_target_pairs={{0,16},{16,0},{1,17},{17,1},{2,18},{18,2},{3,19},{19,3},{4,20},{20... | collective-permute-start | bytes 1179656 | tf_op jit(solution)/shard_map/ppermute | solution.py:148
  194.9 11.5 %collective-permute-start.40 = (bf16[256,768]{1,0:T(8,128)(2,1)S(1)}, bf16[256,768]{1,0:T(8,128)(2,1)S(1)}, u32[]{:S(2)}, u32[]{:S(2)}) collective-permute-start(bf16[256,768]{1,0:T(8,128)(2,1)S(1)} %get-tuple-element.191.refs_0_), channel_id=1, source_target_pairs={{0,1},{1,0},{2,3},{3,2},{4,5},{5,4},{6,7},{7,6},{8,9},{9,8},{10,11... | collective-permute-start | bytes 1179656 | tf_op jit(solution)/shard_map/ppermute | solution.py:152
  195.7 10.8 %collective-permute-start.42 = (bf16[256,768]{1,0:T(8,128)(2,1)S(1)}, bf16[256,768]{1,0:T(8,128)(2,1)S(1)}, u32[]{:S(2)}, u32[]{:S(2)}) collective-permute-start(bf16[256,768]{1,0:T(8,128)(2,1)S(1)} %copy-done.10), channel_id=1, source_target_pairs={{0,16},{16,0},{1,17},{17,1},{2,18},{18,2},{3,19},{19,3},{4,20},{20... | collective-permute-start | bytes 1179656 | tf_op jit(solution)/shard_map/ppermute | solution.py:148
  220.4 11.2 %collective-permute-start.49 = (bf16[256,768]{1,0:T(8,128)(2,1)S(1)}, bf16[256,768]{1,0:T(8,128)(2,1)S(1)}, u32[]{:S(2)}, u32[]{:S(2)}) collective-permute-start(bf16[256,768]{1,0:T(8,128)(2,1)S(1)} %pair_sum.12.refs_7_), channel_id=1, source_target_pairs={{0,1},{1,0},{2,3},{3,2},{4,5},{5,4},{6,7},{7,6},{8,9},{9,8},{10,11... | collective-permute-start | bytes 1179656 | tf_op jit(solution)/shard_map/ppermute | solution.py:152
  223.6 8.0 %collective-permute-start.48 = (bf16[256,768]{1,0:T(8,128)(2,1)S(1)}, bf16[256,768]{1,0:T(8,128)(2,1)S(1)}, u32[]{:S(2)}, u32[]{:S(2)}) collective-permute-start(bf16[256,768]{1,0:T(8,128)(2,1)S(1)} %get-tuple-element.205), channel_id=1, source_target_pairs={{0,16},{16,0},{1,17},{17,1},{2,18},{18,2},{3,19},{19,3},{4,20},{20... | collective-permute-start | bytes 1179656 | tf_op jit(solution)/shard_map/ppermute | solution.py:148
  232.8 12.1 %collective-permute-start.51 = (bf16[272,768]{1,0:T(8,128)(2,1)S(1)}, bf16[272,768]{1,0:T(8,128)(2,1)S(1)}, u32[]{:S(2)}, u32[]{:S(2)}) collective-permute-start(bf16[272,768]{1,0:T(8,128)(2,1)S(1)} %get-tuple-element.210.refs_0_.refs_12_.refs_6_), channel_id=1, source_target_pairs={{0,1},{1,0},{2,3},{3,2},{4,5},{5,4},{6,7},{7,6},{8,9},{9,8},{10,11... | collective-permute-start | bytes 1253384 | tf_op jit(solution)/shard_map/ppermute | solution.py:152
  233.7 11.3 %collective-permute-start.43 = (bf16[272,768]{1,0:T(8,128)(2,1)S(1)}, bf16[272,768]{1,0:T(8,128)(2,1)S(1)}, u32[]{:S(2)}, u32[]{:S(2)}) collective-permute-start(bf16[272,768]{1,0:T(8,128)(2,1)S(1)} %get-tuple-element.198), channel_id=1, source_target_pairs={{0,16},{16,0},{1,17},{17,1},{2,18},{18,2},{3,19},{19,3},{4,20},{20... | collective-permute-start | bytes 1253384 | tf_op jit(solution)/shard_map/ppermute | solution.py:148
  245.2 15.9 %collective-permute-start.44 = (bf16[272,768]{1,0:T(8,128)(2,1)S(1)}, bf16[272,768]{1,0:T(8,128)(2,1)S(1)}, u32[]{:S(2)}, u32[]{:S(2)}) collective-permute-start(bf16[272,768]{1,0:T(8,128)(2,1)S(1)} %pair_sum.11.refs_7_), channel_id=1, source_target_pairs={{0,1},{1,0},{2,3},{3,2},{4,5},{5,4},{6,7},{7,6},{8,9},{9,8},{10,11... | collective-permute-start | bytes 1253384 | tf_op jit(solution)/shard_map/ppermute | solution.py:152
  246.0 33.4 %collective-permute-start.64 = (bf16[768,1536]{1,0:T(8,128)(2,1)S(1)}, bf16[768,1536]{1,0:T(8,128)(2,1)S(1)}, u32[]{:S(2)}, u32[]{:S(2)}) collective-permute-start(bf16[768,1536]{1,0:T(8,128)(2,1)S(1)} %grads.4.refs_2_.refs_1_), channel_id=1, source_target_pairs={{2,0},{3,1},{16,18},{17,19},{6,4},{7,5},{20,22},{21,23},{10,8},{11... | collective-permute-start | bytes 7077896 | tf_op jit(solution)/shard_map/ppermute | solution.py:1306
  265.3 11.5 %collective-permute-start.55 = (bf16[256,768]{1,0:T(8,128)(2,1)S(1)}, bf16[256,768]{1,0:T(8,128)(2,1)S(1)}, u32[]{:S(2)}, u32[]{:S(2)}) collective-permute-start(bf16[256,768]{1,0:T(8,128)(2,1)S(1)} %pair_sum.13.refs_6_.refs_12_), channel_id=1, source_target_pairs={{0,1},{1,0},{2,3},{3,2},{4,5},{5,4},{6,7},{7,6},{8,9},{9,8},{10,11... | collective-permute-start | bytes 1179656 | tf_op jit(solution)/shard_map/ppermute | solution.py:152
  267.5 9.3 %collective-permute-start.54 = (bf16[256,768]{1,0:T(8,128)(2,1)S(1)}, bf16[256,768]{1,0:T(8,128)(2,1)S(1)}, u32[]{:S(2)}, u32[]{:S(2)}) collective-permute-start(bf16[256,768]{1,0:T(8,128)(2,1)S(1)} %get-tuple-element.226), channel_id=1, source_target_pairs={{0,16},{16,0},{1,17},{17,1},{2,18},{18,2},{3,19},{19,3},{4,20},{20... | collective-permute-start | bytes 1179656 | tf_op jit(solution)/shard_map/ppermute | solution.py:148
  269.5 19.8 %collective-permute-start.62 = (bf16[768,768]{1,0:T(8,128)(2,1)S(1)}, bf16[768,768]{1,0:T(8,128)(2,1)S(1)}, u32[]{:S(2)}, u32[]{:S(2)}) collective-permute-start(bf16[768,768]{1,0:T(8,128)(2,1)S(1)} %grads.5.refs_2_.refs_10_.refs_1_), channel_id=1, source_target_pairs={{2,0},{3,1},{16,18},{17,19},{6,4},{7,5},{20,22},{21,23},{10,8},{11... | collective-permute-start | bytes 3538952 | tf_op jit(solution)/shard_map/ppermute | solution.py:1306
  277.9 24.1 %collective-permute-start.56 = (bf16[768,768]{1,0:T(8,128)(2,1)S(1)}, bf16[768,768]{1,0:T(8,128)(2,1)S(1)}, u32[]{:S(2)}, u32[]{:S(2)}) collective-permute-start(bf16[768,768]{1,0:T(8,128)(2,1)S(1)} %pack.1.refs_1_.refs_6_.refs_2_), channel_id=1, source_target_pairs={{2,0},{3,1},{16,18},{17,19},{6,4},{7,5},{20,22},{21,23},{10,8},{11... | collective-permute-start | bytes 3538952 | tf_op jit(solution)/shard_map/ppermute | solution.py:1443
  280.5 22.9 %collective-permute-start.65 = (bf16[384,1536]{1,0:T(8,128)(2,1)S(1)}, bf16[384,1536]{1,0:T(8,128)(2,1)S(1)}, u32[]{:S(2)}, u32[]{:S(2)}) collective-permute-start(bf16[384,1536]{1,0:T(8,128)(2,1)S(1)} %get-tuple-element.242), channel_id=1, source_target_pairs={{0,4},{1,5},{18,22},{19,23},{4,0},{5,1},{22,18},{23,19},{8,12},{9,... | collective-permute-start | bytes 3538952 | tf_op jit(solution)/shard_map/ppermute | solution.py:1188
  282.9 12.1 %collective-permute-start.61 = (bf16[272,768]{1,0:T(8,128)(2,1)S(1)}, bf16[272,768]{1,0:T(8,128)(2,1)S(1)}, u32[]{:S(2)}, u32[]{:S(2)}) collective-permute-start(bf16[272,768]{1,0:T(8,128)(2,1)S(1)} %get-tuple-element.235.refs_0_.refs_6_), channel_id=1, source_target_pairs={{0,1},{1,0},{2,3},{3,2},{4,5},{5,4},{6,7},{7,6},{8,9},{9,8},{10,11... | collective-permute-start | bytes 1253384 | tf_op jit(solution)/shard_map/ppermute | solution.py:152
  295.0 8.7 %collective-permute-start.63 = (bf16[272,768]{1,0:T(8,128)(2,1)S(1)}, bf16[272,768]{1,0:T(8,128)(2,1)S(1)}, u32[]{:S(2)}, u32[]{:S(2)}) collective-permute-start(bf16[272,768]{1,0:T(8,128)(2,1)S(1)} %hold.27.refs_0_.refs_8_), channel_id=1, source_target_pairs={{0,16},{16,0},{1,17},{17,1},{2,18},{18,2},{3,19},{19,3},{4,20},{20... | collective-permute-start | bytes 1253384 | tf_op jit(solution)/shard_map/ppermute | solution.py:148
  295.1 17.4 %collective-permute-start.57 = (bf16[768,768]{1,0:T(8,128)(2,1)S(1)}, bf16[768,768]{1,0:T(8,128)(2,1)S(1)}, u32[]{:S(2)}, u32[]{:S(2)}) collective-permute-start(bf16[768,768]{1,0:T(8,128)(2,1)S(1)} %pack.1.refs_1_.refs_6_.refs_2_), channel_id=1, source_target_pairs={{0,16},{1,17},{18,2},{19,3},{4,20},{5,21},{22,6},{23,7},{8,24},{9,... | collective-permute-start | bytes 3538952 | tf_op jit(solution)/shard_map/ppermute | solution.py:1479
  302.0 10.5 %collective-permute-start.58 = (bf16[768,768]{1,0:T(8,128)(2,1)S(1)}, bf16[768,768]{1,0:T(8,128)(2,1)S(1)}, u32[]{:S(2)}, u32[]{:S(2)}) collective-permute-start(bf16[768,768]{1,0:T(8,128)(2,1)S(1)} %collective-permute-done.56.refs_2_.refs_6_), channel_id=1, source_target_pairs={{0,16},{1,17},{18,2},{19,3},{4,20},{5,21},{22,6},{23,7},{8,24},{9,... | collective-permute-start | bytes 3538952 | tf_op jit(solution)/shard_map/ppermute | solution.py:1479
  309.1 11.2 %collective-permute-start.67 = (bf16[256,768]{1,0:T(8,128)(2,1)S(1)}, bf16[256,768]{1,0:T(8,128)(2,1)S(1)}, u32[]{:S(2)}, u32[]{:S(2)}) collective-permute-start(bf16[256,768]{1,0:T(8,128)(2,1)S(1)} %pair_sum.14), channel_id=1, source_target_pairs={{0,1},{1,0},{2,3},{3,2},{4,5},{5,4},{6,7},{7,6},{8,9},{9,8},{10,11... | collective-permute-start | bytes 1179656 | tf_op jit(solution)/shard_map/ppermute | solution.py:152
  310.4 19.7 %collective-permute-start.71 = (bf16[192,1536]{1,0:T(8,128)(2,1)S(1)}, bf16[192,1536]{1,0:T(8,128)(2,1)S(1)}, u32[]{:S(2)}, u32[]{:S(2)}) collective-permute-start(bf16[192,1536]{1,0:T(8,128)(2,1)S(1)} %get-tuple-element.259), channel_id=1, source_target_pairs={{0,8},{1,9},{18,26},{19,27},{4,12},{5,13},{22,30},{23,31},{8,0},{9... | collective-permute-start | bytes 1769480 | tf_op jit(solution)/shard_map/ppermute | solution.py:1188
  322.6 9.8 %collective-permute-start.68 = (bf16[272,768]{1,0:T(8,128)(2,1)S(1)}, bf16[272,768]{1,0:T(8,128)(2,1)S(1)}, u32[]{:S(2)}, u32[]{:S(2)}) collective-permute-start(bf16[272,768]{1,0:T(8,128)(2,1)S(1)} %get-tuple-element.249.refs_0_.refs_12_.refs_6_), channel_id=1, source_target_pairs={{0,16},{16,0},{1,17},{17,1},{2,18},{18,2},{3,19},{19,3},{4,20},{20... | collective-permute-start | bytes 1253384 | tf_op jit(solution)/shard_map/ppermute | solution.py:148
  322.6 12.1 %collective-permute-start.69 = (bf16[272,768]{1,0:T(8,128)(2,1)S(1)}, bf16[272,768]{1,0:T(8,128)(2,1)S(1)}, u32[]{:S(2)}, u32[]{:S(2)}) collective-permute-start(bf16[272,768]{1,0:T(8,128)(2,1)S(1)} %get-tuple-element.249.refs_0_.refs_12_.refs_6_), channel_id=1, source_target_pairs={{0,1},{1,0},{2,3},{3,2},{4,5},{5,4},{6,7},{7,6},{8,9},{9,8},{10,11... | collective-permute-start | bytes 1253384 | tf_op jit(solution)/shard_map/ppermute | solution.py:152
  326.8 33.8 %collective-permute-start.79 = (bf16[768,1536]{1,0:T(8,128)(2,1)S(1)}, bf16[768,1536]{1,0:T(8,128)(2,1)S(1)}, u32[]{:S(2)}, u32[]{:S(2)}) collective-permute-start(bf16[768,1536]{1,0:T(8,128)(2,1)S(1)} %grads.6.refs_2_.refs_1_), channel_id=1, source_target_pairs={{2,0},{3,1},{16,18},{17,19},{6,4},{7,5},{20,22},{21,23},{10,8},{11... | collective-permute-start | bytes 7077896 | tf_op jit(solution)/shard_map/ppermute | solution.py:1306
  328.2 11.8 %collective-permute-start.73 = (bf16[384,768]{1,0:T(8,128)(2,1)S(1)}, bf16[384,768]{1,0:T(8,128)(2,1)S(1)}, u32[]{:S(2)}, u32[]{:S(2)}) collective-permute-start(bf16[384,768]{1,0:T(8,128)(2,1)S(1)} %get-tuple-element.261), channel_id=1, source_target_pairs={{0,4},{1,5},{18,22},{19,23},{4,0},{5,1},{22,18},{23,19},{8,12},{9,... | collective-permute-start | bytes 1769480 | tf_op jit(solution)/shard_map/ppermute | solution.py:1188
  330.3 10.6 %collective-permute-start.72 = (bf16[192,1536]{1,0:T(8,128)(2,1)S(1)}, bf16[192,1536]{1,0:T(8,128)(2,1)S(1)}, u32[]{:S(2)}, u32[]{:S(2)}) collective-permute-start(bf16[192,1536]{1,0:T(8,128)(2,1)S(1)} %total.5), channel_id=1, source_target_pairs={{0,16},{1,17},{18,18},{19,19},{4,20},{5,21},{22,22},{23,23},{8,24}... | collective-permute-start | bytes 1769480 | tf_op jit(solution)/shard_map/ppermute | solution.py:1326
  361.7 21.3 %collective-permute-start.80 = (bf16[384,1536]{1,0:T(8,128)(2,1)S(1)}, bf16[384,1536]{1,0:T(8,128)(2,1)S(1)}, u32[]{:S(2)}, u32[]{:S(2)}) collective-permute-start(bf16[384,1536]{1,0:T(8,128)(2,1)S(1)} %get-tuple-element.286), channel_id=1, source_target_pairs={{0,4},{1,5},{18,22},{19,23},{4,0},{5,1},{22,18},{23,19},{8,12},{9,... | collective-permute-start | bytes 3538952 | tf_op jit(solution)/shard_map/ppermute | solution.py:1188
  363.6 21.7 %collective-permute-start.83 = (bf16[768,768]{1,0:T(8,128)(2,1)S(1)}, bf16[768,768]{1,0:T(8,128)(2,1)S(1)}, u32[]{:S(2)}, u32[]{:S(2)}) collective-permute-start(bf16[768,768]{1,0:T(8,128)(2,1)S(1)} %grads.7.refs_2_.refs_3_.refs_11_.refs_1_), channel_id=1, source_target_pairs={{2,0},{3,1},{16,18},{17,19},{6,4},{7,5},{20,22},{21,23},{10,8},{11... | collective-permute-start | bytes 3538952 | tf_op jit(solution)/shard_map/ppermute | solution.py:1306
  364.9 15.6 %collective-permute-start.77 = (bf16[192,768]{1,0:T(8,128)(2,1)S(1)}, bf16[192,768]{1,0:T(8,128)(2,1)S(1)}, u32[]{:S(2)}, u32[]{:S(2)}) collective-permute-start(bf16[192,768]{1,0:T(8,128)(2,1)S(1)} %get-tuple-element.284), channel_id=1, source_target_pairs={{0,8},{1,9},{18,26},{19,27},{4,12},{5,13},{22,30},{23,31},{8,0},{9... | collective-permute-start | bytes 884744 | tf_op jit(solution)/shard_map/ppermute | solution.py:1188
  368.2 13.7 %collective-permute-start.76 = (bf16[288,768]{1,0:T(8,128)(2,1)S(1)}, bf16[288,768]{1,0:T(8,128)(2,1)S(1)}, u32[]{:S(2)}, u32[]{:S(2)}) collective-permute-start(bf16[288,768]{1,0:T(8,128)(2,1)S(1)} %pair_sum.15.refs_12_.refs_6_), channel_id=1, source_target_pairs={{0,1},{1,0},{2,3},{3,2},{4,5},{5,4},{6,7},{7,6},{8,9},{9,8},{10,11... | collective-permute-start | bytes 1327112 | tf_op jit(solution)/shard_map/ppermute | solution.py:152
  369.1 14.1 %collective-permute-start.74 = (bf16[256,768]{1,0:T(8,128)(2,1)S(1)}, bf16[256,768]{1,0:T(8,128)(2,1)S(1)}, u32[]{:S(2)}, u32[]{:S(2)}) collective-permute-start(bf16[256,768]{1,0:T(8,128)(2,1)S(1)} %get-tuple-element.264), channel_id=1, source_target_pairs={{0,16},{16,0},{1,17},{17,1},{2,18},{18,2},{3,19},{19,3},{4,20},{20... | collective-permute-start | bytes 1179656 | tf_op jit(solution)/shard_map/ppermute | solution.py:148
  386.1 17.5 %collective-permute-start.84 = (bf16[384,768]{1,0:T(8,128)(2,1)S(1)}, bf16[384,768]{1,0:T(8,128)(2,1)S(1)}, u32[]{:S(2)}, u32[]{:S(2)}) collective-permute-start(bf16[384,768]{1,0:T(8,128)(2,1)S(1)} %get-tuple-element.292), channel_id=1, source_target_pairs={{0,4},{1,5},{18,22},{19,23},{4,0},{5,1},{22,18},{23,19},{8,12},{9,... | collective-permute-start | bytes 1769480 | tf_op jit(solution)/shard_map/ppermute | solution.py:1188
  389.4 20.0 %collective-permute-start.90 = (bf16[192,1536]{1,0:T(8,128)(2,1)S(1)}, bf16[192,1536]{1,0:T(8,128)(2,1)S(1)}, u32[]{:S(2)}, u32[]{:S(2)}) collective-permute-start(bf16[192,1536]{1,0:T(8,128)(2,1)S(1)} %get-tuple-element.303), channel_id=1, source_target_pairs={{0,8},{1,9},{18,26},{19,27},{4,12},{5,13},{22,30},{23,31},{8,0},{9... | collective-permute-start | bytes 1769480 | tf_op jit(solution)/shard_map/ppermute | solution.py:1188
  403.8 15.0 %collective-permute-start.87 = (bf16[240,768]{1,0:T(8,128)(2,1)S(1)}, bf16[240,768]{1,0:T(8,128)(2,1)S(1)}, u32[]{:S(2)}, u32[]{:S(2)}) collective-permute-start(bf16[240,768]{1,0:T(8,128)(2,1)S(1)} %get-tuple-element.294), channel_id=1, source_target_pairs={{0,8},{1,9},{18,26},{19,27},{4,12},{5,13},{22,30},{23,31},{8,0},{9... | collective-permute-start | bytes 1105928 | tf_op jit(solution)/shard_map/ppermute | solution.py:1188
  409.5 16.7 %collective-permute-start.91 = (bf16[192,1536]{1,0:T(8,128)(2,1)S(1)}, bf16[192,1536]{1,0:T(8,128)(2,1)}, u32[]{:S(2)}, u32[]{:S(2)}) collective-permute-start(bf16[192,1536]{1,0:T(8,128)(2,1)S(1)} %total.9), channel_id=1, source_target_pairs={{0,0},{1,1},{18,2},{19,3},{4,4},{5,5},{22,6},{23,7},{8,8},{9,9},{2... | collective-permute-start | bytes 1769480 | tf_op jit(solution)/shard_map/ppermute | solution.py:1326
  411.0 13.7 %collective-permute-start.81 = (bf16[256,768]{1,0:T(8,128)(2,1)}, bf16[256,768]{1,0:T(8,128)(2,1)S(1)}, u32[]{:S(2)}, u32[]{:S(2)}) collective-permute-start(bf16[256,768]{1,0:T(8,128)(2,1)} %get-tuple-element.288), channel_id=1, source_target_pairs={{0,0},{1,1},{16,2},{17,3},{4,4},{5,5},{20,6},{21,7},{8,8},{9,9},{2... | collective-permute-start | bytes 1179656 | tf_op jit(solution)/shard_map/ppermute | solution.py:1160
  412.7 12.0 %collective-permute-start.82 = (bf16[256,768]{1,0:T(8,128)(2,1)}, bf16[256,768]{1,0:T(8,128)(2,1)S(1)}, u32[]{:S(2)}, u32[]{:S(2)}) collective-permute-start(bf16[256,768]{1,0:T(8,128)(2,1)} %get-tuple-element.288), channel_id=1, source_target_pairs={{2,0},{3,1},{18,2},{19,3},{6,4},{7,5},{22,6},{23,7},{10,8},{11,9},... | collective-permute-start | bytes 1179656 | tf_op jit(solution)/shard_map/ppermute | solution.py:1160
  419.6 9.8 %collective-permute-start.88 = (bf16[192,768]{1,0:T(8,128)(2,1)}, bf16[192,768]{1,0:T(8,128)(2,1)}, u32[]{:S(2)}, u32[]{:S(2)}) collective-permute-start(bf16[192,768]{1,0:T(8,128)(2,1)} %get-tuple-element.296), channel_id=1, source_target_pairs={{0,0},{1,1},{18,2},{19,3},{4,4},{5,5},{22,6},{23,7},{8,8},{9,9},{2... | collective-permute-start | bytes 884744 | tf_op jit(solution)/shard_map/ppermute | solution.py:1517
  (128 other events, 853.2 us)
Sparse Core Ops, SparseCore 0:
  42.7 38.3 all-gather.2
  99.7 27.3 all-gather.4
